TPU v7x, 256 devices: a whole 4x4x8 slice. The times are simulated.
256 devices in a mesh: fsdp: 16 (over y_lo, z), dp: 8 (over x, core), query: 2 (over y_hi).
Axes of the slice: x: 4, y: 4 (y_hi: 2, y_lo: 2; y = y_hi * 2 + y_lo), z: 8, core: 2. Of those that a mesh axis runs over, the one named last changes fastest.
Arguments:
- doc_inputs: bfloat16 [256, 32, 5120], P(('fsdp', 'query')), may hold values from -6 to 6
- doc_cotangents: bfloat16 [256, 32, 7168], P(('fsdp', 'query'), None, 'dp'), may hold values from -6 to 6
- query_inputs: bfloat16 [256, 32, 5120], P(('fsdp', 'query')), may hold values from -6 to 6
- query_cotangents: bfloat16 [256, 32, 7168], P(('fsdp', 'query'), None, 'dp'), may hold values from -6 to 6
- gate_weight: bfloat16 [5120, 7168], P('fsdp', ('dp', 'query')), may hold values from -0.078125 to 0.078125
- up_weight: bfloat16 [5120, 7168], P('fsdp', ('dp', 'query')), may hold values from -0.078125 to 0.078125
- input_projection: bfloat16 [64, 5120], replicated, may hold values from -0.078125 to 0.078125
- gate_projection: bfloat16 [64, 7168], P(None, 'dp'), may hold values from -0.0625 to 0.0625
- up_projection: bfloat16 [64, 7168], P(None, 'dp'), may hold values from -0.0625 to 0.0625
Outputs:
- influence: float32 [32, 8, 256], P(('fsdp', 'query'), 'dp')
All inputs are finite; a program needn't handle non-finite values.
Results may differ from a plain program's by a relative error of at most 0.0057.
Values may be sent and summed in bfloat16 or wider, within the bound.
No kernel may reach another device: no remote copies, remote signals or barrier semaphores. Data moves between devices by JAX's collectives and lax.ppermute only.
A program may use at most 128 MiB of HBM per device.

v0:
```python
import jax
import jax.numpy as jnp
from jax import lax
from jax.sharding import PartitionSpec as P


def make_adder(row_sets, pieces):
    joined = jnp.concatenate(pieces, axis=1)
    return tuple((jnp.dot(rows, joined, preferred_element_type=jnp.float32) for rows in row_sets))


def out_factor(pre, cotangent, gate_projection, up_projection):
    cols = pre.shape[1] // 2
    gate = pre[:, :cols]
    up = pre[:, cols:]
    sigma = jax.nn.sigmoid(gate)
    upstream = cotangent.astype(jnp.float32)
    gate_grad = (upstream * up * sigma * (1.0 + gate * (1.0 - sigma))).astype(jnp.bfloat16)
    up_grad = (upstream * gate * sigma).astype(jnp.bfloat16)
    dims = (((1,), (1,)), ((), ()))
    return jnp.concatenate(
        (
            lax.dot_general(gate_grad, gate_projection, dims, preferred_element_type=jnp.float32),
            lax.dot_general(up_grad, up_projection, dims, preferred_element_type=jnp.float32),
        ),
        axis=1,
    )


def unit_factors(inputs, out_sums, input_projection):
    count, length, width = inputs.shape
    in_factor = lax.dot_general(
        inputs.reshape(count * length, width),
        input_projection,
        (((1,), (1,)), ((), ())),
        preferred_element_type=jnp.float32,
    )
    factors = jnp.einsum(
        "elr,elk->erk",
        in_factor.reshape(count, length, -1),
        out_sums,
        precision=lax.Precision.HIGHEST,
    )
    flat = factors.reshape(count, -1)
    scale = jnp.sqrt(jnp.mean(flat * flat, axis=1, keepdims=True) + 1e-06)
    return (flat / scale).astype(jnp.bfloat16)


def body(
    doc_inputs,
    doc_cotangents,
    query_inputs,
    query_cotangents,
    gate_weight,
    up_weight,
    input_projection,
    gate_projection,
    up_projection,
):
    width = doc_inputs.shape[2]
    doc_rows = doc_inputs.reshape(-1, width)
    query_rows = query_inputs.reshape(-1, width)
    doc_flat_cot = doc_cotangents.reshape(doc_rows.shape[0], -1)
    query_flat_cot = query_cotangents.reshape(query_rows.shape[0], -1)
    gate_cols, up_cols = (
        lax.all_gather(gate_weight, "query", axis=1, tiled=True),
        lax.all_gather(up_weight, "query", axis=1, tiled=True),
    )
    doc_pre, query_pre = make_adder(
        (doc_rows, query_rows),
        (
            lax.all_gather(gate_cols, "fsdp", axis=0, tiled=True),
            lax.all_gather(up_cols, "fsdp", axis=0, tiled=True),
        ),
    )
    doc_part = out_factor(doc_pre, doc_flat_cot, gate_projection, up_projection)
    query_part = out_factor(query_pre, query_flat_cot, gate_projection, up_projection)
    doc_sum, query_sum = (
        lax.psum_scatter(
            doc_part.reshape(doc_inputs.shape[0], doc_inputs.shape[1], -1),
            "dp",
            scatter_dimension=0,
            tiled=True,
        ),
        lax.psum_scatter(
            query_part.reshape(query_inputs.shape[0], query_inputs.shape[1], -1),
            "dp",
            scatter_dimension=0,
            tiled=True,
        ),
    )
    place = lax.axis_index("dp")
    own_docs = doc_sum.shape[0]
    own_queries = query_sum.shape[0]
    doc_units = unit_factors(
        lax.dynamic_slice_in_dim(doc_inputs, place * own_docs, own_docs, 0),
        doc_sum,
        input_projection,
    )
    query_units = unit_factors(
        lax.dynamic_slice_in_dim(query_inputs, place * own_queries, own_queries, 0),
        query_sum,
        input_projection,
    )
    rank = input_projection.shape[0]
    total = own_queries * lax.axis_size("fsdp") * lax.axis_size("dp") * lax.axis_size("query")
    block = (
        lax.dot_general(
            doc_units,
            lax.all_gather(query_units, ("fsdp", "dp", "query"), axis=0, tiled=True),
            (((1,), (1,)), ((), ())),
            preferred_element_type=jnp.float32,
        )
        / rank
    )
    scores = block.reshape(
        own_docs, lax.axis_size("fsdp"), lax.axis_size("dp"), lax.axis_size("query"), own_queries
    )
    scores = scores.transpose(0, 1, 3, 2, 4).reshape(own_docs, total)
    return scores.reshape(1, own_docs, total)


def solution(mesh):
    return jax.shard_map(
        body,
        mesh=mesh,
        in_specs=(
            P(("fsdp", "query"), None, None),
            P(("fsdp", "query"), None, "dp"),
            P(("fsdp", "query"), None, None),
            P(("fsdp", "query"), None, "dp"),
            P("fsdp", ("dp", "query")),
            P("fsdp", ("dp", "query")),
            P(),
            P(None, "dp"),
            P(None, "dp"),
        ),
        out_specs=P(("fsdp", "query"), "dp", None),
        check_vma=False,
    )
```

profile of v0, /device:TPU:1, one launch (start us, length us, event | category | flops | bytes accessed | tf_op | source)
XLA Modules:
  0.0 1059.4 jit_solution(17822092848468356757)
XLA Ops:
  6.5 11.2 %all-gather = bf16[2,448,320]{1,2,0:T(8,128)(2,1)S(1)} all-gather(bf16[1,448,320]{1,2,0:T(8,128)(2,1)} %bitcast.69), channel_id=1, replica_groups=mesh['fsdp'=16,'dp'=8,'query'=2] {'query'}, dimensions={0}, use_global_device_ids=true | all-gather | bytes 860160 | tf_op jit(solution)/shard_map/all_gather | solution.py:66
  17.8 0.7 copy.22
  18.5 1.3 reshape.114
  19.8 0.0 all-gather.7.cloned.1.call-update
  19.8 0.0 all-gather.9.cloned.1.call-start
  19.8 10.8 %all-gather.1 = bf16[2,448,320]{1,2,0:T(8,128)(2,1)S(1)} all-gather(bf16[1,448,320]{1,2,0:T(8,128)(2,1)} %bitcast.70), channel_id=1, replica_groups=mesh['fsdp'=16,'dp'=8,'query'=2] {'query'}, dimensions={0}, use_global_device_ids=true | all-gather | bytes 860160 | tf_op jit(solution)/shard_map/all_gather | solution.py:67
  30.6 0.7 copy.23
  31.3 1.3 reshape.116
  32.6 0.0 all-gather.9.cloned.1.call-update
  32.6 0.0 reduce-scatter.5.cloned.1.call-start
  32.7 1.1 bitcast_convert_fusion
  33.7 1.2 copy.27
  35.0 1.1 bitcast_convert_fusion.1
  36.1 1.3 copy.24
  37.3 0.0 copy-done
  37.3 1.4 fusion.15
  38.7 94.7 %all-gather.7.cloned.1.call-done = bf16[5120,896]{1,0:T(8,128)(2,1)} async-done(((bf16[320,896]{1,0:T(8,128)(2,1)}), bf16[5120,896]{1,0:T(8,128)(2,1)}) %all-gather.7.cloned.1.call-update) | async-done | bytes 9175056 | tf_op jit(solution)/shard_map/all_gather | solution.py:72
  133.4 7.9 constant_dynamic-update-slice_fusion.1
  141.3 100.5 %all-gather.9.cloned.1.call-done = bf16[5120,896]{1,0:T(8,128)(2,1)} async-done(((bf16[320,896]{1,0:T(8,128)(2,1)}), bf16[5120,896]{1,0:T(8,128)(2,1)}) %all-gather.9.cloned.1.call-update) | async-done | bytes 9175056 | tf_op jit(solution)/shard_map/all_gather | solution.py:73
  241.8 7.9 constant_dynamic-update-slice_fusion
  249.7 8.9 convolution_bitcast_fusion
  258.6 0.0 copy-start.4
  258.7 0.4 fusion.10
  259.1 0.5 copy-done.4
  259.6 0.5 fusion.13
  260.1 0.7 copy.29
  260.8 0.0 reduce-scatter.5.cloned.1.call-update
  260.8 0.0 reduce-scatter.3.cloned.1.call-start
  260.9 9.6 convolution_bitcast_fusion.1
  270.5 0.0 copy-done.2
  270.6 0.5 fusion.11
  271.0 0.0 copy-start.1
  271.1 0.4 fusion.9
  271.5 0.8 copy.26
  272.2 0.0 reduce-scatter.3.cloned.1.call-update
  272.2 0.2 all-gather.11.cloned.1.call-start
  272.5 16.8 %reduce-scatter.5.cloned.1.call-done = f32[1,32,128]{2,1,0:T(8,128)} async-done(((f32[8,32,128]{2,1,0:T(8,128)}), f32[1,32,128]{2,1,0:T(8,128)}) %reduce-scatter.5.cloned.1.call-update) | async-done | bytes 16400 | tf_op jit(solution)/shard_map/reduce_scatter | solution.py:85
  289.2 1.6 multiply_reduce_fusion
  291.5 0.6 reshape.117
  292.1 0.0 all-gather.11.cloned.1.call-update
  292.1 1.3 fusion.17
  293.4 30.0 %reduce-scatter.3.cloned.1.call-done = f32[1,32,128]{2,1,0:T(8,128)} async-done(((f32[8,32,128]{2,1,0:T(8,128)}), f32[1,32,128]{2,1,0:T(8,128)}) %reduce-scatter.3.cloned.1.call-update) | async-done | bytes 16400 | tf_op jit(solution)/shard_map/reduce_scatter | solution.py:79
  323.4 1.6 multiply_reduce_fusion.1
  325.7 718.4 %all-gather.11.cloned.1.call-done = bf16[256,1,8192]{2,1,0:T(2,128)(2,1)} async-done(((bf16[1,1,8192]{2,1,0:T(2,128)(2,1)}), bf16[256,1,8192]{2,1,0:T(2,128)(2,1)}) %all-gather.11.cloned.1.call-update) | async-done | bytes 4194320 | tf_op jit(solution)/shard_map/all_gather | solution.py:110
  1044.1 7.8 fusion
  1051.9 0.1 reshape.110
  1052.1 0.2 copy.30
  1052.2 0.7 reshape_reshape.3
  (14 shorter events, 0.1 us)
Async XLA Ops:
  6.5 30.8 %copy-start = (bf16[8,32,5120]{2,1,0:T(8,128)(2,1)S(1)}, bf16[8,32,5120]{2,1,0:T(8,128)(2,1)}, u32[]{:S(2)}) copy-start(bf16[8,32,5120]{2,1,0:T(8,128)(2,1)} %param.11) | copy-start | bytes 7864324
  6.5 126.8 %all-gather.7.cloned.1.call-start = ((), (), s32[]{:S(2)}) async-start(), calls=%async_computation.2 | async-start | bytes 9748480 | tf_op jit(solution)/shard_map/all_gather | solution.py:72
  19.8 222.0 %all-gather.9.cloned.1.call-start = ((), (), s32[]{:S(2)}) async-start(), calls=%async_computation.3 | async-start | bytes 9748480 | tf_op jit(solution)/shard_map/all_gather | solution.py:73
  32.6 256.6 %reduce-scatter.5.cloned.1.call-start = ((), (), s32[]{:S(2)}) async-start(), calls=%async_computation.5 | async-start | bytes 147456 | tf_op jit(solution)/shard_map/reduce_scatter | solution.py:85
  249.7 8.9 copy-start.3
  249.7 8.9 copy-start.5
  258.6 0.9 copy-start.4
  260.8 62.6 %reduce-scatter.3.cloned.1.call-start = ((), (), s32[]{:S(2)}) async-start(), calls=%async_computation.4 | async-start | bytes 147456 | tf_op jit(solution)/shard_map/reduce_scatter | solution.py:79
  260.9 9.7 copy-start.2
  271.0 21.1 %copy-start.1 = (bf16[64,5120]{1,0:T(8,128)(2,1)S(1)}, bf16[64,5120]{1,0:T(8,128)(2,1)}, u32[]{:S(2)}) copy-start(bf16[64,5120]{1,0:T(8,128)(2,1)} %param.15) | copy-start | bytes 1966084
  272.2 771.8 %all-gather.11.cloned.1.call-start = ((), (), s32[]{:S(2)}) async-start(), calls=%async_computation.6 | async-start | bytes 8421376 | tf_op jit(solution)/shard_map/all_gather | solution.py:110
Sparse Core Ops, SparseCore 0:
  19.9 113.4 all-gather.6
  135.2 106.5 all-gather.8
  261.0 28.2 reduce-scatter.4
  291.7 31.6 reduce-scatter.2
  325.1 718.8 all-gather.10
where the time goes:
time: 1060 us
  waiting for transfers between devices  960 us (91%)
  matrix products  33.9 us (3%)
  local copies, waits for them, and re-layouts  26 us (2%)
  blocking collectives  22 us (2%)
  between operations  14.7 us (1%)
    all_gather x1, waiting for transfers between devices, body(): lax.all_gather(query_units, ('fsdp', 'dp', 'query'), axis=0, tiled=True)  718 us
    all_gather x1, waiting for transfers between devices, body(): lax.all_gather(up_cols, 'fsdp', axis=0, tiled=True)  100 us
    all_gather x1, waiting for transfers between devices, body(): lax.all_gather(gate_cols, 'fsdp', axis=0, tiled=True)  94.7 us
    reduce_scatter x1, waiting for transfers between devices, body(): lax.psum_scatter(doc_part.reshape(doc_inputs.shape[0], doc_inputs.shape[1...  30 us
  transfers between devices with their start and end apart: 5, of which 5 were waited for; matrix products, arithmetic and copies ran while one was open for 3% of the time, Pallas kernels for 0%

commit v1 on v0

v1 whole, which is shorter than its diff:
```python
import jax
import jax.numpy as jnp
from jax import lax
from jax.sharding import PartitionSpec as P

F32 = jnp.float32
BF16 = jnp.bfloat16
SWAP = ((0, 1), (1, 0))


def ring_perm(size, inner, step):
    outer = size // inner
    return [
        (o * inner + i, o * inner + (i + step) % inner)
        for o in range(outer)
        for i in range(inner)
    ]


def x_shift(value, chips, step):
    perm = [
        (x * 2 + c, ((x + step) % chips) * 2 + c) for x in range(chips) for c in range(2)
    ]
    return lax.ppermute(value, "dp", perm)


def core_swap(value, size):
    return lax.ppermute(value, "dp", [(i, i ^ 1) for i in range(size)])


def partner_rows(rows):
    size = lax.axis_size("dp")
    chips = size // 2
    place = lax.axis_index("dp")
    chip, core = place // 2, place % 2
    mine = lax.dynamic_slice_in_dim(rows, place, 1, 0)
    here = lax.ppermute(mine, "query", SWAP)
    half = rows.shape[1] // 2
    left = x_shift(here, chips, 1)
    right = x_shift(here, chips, -1)
    far_a = x_shift(left[:, :half], chips, 1)
    far_b = x_shift(right[:, half:], chips, -1)
    far = jnp.concatenate((far_a, far_b), axis=1)
    result = jnp.zeros_like(rows)
    for offset, piece in ((0, here), (-1, left), (1, right), (2, far)):
        other = core_swap(piece, size)
        owner = (chip + offset + chips) % chips
        result = lax.dynamic_update_slice(result, piece, (owner * 2 + core, 0, 0))
        result = lax.dynamic_update_slice(result, other, (owner * 2 + 1 - core, 0, 0))
    return result


def projected(pre, cotangent, gate_projection, up_projection):
    cols = pre.shape[1] // 2
    gate = pre[:, :cols]
    up = pre[:, cols:]
    sigma = jax.nn.sigmoid(gate)
    upstream = cotangent.astype(F32)
    gate_grad = (upstream * up * sigma * (1.0 + gate * (1.0 - sigma))).astype(BF16)
    up_grad = (upstream * gate * sigma).astype(BF16)
    dims = (((1,), (1,)), ((), ()))
    return jnp.concatenate(
        (
            lax.dot_general(gate_projection, gate_grad, dims, preferred_element_type=F32),
            lax.dot_general(up_projection, up_grad, dims, preferred_element_type=F32),
        ),
        axis=0,
    )


def body(
    doc_inputs,
    doc_cotangents,
    query_inputs,
    query_cotangents,
    gate_weight,
    up_weight,
    input_projection,
    gate_projection,
    up_projection,
):
    count, length, width = doc_inputs.shape
    half_index = lax.axis_index("query")
    dq = ("dp", "query")
    n_dq = lax.axis_size("dp") * lax.axis_size("query")
    n_fsdp = lax.axis_size("fsdp")
    rank = input_projection.shape[0]

    weight = jnp.concatenate((gate_weight, up_weight), axis=1)
    weight = lax.all_gather(weight, "fsdp", axis=0, tiled=True)
    cols = gate_weight.shape[1]

    own = jnp.concatenate((doc_inputs, query_inputs), axis=1)
    other = partner_rows(own)
    cot = jnp.concatenate((doc_cotangents, query_cotangents), axis=1)
    cot = cot.reshape(-1, cot.shape[2])
    own_cot = lax.dynamic_slice_in_dim(cot, half_index * cols, cols, 1)
    other_cot = lax.ppermute(
        lax.dynamic_slice_in_dim(cot, (1 - half_index) * cols, cols, 1), "query", SWAP
    )
    gate_proj = lax.dynamic_slice_in_dim(gate_projection, half_index * cols, cols, 1)
    up_proj = lax.dynamic_slice_in_dim(up_projection, half_index * cols, cols, 1)

    parts = []
    factors = []
    for rows, rows_cot in ((own, own_cot), (other, other_cot)):
        flat = rows.reshape(-1, width)
        pre = jnp.dot(flat, weight, preferred_element_type=F32)
        parts.append(projected(pre, rows_cot, gate_proj, up_proj))
        factors.append(
            lax.dot_general(
                flat, input_projection, (((1,), (1,)), ((), ())), preferred_element_type=F32
            )
        )

    first = half_index == 0

    def ordered(pair, axis):
        a = jnp.where(first, pair[0], pair[1])
        b = jnp.where(first, pair[1], pair[0])
        return jnp.concatenate((a, b), axis=axis)

    part = ordered(parts, 1).astype(BF16)
    in_factor = ordered(factors, 0)
    ranks = part.shape[0] // n_dq
    part = part.reshape(n_dq, ranks, -1)
    swapped = lax.all_to_all(part, dq, 0, 0, tiled=True)
    out_sum = jnp.sum(swapped.astype(F32), axis=0)

    pairs = 2 * count
    factor = jnp.einsum(
        "kel,elr->ekr",
        out_sum.reshape(ranks, 2 * pairs, length),
        in_factor.reshape(2 * pairs, length, rank),
        precision=lax.Precision.HIGHEST,
    ).reshape(pairs, 2, ranks * rank)
    docs = factor[:, 0]
    queries = factor[:, 1]
    doc_squares = jnp.sum(docs * docs, axis=1)
    docs = docs.astype(BF16)
    queries = queries.astype(BF16)

    everyone = lax.all_to_all(
        jnp.broadcast_to(queries[None], (n_fsdp,) + queries.shape), "fsdp", 0, 0, tiled=True
    ).reshape(n_fsdp * pairs, -1)
    wide = everyone.astype(F32)
    query_squares = jnp.sum(wide * wide, axis=1)
    scores = lax.dot_general(
        docs, everyone, (((1,), (1,)), ((), ())), preferred_element_type=F32
    )
    total = scores.shape[1]

    def to_destinations(x):
        return x.reshape((2, count) + x.shape[1:]).swapaxes(0, 1).reshape(x.shape)

    payload = jnp.concatenate(
        (
            to_destinations(scores),
            jnp.broadcast_to(query_squares[None], (pairs, total)),
            jnp.broadcast_to(to_destinations(doc_squares)[:, None], (pairs, 128)),
        ),
        axis=1,
    )
    received = lax.all_to_all(payload, dq, 0, 0, tiled=True)
    sums = jnp.sum(received, axis=0)
    entries = 1.0 / (rank * 2 * rank)
    doc_scale = lax.rsqrt(sums[2 * total] * entries + 1e-06)
    query_scale = lax.rsqrt(sums[total : 2 * total] * entries + 1e-06)
    result = sums[:total] * query_scale * (doc_scale / rank)
    return result.reshape(1, 1, total)


def solution(mesh):
    return jax.shard_map(
        body,
        mesh=mesh,
        in_specs=(
            P(("fsdp", "query"), None, None),
            P(("fsdp", "query"), None, "dp"),
            P(("fsdp", "query"), None, None),
            P(("fsdp", "query"), None, "dp"),
            P("fsdp", ("dp", "query")),
            P("fsdp", ("dp", "query")),
            P(),
            P(None, "dp"),
            P(None, "dp"),
        ),
        out_specs=P(("fsdp", "query"), "dp", None),
        check_vma=False,
    )
```

time: 1060 us -> 242 us (0.23)
  waiting for transfers between devices: 960 us -> 126 us
  starting transfers between devices: 0.35 us -> 30.2 us
    all_gather x3 -> x1, waiting for transfers between devices: 914 us -> 0.01 us  [body(): weight = lax.all_gather(weight, 'fsdp', axis=0, tiled=True)]
    ppermute x0 -> x10, waiting for transfers between devices: none -> 112 us  [the longest x1 103 us: partner_rows(): here = lax.ppermute(mine, 'query', SWAP)]
    reduce_scatter x2 -> x0, waiting for transfers between devices: 46.8 us -> none  [the longest x1 30 us: body(): lax.psum_scatter(doc_part.reshape(doc_inputs.shape[0], doc_inputs.shape[1...]
    all_gather x2 -> x0, blocking collectives: 22 us -> none  [the longest x1 11.2 us: body(): lax.all_gather(gate_weight, 'query', axis=1, tiled=True)]
    ppermute x0 -> x10, starting transfers between devices: none -> 17.9 us  [the longest x4 8.56 us: core_swap(): return lax.ppermute(value, 'dp', [(i, i ^ 1) for i in range(size)])]
    all_to_all x0 -> x2, waiting for transfers between devices: none -> 13.4 us  [the longest x1 8.5 us: body(): lax.all_to_all(jnp.broadcast_to(queries[None], (n_fsdp,) + queries.shape)...]
    all_to_all x0 -> x1, blocking collectives: none -> 12.5 us  [body(): received = lax.all_to_all(payload, dq, 0, 0, tiled=True)]
    all_to_all x0 -> x2, starting transfers between devices: none -> 12.3 us  [the longest x1 7.06 us: body(): lax.all_to_all(jnp.broadcast_to(queries[None], (n_fsdp,) + queries.shape)...]
  transfers between devices with their start and end apart: 5 -> 13, of which waited for: 5 -> 5; matrix products, arithmetic and copies ran while one was open for 3% -> 19% of each run, Pallas kernels for 0% -> 0%
where the time goes in v1:
time: 242 us
  waiting for transfers between devices  126 us (52%)
  matrix products  34.4 us (14%)
  starting transfers between devices  30.2 us (12%)
  local copies, waits for them, and re-layouts  19.5 us (8%)
  between operations  14.4 us (6%)
  blocking collectives  12.5 us (5%)
  other arithmetic  5.19 us (2%)
    ppermute x1, waiting for transfers between devices, partner_rows(): here = lax.ppermute(mine, 'query', SWAP)  103 us
    dot_general x2, matrix products, body(): pre = jnp.dot(flat, weight, preferred_element_type=F32)  20.1 us
    all_to_all x1, blocking collectives, body(): received = lax.all_to_all(payload, dq, 0, 0, tiled=True)  12.5 us
    dot_general x2, matrix products, body(): lax.dot_general(flat, input_projection, (((1,), (1,)), ((), ())), preferr...  9.05 us
    ppermute x4, waiting for transfers between devices, x_shift(): return lax.ppermute(value, 'dp', perm)  8.86 us
    ppermute x4, starting transfers between devices, core_swap(): return lax.ppermute(value, 'dp', [(i, i ^ 1) for i in range(size)])  8.56 us
    all_to_all x1, waiting for transfers between devices, body(): lax.all_to_all(jnp.broadcast_to(queries[None], (n_fsdp,) + queries.shape)...  8.5 us
    all_to_all x1, starting transfers between devices, body(): lax.all_to_all(jnp.broadcast_to(queries[None], (n_fsdp,) + queries.shape)...  7.06 us
  transfers between devices with their start and end apart: 13, of which 5 were waited for; matrix products, arithmetic and copies ran while one was open for 19% of the time, Pallas kernels for 0%

profile of v1, /device:TPU:1, one launch (start us, length us, event | category | flops | bytes accessed | tf_op | source)
XLA Modules:
  0.0 241.7 jit_solution(1108142315296422103)
XLA Ops:
  6.5 2.2 pad_maximum_fusion.1
  8.8 1.9 constant_dynamic-update-slice_fusion.1
  10.7 0.2 constant_dynamic-update-slice_fusion
  10.9 2.4 copy-done.1
  13.4 3.8 %collective-permute-start.1 = (bf16[1,64,5120]{2,1,0:T(8,128)(2,1)S(1)}, bf16[1,64,5120]{2,1,0:T(8,128)(2,1)S(1)}, u32[]{:S(2)}, u32[]{:S(2)}) collective-permute-start(bf16[1,64,5120]{2,1,0:T(8,128)(2,1)S(1)} %constant_dynamic-slice_fusion), channel_id=1, source_target_pairs={{0,1},{1,0},{2,3},{3,2},{4,5},{5,4},{6,7},{7,6},{8,9},{9,8},{10,11... | collective-permute-start | bytes 1966088 | tf_op jit(solution)/shard_map/ppermute | solution.py:37
  17.2 1.3 pad_maximum_fusion
  18.4 1.1 constant_dynamic-slice_fusion.1
  19.6 103.2 %collective-permute-done.1 = bf16[1,64,5120]{2,1,0:T(8,128)(2,1)S(1)} collective-permute-done((bf16[1,64,5120]{2,1,0:T(8,128)(2,1)S(1)}, bf16[1,64,5120]{2,1,0:T(8,128)(2,1)S(1)}, u32[]{:S(2)}, u32[]{:S(2)}) %collective-permute-start.1) | collective-permute-done | bytes 655392 | tf_op jit(solution)/shard_map/ppermute | solution.py:37
  122.7 5.3 %collective-permute-start.2 = (bf16[1,64,5120]{2,1,0:T(8,128)(2,1)S(1)}, bf16[1,64,5120]{2,1,0:T(8,128)(2,1)}, u32[]{:S(2)}, u32[]{:S(2)}) collective-permute-start(bf16[1,64,5120]{2,1,0:T(8,128)(2,1)S(1)} %collective-permute-done.1), channel_id=1, source_target_pairs={{0,2},{2,0},{4,6},{6,4},{8,10},{10,8},{12,14},{14,12},{1,3},{3,1},... | collective-permute-start | bytes 1966088 | tf_op jit(solution)/shard_map/ppermute | solution.py:28
  128.0 2.7 %collective-permute-start.5 = (bf16[1,64,5120]{2,1,0:T(8,128)(2,1)S(1)}, bf16[1,64,5120]{2,1,0:T(8,128)(2,1)S(1)}, u32[]{:S(2)}, u32[]{:S(2)}) collective-permute-start(bf16[1,64,5120]{2,1,0:T(8,128)(2,1)S(1)} %collective-permute-done.1), channel_id=1, source_target_pairs={{0,12},{2,14},{4,0},{6,2},{8,4},{10,6},{12,8},{14,10},{1,13},{3,15... | collective-permute-start | bytes 1966088 | tf_op jit(solution)/shard_map/ppermute | solution.py:24
  130.7 4.9 %fusion.41 = f32[512,64]{0,1:T(8,128)} fusion(bf16[512,5120]{1,0:T(8,128)(2,1)} %bitcast.34, bf16[64,5120]{1,0:T(8,128)(2,1)S(1)} %copy-done), kind=kOutput, calls=%fused_computation.74 | convolution fusion | flops 335544320 | bytes 6029312 | tf_op jit(solution)/shard_map/dot_general | solution.py:111
  135.6 2.9 %broadcast_in_dim.24 = bf16[8,64,5120]{2,1,0:T(8,128)(2,1)} broadcast(bf16[]{:T(256)} %constant.73.clone.1), dimensions={} | broadcast | bytes 5242882 | tf_op jit(solution)/shard_map/broadcast_in_dim | solution.py:44
  138.5 0.9 constant_dynamic-update-slice_fusion.11
  139.4 6.2 %collective-permute-done.3 = bf16[1,64,5120]{2,1,0:T(8,128)(2,1)S(1)} collective-permute-done((bf16[1,64,5120]{2,1,0:T(8,128)(2,1)S(1)}, bf16[1,64,5120]{2,1,0:T(8,128)(2,1)S(1)}, u32[]{:S(2)}, u32[]{:S(2)}) %collective-permute-start.3) | collective-permute-done | bytes 655392 | tf_op jit(solution)/shard_map/ppermute | solution.py:24
  145.8 2.7 %collective-permute-start.8 = (bf16[1,32,5120]{2,1,0:T(8,128)(2,1)S(1)}, bf16[1,32,5120]{2,1,0:T(8,128)(2,1)S(1)}, u32[]{:S(2)}, u32[]{:S(2)}) collective-permute-start(bf16[1,32,5120]{2,1,0:T(8,128)(2,1)S(1)} %slice.48), channel_id=1, source_target_pairs={{0,12},{2,14},{4,0},{6,2},{8,4},{10,6},{12,8},{14,10},{1,13},{3,15... | collective-permute-start | bytes 983048 | tf_op jit(solution)/shard_map/ppermute | solution.py:24
  148.5 1.3 collective-permute-start.4
  149.8 2.0 constant_dynamic-update-slice_fusion.10
  151.8 0.9 constant_dynamic-update-slice_fusion.9
  152.7 2.6 %collective-permute-done.7 = bf16[1,32,5120]{2,1,0:T(8,128)(2,1)S(1)} collective-permute-done((bf16[1,32,5120]{2,1,0:T(8,128)(2,1)S(1)}, bf16[1,32,5120]{2,1,0:T(8,128)(2,1)S(1)}, u32[]{:S(2)}, u32[]{:S(2)}) %collective-permute-start.7) | collective-permute-done | bytes 327712 | tf_op jit(solution)/shard_map/ppermute | solution.py:24
  155.4 1.9 collective-permute-start.9
  157.4 0.9 constant_dynamic-update-slice_fusion.8
  158.3 0.9 constant_dynamic-update-slice_fusion.7
  159.2 0.9 constant_dynamic-update-slice_fusion.6
  160.1 0.9 constant_dynamic-update-slice_fusion.5
  161.0 0.9 constant_dynamic-update-slice_fusion.4
  161.9 12.5 %fusion.39 = f32[512,896]{1,0:T(8,128)S(1)} fusion(bf16[512,5120]{1,0:T(8,128)(2,1)} %bitcast.35, bf16[5120,896]{1,0:T(8,128)(2,1)} %all-gather.2.cloned.1.call-done), kind=kOutput, calls=%fused_computation.72 | convolution fusion | flops 4697620480 | bytes 16252928 | tf_op jit(solution)/shard_map/dot_general | solution.py:108
  174.4 7.7 %fusion.40 = f32[512,896]{1,0:T(8,128)S(1)} fusion(bf16[512,5120]{1,0:T(8,128)(2,1)} %bitcast.2, bf16[5120,896]{1,0:T(8,128)(2,1)S(1)} %copy-done.4), kind=kOutput, calls=%fused_computation.73 | convolution fusion | flops 4697620480 | bytes 16252928 | tf_op jit(solution)/shard_map/dot_general | solution.py:108
  182.1 0.5 fusion.12
  182.6 0.4 copy-done.6
  183.0 0.7 fusion.16
  183.7 1.5 fusion.10
  185.2 1.7 fusion.14
  187.0 0.7 pad_maximum_fusion.4
  187.7 5.3 %all-to-all-start = ((bf16[16,8,1024]{2,1,0:T(8,128)(2,1)}), bf16[16,8,1024]{2,1,0:T(8,128)(2,1)S(1)}, u32[]{:S(2)}, u32[]{:S(2)}) async-start(bf16[16,8,1024]{2,1,0:T(8,128)(2,1)} %pad_maximum_fusion.4), calls=%async_computation | async-start | bytes 524288 | tf_op jit(solution)/shard_map/all_to_all | solution.py:127
  193.0 4.2 %broadcast_select_fusion.1 = (f32[512,64]{0,1:T(8,128)S(1)}, f32[512,64]{0,1:T(8,128)S(1)}) fusion(f32[512,64]{0,1:T(8,128)S(1)} %copy-done.3, pred[]{:T(512)S(6)} %eq.9, bf16[512,5120]{1,0:T(8,128)(2,1)} %bitcast.2, bf16[64,5120]{1,0:T(8,128)(2,1)S(1)} %copy-done), kind=kOutput, calls=%fused_computation.38 | convolution fusion | flops 335609856 | bytes 6291457 | tf_op jit(solution)/shard_map/dot_general | solution.py:111
  197.2 0.2 copy.18
  197.4 4.9 %all-to-all-done = bf16[16,8,1024]{2,1,0:T(8,128)(2,1)S(1)} async-done(((bf16[16,8,1024]{2,1,0:T(8,128)(2,1)}), bf16[16,8,1024]{2,1,0:T(8,128)(2,1)S(1)}, u32[]{:S(2)}, u32[]{:S(2)}) %all-to-all-start) | async-done | bytes 262176 | tf_op jit(solution)/shard_map/all_to_all | solution.py:127
  202.5 0.6 fusion.22
  203.1 0.1 reshape.72
  203.3 0.7 broadcast_in_dim.25
  204.0 7.1 %all-to-all-start.1 = ((bf16[16,16,512]{2,1,0:T(8,128)(2,1)}), bf16[16,16,512]{2,1,0:T(8,128)(2,1)S(1)}, u32[]{:S(2)}, u32[]{:S(2)}) async-start(bf16[16,16,512]{2,1,0:T(8,128)(2,1)} %broadcast_in_dim.25), calls=%async_computation.1 | async-start | bytes 524288 | tf_op jit(solution)/shard_map/all_to_all | solution.py:143
  211.1 0.1 multiply_reduce_fusion.1
  211.5 8.5 %all-to-all-done.1 = bf16[16,16,512]{2,1,0:T(8,128)(2,1)S(1)} async-done(((bf16[16,16,512]{2,1,0:T(8,128)(2,1)}), bf16[16,16,512]{2,1,0:T(8,128)(2,1)S(1)}, u32[]{:S(2)}, u32[]{:S(2)}) %all-to-all-start.1) | async-done | bytes 262176 | tf_op jit(solution)/shard_map/all_to_all | solution.py:143
  220.0 0.2 convolution_bitcast_fusion
  220.2 0.1 multiply_reduce_fusion
  220.5 12.5 %all_to_all.19 = f32[16,1,640]{2,1,0:T(1,128)S(1)} all-to-all(f32[16,1,640]{2,1,0:T(1,128)S(1)} %copy.24), channel_id=1, replica_groups=mesh['fsdp'=16,'dp'=8,'query'=2] {'dp','query'}, dimensions={0} | all-to-all | bytes 81920 | tf_op jit(solution)/shard_map/all_to_all | solution.py:164
  233.1 0.5 slice.44
  234.3 0.6 multiply_multiply_fusion
  (49 shorter events, 1.1 us)
Async XLA Ops:
  6.5 124.2 %copy-start = (bf16[64,5120]{1,0:T(8,128)(2,1)S(1)}, bf16[64,5120]{1,0:T(8,128)(2,1)}, u32[]{:S(2)}) copy-start(bf16[64,5120]{1,0:T(8,128)(2,1)} %param.15) | copy-start | bytes 1966084
  6.5 4.2 %copy-start.2 = (bf16[8,32,5120]{2,1,0:T(8,128)(2,1)S(1)}, bf16[8,32,5120]{2,1,0:T(8,128)(2,1)}, u32[]{:S(2)}) copy-start(bf16[8,32,5120]{2,1,0:T(8,128)(2,1)} %param.11) | copy-start | bytes 7864324
  6.5 155.4 %all-gather.2.cloned.1.call-start = ((), (), s32[]{:S(2)}) async-start(), calls=%async_computation.3 | async-start | bytes 9748480 | tf_op jit(solution)/shard_map/all_gather | solution.py:90
  10.9 2.4 copy-start.1
  13.4 109.4 %collective-permute-start.1 = (bf16[1,64,5120]{2,1,0:T(8,128)(2,1)S(1)}, bf16[1,64,5120]{2,1,0:T(8,128)(2,1)S(1)}, u32[]{:S(2)}, u32[]{:S(2)}) collective-permute-start(bf16[1,64,5120]{2,1,0:T(8,128)(2,1)S(1)} %constant_dynamic-slice_fusion), channel_id=1, source_target_pairs={{0,1},{1,0},{2,3},{3,2},{4,5},{5,4},{6,7},{7,6},{8,9},{9,8},{10,11... | collective-permute-start | bytes 1966088 | tf_op jit(solution)/shard_map/ppermute | solution.py:37
  19.5 164.2 %collective-permute-start = (bf16[512,448]{1,0:T(8,128)(2,1)}, bf16[512,448]{1,0:T(8,128)(2,1)}, u32[]{:S(2)}, u32[]{:S(2)}) collective-permute-start(bf16[512,448]{1,0:T(8,128)(2,1)} %constant_dynamic-slice_fusion.1), channel_id=1, source_target_pairs={{0,1},{1,0},{2,3},{3,2},{4,5},{5,4},{6,7},{7,6},{8,9},{9,8},{10,11... | collective-permute-start | bytes 1376264 | tf_op jit(solution)/shard_map/ppermute | solution.py:98
  122.7 27.1 %collective-permute-start.2 = (bf16[1,64,5120]{2,1,0:T(8,128)(2,1)S(1)}, bf16[1,64,5120]{2,1,0:T(8,128)(2,1)}, u32[]{:S(2)}, u32[]{:S(2)}) collective-permute-start(bf16[1,64,5120]{2,1,0:T(8,128)(2,1)S(1)} %collective-permute-done.1), channel_id=1, source_target_pairs={{0,2},{2,0},{4,6},{6,4},{8,10},{10,8},{12,14},{14,12},{1,3},{3,1},... | collective-permute-start | bytes 1966088 | tf_op jit(solution)/shard_map/ppermute | solution.py:28
  128.0 17.6 %collective-permute-start.3 = (bf16[1,64,5120]{2,1,0:T(8,128)(2,1)S(1)}, bf16[1,64,5120]{2,1,0:T(8,128)(2,1)S(1)}, u32[]{:S(2)}, u32[]{:S(2)}) collective-permute-start(bf16[1,64,5120]{2,1,0:T(8,128)(2,1)S(1)} %collective-permute-done.1), channel_id=1, source_target_pairs={{0,4},{2,6},{4,8},{6,10},{8,12},{10,14},{12,0},{14,2},{1,5},{3,7},... | collective-permute-start | bytes 1966088 | tf_op jit(solution)/shard_map/ppermute | solution.py:24
  128.0 17.7 %collective-permute-start.5 = (bf16[1,64,5120]{2,1,0:T(8,128)(2,1)S(1)}, bf16[1,64,5120]{2,1,0:T(8,128)(2,1)S(1)}, u32[]{:S(2)}, u32[]{:S(2)}) collective-permute-start(bf16[1,64,5120]{2,1,0:T(8,128)(2,1)S(1)} %collective-permute-done.1), channel_id=1, source_target_pairs={{0,12},{2,14},{4,0},{6,2},{8,4},{10,6},{12,8},{14,10},{1,13},{3,15... | collective-permute-start | bytes 1966088 | tf_op jit(solution)/shard_map/ppermute | solution.py:24
  145.6 9.7 %collective-permute-start.7 = (bf16[1,32,5120]{2,1,0:T(8,128)(2,1)S(1)}, bf16[1,32,5120]{2,1,0:T(8,128)(2,1)S(1)}, u32[]{:S(2)}, u32[]{:S(2)}) collective-permute-start(bf16[1,32,5120]{2,1,0:T(8,128)(2,1)S(1)} %slice.47), channel_id=1, source_target_pairs={{0,4},{2,6},{4,8},{6,10},{8,12},{10,14},{12,0},{14,2},{1,5},{3,7},... | collective-permute-start | bytes 983048 | tf_op jit(solution)/shard_map/ppermute | solution.py:24
  145.8 9.6 %collective-permute-start.8 = (bf16[1,32,5120]{2,1,0:T(8,128)(2,1)S(1)}, bf16[1,32,5120]{2,1,0:T(8,128)(2,1)S(1)}, u32[]{:S(2)}, u32[]{:S(2)}) collective-permute-start(bf16[1,32,5120]{2,1,0:T(8,128)(2,1)S(1)} %slice.48), channel_id=1, source_target_pairs={{0,12},{2,14},{4,0},{6,2},{8,4},{10,6},{12,8},{14,10},{1,13},{3,15... | collective-permute-start | bytes 983048 | tf_op jit(solution)/shard_map/ppermute | solution.py:24
  148.5 8.9 %collective-permute-start.4 = (bf16[1,64,5120]{2,1,0:T(8,128)(2,1)S(1)}, bf16[1,64,5120]{2,1,0:T(8,128)(2,1)S(1)}, u32[]{:S(2)}, u32[]{:S(2)}) collective-permute-start(bf16[1,64,5120]{2,1,0:T(8,128)(2,1)S(1)} %collective-permute-done.3), channel_id=1, source_target_pairs={{0,2},{2,0},{4,6},{6,4},{8,10},{10,8},{12,14},{14,12},{1,3},{3,1},... | collective-permute-start | bytes 1966088 | tf_op jit(solution)/shard_map/ppermute | solution.py:28
  149.8 9.3 %collective-permute-start.6 = (bf16[1,64,5120]{2,1,0:T(8,128)(2,1)S(1)}, bf16[1,64,5120]{2,1,0:T(8,128)(2,1)S(1)}, u32[]{:S(2)}, u32[]{:S(2)}) collective-permute-start(bf16[1,64,5120]{2,1,0:T(8,128)(2,1)S(1)} %collective-permute-done.5), channel_id=1, source_target_pairs={{0,2},{2,0},{4,6},{6,4},{8,10},{10,8},{12,14},{14,12},{1,3},{3,1},... | collective-permute-start | bytes 1966088 | tf_op jit(solution)/shard_map/ppermute | solution.py:28
  155.4 5.6 %collective-permute-start.9 = (bf16[1,64,5120]{2,1,0:T(8,128)(2,1)S(1)}, bf16[1,64,5120]{2,1,0:T(8,128)(2,1)S(1)}, u32[]{:S(2)}, u32[]{:S(2)}) collective-permute-start(bf16[1,64,5120]{2,1,0:T(8,128)(2,1)S(1)} %constant_dynamic-update-slice_fusion.2), channel_id=1, source_target_pairs={{0,2},{2,0},{4,6},{6,4},{8,10},{10,8},{12,14},{14,12},{1,3},{3,1},... | collective-permute-start | bytes 1966088 | tf_op jit(solution)/shard_map/ppermute | solution.py:28
  161.9 12.5 %copy-start.4 = (bf16[5120,896]{1,0:T(8,128)(2,1)S(1)}, bf16[5120,896]{1,0:T(8,128)(2,1)}, u32[]{:S(2)}) copy-start(bf16[5120,896]{1,0:T(8,128)(2,1)} %all-gather.2.cloned.1.call-done) | copy-start | bytes 27525124
  174.4 7.7 %copy-start.5 = (bf16[64,896]{1,0:T(8,128)(2,1)S(1)}, bf16[64,896]{1,0:T(8,128)(2,1)}, u32[]{:S(2)}) copy-start(bf16[64,896]{1,0:T(8,128)(2,1)} %param.17) | copy-start | bytes 344068
  182.1 0.9 copy-start.6
  185.2 7.8 %copy-start.3 = (f32[512,64]{0,1:T(8,128)S(1)}, f32[512,64]{0,1:T(8,128)}, u32[]{:S(2)}) copy-start(f32[512,64]{0,1:T(8,128)} %fusion.41) | copy-start | bytes 393220
  187.7 14.6 %all-to-all-start = ((bf16[16,8,1024]{2,1,0:T(8,128)(2,1)}), bf16[16,8,1024]{2,1,0:T(8,128)(2,1)S(1)}, u32[]{:S(2)}, u32[]{:S(2)}) async-start(bf16[16,8,1024]{2,1,0:T(8,128)(2,1)} %pad_maximum_fusion.4), calls=%async_computation | async-start | bytes 524288 | tf_op jit(solution)/shard_map/all_to_all | solution.py:127
  204.0 16.0 %all-to-all-start.1 = ((bf16[16,16,512]{2,1,0:T(8,128)(2,1)}), bf16[16,16,512]{2,1,0:T(8,128)(2,1)S(1)}, u32[]{:S(2)}, u32[]{:S(2)}) async-start(bf16[16,16,512]{2,1,0:T(8,128)(2,1)} %broadcast_in_dim.25), calls=%async_computation.1 | async-start | bytes 524288 | tf_op jit(solution)/shard_map/all_to_all | solution.py:143
Sparse Core Ops, SparseCore 0:
  9.1 112.7 all-gather.1

commit v2 on v1

v2 whole, which is shorter than its diff:
```python
import jax
import jax.numpy as jnp
from jax import lax
from jax.sharding import PartitionSpec as P

F32 = jnp.float32
BF16 = jnp.bfloat16

def shift(value, axis, step):
    size = lax.axis_size(axis)
    return lax.ppermute(value, axis, [(i, (i + step) % size) for i in range(size)])


def gathered(weight, cot, rows):
    barrier = lax.optimization_barrier
    n_z = lax.axis_size("z")
    n_x = lax.axis_size("x")
    z = lax.axis_index("z")
    chip = lax.axis_index("x")
    core = lax.axis_index("core")
    half = weight.shape[0] // 2

    def up(value):
        return shift(value, "z", 1)

    def down(value):
        return shift(value, "z", -1)

    def across(value):
        return shift(value, "ylo", 1)

    mine = lax.dynamic_slice_in_dim(rows, chip * 2 + core, 1, 0)
    a1, b1, here, w0 = barrier((up(weight), down(weight), shift(mine, "yhi", 1), weight))
    left, right, far = shift(here, "x", 1), shift(here, "x", -1), shift(here, "x", 2)
    a2, b2, o0 = barrier((up(a1), down(b1), across(w0)))
    a3, b3, oa2, o0, b2, left, right, far = barrier(
        (up(a2), down(b2), across(a2), o0, b2, left, right, far)
    )
    pieces = jnp.concatenate((here, left, right, far), axis=0)
    oa1, ob1, ob2, others, a3, b3, oa2 = barrier(
        (up(o0), down(o0), across(b2), shift(pieces, "core", 1), a3, b3, oa2)
    )
    up_pair = up(jnp.concatenate((oa2, a3[:half]), axis=0))
    down_pair = down(jnp.concatenate((ob2, b3[half:]), axis=0))
    up_pair, down_pair, cot = barrier((up_pair, down_pair, shift(cot, "yhi", 1)))
    full = 2 * half
    oa3, a4 = up_pair[:full], up_pair[full:]
    ob3, b4 = down_pair[:full], down_pair[full:]
    oa4 = up(oa3[:half])
    ob4 = down(ob3[half:])

    def placed(by_offset, high, low):
        result = jnp.zeros((n_z,) + weight.shape, weight.dtype)
        for offset, shard in by_offset:
            result = lax.dynamic_update_slice(result, shard[None], ((z + offset) % n_z, 0, 0))
        far_z = (z + n_z // 2) % n_z
        result = lax.dynamic_update_slice(result, high[None], (far_z, 0, 0))
        result = lax.dynamic_update_slice(result, low[None], (far_z, half, 0))
        return result.reshape(n_z * full, -1)

    this_row = placed(
        ((0, w0), (n_z - 1, a1), (1, b1), (n_z - 2, a2), (2, b2), (n_z - 3, a3), (3, b3)), a4, b4
    )
    other_row = placed(
        ((0, o0), (n_z - 1, oa1), (1, ob1), (n_z - 2, oa2), (2, ob2), (n_z - 3, oa3), (3, ob3)),
        oa4,
        ob4,
    )
    partner = jnp.zeros_like(rows)
    for index, offset in enumerate((0, n_x - 1, 1, 2)):
        owner = ((chip + offset) % n_x) * 2
        partner = lax.dynamic_update_slice(
            partner, pieces[index : index + 1], (owner + core, 0, 0)
        )
        partner = lax.dynamic_update_slice(
            partner, others[index : index + 1], (owner + 1 - core, 0, 0)
        )
    return this_row, other_row, cot, partner


def projected(pre, cotangent, gate_projection, up_projection):
    cols = pre.shape[1] // 2
    gate = pre[:, :cols]
    up = pre[:, cols:]
    sigma = jax.nn.sigmoid(gate)
    upstream = cotangent.astype(F32)
    gate_grad = (upstream * up * sigma * (1.0 + gate * (1.0 - sigma))).astype(BF16)
    up_grad = (upstream * gate * sigma).astype(BF16)
    dims = (((1,), (1,)), ((), ()))
    return jnp.concatenate(
        (
            lax.dot_general(gate_projection, gate_grad, dims, preferred_element_type=F32),
            lax.dot_general(up_projection, up_grad, dims, preferred_element_type=F32),
        ),
        axis=0,
    )


def body(
    doc_inputs,
    doc_cotangents,
    query_inputs,
    query_cotangents,
    gate_weight,
    up_weight,
    input_projection,
    gate_projection,
    up_projection,
):
    count, length, width = doc_inputs.shape
    half_index = lax.axis_index("yhi")
    row_index = lax.axis_index("ylo")
    dq = ("x", "core", "yhi")
    fsdp = ("ylo", "z")
    n_dq = lax.axis_size(dq)
    n_fsdp = lax.axis_size(fsdp)
    rank = input_projection.shape[0]
    cols = gate_weight.shape[1]

    own = jnp.concatenate((doc_inputs, query_inputs), axis=1)
    cot = jnp.concatenate((doc_cotangents, query_cotangents), axis=1)
    cot = cot.reshape(-1, cot.shape[2])
    own_cot = lax.dynamic_slice_in_dim(cot, half_index * cols, cols, 1)
    sent_cot = lax.dynamic_slice_in_dim(cot, (1 - half_index) * cols, cols, 1)
    weight = jnp.concatenate((gate_weight, up_weight), axis=1)
    this_row, other_row, other_cot, other = gathered(weight, sent_cot, own)
    gate_proj = lax.dynamic_slice_in_dim(gate_projection, half_index * cols, cols, 1)
    up_proj = lax.dynamic_slice_in_dim(up_projection, half_index * cols, cols, 1)

    parts = []
    factors = []
    depth = this_row.shape[0]
    for rows, rows_cot in ((own, own_cot), (other, other_cot)):
        flat = rows.reshape(-1, width)
        this_flat = lax.dynamic_slice_in_dim(flat, row_index * depth, depth, 1)
        other_flat = lax.dynamic_slice_in_dim(flat, (1 - row_index) * depth, depth, 1)
        pre = jnp.dot(this_flat, this_row, preferred_element_type=F32)
        pre = pre + jnp.dot(other_flat, other_row, preferred_element_type=F32)
        parts.append(projected(pre, rows_cot, gate_proj, up_proj))
        factors.append(
            lax.dot_general(
                flat, input_projection, (((1,), (1,)), ((), ())), preferred_element_type=F32
            )
        )

    first = half_index == 0

    def ordered(pair, axis):
        a = jnp.where(first, pair[0], pair[1])
        b = jnp.where(first, pair[1], pair[0])
        return jnp.concatenate((a, b), axis=axis)

    part = ordered(parts, 1).astype(BF16)
    in_factor = ordered(factors, 0)
    ranks = part.shape[0] // n_dq
    part = part.reshape(n_dq, ranks, -1)
    swapped = lax.all_to_all(part, dq, 0, 0, tiled=True)
    out_sum = jnp.sum(swapped.astype(F32), axis=0)

    pairs = 2 * count
    factor = jnp.einsum(
        "kel,elr->ekr",
        out_sum.reshape(ranks, 2 * pairs, length),
        in_factor.reshape(2 * pairs, length, rank),
        precision=lax.Precision.HIGHEST,
    ).reshape(pairs, 2, ranks * rank)
    docs = factor[:, 0]
    queries = factor[:, 1]
    doc_squares = jnp.sum(docs * docs, axis=1)
    docs = docs.astype(BF16)
    queries = queries.astype(BF16)

    everyone = lax.all_to_all(
        jnp.broadcast_to(queries[None], (n_fsdp,) + queries.shape), fsdp, 0, 0, tiled=True
    ).reshape(n_fsdp * pairs, -1)
    wide = everyone.astype(F32)
    query_squares = jnp.sum(wide * wide, axis=1)
    scores = lax.dot_general(
        docs, everyone, (((1,), (1,)), ((), ())), preferred_element_type=F32
    )
    total = scores.shape[1]

    def to_destinations(x):
        return x.reshape((2, count) + x.shape[1:]).swapaxes(0, 1).reshape(x.shape)

    payload = jnp.concatenate(
        (
            to_destinations(scores),
            jnp.broadcast_to(query_squares[None], (pairs, total)),
            jnp.broadcast_to(to_destinations(doc_squares)[:, None], (pairs, 128)),
        ),
        axis=1,
    )
    received = lax.all_to_all(payload, dq, 0, 0, tiled=True)
    sums = jnp.sum(received, axis=0)
    entries = 1.0 / (rank * 2 * rank)
    doc_scale = lax.rsqrt(sums[2 * total] * entries + 1e-06)
    query_scale = lax.rsqrt(sums[total : 2 * total] * entries + 1e-06)
    result = sums[:total] * query_scale * (doc_scale / rank)
    return result.reshape(1, 1, total)


def solution(mesh):
    fine = jax.sharding.Mesh(
        mesh.devices.reshape(2, mesh.shape["fsdp"] // 2, mesh.shape["dp"] // 2, 2, 2),
        ("ylo", "z", "x", "core", "yhi"),
    )
    fsdp = ("ylo", "z")
    dp = ("x", "core")
    return jax.shard_map(
        body,
        mesh=fine,
        in_specs=(
            P(fsdp + ("yhi",), None, None),
            P(fsdp + ("yhi",), None, dp),
            P(fsdp + ("yhi",), None, None),
            P(fsdp + ("yhi",), None, dp),
            P(fsdp, dp + ("yhi",)),
            P(fsdp, dp + ("yhi",)),
            P(),
            P(None, dp),
            P(None, dp),
        ),
        out_specs=P(fsdp + ("yhi",), dp, None),
        check_vma=False,
    )
```

time: 242 us -> 197 us (0.81)
  waiting for transfers between devices: 126 us -> 81 us
  starting transfers between devices: 30.2 us -> 49.8 us
  between operations: 14.4 us -> 1.28 us
  matrix products: 34.4 us -> 22.6 us
  local copies, waits for them, and re-layouts: 19.5 us -> 23.3 us
    ppermute x10 -> x21, waiting for transfers between devices: 112 us -> 67.5 us  [shift(): lax.ppermute(value, axis, [(i, (i + step) % size) for i in range(size)])]
    ppermute x10 -> x21, starting transfers between devices: 17.9 us -> 36.2 us  [shift(): lax.ppermute(value, axis, [(i, (i + step) % size) for i in range(size)])]
    dot_general x2 -> x4, matrix products: 20.1 us -> 11.6 us  [the longest x2 5.8 us: body(): pre = pre + jnp.dot(other_flat, other_row, preferred_element_type=F32)]
    all_to_all x1, starting transfers between devices: 5.26 us -> 9.03 us  [body(): swapped = lax.all_to_all(part, dq, 0, 0, tiled=True)]
    dot_general x2, matrix products: 9.05 us -> 5.93 us  [body(): lax.dot_general(flat, input_projection, (((1,), (1,)), ((), ())), preferr...]
    concatenate x0 -> x3, other arithmetic: none -> 3.09 us  [the longest x1 1.89 us: gathered(): pieces = jnp.concatenate((here, left, right, far), axis=0)]
    all_to_all x1, starting transfers between devices: 7.06 us -> 4.55 us  [body(): lax.all_to_all(jnp.broadcast_to(queries[None], (n_fsdp,) + queries.shape)...]
    unnamed x17 -> x50, local copies, waits for them, and re-layouts: 4.71 us -> 6.28 us
  transfers between devices with their start and end apart: 13 -> 23, of which waited for: 5 -> 11; matrix products, arithmetic and copies ran while one was open for 19% -> 14% of each run, Pallas kernels for 0% -> 0%
where the time goes in v2:
time: 197 us; the launch traced here: 196 us
  waiting for transfers between devices  81 us (41%)
  starting transfers between devices  49.8 us (25%)
  local copies, waits for them, and re-layouts  23.3 us (12%)
  matrix products  22.6 us (11%)
  blocking collectives  12.1 us (6%)
  other arithmetic  6.23 us (3%)
    ppermute x21, waiting for transfers between devices, shift(): lax.ppermute(value, axis, [(i, (i + step) % size) for i in range(size)])  67.5 us
    ppermute x21, starting transfers between devices, shift(): lax.ppermute(value, axis, [(i, (i + step) % size) for i in range(size)])  36.2 us
    all_to_all x1, blocking collectives, body(): received = lax.all_to_all(payload, dq, 0, 0, tiled=True)  12.1 us
    all_to_all x1, starting transfers between devices, body(): swapped = lax.all_to_all(part, dq, 0, 0, tiled=True)  9.03 us
    all_to_all x1, waiting for transfers between devices, body(): lax.all_to_all(jnp.broadcast_to(queries[None], (n_fsdp,) + queries.shape)...  8.5 us
    unnamed x50, local copies, waits for them, and re-layouts  6.28 us
    dot_general x2, matrix products, body(): lax.dot_general(flat, input_projection, (((1,), (1,)), ((), ())), preferr...  5.93 us
    dot_general x2, matrix products, body(): pre = pre + jnp.dot(other_flat, other_row, preferred_element_type=F32)  5.8 us
  transfers between devices with their start and end apart: 23, of which 11 were waited for; matrix products, arithmetic and copies ran while one was open for 14% of the time, Pallas kernels for 0%

profile of v2, /device:TPU:1, one launch (start us, length us, event | category | flops | bytes accessed | tf_op | source)
XLA Modules:
  0.0 196.3 jit_solution(7279550828675468083)
XLA Ops:
  0.0 3.6 %constant_dynamic-update-slice_fusion.5 = bf16[8,64,5120]{2,1,0:T(8,128)(2,1)} fusion(bf16[8,32,5120]{2,1,0:T(8,128)(2,1)} %param.9), kind=kLoop, calls=%fused_computation.99 | loop fusion | bytes 5242880
  3.6 1.7 constant_dynamic-update-slice_fusion.4
  5.3 1.1 constant_dynamic-slice_fusion.1
  6.4 3.8 %collective-permute-start.2 = (bf16[1,64,5120]{2,1,0:T(8,128)(2,1)S(1)}, bf16[1,64,5120]{2,1,0:T(8,128)(2,1)S(1)}, u32[]{:S(2)}, u32[]{:S(2)}) collective-permute-start(bf16[1,64,5120]{2,1,0:T(8,128)(2,1)S(1)} %constant_dynamic-slice_fusion.1), channel_id=1, source_target_pairs={{0,1},{1,0},{2,3},{3,2},{4,5},{5,4},{6,7},{7,6},{8,9},{9,8},{10,11... | collective-permute-start | bytes 1966088 | tf_op jit(solution)/shard_map/ppermute | solution.py:11
  10.5 1.7 collective-permute-start
  12.2 4.0 %collective-permute-start.1 = (bf16[320,896]{1,0:T(8,128)(2,1)S(1)}, bf16[320,896]{1,0:T(8,128)(2,1)S(1)}, u32[]{:S(2)}, u32[]{:S(2)}) collective-permute-start(bf16[320,896]{1,0:T(8,128)(2,1)S(1)} %pad_maximum_fusion.4), channel_id=1, source_target_pairs={{0,112},{16,0},{32,16},{48,32},{64,48},{80,64},{96,80},{112,96},{1... | collective-permute-start | bytes 1720328 | tf_op jit(solution)/shard_map/ppermute | solution.py:11
  16.2 12.3 %collective-permute-done = bf16[320,896]{1,0:T(8,128)(2,1)S(1)} collective-permute-done((bf16[320,896]{1,0:T(8,128)(2,1)S(1)}, bf16[320,896]{1,0:T(8,128)(2,1)S(1)}, u32[]{:S(2)}, u32[]{:S(2)}) %collective-permute-start) | collective-permute-done | bytes 573472 | tf_op jit(solution)/shard_map/ppermute | solution.py:11
  28.6 2.6 %collective-permute-start.10 = (bf16[1,64,5120]{2,1,0:T(8,128)(2,1)S(1)}, bf16[1,64,5120]{2,1,0:T(8,128)(2,1)S(1)}, u32[]{:S(2)}, u32[]{:S(2)}) collective-permute-start(bf16[1,64,5120]{2,1,0:T(8,128)(2,1)S(1)} %collective-permute-done.2), channel_id=1, source_target_pairs={{0,12},{4,0},{8,4},{12,8},{1,13},{5,1},{9,5},{13,9},{2,14},{6,2},{... | collective-permute-start | bytes 1966088 | tf_op jit(solution)/shard_map/ppermute | solution.py:11
  31.2 2.6 %collective-permute-start.4 = (bf16[320,896]{1,0:T(8,128)(2,1)S(1)}, bf16[320,896]{1,0:T(8,128)(2,1)S(1)}, u32[]{:S(2)}, u32[]{:S(2)}) collective-permute-start(bf16[320,896]{1,0:T(8,128)(2,1)S(1)} %collective-permute-done.1), channel_id=1, source_target_pairs={{0,112},{16,0},{32,16},{48,32},{64,48},{80,64},{96,80},{112,96},{1... | collective-permute-start | bytes 1720328 | tf_op jit(solution)/shard_map/ppermute | solution.py:11
  34.7 8.1 %collective-permute-done.3 = bf16[320,896]{1,0:T(8,128)(2,1)S(1)} collective-permute-done((bf16[320,896]{1,0:T(8,128)(2,1)S(1)}, bf16[320,896]{1,0:T(8,128)(2,1)S(1)}, u32[]{:S(2)}, u32[]{:S(2)}) %collective-permute-start.3) | collective-permute-done | bytes 573472 | tf_op jit(solution)/shard_map/ppermute | solution.py:11
  42.7 1.2 collective-permute-start.9
  43.9 1.9 collective-permute-done.5
  46.3 2.6 %collective-permute-start.7 = (bf16[320,896]{1,0:T(8,128)(2,1)S(1)}, bf16[320,896]{1,0:T(8,128)(2,1)}, u32[]{:S(2)}, u32[]{:S(2)}) collective-permute-start(bf16[320,896]{1,0:T(8,128)(2,1)S(1)} %collective-permute-done.4), channel_id=1, source_target_pairs={{0,112},{16,0},{32,16},{48,32},{64,48},{80,64},{96,80},{112,96},{1... | collective-permute-start | bytes 1720328 | tf_op jit(solution)/shard_map/ppermute | solution.py:11
  49.3 17.0 %collective-permute-done.9 = bf16[1,64,5120]{2,1,0:T(8,128)(2,1)S(1)} collective-permute-done((bf16[1,64,5120]{2,1,0:T(8,128)(2,1)S(1)}, bf16[1,64,5120]{2,1,0:T(8,128)(2,1)S(1)}, u32[]{:S(2)}, u32[]{:S(2)}) %collective-permute-start.9) | collective-permute-done | bytes 655392 | tf_op jit(solution)/shard_map/ppermute | solution.py:11
  67.1 1.9 pad_maximum_fusion
  69.0 3.2 %collective-permute-start.15 = (bf16[4,64,5120]{2,1,0:T(8,128)(2,1)}, bf16[4,64,5120]{2,1,0:T(8,128)(2,1)}, u32[]{:S(2)}, u32[]{:S(2)}) collective-permute-start(bf16[4,64,5120]{2,1,0:T(8,128)(2,1)} %pad_maximum_fusion), channel_id=1, source_target_pairs={{0,2},{2,0},{1,3},{3,1},{4,6},{6,4},{5,7},{7,5},{8,10},{10,8},{9,1... | collective-permute-start | bytes 7864328 | tf_op jit(solution)/shard_map/ppermute | solution.py:11
  72.2 1.3 pad_maximum_fusion.1
  73.4 0.9 copy-done.4
  74.4 1.1 constant_dynamic-slice_fusion
  75.4 1.7 collective-permute-start.18
  79.8 3.2 %collective-permute-start.13 = (bf16[320,896]{1,0:T(8,128)(2,1)S(1)}, bf16[320,896]{1,0:T(8,128)(2,1)S(1)}, u32[]{:S(2)}, u32[]{:S(2)}) collective-permute-start(bf16[320,896]{1,0:T(8,128)(2,1)S(1)} %copy-done.17), channel_id=1, source_target_pairs={{0,112},{16,0},{32,16},{48,32},{64,48},{80,64},{96,80},{112,96},{1... | collective-permute-start | bytes 1720328 | tf_op jit(solution)/shard_map/ppermute | solution.py:11
  84.4 11.7 %collective-permute-done.12 = bf16[320,896]{1,0:T(8,128)(2,1)S(1)} collective-permute-done((bf16[320,896]{1,0:T(8,128)(2,1)S(1)}, bf16[320,896]{1,0:T(8,128)(2,1)S(1)}, u32[]{:S(2)}, u32[]{:S(2)}) %collective-permute-start.12) | collective-permute-done | bytes 573472 | tf_op jit(solution)/shard_map/ppermute | solution.py:11
  96.1 6.0 %collective-permute-done.14 = bf16[320,896]{1,0:T(8,128)(2,1)S(1)} collective-permute-done((bf16[320,896]{1,0:T(8,128)(2,1)S(1)}, bf16[320,896]{1,0:T(8,128)(2,1)S(1)}, u32[]{:S(2)}, u32[]{:S(2)}) %collective-permute-start.14) | collective-permute-done | bytes 573472 | tf_op jit(solution)/shard_map/ppermute | solution.py:11
  102.3 1.1 bitcast_dynamic-update-slice_fusion.3
  103.4 1.1 pad_maximum_fusion.2
  104.6 1.4 collective-permute-start.16
  106.0 1.0 slice.67
  107.1 2.3 %collective-permute-start.17 = (bf16[480,896]{1,0:T(8,128)(2,1)S(1)}, bf16[480,896]{1,0:T(8,128)(2,1)S(1)}, u32[]{:S(2)}, u32[]{:S(2)}) collective-permute-start(bf16[480,896]{1,0:T(8,128)(2,1)S(1)} %pad_maximum_fusion.3), channel_id=1, source_target_pairs={{0,112},{16,0},{32,16},{48,32},{64,48},{80,64},{96,80},{112,96},{1... | collective-permute-start | bytes 2580488 | tf_op jit(solution)/shard_map/ppermute | solution.py:11
  109.4 1.1 slice_dynamic-update-slice_fusion.3
  110.6 1.1 slice_dynamic-update-slice_fusion.2
  111.8 1.1 slice_dynamic-update-slice_fusion.1
  113.0 1.1 slice_dynamic-update-slice_fusion
  114.3 1.1 bitcast_dynamic-update-slice_fusion.7
  115.4 1.7 fusion.57
  117.2 9.7 %collective-permute-done.16 = bf16[480,896]{1,0:T(8,128)(2,1)S(1)} collective-permute-done((bf16[480,896]{1,0:T(8,128)(2,1)S(1)}, bf16[480,896]{1,0:T(8,128)(2,1)S(1)}, u32[]{:S(2)}, u32[]{:S(2)}) %collective-permute-start.16) | collective-permute-done | bytes 860192 | tf_op jit(solution)/shard_map/ppermute | solution.py:11
  127.4 2.7 %collective-permute-start.19 = (bf16[160,896]{1,0:T(8,128)(2,1)S(1)}, bf16[160,896]{1,0:T(8,128)(2,1)S(1)}, u32[]{:S(2)}, u32[]{:S(2)}) collective-permute-start(bf16[160,896]{1,0:T(8,128)(2,1)S(1)} %slice.72), channel_id=1, source_target_pairs={{0,16},{16,32},{32,48},{48,64},{64,80},{80,96},{96,112},{112,0},{1... | collective-permute-start | bytes 860168 | tf_op jit(solution)/shard_map/ppermute | solution.py:11
  131.0 2.9 %fusion.2 = f32[512,896]{1,0:T(8,128)S(1)} fusion(bf16[2560,896]{1,0:T(8,128)(2,1)S(1)} %bitcast.82, bf16[512,5120]{1,0:T(8,128)(2,1)S(1)} %bitcast.73, s32[]{:T(128)S(6)} %select_n.178), kind=kOutput, calls=%fused_computation.3 | convolution fusion | flops 2348810240 | bytes 9043972 | tf_op jit(solution)/shard_map/dot_general | solution.py:137
  133.9 2.9 %fusion.6 = f32[512,896]{1,0:T(8,128)S(1)} fusion(bf16[2560,896]{1,0:T(8,128)(2,1)S(1)} %bitcast.83, bf16[512,5120]{1,0:T(8,128)(2,1)S(1)} %bitcast.78, s32[]{:T(128)S(6)} %select_n.178), kind=kOutput, calls=%fused_computation.7 | convolution fusion | flops 2348810240 | bytes 9043972 | tf_op jit(solution)/shard_map/dot_general | solution.py:137
  137.1 2.9 %fusion.8 = f32[512,896]{1,0:T(8,128)S(1)} fusion(f32[512,896]{1,0:T(8,128)S(1)} %fusion.6, bf16[2560,896]{1,0:T(8,128)(2,1)S(1)} %bitcast.80, bf16[512,5120]{1,0:T(8,128)(2,1)S(1)} %bitcast.79, s32[]{:T(128)S(6)} %select_n.197), kind=kOutput, calls=%fused_computation.9 | convolution fusion | flops 2349268992 | bytes 10878980 | tf_op jit(solution)/shard_map/dot_general | solution.py:138
  141.4 2.9 %fusion.11 = f32[512,896]{1,0:T(8,128)S(1)} fusion(f32[512,896]{1,0:T(8,128)S(1)} %fusion.2, bf16[2560,896]{1,0:T(8,128)(2,1)S(1)} %bitcast.81, bf16[512,5120]{1,0:T(8,128)(2,1)S(1)} %bitcast.74, s32[]{:T(128)S(6)} %select_n.197), kind=kOutput, calls=%fused_computation.10 | convolution fusion | flops 2349268992 | bytes 10878980 | tf_op jit(solution)/shard_map/dot_general | solution.py:138
  144.4 1.7 fusion.28
  146.0 1.5 fusion.24
  148.3 9.0 %all-to-all-start = ((bf16[16,8,1024]{2,1,0:T(8,128)(2,1)}), bf16[16,8,1024]{2,1,0:T(8,128)(2,1)S(1)}, u32[]{:S(2)}, u32[]{:S(2)}) async-start(bf16[16,8,1024]{2,1,0:T(8,128)(2,1)} %pad_maximum_fusion.7), calls=%async_computation | async-start | bytes 524288 | tf_op jit(solution)/shard_map/all_to_all | solution.py:157
  157.3 4.2 %broadcast_select_fusion.1 = (f32[512,64]{0,1:T(8,128)S(1)}, f32[512,64]{0,1:T(8,128)S(1)}) fusion(f32[512,64]{0,1:T(8,128)S(1)} %fusion.57, pred[]{:T(512)S(6)} %eq.24, bf16[512,5120]{1,0:T(8,128)(2,1)} %bitcast.75, bf16[64,5120]{1,0:T(8,128)(2,1)S(1)} %copy-done), kind=kOutput, calls=%fused_computation.73 | convolution fusion | flops 335609856 | bytes 6291457 | tf_op jit(solution)/shard_map/dot_general | solution.py:141
  161.8 4.9 %all-to-all-done = bf16[16,8,1024]{2,1,0:T(8,128)(2,1)S(1)} async-done(((bf16[16,8,1024]{2,1,0:T(8,128)(2,1)}), bf16[16,8,1024]{2,1,0:T(8,128)(2,1)S(1)}, u32[]{:S(2)}, u32[]{:S(2)}) %all-to-all-start) | async-done | bytes 262176 | tf_op jit(solution)/shard_map/all_to_all | solution.py:157
  168.3 4.6 %all-to-all-start.1 = ((bf16[16,16,512]{2,1,0:T(8,128)(2,1)}), bf16[16,16,512]{2,1,0:T(8,128)(2,1)S(1)}, u32[]{:S(2)}, u32[]{:S(2)}) async-start(bf16[16,16,512]{2,1,0:T(8,128)(2,1)} %broadcast_in_dim.97), calls=%async_computation.1 | async-start | bytes 524288 | tf_op jit(solution)/shard_map/all_to_all | solution.py:173
  173.3 8.5 %all-to-all-done.1 = bf16[16,16,512]{2,1,0:T(8,128)(2,1)S(1)} async-done(((bf16[16,16,512]{2,1,0:T(8,128)(2,1)}), bf16[16,16,512]{2,1,0:T(8,128)(2,1)S(1)}, u32[]{:S(2)}, u32[]{:S(2)}) %all-to-all-start.1) | async-done | bytes 262176 | tf_op jit(solution)/shard_map/all_to_all | solution.py:173
  182.4 12.1 %all_to_all.19 = f32[16,1,640]{2,1,0:T(1,128)S(1)} all-to-all(f32[16,1,640]{2,1,0:T(1,128)S(1)} %copy.24), channel_id=1, replica_groups=mesh['ylo'=2,'z'=8,'x'=4,'core'=2,'yhi'=2] {'x','core','yhi'}, dimensions={0} | all-to-all | bytes 81920 | tf_op jit(solution)/shard_map/all_to_all | solution.py:194
  (128 shorter events, 15.1 us)
Async XLA Ops:
  0.0 115.4 %copy-start = (bf16[64,5120]{1,0:T(8,128)(2,1)S(1)}, bf16[64,5120]{1,0:T(8,128)(2,1)}, u32[]{:S(2)}) copy-start(bf16[64,5120]{1,0:T(8,128)(2,1)} %param.15) | copy-start | bytes 1966084
  0.0 3.6 %copy-start.1 = (bf16[8,32,5120]{2,1,0:T(8,128)(2,1)S(1)}, bf16[8,32,5120]{2,1,0:T(8,128)(2,1)}, u32[]{:S(2)}) copy-start(bf16[8,32,5120]{2,1,0:T(8,128)(2,1)} %param.11) | copy-start | bytes 7864324
  3.6 6.7 %copy-start.18 = (bf16[320,448]{1,0:T(8,128)(2,1)S(1)}, bf16[320,448]{1,0:T(8,128)(2,1)}, u32[]{:S(2)}) copy-start(bf16[320,448]{1,0:T(8,128)(2,1)} %param.14) | copy-start | bytes 860164
  3.6 6.7 %copy-start.19 = (bf16[320,448]{1,0:T(8,128)(2,1)S(1)}, bf16[320,448]{1,0:T(8,128)(2,1)}, u32[]{:S(2)}) copy-start(bf16[320,448]{1,0:T(8,128)(2,1)} %param.13) | copy-start | bytes 860164
  6.4 22.1 %collective-permute-start.2 = (bf16[1,64,5120]{2,1,0:T(8,128)(2,1)S(1)}, bf16[1,64,5120]{2,1,0:T(8,128)(2,1)S(1)}, u32[]{:S(2)}, u32[]{:S(2)}) collective-permute-start(bf16[1,64,5120]{2,1,0:T(8,128)(2,1)S(1)} %constant_dynamic-slice_fusion.1), channel_id=1, source_target_pairs={{0,1},{1,0},{2,3},{3,2},{4,5},{5,4},{6,7},{7,6},{8,9},{9,8},{10,11... | collective-permute-start | bytes 1966088 | tf_op jit(solution)/shard_map/ppermute | solution.py:11
  10.5 55.8 %copy-start.2 = (bf16[320,896]{1,0:T(8,128)(2,1)}, bf16[320,896]{1,0:T(8,128)(2,1)S(1)}, u32[]{:S(2)}) copy-start(bf16[320,896]{1,0:T(8,128)(2,1)S(1)} %pad_maximum_fusion.4) | copy-start | bytes 1720324
  10.5 18.0 %collective-permute-start = (bf16[320,896]{1,0:T(8,128)(2,1)S(1)}, bf16[320,896]{1,0:T(8,128)(2,1)S(1)}, u32[]{:S(2)}, u32[]{:S(2)}) collective-permute-start(bf16[320,896]{1,0:T(8,128)(2,1)S(1)} %pad_maximum_fusion.4), channel_id=1, source_target_pairs={{0,16},{16,32},{32,48},{48,64},{64,80},{80,96},{96,112},{112,0},{1... | collective-permute-start | bytes 1720328 | tf_op jit(solution)/shard_map/ppermute | solution.py:11
  12.2 16.3 %collective-permute-start.1 = (bf16[320,896]{1,0:T(8,128)(2,1)S(1)}, bf16[320,896]{1,0:T(8,128)(2,1)S(1)}, u32[]{:S(2)}, u32[]{:S(2)}) collective-permute-start(bf16[320,896]{1,0:T(8,128)(2,1)S(1)} %pad_maximum_fusion.4), channel_id=1, source_target_pairs={{0,112},{16,0},{32,16},{48,32},{64,48},{80,64},{96,80},{112,96},{1... | collective-permute-start | bytes 1720328 | tf_op jit(solution)/shard_map/ppermute | solution.py:11
  28.5 6.2 %copy-start.12 = (bf16[320,896]{1,0:T(8,128)(2,1)}, bf16[320,896]{1,0:T(8,128)(2,1)S(1)}, u32[]{:S(2)}) copy-start(bf16[320,896]{1,0:T(8,128)(2,1)S(1)} %collective-permute-done) | copy-start | bytes 1720324
  28.5 15.4 %copy-start.8 = (bf16[320,896]{1,0:T(8,128)(2,1)}, bf16[320,896]{1,0:T(8,128)(2,1)S(1)}, u32[]{:S(2)}) copy-start(bf16[320,896]{1,0:T(8,128)(2,1)S(1)} %collective-permute-done.1) | copy-start | bytes 1720324
  28.5 14.2 %collective-permute-start.3 = (bf16[320,896]{1,0:T(8,128)(2,1)S(1)}, bf16[320,896]{1,0:T(8,128)(2,1)S(1)}, u32[]{:S(2)}, u32[]{:S(2)}) collective-permute-start(bf16[320,896]{1,0:T(8,128)(2,1)S(1)} %collective-permute-done), channel_id=1, source_target_pairs={{0,16},{16,32},{32,48},{48,64},{64,80},{80,96},{96,112},{112,0},{1... | collective-permute-start | bytes 1720328 | tf_op jit(solution)/shard_map/ppermute | solution.py:11
  28.6 17.7 %collective-permute-start.10 = (bf16[1,64,5120]{2,1,0:T(8,128)(2,1)S(1)}, bf16[1,64,5120]{2,1,0:T(8,128)(2,1)S(1)}, u32[]{:S(2)}, u32[]{:S(2)}) collective-permute-start(bf16[1,64,5120]{2,1,0:T(8,128)(2,1)S(1)} %collective-permute-done.2), channel_id=1, source_target_pairs={{0,12},{4,0},{8,4},{12,8},{1,13},{5,1},{9,5},{13,9},{2,14},{6,2},{... | collective-permute-start | bytes 1966088 | tf_op jit(solution)/shard_map/ppermute | solution.py:11
  31.2 12.8 %collective-permute-start.4 = (bf16[320,896]{1,0:T(8,128)(2,1)S(1)}, bf16[320,896]{1,0:T(8,128)(2,1)S(1)}, u32[]{:S(2)}, u32[]{:S(2)}) collective-permute-start(bf16[320,896]{1,0:T(8,128)(2,1)S(1)} %collective-permute-done.1), channel_id=1, source_target_pairs={{0,112},{16,0},{32,16},{48,32},{64,48},{80,64},{96,80},{112,96},{1... | collective-permute-start | bytes 1720328 | tf_op jit(solution)/shard_map/ppermute | solution.py:11
  33.7 12.1 %collective-permute-start.5 = (bf16[320,896]{1,0:T(8,128)(2,1)S(1)}, bf16[320,896]{1,0:T(8,128)(2,1)S(1)}, u32[]{:S(2)}, u32[]{:S(2)}) collective-permute-start(bf16[320,896]{1,0:T(8,128)(2,1)S(1)} %pad_maximum_fusion.4), channel_id=1, source_target_pairs={{0,128},{128,0},{1,129},{129,1},{2,130},{130,2},{3,131},{131,3},{4... | collective-permute-start | bytes 1720328 | tf_op jit(solution)/shard_map/ppermute | solution.py:11
  34.1 15.1 %collective-permute-start.11 = (bf16[1,64,5120]{2,1,0:T(8,128)(2,1)S(1)}, bf16[1,64,5120]{2,1,0:T(8,128)(2,1)S(1)}, u32[]{:S(2)}, u32[]{:S(2)}) collective-permute-start(bf16[1,64,5120]{2,1,0:T(8,128)(2,1)S(1)} %collective-permute-done.2), channel_id=1, source_target_pairs={{0,8},{4,12},{8,0},{12,4},{1,9},{5,13},{9,1},{13,5},{2,10},{6,14},... | collective-permute-start | bytes 1966088 | tf_op jit(solution)/shard_map/ppermute | solution.py:11
  42.7 24.3 %copy-start.10 = (bf16[320,896]{1,0:T(8,128)(2,1)}, bf16[320,896]{1,0:T(8,128)(2,1)S(1)}, u32[]{:S(2)}) copy-start(bf16[320,896]{1,0:T(8,128)(2,1)S(1)} %collective-permute-done.3) | copy-start | bytes 1720324
  42.7 23.5 %collective-permute-start.9 = (bf16[1,64,5120]{2,1,0:T(8,128)(2,1)S(1)}, bf16[1,64,5120]{2,1,0:T(8,128)(2,1)S(1)}, u32[]{:S(2)}, u32[]{:S(2)}) collective-permute-start(bf16[1,64,5120]{2,1,0:T(8,128)(2,1)S(1)} %collective-permute-done.2), channel_id=1, source_target_pairs={{0,4},{4,8},{8,12},{12,0},{1,5},{5,9},{9,13},{13,1},{2,6},{6,10},{... | collective-permute-start | bytes 1966088 | tf_op jit(solution)/shard_map/ppermute | solution.py:11
  43.9 23.1 %copy-start.14 = (bf16[320,896]{1,0:T(8,128)(2,1)}, bf16[320,896]{1,0:T(8,128)(2,1)S(1)}, u32[]{:S(2)}) copy-start(bf16[320,896]{1,0:T(8,128)(2,1)S(1)} %collective-permute-done.4) | copy-start | bytes 1720324
  45.8 21.3 %copy-start.16 = (bf16[320,896]{1,0:T(8,128)(2,1)}, bf16[320,896]{1,0:T(8,128)(2,1)S(1)}, u32[]{:S(2)}) copy-start(bf16[320,896]{1,0:T(8,128)(2,1)S(1)} %collective-permute-done.5) | copy-start | bytes 1720324
  45.8 20.4 %collective-permute-start.6 = (bf16[320,896]{1,0:T(8,128)(2,1)S(1)}, bf16[320,896]{1,0:T(8,128)(2,1)S(1)}, u32[]{:S(2)}, u32[]{:S(2)}) collective-permute-start(bf16[320,896]{1,0:T(8,128)(2,1)S(1)} %collective-permute-done.3), channel_id=1, source_target_pairs={{0,16},{16,32},{32,48},{48,64},{64,80},{80,96},{96,112},{112,0},{1... | collective-permute-start | bytes 1720328 | tf_op jit(solution)/shard_map/ppermute | solution.py:11
  45.9 21.2 %collective-permute-start.8 = (bf16[320,896]{1,0:T(8,128)(2,1)S(1)}, bf16[320,896]{1,0:T(8,128)(2,1)}, u32[]{:S(2)}, u32[]{:S(2)}) collective-permute-start(bf16[320,896]{1,0:T(8,128)(2,1)S(1)} %collective-permute-done.3), channel_id=1, source_target_pairs={{0,128},{128,0},{1,129},{129,1},{2,130},{130,2},{3,131},{131,3},{4... | collective-permute-start | bytes 1720328 | tf_op jit(solution)/shard_map/ppermute | solution.py:11
  46.3 20.8 %collective-permute-start.7 = (bf16[320,896]{1,0:T(8,128)(2,1)S(1)}, bf16[320,896]{1,0:T(8,128)(2,1)}, u32[]{:S(2)}, u32[]{:S(2)}) collective-permute-start(bf16[320,896]{1,0:T(8,128)(2,1)S(1)} %collective-permute-done.4), channel_id=1, source_target_pairs={{0,112},{16,0},{32,16},{48,32},{64,48},{80,64},{96,80},{112,96},{1... | collective-permute-start | bytes 1720328 | tf_op jit(solution)/shard_map/ppermute | solution.py:11
  66.2 0.8 copy-start.6
  69.0 33.1 %collective-permute-start.15 = (bf16[4,64,5120]{2,1,0:T(8,128)(2,1)}, bf16[4,64,5120]{2,1,0:T(8,128)(2,1)}, u32[]{:S(2)}, u32[]{:S(2)}) collective-permute-start(bf16[4,64,5120]{2,1,0:T(8,128)(2,1)} %pad_maximum_fusion), channel_id=1, source_target_pairs={{0,2},{2,0},{1,3},{3,1},{4,6},{6,4},{5,7},{7,5},{8,10},{10,8},{9,1... | collective-permute-start | bytes 7864328 | tf_op jit(solution)/shard_map/ppermute | solution.py:11
  73.4 0.9 copy-start.4
  75.4 41.7 %collective-permute-start.18 = (bf16[512,448]{1,0:T(8,128)(2,1)}, bf16[512,448]{1,0:T(8,128)(2,1)}, u32[]{:S(2)}, u32[]{:S(2)}) collective-permute-start(bf16[512,448]{1,0:T(8,128)(2,1)} %constant_dynamic-slice_fusion), channel_id=1, source_target_pairs={{0,1},{1,0},{2,3},{3,2},{4,5},{5,4},{6,7},{7,6},{8,9},{9,8},{10,11... | collective-permute-start | bytes 1376264 | tf_op jit(solution)/shard_map/ppermute | solution.py:11
  77.1 1.1 copy-start.3
  77.1 1.2 copy-start.13
  78.2 1.1 copy-start.17
  78.2 4.8 %copy-start.15 = (bf16[320,896]{1,0:T(8,128)(2,1)S(1)}, bf16[320,896]{1,0:T(8,128)(2,1)}, u32[]{:S(2)}) copy-start(bf16[320,896]{1,0:T(8,128)(2,1)} %copy-done.14) | copy-start | bytes 1720324
  78.2 5.2 %copy-start.9 = (bf16[320,896]{1,0:T(8,128)(2,1)S(1)}, bf16[320,896]{1,0:T(8,128)(2,1)}, u32[]{:S(2)}) copy-start(bf16[320,896]{1,0:T(8,128)(2,1)} %copy-done.8) | copy-start | bytes 1720324
  78.4 5.1 %copy-start.11 = (bf16[320,896]{1,0:T(8,128)(2,1)S(1)}, bf16[320,896]{1,0:T(8,128)(2,1)}, u32[]{:S(2)}) copy-start(bf16[320,896]{1,0:T(8,128)(2,1)} %copy-done.10) | copy-start | bytes 1720324
  79.3 16.8 %collective-permute-start.12 = (bf16[320,896]{1,0:T(8,128)(2,1)S(1)}, bf16[320,896]{1,0:T(8,128)(2,1)S(1)}, u32[]{:S(2)}, u32[]{:S(2)}) collective-permute-start(bf16[320,896]{1,0:T(8,128)(2,1)S(1)} %copy-done.17), channel_id=1, source_target_pairs={{0,16},{16,32},{32,48},{48,64},{64,80},{80,96},{96,112},{112,0},{1... | collective-permute-start | bytes 1720328 | tf_op jit(solution)/shard_map/ppermute | solution.py:11
  79.8 16.2 %collective-permute-start.13 = (bf16[320,896]{1,0:T(8,128)(2,1)S(1)}, bf16[320,896]{1,0:T(8,128)(2,1)S(1)}, u32[]{:S(2)}, u32[]{:S(2)}) collective-permute-start(bf16[320,896]{1,0:T(8,128)(2,1)S(1)} %copy-done.17), channel_id=1, source_target_pairs={{0,112},{16,0},{32,16},{48,32},{64,48},{80,64},{96,80},{112,96},{1... | collective-permute-start | bytes 1720328 | tf_op jit(solution)/shard_map/ppermute | solution.py:11
  83.0 19.1 %collective-permute-start.14 = (bf16[320,896]{1,0:T(8,128)(2,1)S(1)}, bf16[320,896]{1,0:T(8,128)(2,1)S(1)}, u32[]{:S(2)}, u32[]{:S(2)}) collective-permute-start(bf16[320,896]{1,0:T(8,128)(2,1)S(1)} %copy-done.15), channel_id=1, source_target_pairs={{0,128},{128,0},{1,129},{129,1},{2,130},{130,2},{3,131},{131,3},{4... | collective-permute-start | bytes 1720328 | tf_op jit(solution)/shard_map/ppermute | solution.py:11
  83.6 19.8 %slice-start.2 = ((bf16[320,896]{1,0:T(8,128)(2,1)}), bf16[160,896]{1,0:T(8,128)(2,1)S(1)}, s32[]{:S(2)}) async-start(bf16[320,896]{1,0:T(8,128)(2,1)} %copy-done.6), calls=%async_computation.5 | async-start | bytes 573440 | tf_op jit(solution)/shard_map/slice | solution.py:43
  104.6 22.3 %collective-permute-start.16 = (bf16[480,896]{1,0:T(8,128)(2,1)S(1)}, bf16[480,896]{1,0:T(8,128)(2,1)S(1)}, u32[]{:S(2)}, u32[]{:S(2)}) collective-permute-start(bf16[480,896]{1,0:T(8,128)(2,1)S(1)} %pad_maximum_fusion.2), channel_id=1, source_target_pairs={{0,16},{16,32},{32,48},{48,64},{64,80},{80,96},{96,112},{112,0},{1... | collective-permute-start | bytes 2580488 | tf_op jit(solution)/shard_map/ppermute | solution.py:11
  107.1 7.1 %copy-start.7 = (bf16[320,896]{1,0:T(8,128)(2,1)S(1)}, bf16[320,896]{1,0:T(8,128)(2,1)}, u32[]{:S(2)}) copy-start(bf16[320,896]{1,0:T(8,128)(2,1)} %copy-done.6) | copy-start | bytes 1720324
  107.1 20.2 %collective-permute-start.17 = (bf16[480,896]{1,0:T(8,128)(2,1)S(1)}, bf16[480,896]{1,0:T(8,128)(2,1)S(1)}, u32[]{:S(2)}, u32[]{:S(2)}) collective-permute-start(bf16[480,896]{1,0:T(8,128)(2,1)S(1)} %pad_maximum_fusion.3), channel_id=1, source_target_pairs={{0,112},{16,0},{32,16},{48,32},{64,48},{80,64},{96,80},{112,96},{1... | collective-permute-start | bytes 2580488 | tf_op jit(solution)/shard_map/ppermute | solution.py:11
  127.4 9.6 %collective-permute-start.19 = (bf16[160,896]{1,0:T(8,128)(2,1)S(1)}, bf16[160,896]{1,0:T(8,128)(2,1)S(1)}, u32[]{:S(2)}, u32[]{:S(2)}) collective-permute-start(bf16[160,896]{1,0:T(8,128)(2,1)S(1)} %slice.72), channel_id=1, source_target_pairs={{0,16},{16,32},{32,48},{48,64},{64,80},{80,96},{96,112},{112,0},{1... | collective-permute-start | bytes 860168 | tf_op jit(solution)/shard_map/ppermute | solution.py:11
  130.1 6.9 %collective-permute-start.20 = (bf16[160,896]{1,0:T(8,128)(2,1)S(1)}, bf16[160,896]{1,0:T(8,128)(2,1)S(1)}, u32[]{:S(2)}, u32[]{:S(2)}) collective-permute-start(bf16[160,896]{1,0:T(8,128)(2,1)S(1)} %slice.73), channel_id=1, source_target_pairs={{0,112},{16,0},{32,16},{48,32},{64,48},{80,64},{96,80},{112,96},{1... | collective-permute-start | bytes 860168 | tf_op jit(solution)/shard_map/ppermute | solution.py:11
  130.9 3.0 %slice-start = ((s8[5242880]{0:T(1024)(128)(4,1)}), s8[4194304]{0:T(1024)(128)(4,1)S(1)}, s32[]{:S(2)}) async-start(s8[5242880]{0:T(1024)(128)(4,1)} %bitcast.76), calls=%async_computation.3 | async-start | bytes 8388608
  131.0 2.9 %slice-start.1 = ((s8[5242880]{0:T(1024)(128)(4,1)}), s8[1048576]{0:T(1024)(128)(4,1)S(1)}, s32[]{:S(2)}) async-start(s8[5242880]{0:T(1024)(128)(4,1)} %bitcast.76), calls=%async_computation.4 | async-start | bytes 2097152
  137.1 2.9 %copy-start.5 = (bf16[8,64,896]{2,1,0:T(8,128)(2,1)S(1)}, bf16[8,64,896]{2,1,0:T(8,128)(2,1)}, u32[]{:S(2)}) copy-start(bf16[8,64,896]{2,1,0:T(8,128)(2,1)} %copy-done.4) | copy-start | bytes 2752516
  137.1 2.9 %copy-start.20 = (bf16[64,896]{1,0:T(8,128)(2,1)S(1)}, bf16[64,896]{1,0:T(8,128)(2,1)}, u32[]{:S(2)}) copy-start(bf16[64,896]{1,0:T(8,128)(2,1)} %param.16) | copy-start | bytes 344068
  140.0 0.9 copy-start.21
  148.3 18.4 %all-to-all-start = ((bf16[16,8,1024]{2,1,0:T(8,128)(2,1)}), bf16[16,8,1024]{2,1,0:T(8,128)(2,1)S(1)}, u32[]{:S(2)}, u32[]{:S(2)}) async-start(bf16[16,8,1024]{2,1,0:T(8,128)(2,1)} %pad_maximum_fusion.7), calls=%async_computation | async-start | bytes 524288 | tf_op jit(solution)/shard_map/all_to_all | solution.py:157
  168.3 13.5 %all-to-all-start.1 = ((bf16[16,16,512]{2,1,0:T(8,128)(2,1)}), bf16[16,16,512]{2,1,0:T(8,128)(2,1)S(1)}, u32[]{:S(2)}, u32[]{:S(2)}) async-start(bf16[16,16,512]{2,1,0:T(8,128)(2,1)} %broadcast_in_dim.97), calls=%async_computation.1 | async-start | bytes 524288 | tf_op jit(solution)/shard_map/all_to_all | solution.py:173

commit v3 on v2

--- a/solution.py
+++ b/solution.py
@@ -11,14 +11,12 @@
     return lax.ppermute(value, axis, [(i, (i + step) % size) for i in range(size)])
 
 
-def gathered(weight, cot, rows):
+def gathered(weight, piece, cot):
     barrier = lax.optimization_barrier
     n_z = lax.axis_size("z")
-    n_x = lax.axis_size("x")
     z = lax.axis_index("z")
-    chip = lax.axis_index("x")
-    core = lax.axis_index("core")
-    half = weight.shape[0] // 2
+    full = weight.shape[0]
+    half = full // 2
 
     def up(value):
         return shift(value, "z", 1)
@@ -29,53 +27,35 @@
     def across(value):
         return shift(value, "ylo", 1)
 
-    mine = lax.dynamic_slice_in_dim(rows, chip * 2 + core, 1, 0)
-    a1, b1, here, w0 = barrier((up(weight), down(weight), shift(mine, "yhi", 1), weight))
-    left, right, far = shift(here, "x", 1), shift(here, "x", -1), shift(here, "x", 2)
-    a2, b2, o0 = barrier((up(a1), down(b1), across(w0)))
-    a3, b3, oa2, o0, b2, left, right, far = barrier(
-        (up(a2), down(b2), across(a2), o0, b2, left, right, far)
-    )
-    pieces = jnp.concatenate((here, left, right, far), axis=0)
-    oa1, ob1, ob2, others, a3, b3, oa2 = barrier(
-        (up(o0), down(o0), across(b2), shift(pieces, "core", 1), a3, b3, oa2)
-    )
-    up_pair = up(jnp.concatenate((oa2, a3[:half]), axis=0))
-    down_pair = down(jnp.concatenate((ob2, b3[half:]), axis=0))
-    up_pair, down_pair, cot = barrier((up_pair, down_pair, shift(cot, "yhi", 1)))
-    full = 2 * half
-    oa3, a4 = up_pair[:full], up_pair[full:]
-    ob3, b4 = down_pair[:full], down_pair[full:]
-    oa4 = up(oa3[:half])
-    ob4 = down(ob3[half:])
-
-    def placed(by_offset, high, low):
+    def placed(by_offset):
         result = jnp.zeros((n_z,) + weight.shape, weight.dtype)
         for offset, shard in by_offset:
             result = lax.dynamic_update_slice(result, shard[None], ((z + offset) % n_z, 0, 0))
-        far_z = (z + n_z // 2) % n_z
-        result = lax.dynamic_update_slice(result, high[None], (far_z, 0, 0))
-        result = lax.dynamic_update_slice(result, low[None], (far_z, half, 0))
-        return result.reshape(n_z * full, -1)
+        return result
+
+    a1, b1, here, w0, cot = barrier(
+        (up(weight), down(weight), shift(piece, "yhi", 1), weight, cot)
+    )
+    partner = lax.all_gather(here, ("x", "core"), axis=0, tiled=True)
+    a2, b2, o0 = barrier((up(a1), down(b1), across(w0)))
+    a3, b3, oa2, o0, b2 = barrier((up(a2), down(b2), across(a2), o0, b2))
+    oa1, ob1, ob2, a4, b4, oa2, cot = barrier(
+        (up(o0), down(o0), across(b2), up(a3[:half]), down(b3[half:]), oa2, cot)
+    )
+    oa3, ob3, other_cot = barrier((up(oa2), down(ob2), shift(cot, "yhi", 1)))
+    far = (up(oa3[:half]), down(ob3[half:]))
 
     this_row = placed(
-        ((0, w0), (n_z - 1, a1), (1, b1), (n_z - 2, a2), (2, b2), (n_z - 3, a3), (3, b3)), a4, b4
-    )
+        ((0, w0), (n_z - 1, a1), (1, b1), (n_z - 2, a2), (2, b2), (n_z - 3, a3), (3, b3))
+    )
+    far_z = (z + n_z // 2) % n_z
+    this_row = lax.dynamic_update_slice(this_row, a4[None], (far_z, 0, 0))
+    this_row = lax.dynamic_update_slice(this_row, b4[None], (far_z, half, 0))
     other_row = placed(
-        ((0, o0), (n_z - 1, oa1), (1, ob1), (n_z - 2, oa2), (2, ob2), (n_z - 3, oa3), (3, ob3)),
-        oa4,
-        ob4,
-    )
-    partner = jnp.zeros_like(rows)
-    for index, offset in enumerate((0, n_x - 1, 1, 2)):
-        owner = ((chip + offset) % n_x) * 2
-        partner = lax.dynamic_update_slice(
-            partner, pieces[index : index + 1], (owner + core, 0, 0)
-        )
-        partner = lax.dynamic_update_slice(
-            partner, others[index : index + 1], (owner + 1 - core, 0, 0)
-        )
-    return this_row, other_row, cot, partner
+        ((0, o0), (n_z - 1, oa1), (1, ob1), (n_z - 2, oa2), (2, ob2), (n_z - 3, oa3), (3, ob3))
+    )
+    flat = (n_z * full, -1)
+    return this_row.reshape(flat), other_row.reshape(flat), far, far_z, other_cot, partner
 
 
 def projected(pre, cotangent, gate_projection, up_projection):
@@ -117,31 +97,56 @@
     rank = input_projection.shape[0]
     cols = gate_weight.shape[1]
 
+    place = lax.axis_index(("x", "core"))
+    piece = jnp.concatenate(
+        (
+            lax.dynamic_slice_in_dim(doc_inputs, place, 1, 0),
+            lax.dynamic_slice_in_dim(query_inputs, place, 1, 0),
+        ),
+        axis=1,
+    )
     own = jnp.concatenate((doc_inputs, query_inputs), axis=1)
-    cot = jnp.concatenate((doc_cotangents, query_cotangents), axis=1)
-    cot = cot.reshape(-1, cot.shape[2])
-    own_cot = lax.dynamic_slice_in_dim(cot, half_index * cols, cols, 1)
-    sent_cot = lax.dynamic_slice_in_dim(cot, (1 - half_index) * cols, cols, 1)
+
+    def columns(value, index):
+        return lax.dynamic_slice_in_dim(value, index * cols, cols, value.ndim - 1)
+
+    def cotangents(index):
+        joined = jnp.concatenate(
+            (columns(doc_cotangents, index), columns(query_cotangents, index)), axis=1
+        )
+        return joined.reshape(-1, cols)
+
+    own_cot = cotangents(half_index)
     weight = jnp.concatenate((gate_weight, up_weight), axis=1)
-    this_row, other_row, other_cot, other = gathered(weight, sent_cot, own)
+    this_row, other_row, far, far_z, other_cot, other = gathered(
+        weight, piece, cotangents(1 - half_index)
+    )
     gate_proj = lax.dynamic_slice_in_dim(gate_projection, half_index * cols, cols, 1)
     up_proj = lax.dynamic_slice_in_dim(up_projection, half_index * cols, cols, 1)
 
-    parts = []
-    factors = []
     depth = this_row.shape[0]
-    for rows, rows_cot in ((own, own_cot), (other, other_cot)):
+    both = []
+    for rows in (own, other):
         flat = rows.reshape(-1, width)
         this_flat = lax.dynamic_slice_in_dim(flat, row_index * depth, depth, 1)
         other_flat = lax.dynamic_slice_in_dim(flat, (1 - row_index) * depth, depth, 1)
         pre = jnp.dot(this_flat, this_row, preferred_element_type=F32)
         pre = pre + jnp.dot(other_flat, other_row, preferred_element_type=F32)
+        far_flat = lax.dynamic_slice_in_dim(
+            other_flat, far_z * weight.shape[0], weight.shape[0], 1
+        )
+        in_factor = lax.dot_general(
+            flat, input_projection, (((1,), (1,)), ((), ())), preferred_element_type=F32
+        )
+        both.append((pre, far_flat, in_factor))
+    both, far = lax.optimization_barrier((both, far))
+    far = jnp.concatenate(far, axis=0)
+    parts = []
+    factors = []
+    for (pre, far_flat, in_factor), rows_cot in zip(both, (own_cot, other_cot)):
+        pre = pre + jnp.dot(far_flat, far, preferred_element_type=F32)
         parts.append(projected(pre, rows_cot, gate_proj, up_proj))
-        factors.append(
-            lax.dot_general(
-                flat, input_projection, (((1,), (1,)), ((), ())), preferred_element_type=F32
-            )
-        )
+        factors.append(in_factor)
 
     first = half_index == 0
 

time: 197 us -> 188 us (0.954)
  waiting for transfers between devices: 81 us -> 63 us
  between operations: 1.28 us -> 14.7 us
  local copies, waits for them, and re-layouts: 23.3 us -> 15.8 us
  other arithmetic: 6.23 us -> 9.57 us
    ppermute x21 -> x19, waiting for transfers between devices: 67.5 us -> 45.3 us  [shift(): lax.ppermute(value, axis, [(i, (i + step) % size) for i in range(size)])]
    ppermute x21 -> x19, starting transfers between devices: 36.2 us -> 29.1 us  [shift(): lax.ppermute(value, axis, [(i, (i + step) % size) for i in range(size)])]
    all_to_all x1, starting transfers between devices: 9.03 us -> 14.4 us  [body(): swapped = lax.all_to_all(part, dq, 0, 0, tiled=True)]
    unnamed x50 -> x30, local copies, waits for them, and re-layouts: 6.28 us -> 1.38 us
    dynamic_update_slice x12 -> x2, local copies, waits for them, and re-layouts: 4.91 us -> 0.07 us  [the longest x1 0.04 us: gathered(): this_row = lax.dynamic_update_slice(this_row, a4[None], (far_z, 0, 0))]
    all_to_all x1, waiting for transfers between devices: 4.95 us -> 9.12 us  [body(): swapped = lax.all_to_all(part, dq, 0, 0, tiled=True)]
    dot_general x2, matrix products: 5.8 us -> 8.96 us  [body(): pre = pre + jnp.dot(other_flat, other_row, preferred_element_type=F32)]
    dot_general x2, matrix products: 5.93 us -> 3.42 us  [body(): lax.dot_general(flat, input_projection, (((1,), (1,)), ((), ())), preferr...]
  transfers between devices with their start and end apart: 23 -> 22, of which waited for: 11 -> 8; matrix products, arithmetic and copies ran while one was open for 14% -> 19% of each run, Pallas kernels for 0% -> 0%
where the time goes in v3:
time: 188 us; the launch traced here: 187 us
  waiting for transfers between devices  63 us (34%)
  starting transfers between devices  48.6 us (26%)
  matrix products  23.3 us (12%)
  local copies, waits for them, and re-layouts  15.8 us (8%)
  between operations  14.7 us (8%)
  blocking collectives  12.1 us (6%)
  other arithmetic  9.57 us (5%)
    ppermute x19, waiting for transfers between devices, shift(): lax.ppermute(value, axis, [(i, (i + step) % size) for i in range(size)])  45.3 us
    ppermute x19, starting transfers between devices, shift(): lax.ppermute(value, axis, [(i, (i + step) % size) for i in range(size)])  29.1 us
    all_to_all x1, starting transfers between devices, body(): swapped = lax.all_to_all(part, dq, 0, 0, tiled=True)  14.4 us
    all_to_all x1, blocking collectives, body(): received = lax.all_to_all(payload, dq, 0, 0, tiled=True)  12.1 us
    all_to_all x1, waiting for transfers between devices, body(): swapped = lax.all_to_all(part, dq, 0, 0, tiled=True)  9.12 us
    dot_general x2, matrix products, body(): pre = pre + jnp.dot(other_flat, other_row, preferred_element_type=F32)  8.96 us
    all_to_all x1, waiting for transfers between devices, body(): lax.all_to_all(jnp.broadcast_to(queries[None], (n_fsdp,) + queries.shape)...  8.5 us
    dot_general x2, matrix products, body(): pre = jnp.dot(this_flat, this_row, preferred_element_type=F32)  7.05 us
  transfers between devices with their start and end apart: 22, of which 8 were waited for; matrix products, arithmetic and copies ran while one was open for 19% of the time, Pallas kernels for 0%

profile of v3, /device:TPU:1, one launch (start us, length us, event | category | flops | bytes accessed | tf_op | source)
XLA Modules:
  0.0 187.2 jit_solution(17807615117367914510)
XLA Ops:
  6.5 1.3 constant_dynamic-slice_fusion.4
  7.8 0.9 pad_maximum_fusion.1
  8.7 3.7 %collective-permute-start.2 = (bf16[1,64,5120]{2,1,0:T(8,128)(2,1)}, bf16[1,64,5120]{2,1,0:T(8,128)(2,1)}, u32[]{:S(2)}, u32[]{:S(2)}) collective-permute-start(bf16[1,64,5120]{2,1,0:T(8,128)(2,1)} %pad_maximum_fusion.1), channel_id=1, source_target_pairs={{0,1},{1,0},{2,3},{3,2},{4,5},{5,4},{6,7},{7,6},{8,9},{9,8},{10,11... | collective-permute-start | bytes 1966088 | tf_op jit(solution)/shard_map/ppermute | solution.py:11
  12.4 2.1 %pad_maximum_fusion.2 = bf16[320,896]{1,0:T(8,128)(2,1)} fusion(bf16[320,448]{1,0:T(8,128)(2,1)} %param.14, bf16[320,448]{1,0:T(8,128)(2,1)} %param.13), kind=kLoop, calls=%fused_computation.29 | loop fusion | flops 1146880 | bytes 1146880 | tf_op jit(solution)/shard_map/concatenate | solution.py:120
  14.5 1.6 collective-permute-start
  16.2 3.9 %collective-permute-start.1 = (bf16[320,896]{1,0:T(8,128)(2,1)}, bf16[320,896]{1,0:T(8,128)(2,1)}, u32[]{:S(2)}, u32[]{:S(2)}) collective-permute-start(bf16[320,896]{1,0:T(8,128)(2,1)} %pad_maximum_fusion.2), channel_id=1, source_target_pairs={{0,112},{16,0},{32,16},{48,32},{64,48},{80,64},{96,80},{112,96},{1... | collective-permute-start | bytes 1720328 | tf_op jit(solution)/shard_map/ppermute | solution.py:11
  20.1 2.4 %constant_dynamic-slice_fusion.6 = (bf16[8,32,448]{2,1,0:T(8,128)(2,1)S(1)}, bf16[8,32,448]{2,1,0:T(8,128)(2,1)S(1)}, bf16[8,32,448]{2,1,0:T(8,128)(2,1)S(1)}, bf16[8,32,448]{2,1,0:T(8,128)(2,1)}) fusion(bf16[8,32,896]{2,1,0:T(8,128)(2,1)} %param.12, s32[]{:T(128)S(6)} %select_n.144, s32[]{:T(128)S(6)} %select_n.147, bf16[8,32,896]{2,1,0:T(8,128)(2,1)} %param.10), kind=kLoop, calls=%fused_computation.89 | loop fusion | bytes 1835016 | tf_op jit(solution)/shard_map/dynamic_slice | solution.py:111
  22.5 0.9 pad_maximum_fusion.4
  23.3 9.4 %collective-permute-done = bf16[320,896]{1,0:T(8,128)(2,1)} collective-permute-done((bf16[320,896]{1,0:T(8,128)(2,1)}, bf16[320,896]{1,0:T(8,128)(2,1)}, u32[]{:S(2)}, u32[]{:S(2)}) %collective-permute-start) | collective-permute-done | bytes 573472 | tf_op jit(solution)/shard_map/ppermute | solution.py:11
  33.0 2.1 %pad_maximum_fusion = bf16[8,64,5120]{2,1,0:T(8,128)(2,1)S(1)} fusion(bf16[8,32,5120]{2,1,0:T(8,128)(2,1)S(1)} %copy-done.5, bf16[8,32,5120]{2,1,0:T(8,128)(2,1)} %param.9), kind=kLoop, calls=%fused_computation | loop fusion | flops 10485760 | bytes 10485760 | tf_op jit(solution)/shard_map/concatenate | solution.py:108
  35.3 0.8 pad_maximum_fusion.3
  36.2 2.7 %collective-permute-start.4 = (bf16[320,896]{1,0:T(8,128)(2,1)}, bf16[320,896]{1,0:T(8,128)(2,1)S(1)}, u32[]{:S(2)}, u32[]{:S(2)}) collective-permute-start(bf16[320,896]{1,0:T(8,128)(2,1)} %collective-permute-done.1), channel_id=1, source_target_pairs={{0,112},{16,0},{32,16},{48,32},{64,48},{80,64},{96,80},{112,96},{1... | collective-permute-start | bytes 1720328 | tf_op jit(solution)/shard_map/ppermute | solution.py:11
  39.3 1.7 fusion.51
  41.6 1.1 bitcast_dynamic-update-slice_fusion.13
  42.7 7.9 %collective-permute-done.3 = bf16[320,896]{1,0:T(8,128)(2,1)S(1)} collective-permute-done((bf16[320,896]{1,0:T(8,128)(2,1)}, bf16[320,896]{1,0:T(8,128)(2,1)S(1)}, u32[]{:S(2)}, u32[]{:S(2)}) %collective-permute-start.3) | collective-permute-done | bytes 573472 | tf_op jit(solution)/shard_map/ppermute | solution.py:11
  50.6 0.9 collective-permute-done.5
  52.0 2.6 %collective-permute-start.7 = (bf16[320,896]{1,0:T(8,128)(2,1)S(1)}, bf16[320,896]{1,0:T(8,128)(2,1)S(1)}, u32[]{:S(2)}, u32[]{:S(2)}) collective-permute-start(bf16[320,896]{1,0:T(8,128)(2,1)S(1)} %collective-permute-done.4), channel_id=1, source_target_pairs={{0,112},{16,0},{32,16},{48,32},{64,48},{80,64},{96,80},{112,96},{1... | collective-permute-start | bytes 1720328 | tf_op jit(solution)/shard_map/ppermute | solution.py:11
  54.6 1.1 bitcast_dynamic-update-slice_fusion.12
  55.8 1.2 bitcast_dynamic-update-slice_fusion.11
  57.1 7.3 %collective-permute-done.6 = bf16[320,896]{1,0:T(8,128)(2,1)S(1)} collective-permute-done((bf16[320,896]{1,0:T(8,128)(2,1)S(1)}, bf16[320,896]{1,0:T(8,128)(2,1)S(1)}, u32[]{:S(2)}, u32[]{:S(2)}) %collective-permute-start.6) | collective-permute-done | bytes 573472 | tf_op jit(solution)/shard_map/ppermute | solution.py:11
  64.4 2.5 %collective-permute-start.10 = (bf16[320,896]{1,0:T(8,128)(2,1)S(1)}, bf16[320,896]{1,0:T(8,128)(2,1)S(1)}, u32[]{:S(2)}, u32[]{:S(2)}) collective-permute-start(bf16[320,896]{1,0:T(8,128)(2,1)S(1)} %collective-permute-done.5), channel_id=1, source_target_pairs={{0,112},{16,0},{32,16},{48,32},{64,48},{80,64},{96,80},{112,96},{1... | collective-permute-start | bytes 1720328 | tf_op jit(solution)/shard_map/ppermute | solution.py:11
  66.9 1.1 collective-permute-start.11
  68.3 2.7 %collective-permute-start.13 = (bf16[160,896]{1,0:T(8,128)(2,1)S(1)}, bf16[160,896]{1,0:T(8,128)(2,1)S(1)}, u32[]{:S(2)}, u32[]{:S(2)}) collective-permute-start(bf16[160,896]{1,0:T(8,128)(2,1)S(1)} %slice.41), channel_id=1, source_target_pairs={{0,112},{16,0},{32,16},{48,32},{64,48},{80,64},{96,80},{112,96},{1... | collective-permute-start | bytes 860168 | tf_op jit(solution)/shard_map/ppermute | solution.py:11
  72.0 12.1 %collective-permute-done.12 = bf16[160,896]{1,0:T(8,128)(2,1)S(1)} collective-permute-done((bf16[160,896]{1,0:T(8,128)(2,1)S(1)}, bf16[160,896]{1,0:T(8,128)(2,1)S(1)}, u32[]{:S(2)}, u32[]{:S(2)}) %collective-permute-start.12) | collective-permute-done | bytes 286752 | tf_op jit(solution)/shard_map/ppermute | solution.py:11
  84.3 2.7 %collective-permute-start.15 = (bf16[320,896]{1,0:T(8,128)(2,1)S(1)}, bf16[320,896]{1,0:T(8,128)(2,1)S(1)}, u32[]{:S(2)}, u32[]{:S(2)}) collective-permute-start(bf16[320,896]{1,0:T(8,128)(2,1)S(1)} %collective-permute-done.11), channel_id=1, source_target_pairs={{0,112},{16,0},{32,16},{48,32},{64,48},{80,64},{96,80},{112,96},{1... | collective-permute-start | bytes 1720328 | tf_op jit(solution)/shard_map/ppermute | solution.py:11
  86.9 1.6 collective-permute-start.16
  88.9 7.5 %collective-permute-done.16 = bf16[512,448]{1,0:T(8,128)(2,1)S(1)} collective-permute-done((bf16[512,448]{1,0:T(8,128)(2,1)S(1)}, bf16[512,448]{1,0:T(8,128)(2,1)S(1)}, u32[]{:S(2)}, u32[]{:S(2)}) %collective-permute-start.16) | collective-permute-done | bytes 458784 | tf_op jit(solution)/shard_map/ppermute | solution.py:11
  96.5 0.8 slice.42
  97.3 0.8 slice.43
  98.1 2.7 %collective-permute-start.18 = (bf16[160,896]{1,0:T(8,128)(2,1)}, bf16[160,896]{1,0:T(8,128)(2,1)}, u32[]{:S(2)}, u32[]{:S(2)}) collective-permute-start(bf16[160,896]{1,0:T(8,128)(2,1)} %slice.43), channel_id=1, source_target_pairs={{0,112},{16,0},{32,16},{48,32},{64,48},{80,64},{96,80},{112,96},{1... | collective-permute-start | bytes 860168 | tf_op jit(solution)/shard_map/ppermute | solution.py:11
  100.9 2.9 %fusion.4 = f32[512,896]{1,0:T(8,128)S(1)} fusion(bf16[2560,896]{1,0:T(8,128)(2,1)S(1)} %bitcast.86, bf16[512,5120]{1,0:T(8,128)(2,1)S(1)} %bitcast.80, s32[]{:T(128)S(6)} %select_n.164), kind=kOutput, calls=%fused_computation.5 | convolution fusion | flops 2348810240 | bytes 9043972 | tf_op jit(solution)/shard_map/dot_general | solution.py:134
  103.8 4.1 %fusion.8 = f32[512,896]{1,0:T(8,128)} fusion(f32[512,896]{1,0:T(8,128)S(1)} %fusion.4, bf16[2560,896]{1,0:T(8,128)(2,1)S(1)} %bitcast.88, bf16[512,5120]{1,0:T(8,128)(2,1)S(1)} %bitcast.81, s32[]{:T(128)S(6)} %select_n.145), kind=kOutput, calls=%fused_computation.9 | convolution fusion | flops 2349268992 | bytes 10878980 | tf_op jit(solution)/shard_map/dot_general | solution.py:133
  108.0 6.1 %fusion = f32[512,896]{1,0:T(8,128)S(1)} fusion(bf16[2560,896]{1,0:T(8,128)(2,1)} %bitcast.87, bf16[512,5120]{1,0:T(8,128)(2,1)} %bitcast.82, s32[]{:T(128)S(6)} %select_n.164), kind=kOutput, calls=%fused_computation.1 | convolution fusion | flops 2348810240 | bytes 9043972 | tf_op jit(solution)/shard_map/dot_general | solution.py:134
  114.3 2.9 %fusion.11 = f32[512,896]{1,0:T(8,128)S(1)} fusion(f32[512,896]{1,0:T(8,128)S(1)} %fusion, bf16[2560,896]{1,0:T(8,128)(2,1)S(1)} %bitcast.89, bf16[512,5120]{1,0:T(8,128)(2,1)S(1)} %bitcast.84, s32[]{:T(128)S(6)} %select_n.145), kind=kOutput, calls=%fused_computation.10 | convolution fusion | flops 2349268992 | bytes 10878980 | tf_op jit(solution)/shard_map/dot_general | solution.py:133
  117.2 1.7 fusion.52
  118.9 1.1 constant_dynamic-update-slice_fusion.1
  120.1 1.0 constant_dynamic-update-slice_fusion
  121.0 0.7 fusion.53
  121.7 0.7 fusion.54
  122.8 0.6 fusion.21
  124.0 0.8 fusion.26
  125.6 0.7 pad_maximum_fusion.7
  126.4 14.4 %all-to-all-start = ((bf16[16,8,1024]{2,1,0:T(8,128)(2,1)}), bf16[16,8,1024]{2,1,0:T(8,128)(2,1)S(1)}, u32[]{:S(2)}, u32[]{:S(2)}) async-start(bf16[16,8,1024]{2,1,0:T(8,128)(2,1)} %pad_maximum_fusion.7), calls=%async_computation | async-start | bytes 524288 | tf_op jit(solution)/shard_map/all_to_all | solution.py:162
  141.0 9.1 %all-to-all-done = bf16[16,8,1024]{2,1,0:T(8,128)(2,1)S(1)} async-done(((bf16[16,8,1024]{2,1,0:T(8,128)(2,1)}), bf16[16,8,1024]{2,1,0:T(8,128)(2,1)S(1)}, u32[]{:S(2)}, u32[]{:S(2)}) %all-to-all-start) | async-done | bytes 262176 | tf_op jit(solution)/shard_map/all_to_all | solution.py:162
  151.1 0.7 broadcast_in_dim.85
  151.8 5.1 %all-to-all-start.1 = ((bf16[16,16,512]{2,1,0:T(8,128)(2,1)}), bf16[16,16,512]{2,1,0:T(8,128)(2,1)S(1)}, u32[]{:S(2)}, u32[]{:S(2)}) async-start(bf16[16,16,512]{2,1,0:T(8,128)(2,1)} %broadcast_in_dim.85), calls=%async_computation.1 | async-start | bytes 524288 | tf_op jit(solution)/shard_map/all_to_all | solution.py:178
  157.3 8.5 %all-to-all-done.1 = bf16[16,16,512]{2,1,0:T(8,128)(2,1)S(1)} async-done(((bf16[16,16,512]{2,1,0:T(8,128)(2,1)}), bf16[16,16,512]{2,1,0:T(8,128)(2,1)S(1)}, u32[]{:S(2)}, u32[]{:S(2)}) %all-to-all-start.1) | async-done | bytes 262176 | tf_op jit(solution)/shard_map/all_to_all | solution.py:178
  166.4 12.1 %all_to_all.19 = f32[16,1,640]{2,1,0:T(1,128)S(1)} all-to-all(f32[16,1,640]{2,1,0:T(1,128)S(1)} %copy.24), channel_id=1, replica_groups=mesh['ylo'=2,'z'=8,'x'=4,'core'=2,'yhi'=2] {'x','core','yhi'}, dimensions={0} | all-to-all | bytes 81920 | tf_op jit(solution)/shard_map/all_to_all | solution.py:199
  (103 shorter events, 8.7 us)
Async XLA Ops:
  6.5 32.7 %copy-start = (bf16[64,5120]{1,0:T(8,128)(2,1)S(1)}, bf16[64,5120]{1,0:T(8,128)(2,1)}, u32[]{:S(2)}) copy-start(bf16[64,5120]{1,0:T(8,128)(2,1)} %param.15) | copy-start | bytes 1966084
  6.5 26.4 %copy-start.5 = (bf16[8,32,5120]{2,1,0:T(8,128)(2,1)S(1)}, bf16[8,32,5120]{2,1,0:T(8,128)(2,1)}, u32[]{:S(2)}) copy-start(bf16[8,32,5120]{2,1,0:T(8,128)(2,1)} %param.11) | copy-start | bytes 7864324
  6.5 101.4 %all-gather.2.cloned.1.call-start = ((), (), s32[]{:S(2)}) async-start(), calls=%async_computation.3 | async-start | bytes 5898240 | tf_op jit(solution)/shard_map/all_gather | solution.py:39
  8.7 24.1 %collective-permute-start.2 = (bf16[1,64,5120]{2,1,0:T(8,128)(2,1)}, bf16[1,64,5120]{2,1,0:T(8,128)(2,1)}, u32[]{:S(2)}, u32[]{:S(2)}) collective-permute-start(bf16[1,64,5120]{2,1,0:T(8,128)(2,1)} %pad_maximum_fusion.1), channel_id=1, source_target_pairs={{0,1},{1,0},{2,3},{3,2},{4,5},{5,4},{6,7},{7,6},{8,9},{9,8},{10,11... | collective-permute-start | bytes 1966088 | tf_op jit(solution)/shard_map/ppermute | solution.py:11
  14.5 18.3 %collective-permute-start = (bf16[320,896]{1,0:T(8,128)(2,1)}, bf16[320,896]{1,0:T(8,128)(2,1)}, u32[]{:S(2)}, u32[]{:S(2)}) collective-permute-start(bf16[320,896]{1,0:T(8,128)(2,1)} %pad_maximum_fusion.2), channel_id=1, source_target_pairs={{0,16},{16,32},{32,48},{48,64},{64,80},{80,96},{96,112},{112,0},{1... | collective-permute-start | bytes 1720328 | tf_op jit(solution)/shard_map/ppermute | solution.py:11
  16.2 16.6 %collective-permute-start.1 = (bf16[320,896]{1,0:T(8,128)(2,1)}, bf16[320,896]{1,0:T(8,128)(2,1)}, u32[]{:S(2)}, u32[]{:S(2)}) collective-permute-start(bf16[320,896]{1,0:T(8,128)(2,1)} %pad_maximum_fusion.2), channel_id=1, source_target_pairs={{0,112},{16,0},{32,16},{48,32},{64,48},{80,64},{96,80},{112,96},{1... | collective-permute-start | bytes 1720328 | tf_op jit(solution)/shard_map/ppermute | solution.py:11
  33.0 2.4 %copy-start.8 = (bf16[8,32,448]{2,1,0:T(8,128)(2,1)S(1)}, bf16[8,32,448]{2,1,0:T(8,128)(2,1)}, u32[]{:S(2)}) copy-start(bf16[8,32,448]{2,1,0:T(8,128)(2,1)} %get-tuple-element.80) | copy-start | bytes 688132
  36.2 14.4 %collective-permute-start.3 = (bf16[320,896]{1,0:T(8,128)(2,1)}, bf16[320,896]{1,0:T(8,128)(2,1)S(1)}, u32[]{:S(2)}, u32[]{:S(2)}) collective-permute-start(bf16[320,896]{1,0:T(8,128)(2,1)} %collective-permute-done), channel_id=1, source_target_pairs={{0,16},{16,32},{32,48},{48,64},{64,80},{80,96},{96,112},{112,0},{1... | collective-permute-start | bytes 1720328 | tf_op jit(solution)/shard_map/ppermute | solution.py:11
  36.2 14.4 %collective-permute-start.4 = (bf16[320,896]{1,0:T(8,128)(2,1)}, bf16[320,896]{1,0:T(8,128)(2,1)S(1)}, u32[]{:S(2)}, u32[]{:S(2)}) collective-permute-start(bf16[320,896]{1,0:T(8,128)(2,1)} %collective-permute-done.1), channel_id=1, source_target_pairs={{0,112},{16,0},{32,16},{48,32},{64,48},{80,64},{96,80},{112,96},{1... | collective-permute-start | bytes 1720328 | tf_op jit(solution)/shard_map/ppermute | solution.py:11
  38.9 12.7 %collective-permute-start.5 = (bf16[320,896]{1,0:T(8,128)(2,1)}, bf16[320,896]{1,0:T(8,128)(2,1)S(1)}, u32[]{:S(2)}, u32[]{:S(2)}) collective-permute-start(bf16[320,896]{1,0:T(8,128)(2,1)} %pad_maximum_fusion.2), channel_id=1, source_target_pairs={{0,128},{128,0},{1,129},{129,1},{2,130},{130,2},{3,131},{131,3},{4... | collective-permute-start | bytes 1720328 | tf_op jit(solution)/shard_map/ppermute | solution.py:11
  51.5 12.9 %collective-permute-start.6 = (bf16[320,896]{1,0:T(8,128)(2,1)S(1)}, bf16[320,896]{1,0:T(8,128)(2,1)S(1)}, u32[]{:S(2)}, u32[]{:S(2)}) collective-permute-start(bf16[320,896]{1,0:T(8,128)(2,1)S(1)} %collective-permute-done.3), channel_id=1, source_target_pairs={{0,16},{16,32},{32,48},{48,64},{64,80},{80,96},{96,112},{112,0},{1... | collective-permute-start | bytes 1720328 | tf_op jit(solution)/shard_map/ppermute | solution.py:11
  51.6 12.8 %collective-permute-start.8 = (bf16[320,896]{1,0:T(8,128)(2,1)S(1)}, bf16[320,896]{1,0:T(8,128)(2,1)S(1)}, u32[]{:S(2)}, u32[]{:S(2)}) collective-permute-start(bf16[320,896]{1,0:T(8,128)(2,1)S(1)} %collective-permute-done.3), channel_id=1, source_target_pairs={{0,128},{128,0},{1,129},{129,1},{2,130},{130,2},{3,131},{131,3},{4... | collective-permute-start | bytes 1720328 | tf_op jit(solution)/shard_map/ppermute | solution.py:11
  52.0 12.4 %collective-permute-start.7 = (bf16[320,896]{1,0:T(8,128)(2,1)S(1)}, bf16[320,896]{1,0:T(8,128)(2,1)S(1)}, u32[]{:S(2)}, u32[]{:S(2)}) collective-permute-start(bf16[320,896]{1,0:T(8,128)(2,1)S(1)} %collective-permute-done.4), channel_id=1, source_target_pairs={{0,112},{16,0},{32,16},{48,32},{64,48},{80,64},{96,80},{112,96},{1... | collective-permute-start | bytes 1720328 | tf_op jit(solution)/shard_map/ppermute | solution.py:11
  64.4 19.8 %collective-permute-start.10 = (bf16[320,896]{1,0:T(8,128)(2,1)S(1)}, bf16[320,896]{1,0:T(8,128)(2,1)S(1)}, u32[]{:S(2)}, u32[]{:S(2)}) collective-permute-start(bf16[320,896]{1,0:T(8,128)(2,1)S(1)} %collective-permute-done.5), channel_id=1, source_target_pairs={{0,112},{16,0},{32,16},{48,32},{64,48},{80,64},{96,80},{112,96},{1... | collective-permute-start | bytes 1720328 | tf_op jit(solution)/shard_map/ppermute | solution.py:11
  66.9 17.2 %collective-permute-start.9 = (bf16[320,896]{1,0:T(8,128)(2,1)S(1)}, bf16[320,896]{1,0:T(8,128)(2,1)S(1)}, u32[]{:S(2)}, u32[]{:S(2)}) collective-permute-start(bf16[320,896]{1,0:T(8,128)(2,1)S(1)} %collective-permute-done.5), channel_id=1, source_target_pairs={{0,16},{16,32},{32,48},{48,64},{64,80},{80,96},{96,112},{112,0},{1... | collective-permute-start | bytes 1720328 | tf_op jit(solution)/shard_map/ppermute | solution.py:11
  66.9 17.2 %collective-permute-start.11 = (bf16[320,896]{1,0:T(8,128)(2,1)S(1)}, bf16[320,896]{1,0:T(8,128)(2,1)S(1)}, u32[]{:S(2)}, u32[]{:S(2)}) collective-permute-start(bf16[320,896]{1,0:T(8,128)(2,1)S(1)} %collective-permute-done.4), channel_id=1, source_target_pairs={{0,128},{128,0},{1,129},{129,1},{2,130},{130,2},{3,131},{131,3},{4... | collective-permute-start | bytes 1720328 | tf_op jit(solution)/shard_map/ppermute | solution.py:11
  68.0 16.1 %collective-permute-start.12 = (bf16[160,896]{1,0:T(8,128)(2,1)S(1)}, bf16[160,896]{1,0:T(8,128)(2,1)S(1)}, u32[]{:S(2)}, u32[]{:S(2)}) collective-permute-start(bf16[160,896]{1,0:T(8,128)(2,1)S(1)} %slice.40), channel_id=1, source_target_pairs={{0,16},{16,32},{32,48},{48,64},{64,80},{80,96},{96,112},{112,0},{1... | collective-permute-start | bytes 860168 | tf_op jit(solution)/shard_map/ppermute | solution.py:11
  68.3 18.6 %copy-start.9 = (bf16[8,64,448]{2,1,0:T(8,128)(2,1)S(1)}, bf16[8,64,448]{2,1,0:T(8,128)(2,1)}, u32[]{:S(2)}) copy-start(bf16[8,64,448]{2,1,0:T(8,128)(2,1)} %pad_maximum_fusion.4) | copy-start | bytes 1376260
  68.3 15.8 %collective-permute-start.13 = (bf16[160,896]{1,0:T(8,128)(2,1)S(1)}, bf16[160,896]{1,0:T(8,128)(2,1)S(1)}, u32[]{:S(2)}, u32[]{:S(2)}) collective-permute-start(bf16[160,896]{1,0:T(8,128)(2,1)S(1)} %slice.41), channel_id=1, source_target_pairs={{0,112},{16,0},{32,16},{48,32},{64,48},{80,64},{96,80},{112,96},{1... | collective-permute-start | bytes 860168 | tf_op jit(solution)/shard_map/ppermute | solution.py:11
  84.2 12.3 %collective-permute-start.14 = (bf16[320,896]{1,0:T(8,128)(2,1)S(1)}, bf16[320,896]{1,0:T(8,128)(2,1)S(1)}, u32[]{:S(2)}, u32[]{:S(2)}) collective-permute-start(bf16[320,896]{1,0:T(8,128)(2,1)S(1)} %collective-permute-done.8), channel_id=1, source_target_pairs={{0,16},{16,32},{32,48},{48,64},{64,80},{80,96},{96,112},{112,0},{1... | collective-permute-start | bytes 1720328 | tf_op jit(solution)/shard_map/ppermute | solution.py:11
  84.3 12.2 %collective-permute-start.15 = (bf16[320,896]{1,0:T(8,128)(2,1)S(1)}, bf16[320,896]{1,0:T(8,128)(2,1)S(1)}, u32[]{:S(2)}, u32[]{:S(2)}) collective-permute-start(bf16[320,896]{1,0:T(8,128)(2,1)S(1)} %collective-permute-done.11), channel_id=1, source_target_pairs={{0,112},{16,0},{32,16},{48,32},{64,48},{80,64},{96,80},{112,96},{1... | collective-permute-start | bytes 1720328 | tf_op jit(solution)/shard_map/ppermute | solution.py:11
  86.9 9.5 %collective-permute-start.16 = (bf16[512,448]{1,0:T(8,128)(2,1)S(1)}, bf16[512,448]{1,0:T(8,128)(2,1)S(1)}, u32[]{:S(2)}, u32[]{:S(2)}) collective-permute-start(bf16[512,448]{1,0:T(8,128)(2,1)S(1)} %bitcast.92), channel_id=1, source_target_pairs={{0,1},{1,0},{2,3},{3,2},{4,5},{5,4},{6,7},{7,6},{8,9},{9,8},{10,11... | collective-permute-start | bytes 1376264 | tf_op jit(solution)/shard_map/ppermute | solution.py:11
  88.8 14.9 %copy-start.3 = (bf16[8,320,896]{2,1,0:T(8,128)(2,1)}, bf16[8,320,896]{2,1,0:T(8,128)(2,1)S(1)}, u32[]{:S(2)}) copy-start(bf16[8,320,896]{2,1,0:T(8,128)(2,1)S(1)} %bitcast_dynamic-update-slice_fusion.14) | copy-start | bytes 13762564
  96.5 7.3 %copy-start.12 = (bf16[512,448]{1,0:T(8,128)(2,1)}, bf16[512,448]{1,0:T(8,128)(2,1)S(1)}, u32[]{:S(2)}) copy-start(bf16[512,448]{1,0:T(8,128)(2,1)S(1)} %collective-permute-done.16) | copy-start | bytes 1376260
  97.3 21.6 %collective-permute-start.17 = (bf16[160,896]{1,0:T(8,128)(2,1)}, bf16[160,896]{1,0:T(8,128)(2,1)}, u32[]{:S(2)}, u32[]{:S(2)}) collective-permute-start(bf16[160,896]{1,0:T(8,128)(2,1)} %slice.42), channel_id=1, source_target_pairs={{0,16},{16,32},{32,48},{48,64},{64,80},{80,96},{96,112},{112,0},{1... | collective-permute-start | bytes 860168 | tf_op jit(solution)/shard_map/ppermute | solution.py:11
  98.1 20.9 %collective-permute-start.18 = (bf16[160,896]{1,0:T(8,128)(2,1)}, bf16[160,896]{1,0:T(8,128)(2,1)}, u32[]{:S(2)}, u32[]{:S(2)}) collective-permute-start(bf16[160,896]{1,0:T(8,128)(2,1)} %slice.43), channel_id=1, source_target_pairs={{0,112},{16,0},{32,16},{48,32},{64,48},{80,64},{96,80},{112,96},{1... | collective-permute-start | bytes 860168 | tf_op jit(solution)/shard_map/ppermute | solution.py:11
  100.9 2.9 %copy-start.2 = (bf16[8,320,896]{2,1,0:T(8,128)(2,1)}, bf16[8,320,896]{2,1,0:T(8,128)(2,1)S(1)}, u32[]{:S(2)}) copy-start(bf16[8,320,896]{2,1,0:T(8,128)(2,1)S(1)} %bitcast_dynamic-update-slice_fusion) | copy-start | bytes 13762564
  107.9 6.1 %copy-start.1 = (bf16[8,64,5120]{2,1,0:T(8,128)(2,1)S(1)}, bf16[8,64,5120]{2,1,0:T(8,128)(2,1)}, u32[]{:S(2)}) copy-start(bf16[8,64,5120]{2,1,0:T(8,128)(2,1)} %all-gather.2.cloned.1.call-done) | copy-start | bytes 15728644
  107.9 6.3 %copy-start.4 = (bf16[8,320,896]{2,1,0:T(8,128)(2,1)S(1)}, bf16[8,320,896]{2,1,0:T(8,128)(2,1)}, u32[]{:S(2)}) copy-start(bf16[8,320,896]{2,1,0:T(8,128)(2,1)} %copy-done.3) | copy-start | bytes 13762564
  118.9 3.5 %copy-start.7 = (f32[512,896]{1,0:T(8,128)S(1)}, f32[512,896]{1,0:T(8,128)}, u32[]{:S(2)}) copy-start(f32[512,896]{1,0:T(8,128)} %fusion.8) | copy-start | bytes 5505028
  121.7 1.0 copy-start.6
  122.4 1.0 copy-start.10
  122.8 1.2 copy-start.13
  124.0 0.9 copy-start.11
  126.4 23.8 %all-to-all-start = ((bf16[16,8,1024]{2,1,0:T(8,128)(2,1)}), bf16[16,8,1024]{2,1,0:T(8,128)(2,1)S(1)}, u32[]{:S(2)}, u32[]{:S(2)}) async-start(bf16[16,8,1024]{2,1,0:T(8,128)(2,1)} %pad_maximum_fusion.7), calls=%async_computation | async-start | bytes 524288 | tf_op jit(solution)/shard_map/all_to_all | solution.py:162
  151.8 14.0 %all-to-all-start.1 = ((bf16[16,16,512]{2,1,0:T(8,128)(2,1)}), bf16[16,16,512]{2,1,0:T(8,128)(2,1)S(1)}, u32[]{:S(2)}, u32[]{:S(2)}) async-start(bf16[16,16,512]{2,1,0:T(8,128)(2,1)} %broadcast_in_dim.85), calls=%async_computation.1 | async-start | bytes 524288 | tf_op jit(solution)/shard_map/all_to_all | solution.py:178
Sparse Core Ops, SparseCore 0:
  32.9 38.5 all-gather.1

commit v4 on v3

--- a/solution.py
+++ b/solution.py
@@ -11,12 +11,12 @@
     return lax.ppermute(value, axis, [(i, (i + step) % size) for i in range(size)])
 
 
-def gathered(weight, piece, cot):
+def gathered(weight, piece, cot, early):
     barrier = lax.optimization_barrier
     n_z = lax.axis_size("z")
     z = lax.axis_index("z")
-    full = weight.shape[0]
-    half = full // 2
+    half = weight.shape[0] // 2
+    far_z = (z + n_z // 2) % n_z
 
     def up(value):
         return shift(value, "z", 1)
@@ -31,31 +31,38 @@
         result = jnp.zeros((n_z,) + weight.shape, weight.dtype)
         for offset, shard in by_offset:
             result = lax.dynamic_update_slice(result, shard[None], ((z + offset) % n_z, 0, 0))
-        return result
-
-    a1, b1, here, w0, cot = barrier(
-        (up(weight), down(weight), shift(piece, "yhi", 1), weight, cot)
+        return result.reshape(n_z * weight.shape[0], -1)
+
+    a1, b1, here, w0, cot, early = barrier(
+        (up(weight), down(weight), shift(piece, "yhi", 1), weight, cot, early)
     )
     partner = lax.all_gather(here, ("x", "core"), axis=0, tiled=True)
-    a2, b2, o0 = barrier((up(a1), down(b1), across(w0)))
+    a2, b2, o0, cot = barrier((up(a1), down(b1), across(w0), cot))
     a3, b3, oa2, o0, b2 = barrier((up(a2), down(b2), across(a2), o0, b2))
-    oa1, ob1, ob2, a4, b4, oa2, cot = barrier(
-        (up(o0), down(o0), across(b2), up(a3[:half]), down(b3[half:]), oa2, cot)
-    )
-    oa3, ob3, other_cot = barrier((up(oa2), down(ob2), shift(cot, "yhi", 1)))
-    far = (up(oa3[:half]), down(ob3[half:]))
-
+    other_cot = shift(cot, "yhi", 1)
+    oa1, ob1, ob2, a4, b4, oa2, other_cot = barrier(
+        (up(o0), down(o0), across(b2), up(a3[:half]), down(b3[half:]), oa2, other_cot)
+    )
+    a4 = jnp.concatenate((a4, b4), axis=0)
+    last = (
+        (across(a4), far_z),
+        (up(oa2), (z + n_z - 3) % n_z),
+        (down(ob2), (z + 3) % n_z),
+    )
     this_row = placed(
-        ((0, w0), (n_z - 1, a1), (1, b1), (n_z - 2, a2), (2, b2), (n_z - 3, a3), (3, b3))
-    )
-    far_z = (z + n_z // 2) % n_z
-    this_row = lax.dynamic_update_slice(this_row, a4[None], (far_z, 0, 0))
-    this_row = lax.dynamic_update_slice(this_row, b4[None], (far_z, half, 0))
-    other_row = placed(
-        ((0, o0), (n_z - 1, oa1), (1, ob1), (n_z - 2, oa2), (2, ob2), (n_z - 3, oa3), (3, ob3))
-    )
-    flat = (n_z * full, -1)
-    return this_row.reshape(flat), other_row.reshape(flat), far, far_z, other_cot, partner
+        (
+            (0, w0),
+            (n_z - 1, a1),
+            (1, b1),
+            (n_z - 2, a2),
+            (2, b2),
+            (n_z - 3, a3),
+            (3, b3),
+            (n_z // 2, a4),
+        )
+    )
+    other_row = placed(((0, o0), (n_z - 1, oa1), (1, ob1), (n_z - 2, oa2), (2, ob2)))
+    return this_row, other_row, last, other_cot, partner, early
 
 
 def projected(pre, cotangent, gate_projection, up_projection):
@@ -118,35 +125,41 @@
 
     own_cot = cotangents(half_index)
     weight = jnp.concatenate((gate_weight, up_weight), axis=1)
-    this_row, other_row, far, far_z, other_cot, other = gathered(
-        weight, piece, cotangents(1 - half_index)
-    )
-    gate_proj = lax.dynamic_slice_in_dim(gate_projection, half_index * cols, cols, 1)
-    up_proj = lax.dynamic_slice_in_dim(up_projection, half_index * cols, cols, 1)
+    this_row, other_row, last, other_cot, other, (own, own_cot) = gathered(
+        weight, piece, cotangents(1 - half_index), (own, own_cot)
+    )
+    gate_proj = columns(gate_projection, half_index)
+    up_proj = columns(up_projection, half_index)
 
     depth = this_row.shape[0]
-    both = []
+    shard_depth = weight.shape[0]
+    pres = []
+    factors = []
+    chunks = []
     for rows in (own, other):
         flat = rows.reshape(-1, width)
         this_flat = lax.dynamic_slice_in_dim(flat, row_index * depth, depth, 1)
         other_flat = lax.dynamic_slice_in_dim(flat, (1 - row_index) * depth, depth, 1)
         pre = jnp.dot(this_flat, this_row, preferred_element_type=F32)
-        pre = pre + jnp.dot(other_flat, other_row, preferred_element_type=F32)
-        far_flat = lax.dynamic_slice_in_dim(
-            other_flat, far_z * weight.shape[0], weight.shape[0], 1
-        )
-        in_factor = lax.dot_general(
-            flat, input_projection, (((1,), (1,)), ((), ())), preferred_element_type=F32
-        )
-        both.append((pre, far_flat, in_factor))
-    both, far = lax.optimization_barrier((both, far))
-    far = jnp.concatenate(far, axis=0)
+        pres.append(pre + jnp.dot(other_flat, other_row, preferred_element_type=F32))
+        factors.append(
+            lax.dot_general(
+                flat, input_projection, (((1,), (1,)), ((), ())), preferred_element_type=F32
+            )
+        )
+        chunks.append(
+            [
+                lax.dynamic_slice_in_dim(other_flat, place * shard_depth, shard_depth, 1)
+                for _, place in last
+            ]
+        )
+    shards = [shard for shard, _ in last]
+    pres, factors, chunks, shards = lax.optimization_barrier((pres, factors, chunks, shards))
     parts = []
-    factors = []
-    for (pre, far_flat, in_factor), rows_cot in zip(both, (own_cot, other_cot)):
-        pre = pre + jnp.dot(far_flat, far, preferred_element_type=F32)
+    for pre, pieces, rows_cot in zip(pres, chunks, (own_cot, other_cot)):
+        for chunk, shard in zip(pieces, shards):
+            pre = pre + jnp.dot(chunk, shard, preferred_element_type=F32)
         parts.append(projected(pre, rows_cot, gate_proj, up_proj))
-        factors.append(in_factor)
 
     first = half_index == 0
 

time: 188 us -> 180 us (0.957)
  waiting for transfers between devices: 63 us -> 51.1 us
  matrix products: 23.3 us -> 28 us
  starting transfers between devices: 48.6 us -> 46.4 us
    ppermute x19 -> x18, waiting for transfers between devices: 45.3 us -> 33.5 us  [shift(): lax.ppermute(value, axis, [(i, (i + step) % size) for i in range(size)])]
    dynamic_update_slice x14 -> x13, local copies, waits for them, and re-layouts: 4.31 us -> 7.8 us  [placed(): lax.dynamic_update_slice(result, shard[None], ((z + offset) % n_z, 0, 0))]
    dot_general x4 -> x8, matrix products: 10.3 us -> 13.2 us  [the longest x2 8.98 us: body(): jnp.dot(other_flat, other_row, preferred_element_type=F32)]
    all_to_all x1, starting transfers between devices: 14.4 us -> 11.7 us  [body(): swapped = lax.all_to_all(part, dq, 0, 0, tiled=True)]
    ppermute x19 -> x18, starting transfers between devices: 29.1 us -> 29.6 us  [shift(): lax.ppermute(value, axis, [(i, (i + step) % size) for i in range(size)])]
  transfers between devices with their start and end apart: 22 -> 21, of which waited for: 8 -> 11; matrix products, arithmetic and copies ran while one was open for 19% -> 23% of each run, Pallas kernels for 0% -> 0%
where the time goes in v4:
time: 180 us; the launch traced here: 179 us
  waiting for transfers between devices  51.1 us (28%)
  starting transfers between devices  46.4 us (26%)
  matrix products  28 us (16%)
  local copies, waits for them, and re-layouts  17.5 us (10%)
  between operations  14.7 us (8%)
  blocking collectives  12.1 us (7%)
  other arithmetic  9.47 us (5%)
    ppermute x18, waiting for transfers between devices, shift(): lax.ppermute(value, axis, [(i, (i + step) % size) for i in range(size)])  33.5 us
    ppermute x18, starting transfers between devices, shift(): lax.ppermute(value, axis, [(i, (i + step) % size) for i in range(size)])  29.6 us
    all_to_all x1, blocking collectives, body(): received = lax.all_to_all(payload, dq, 0, 0, tiled=True)  12.1 us
    all_to_all x1, starting transfers between devices, body(): swapped = lax.all_to_all(part, dq, 0, 0, tiled=True)  11.7 us
    all_to_all x1, waiting for transfers between devices, body(): swapped = lax.all_to_all(part, dq, 0, 0, tiled=True)  9.1 us
    dot_general x2, matrix products, body(): jnp.dot(other_flat, other_row, preferred_element_type=F32)  8.98 us
    all_to_all x1, waiting for transfers between devices, body(): lax.all_to_all(jnp.broadcast_to(queries[None], (n_fsdp,) + queries.shape)...  8.5 us
    dynamic_update_slice x13, local copies, waits for them, and re-layouts, placed(): lax.dynamic_update_slice(result, shard[None], ((z + offset) % n_z, 0, 0))  7.8 us
  transfers between devices with their start and end apart: 21, of which 11 were waited for; matrix products, arithmetic and copies ran while one was open for 23% of the time, Pallas kernels for 0%

profile of v4, /device:TPU:1, one launch (start us, length us, event | category | flops | bytes accessed | tf_op | source)
XLA Modules:
  0.0 179.2 jit_solution(11072799249333209603)
XLA Ops:
  6.5 2.2 %pad_maximum_fusion.2 = bf16[320,896]{1,0:T(8,128)(2,1)} fusion(bf16[320,448]{1,0:T(8,128)(2,1)} %param.14, bf16[320,448]{1,0:T(8,128)(2,1)} %param.13), kind=kLoop, calls=%fused_computation.31 | loop fusion | flops 1146880 | bytes 1146880 | tf_op jit(solution)/shard_map/concatenate | solution.py:127
  8.8 2.5 %collective-permute-start = (bf16[320,896]{1,0:T(8,128)(2,1)}, bf16[320,896]{1,0:T(8,128)(2,1)}, u32[]{:S(2)}, u32[]{:S(2)}) collective-permute-start(bf16[320,896]{1,0:T(8,128)(2,1)} %pad_maximum_fusion.2), channel_id=1, source_target_pairs={{0,16},{16,32},{32,48},{48,64},{64,80},{80,96},{96,112},{112,0},{1... | collective-permute-start | bytes 1720328 | tf_op jit(solution)/shard_map/ppermute | solution.py:11
  11.2 3.9 %collective-permute-start.1 = (bf16[320,896]{1,0:T(8,128)(2,1)}, bf16[320,896]{1,0:T(8,128)(2,1)}, u32[]{:S(2)}, u32[]{:S(2)}) collective-permute-start(bf16[320,896]{1,0:T(8,128)(2,1)} %pad_maximum_fusion.2), channel_id=1, source_target_pairs={{0,112},{16,0},{32,16},{48,32},{64,48},{80,64},{96,80},{112,96},{1... | collective-permute-start | bytes 1720328 | tf_op jit(solution)/shard_map/ppermute | solution.py:11
  15.2 1.1 constant_dynamic-slice_fusion.10
  16.3 0.9 pad_maximum_fusion.1
  17.2 2.9 %collective-permute-start.2 = (bf16[1,64,5120]{2,1,0:T(8,128)(2,1)}, bf16[1,64,5120]{2,1,0:T(8,128)(2,1)}, u32[]{:S(2)}, u32[]{:S(2)}) collective-permute-start(bf16[1,64,5120]{2,1,0:T(8,128)(2,1)} %pad_maximum_fusion.1), channel_id=1, source_target_pairs={{0,1},{1,0},{2,3},{3,2},{4,5},{5,4},{6,7},{7,6},{8,9},{9,8},{10,11... | collective-permute-start | bytes 1966088 | tf_op jit(solution)/shard_map/ppermute | solution.py:11
  20.1 1.8 %constant_dynamic-slice_fusion.6 = (bf16[8,32,448]{2,1,0:T(8,128)(2,1)S(1)}, bf16[8,32,448]{2,1,0:T(8,128)(2,1)S(1)}, bf16[8,32,448]{2,1,0:T(8,128)(2,1)S(1)}, bf16[8,32,448]{2,1,0:T(8,128)(2,1)S(1)}) fusion(bf16[8,32,896]{2,1,0:T(8,128)(2,1)} %param.12, s32[]{:T(128)S(6)} %select_n.155, s32[]{:T(128)S(6)} %select_n.157, bf16[8,32,896]{2,1,0:T(8,128)(2,1)} %param.10), kind=kLoop, calls=%fused_computation.88 | loop fusion | bytes 1835016 | tf_op jit(solution)/shard_map/dynamic_slice | solution.py:118
  22.0 0.9 pad_maximum_fusion.3
  22.9 0.9 pad_maximum_fusion.4
  23.7 2.9 %pad_maximum_fusion = bf16[8,64,5120]{2,1,0:T(8,128)(2,1)} fusion(bf16[8,32,5120]{2,1,0:T(8,128)(2,1)S(1)} %copy-done.6, bf16[8,32,5120]{2,1,0:T(8,128)(2,1)S(1)} %copy-done.7), kind=kLoop, calls=%fused_computation | loop fusion | flops 10485760 | bytes 10485760 | tf_op jit(solution)/shard_map/concatenate | solution.py:115
  26.6 1.6 collective-permute-done
  28.2 6.1 %collective-permute-done.2 = bf16[1,64,5120]{2,1,0:T(8,128)(2,1)} collective-permute-done((bf16[1,64,5120]{2,1,0:T(8,128)(2,1)}, bf16[1,64,5120]{2,1,0:T(8,128)(2,1)}, u32[]{:S(2)}, u32[]{:S(2)}) %collective-permute-start.2) | collective-permute-done | bytes 655392 | tf_op jit(solution)/shard_map/ppermute | solution.py:11
  34.6 2.7 %collective-permute-start.4 = (bf16[320,896]{1,0:T(8,128)(2,1)}, bf16[320,896]{1,0:T(8,128)(2,1)S(1)}, u32[]{:S(2)}, u32[]{:S(2)}) collective-permute-start(bf16[320,896]{1,0:T(8,128)(2,1)} %collective-permute-done.1), channel_id=1, source_target_pairs={{0,112},{16,0},{32,16},{48,32},{64,48},{80,64},{96,80},{112,96},{1... | collective-permute-start | bytes 1720328 | tf_op jit(solution)/shard_map/ppermute | solution.py:11
  37.2 1.3 collective-permute-start.5
  39.1 1.1 bitcast_dynamic-update-slice_fusion.12
  40.3 1.1 bitcast_dynamic-update-slice_fusion.11
  41.4 2.4 %fusion.55 = f32[512,64]{0,1:T(8,128)} fusion(bf16[512,5120]{1,0:T(8,128)(2,1)S(1)} %bitcast.75, bf16[64,5120]{1,0:T(8,128)(2,1)S(1)} %copy-done), kind=kOutput, calls=%fused_computation.102 | convolution fusion | flops 335544320 | bytes 6029312 | tf_op jit(solution)/shard_map/dot_general | solution.py:146
  43.8 4.8 %collective-permute-done.3 = bf16[320,896]{1,0:T(8,128)(2,1)S(1)} collective-permute-done((bf16[320,896]{1,0:T(8,128)(2,1)}, bf16[320,896]{1,0:T(8,128)(2,1)S(1)}, u32[]{:S(2)}, u32[]{:S(2)}) %collective-permute-start.3) | collective-permute-done | bytes 573472 | tf_op jit(solution)/shard_map/ppermute | solution.py:11
  48.6 0.9 collective-permute-done.5
  49.5 1.3 collective-permute-start.8
  50.8 2.7 %collective-permute-start.7 = (bf16[320,896]{1,0:T(8,128)(2,1)S(1)}, bf16[320,896]{1,0:T(8,128)(2,1)S(1)}, u32[]{:S(2)}, u32[]{:S(2)}) collective-permute-start(bf16[320,896]{1,0:T(8,128)(2,1)S(1)} %collective-permute-done.4), channel_id=1, source_target_pairs={{0,112},{16,0},{32,16},{48,32},{64,48},{80,64},{96,80},{112,96},{1... | collective-permute-start | bytes 1720328 | tf_op jit(solution)/shard_map/ppermute | solution.py:11
  54.0 1.2 bitcast_dynamic-update-slice_fusion.10
  55.2 2.7 %collective-permute-start.14 = (bf16[512,448]{1,0:T(8,128)(2,1)S(1)}, bf16[512,448]{1,0:T(8,128)(2,1)S(1)}, u32[]{:S(2)}, u32[]{:S(2)}) collective-permute-start(bf16[512,448]{1,0:T(8,128)(2,1)S(1)} %bitcast.91), channel_id=1, source_target_pairs={{0,1},{1,0},{2,3},{3,2},{4,5},{5,4},{6,7},{7,6},{8,9},{9,8},{10,11... | collective-permute-start | bytes 1376264 | tf_op jit(solution)/shard_map/ppermute | solution.py:11
  58.0 3.8 %collective-permute-done.6 = bf16[320,896]{1,0:T(8,128)(2,1)S(1)} collective-permute-done((bf16[320,896]{1,0:T(8,128)(2,1)S(1)}, bf16[320,896]{1,0:T(8,128)(2,1)S(1)}, u32[]{:S(2)}, u32[]{:S(2)}) %collective-permute-start.6) | collective-permute-done | bytes 573472 | tf_op jit(solution)/shard_map/ppermute | solution.py:11
  61.8 3.4 %collective-permute-start.10 = (bf16[320,896]{1,0:T(8,128)(2,1)S(1)}, bf16[320,896]{1,0:T(8,128)(2,1)S(1)}, u32[]{:S(2)}, u32[]{:S(2)}) collective-permute-start(bf16[320,896]{1,0:T(8,128)(2,1)S(1)} %collective-permute-done.5), channel_id=1, source_target_pairs={{0,112},{16,0},{32,16},{48,32},{64,48},{80,64},{96,80},{112,96},{1... | collective-permute-start | bytes 1720328 | tf_op jit(solution)/shard_map/ppermute | solution.py:11
  66.3 8.3 %collective-permute-done.14 = bf16[512,448]{1,0:T(8,128)(2,1)S(1)} collective-permute-done((bf16[512,448]{1,0:T(8,128)(2,1)S(1)}, bf16[512,448]{1,0:T(8,128)(2,1)S(1)}, u32[]{:S(2)}, u32[]{:S(2)}) %collective-permute-start.14) | collective-permute-done | bytes 458784 | tf_op jit(solution)/shard_map/ppermute | solution.py:11
  74.6 1.9 %collective-permute-start.13 = (bf16[160,896]{1,0:T(8,128)(2,1)S(1)}, bf16[160,896]{1,0:T(8,128)(2,1)S(1)}, u32[]{:S(2)}, u32[]{:S(2)}) collective-permute-start(bf16[160,896]{1,0:T(8,128)(2,1)S(1)} %slice.35), channel_id=1, source_target_pairs={{0,112},{16,0},{32,16},{48,32},{64,48},{80,64},{96,80},{112,96},{1... | collective-permute-start | bytes 860168 | tf_op jit(solution)/shard_map/ppermute | solution.py:11
  76.7 3.2 %collective-permute-done.12 = bf16[160,896]{1,0:T(8,128)(2,1)S(1)} collective-permute-done((bf16[160,896]{1,0:T(8,128)(2,1)S(1)}, bf16[160,896]{1,0:T(8,128)(2,1)S(1)}, u32[]{:S(2)}, u32[]{:S(2)}) %collective-permute-start.12) | collective-permute-done | bytes 286752 | tf_op jit(solution)/shard_map/ppermute | solution.py:11
  79.9 2.2 %collective-permute-done.13 = bf16[160,896]{1,0:T(8,128)(2,1)S(1)} collective-permute-done((bf16[160,896]{1,0:T(8,128)(2,1)S(1)}, bf16[160,896]{1,0:T(8,128)(2,1)S(1)}, u32[]{:S(2)}, u32[]{:S(2)}) %collective-permute-start.13) | collective-permute-done | bytes 286752 | tf_op jit(solution)/shard_map/ppermute | solution.py:11
  82.2 2.4 %collective-permute-done.11 = bf16[320,896]{1,0:T(8,128)(2,1)} collective-permute-done((bf16[320,896]{1,0:T(8,128)(2,1)S(1)}, bf16[320,896]{1,0:T(8,128)(2,1)}, u32[]{:S(2)}, u32[]{:S(2)}) %collective-permute-start.11) | collective-permute-done | bytes 573472 | tf_op jit(solution)/shard_map/ppermute | solution.py:11
  86.0 1.3 collective-permute-start.15
  87.7 2.3 %collective-permute-start.17 = (bf16[320,896]{1,0:T(8,128)(2,1)}, bf16[320,896]{1,0:T(8,128)(2,1)S(1)}, u32[]{:S(2)}, u32[]{:S(2)}) collective-permute-start(bf16[320,896]{1,0:T(8,128)(2,1)} %collective-permute-done.11), channel_id=1, source_target_pairs={{0,112},{16,0},{32,16},{48,32},{64,48},{80,64},{96,80},{112,96},{1... | collective-permute-start | bytes 1720328 | tf_op jit(solution)/shard_map/ppermute | solution.py:11
  90.2 1.1 bitcast_dynamic-update-slice_fusion.1
  91.3 1.1 bitcast_dynamic-update-slice_fusion
  92.5 1.6 bitcast_dynamic-update-slice_fusion.5
  94.0 2.9 %fusion.4 = f32[512,896]{1,0:T(8,128)S(1)} fusion(bf16[2560,896]{1,0:T(8,128)(2,1)S(1)} %bitcast.83, bf16[512,5120]{1,0:T(8,128)(2,1)S(1)} %bitcast.77, s32[]{:T(128)S(6)} %select_n.175), kind=kOutput, calls=%fused_computation.5 | convolution fusion | flops 2348810240 | bytes 9043972 | tf_op jit(solution)/shard_map/dot_general | solution.py:144
  97.0 4.1 %fusion.8 = f32[512,896]{1,0:T(8,128)} fusion(f32[512,896]{1,0:T(8,128)S(1)} %fusion.4, bf16[2560,896]{1,0:T(8,128)(2,1)S(1)} %bitcast.85, bf16[512,5120]{1,0:T(8,128)(2,1)S(1)} %bitcast.78, s32[]{:T(128)S(6)} %select_n.158), kind=kOutput, calls=%fused_computation.11 | convolution fusion | flops 2349268992 | bytes 10878980 | tf_op jit(solution)/shard_map/dot_general | solution.py:143
  101.1 6.1 %fusion = f32[512,896]{1,0:T(8,128)S(1)} fusion(bf16[2560,896]{1,0:T(8,128)(2,1)} %bitcast.84, bf16[512,5120]{1,0:T(8,128)(2,1)} %bitcast.79, s32[]{:T(128)S(6)} %select_n.175), kind=kOutput, calls=%fused_computation.1 | convolution fusion | flops 2348810240 | bytes 9043972 | tf_op jit(solution)/shard_map/dot_general | solution.py:144
  107.8 2.4 %fusion.56 = f32[512,64]{0,1:T(8,128)} fusion(bf16[512,5120]{1,0:T(8,128)(2,1)S(1)} %bitcast.81, bf16[64,5120]{1,0:T(8,128)(2,1)S(1)} %copy-done), kind=kOutput, calls=%fused_computation.103 | convolution fusion | flops 335544320 | bytes 6029312 | tf_op jit(solution)/shard_map/dot_general | solution.py:146
  110.1 2.9 %fusion.11 = f32[512,896]{1,0:T(8,128)S(1)} fusion(f32[512,896]{1,0:T(8,128)S(1)} %fusion, bf16[2560,896]{1,0:T(8,128)(2,1)S(1)} %bitcast.86, bf16[512,5120]{1,0:T(8,128)(2,1)S(1)} %bitcast.82, s32[]{:T(128)S(6)} %select_n.158), kind=kOutput, calls=%fused_computation.12 | convolution fusion | flops 2349268992 | bytes 10878980 | tf_op jit(solution)/shard_map/dot_general | solution.py:143
  114.5 0.8 add_add_fusion.1
  115.6 0.9 fusion.30
  118.3 0.8 add_add_fusion
  121.1 11.7 %all-to-all-start = ((bf16[16,8,1024]{2,1,0:T(8,128)(2,1)}), bf16[16,8,1024]{2,1,0:T(8,128)(2,1)S(1)}, u32[]{:S(2)}, u32[]{:S(2)}) async-start(bf16[16,8,1024]{2,1,0:T(8,128)(2,1)} %pad_maximum_fusion.7), calls=%async_computation | async-start | bytes 524288 | tf_op jit(solution)/shard_map/all_to_all | solution.py:175
  133.1 9.1 %all-to-all-done = bf16[16,8,1024]{2,1,0:T(8,128)(2,1)S(1)} async-done(((bf16[16,8,1024]{2,1,0:T(8,128)(2,1)}), bf16[16,8,1024]{2,1,0:T(8,128)(2,1)S(1)}, u32[]{:S(2)}, u32[]{:S(2)}) %all-to-all-start) | async-done | bytes 262176 | tf_op jit(solution)/shard_map/all_to_all | solution.py:175
  143.8 5.1 %all-to-all-start.1 = ((bf16[16,16,512]{2,1,0:T(8,128)(2,1)}), bf16[16,16,512]{2,1,0:T(8,128)(2,1)S(1)}, u32[]{:S(2)}, u32[]{:S(2)}) async-start(bf16[16,16,512]{2,1,0:T(8,128)(2,1)} %broadcast_in_dim.73), calls=%async_computation.1 | async-start | bytes 524288 | tf_op jit(solution)/shard_map/all_to_all | solution.py:191
  149.4 8.5 %all-to-all-done.1 = bf16[16,16,512]{2,1,0:T(8,128)(2,1)S(1)} async-done(((bf16[16,16,512]{2,1,0:T(8,128)(2,1)}), bf16[16,16,512]{2,1,0:T(8,128)(2,1)S(1)}, u32[]{:S(2)}, u32[]{:S(2)}) %all-to-all-start.1) | async-done | bytes 262176 | tf_op jit(solution)/shard_map/all_to_all | solution.py:191
  158.4 12.1 %all_to_all.19 = f32[16,1,640]{2,1,0:T(1,128)S(1)} all-to-all(f32[16,1,640]{2,1,0:T(1,128)S(1)} %copy.24), channel_id=1, replica_groups=mesh['ylo'=2,'z'=8,'x'=4,'core'=2,'yhi'=2] {'x','core','yhi'}, dimensions={0} | all-to-all | bytes 81920 | tf_op jit(solution)/shard_map/all_to_all | solution.py:212
  (103 shorter events, 14.6 us)
Async XLA Ops:
  6.5 34.9 %copy-start = (bf16[64,5120]{1,0:T(8,128)(2,1)S(1)}, bf16[64,5120]{1,0:T(8,128)(2,1)}, u32[]{:S(2)}) copy-start(bf16[64,5120]{1,0:T(8,128)(2,1)} %param.15) | copy-start | bytes 1966084
  6.5 17.2 %copy-start.6 = (bf16[8,32,5120]{2,1,0:T(8,128)(2,1)S(1)}, bf16[8,32,5120]{2,1,0:T(8,128)(2,1)}, u32[]{:S(2)}) copy-start(bf16[8,32,5120]{2,1,0:T(8,128)(2,1)} %param.11) | copy-start | bytes 7864324
  6.5 94.5 %all-gather.2.cloned.1.call-start = ((), (), s32[]{:S(2)}) async-start(), calls=%async_computation.3 | async-start | bytes 5898240 | tf_op jit(solution)/shard_map/all_gather | solution.py:39
  8.8 19.4 %collective-permute-start = (bf16[320,896]{1,0:T(8,128)(2,1)}, bf16[320,896]{1,0:T(8,128)(2,1)}, u32[]{:S(2)}, u32[]{:S(2)}) collective-permute-start(bf16[320,896]{1,0:T(8,128)(2,1)} %pad_maximum_fusion.2), channel_id=1, source_target_pairs={{0,16},{16,32},{32,48},{48,64},{64,80},{80,96},{96,112},{112,0},{1... | collective-permute-start | bytes 1720328 | tf_op jit(solution)/shard_map/ppermute | solution.py:11
  11.2 17.0 %collective-permute-start.1 = (bf16[320,896]{1,0:T(8,128)(2,1)}, bf16[320,896]{1,0:T(8,128)(2,1)}, u32[]{:S(2)}, u32[]{:S(2)}) collective-permute-start(bf16[320,896]{1,0:T(8,128)(2,1)} %pad_maximum_fusion.2), channel_id=1, source_target_pairs={{0,112},{16,0},{32,16},{48,32},{64,48},{80,64},{96,80},{112,96},{1... | collective-permute-start | bytes 1720328 | tf_op jit(solution)/shard_map/ppermute | solution.py:11
  17.2 17.1 %collective-permute-start.2 = (bf16[1,64,5120]{2,1,0:T(8,128)(2,1)}, bf16[1,64,5120]{2,1,0:T(8,128)(2,1)}, u32[]{:S(2)}, u32[]{:S(2)}) collective-permute-start(bf16[1,64,5120]{2,1,0:T(8,128)(2,1)} %pad_maximum_fusion.1), channel_id=1, source_target_pairs={{0,1},{1,0},{2,3},{3,2},{4,5},{5,4},{6,7},{7,6},{8,9},{9,8},{10,11... | collective-permute-start | bytes 1966088 | tf_op jit(solution)/shard_map/ppermute | solution.py:11
  20.1 3.6 %copy-start.7 = (bf16[8,32,5120]{2,1,0:T(8,128)(2,1)S(1)}, bf16[8,32,5120]{2,1,0:T(8,128)(2,1)}, u32[]{:S(2)}) copy-start(bf16[8,32,5120]{2,1,0:T(8,128)(2,1)} %param.9) | copy-start | bytes 7864324
  34.5 6.9 %copy-start.1 = (bf16[8,64,5120]{2,1,0:T(8,128)(2,1)S(1)}, bf16[8,64,5120]{2,1,0:T(8,128)(2,1)}, u32[]{:S(2)}) copy-start(bf16[8,64,5120]{2,1,0:T(8,128)(2,1)} %pad_maximum_fusion) | copy-start | bytes 15728644
  34.5 14.1 %collective-permute-start.3 = (bf16[320,896]{1,0:T(8,128)(2,1)}, bf16[320,896]{1,0:T(8,128)(2,1)S(1)}, u32[]{:S(2)}, u32[]{:S(2)}) collective-permute-start(bf16[320,896]{1,0:T(8,128)(2,1)} %collective-permute-done), channel_id=1, source_target_pairs={{0,16},{16,32},{32,48},{48,64},{64,80},{80,96},{96,112},{112,0},{1... | collective-permute-start | bytes 1720328 | tf_op jit(solution)/shard_map/ppermute | solution.py:11
  34.6 14.0 %collective-permute-start.4 = (bf16[320,896]{1,0:T(8,128)(2,1)}, bf16[320,896]{1,0:T(8,128)(2,1)S(1)}, u32[]{:S(2)}, u32[]{:S(2)}) collective-permute-start(bf16[320,896]{1,0:T(8,128)(2,1)} %collective-permute-done.1), channel_id=1, source_target_pairs={{0,112},{16,0},{32,16},{48,32},{64,48},{80,64},{96,80},{112,96},{1... | collective-permute-start | bytes 1720328 | tf_op jit(solution)/shard_map/ppermute | solution.py:11
  37.2 12.3 %collective-permute-start.5 = (bf16[320,896]{1,0:T(8,128)(2,1)}, bf16[320,896]{1,0:T(8,128)(2,1)S(1)}, u32[]{:S(2)}, u32[]{:S(2)}) collective-permute-start(bf16[320,896]{1,0:T(8,128)(2,1)} %pad_maximum_fusion.2), channel_id=1, source_target_pairs={{0,128},{128,0},{1,129},{129,1},{2,130},{130,2},{3,131},{131,3},{4... | collective-permute-start | bytes 1720328 | tf_op jit(solution)/shard_map/ppermute | solution.py:11
  41.4 13.8 %copy-start.12 = (bf16[8,64,448]{2,1,0:T(8,128)(2,1)S(1)}, bf16[8,64,448]{2,1,0:T(8,128)(2,1)}, u32[]{:S(2)}) copy-start(bf16[8,64,448]{2,1,0:T(8,128)(2,1)} %pad_maximum_fusion.3) | copy-start | bytes 1376260
  49.5 12.3 %collective-permute-start.6 = (bf16[320,896]{1,0:T(8,128)(2,1)S(1)}, bf16[320,896]{1,0:T(8,128)(2,1)S(1)}, u32[]{:S(2)}, u32[]{:S(2)}) collective-permute-start(bf16[320,896]{1,0:T(8,128)(2,1)S(1)} %collective-permute-done.3), channel_id=1, source_target_pairs={{0,16},{16,32},{32,48},{48,64},{64,80},{80,96},{96,112},{112,0},{1... | collective-permute-start | bytes 1720328 | tf_op jit(solution)/shard_map/ppermute | solution.py:11
  49.5 12.3 %collective-permute-start.8 = (bf16[320,896]{1,0:T(8,128)(2,1)S(1)}, bf16[320,896]{1,0:T(8,128)(2,1)}, u32[]{:S(2)}, u32[]{:S(2)}) collective-permute-start(bf16[320,896]{1,0:T(8,128)(2,1)S(1)} %collective-permute-done.3), channel_id=1, source_target_pairs={{0,128},{128,0},{1,129},{129,1},{2,130},{130,2},{3,131},{131,3},{4... | collective-permute-start | bytes 1720328 | tf_op jit(solution)/shard_map/ppermute | solution.py:11
  50.8 11.0 %collective-permute-start.7 = (bf16[320,896]{1,0:T(8,128)(2,1)S(1)}, bf16[320,896]{1,0:T(8,128)(2,1)S(1)}, u32[]{:S(2)}, u32[]{:S(2)}) collective-permute-start(bf16[320,896]{1,0:T(8,128)(2,1)S(1)} %collective-permute-done.4), channel_id=1, source_target_pairs={{0,112},{16,0},{32,16},{48,32},{64,48},{80,64},{96,80},{112,96},{1... | collective-permute-start | bytes 1720328 | tf_op jit(solution)/shard_map/ppermute | solution.py:11
  55.2 19.4 %collective-permute-start.14 = (bf16[512,448]{1,0:T(8,128)(2,1)S(1)}, bf16[512,448]{1,0:T(8,128)(2,1)S(1)}, u32[]{:S(2)}, u32[]{:S(2)}) collective-permute-start(bf16[512,448]{1,0:T(8,128)(2,1)S(1)} %bitcast.91), channel_id=1, source_target_pairs={{0,1},{1,0},{2,3},{3,2},{4,5},{5,4},{6,7},{7,6},{8,9},{9,8},{10,11... | collective-permute-start | bytes 1376264 | tf_op jit(solution)/shard_map/ppermute | solution.py:11
  61.8 20.4 %collective-permute-start.10 = (bf16[320,896]{1,0:T(8,128)(2,1)S(1)}, bf16[320,896]{1,0:T(8,128)(2,1)S(1)}, u32[]{:S(2)}, u32[]{:S(2)}) collective-permute-start(bf16[320,896]{1,0:T(8,128)(2,1)S(1)} %collective-permute-done.5), channel_id=1, source_target_pairs={{0,112},{16,0},{32,16},{48,32},{64,48},{80,64},{96,80},{112,96},{1... | collective-permute-start | bytes 1720328 | tf_op jit(solution)/shard_map/ppermute | solution.py:11
  65.2 19.4 %collective-permute-start.9 = (bf16[320,896]{1,0:T(8,128)(2,1)S(1)}, bf16[320,896]{1,0:T(8,128)(2,1)S(1)}, u32[]{:S(2)}, u32[]{:S(2)}) collective-permute-start(bf16[320,896]{1,0:T(8,128)(2,1)S(1)} %collective-permute-done.5), channel_id=1, source_target_pairs={{0,16},{16,32},{32,48},{48,64},{64,80},{80,96},{96,112},{112,0},{1... | collective-permute-start | bytes 1720328 | tf_op jit(solution)/shard_map/ppermute | solution.py:11
  65.2 19.4 %collective-permute-start.11 = (bf16[320,896]{1,0:T(8,128)(2,1)S(1)}, bf16[320,896]{1,0:T(8,128)(2,1)}, u32[]{:S(2)}, u32[]{:S(2)}) collective-permute-start(bf16[320,896]{1,0:T(8,128)(2,1)S(1)} %collective-permute-done.4), channel_id=1, source_target_pairs={{0,128},{128,0},{1,129},{129,1},{2,130},{130,2},{3,131},{131,3},{4... | collective-permute-start | bytes 1720328 | tf_op jit(solution)/shard_map/ppermute | solution.py:11
  65.4 14.5 %collective-permute-start.12 = (bf16[160,896]{1,0:T(8,128)(2,1)S(1)}, bf16[160,896]{1,0:T(8,128)(2,1)S(1)}, u32[]{:S(2)}, u32[]{:S(2)}) collective-permute-start(bf16[160,896]{1,0:T(8,128)(2,1)S(1)} %slice.34), channel_id=1, source_target_pairs={{0,16},{16,32},{32,48},{48,64},{64,80},{80,96},{96,112},{112,0},{1... | collective-permute-start | bytes 860168 | tf_op jit(solution)/shard_map/ppermute | solution.py:11
  74.6 19.4 %copy-start.13 = (bf16[512,448]{1,0:T(8,128)(2,1)}, bf16[512,448]{1,0:T(8,128)(2,1)S(1)}, u32[]{:S(2)}) copy-start(bf16[512,448]{1,0:T(8,128)(2,1)S(1)} %collective-permute-done.14) | copy-start | bytes 1376260
  74.6 7.6 %collective-permute-start.13 = (bf16[160,896]{1,0:T(8,128)(2,1)S(1)}, bf16[160,896]{1,0:T(8,128)(2,1)S(1)}, u32[]{:S(2)}, u32[]{:S(2)}) collective-permute-start(bf16[160,896]{1,0:T(8,128)(2,1)S(1)} %slice.35), channel_id=1, source_target_pairs={{0,112},{16,0},{32,16},{48,32},{64,48},{80,64},{96,80},{112,96},{1... | collective-permute-start | bytes 860168 | tf_op jit(solution)/shard_map/ppermute | solution.py:11
  86.0 27.0 %collective-permute-start.15 = (bf16[320,896]{1,0:T(8,128)(2,1)}, bf16[320,896]{1,0:T(8,128)(2,1)S(1)}, u32[]{:S(2)}, u32[]{:S(2)}) collective-permute-start(bf16[320,896]{1,0:T(8,128)(2,1)} %constant_dynamic-update-slice_fusion), channel_id=1, source_target_pairs={{0,128},{128,0},{1,129},{129,1},{2,130},{130,2},{3,131},{131,3},{4... | collective-permute-start | bytes 1720328 | tf_op jit(solution)/shard_map/ppermute | solution.py:11
  87.3 25.7 %collective-permute-start.16 = (bf16[320,896]{1,0:T(8,128)(2,1)}, bf16[320,896]{1,0:T(8,128)(2,1)S(1)}, u32[]{:S(2)}, u32[]{:S(2)}) collective-permute-start(bf16[320,896]{1,0:T(8,128)(2,1)} %collective-permute-done.8), channel_id=1, source_target_pairs={{0,16},{16,32},{32,48},{48,64},{64,80},{80,96},{96,112},{112,0},{1... | collective-permute-start | bytes 1720328 | tf_op jit(solution)/shard_map/ppermute | solution.py:11
  87.7 25.4 %collective-permute-start.17 = (bf16[320,896]{1,0:T(8,128)(2,1)}, bf16[320,896]{1,0:T(8,128)(2,1)S(1)}, u32[]{:S(2)}, u32[]{:S(2)}) collective-permute-start(bf16[320,896]{1,0:T(8,128)(2,1)} %collective-permute-done.11), channel_id=1, source_target_pairs={{0,112},{16,0},{32,16},{48,32},{64,48},{80,64},{96,80},{112,96},{1... | collective-permute-start | bytes 1720328 | tf_op jit(solution)/shard_map/ppermute | solution.py:11
  92.5 4.5 %copy-start.3 = (bf16[8,320,896]{2,1,0:T(8,128)(2,1)}, bf16[8,320,896]{2,1,0:T(8,128)(2,1)S(1)}, u32[]{:S(2)}) copy-start(bf16[8,320,896]{2,1,0:T(8,128)(2,1)S(1)} %bitcast_dynamic-update-slice_fusion) | copy-start | bytes 13762564
  94.0 2.9 %copy-start.4 = (bf16[8,320,896]{2,1,0:T(8,128)(2,1)}, bf16[8,320,896]{2,1,0:T(8,128)(2,1)S(1)}, u32[]{:S(2)}) copy-start(bf16[8,320,896]{2,1,0:T(8,128)(2,1)S(1)} %bitcast_dynamic-update-slice_fusion.5) | copy-start | bytes 13762564
  101.1 6.1 %copy-start.2 = (bf16[8,64,5120]{2,1,0:T(8,128)(2,1)S(1)}, bf16[8,64,5120]{2,1,0:T(8,128)(2,1)}, u32[]{:S(2)}) copy-start(bf16[8,64,5120]{2,1,0:T(8,128)(2,1)} %all-gather.2.cloned.1.call-done) | copy-start | bytes 15728644
  107.2 2.9 %copy-start.5 = (bf16[8,320,896]{2,1,0:T(8,128)(2,1)S(1)}, bf16[8,320,896]{2,1,0:T(8,128)(2,1)}, u32[]{:S(2)}) copy-start(bf16[8,320,896]{2,1,0:T(8,128)(2,1)} %copy-done.4) | copy-start | bytes 13762564
  113.0 1.5 copy-start.8
  114.5 1.0 copy-start.11
  114.5 1.1 copy-start.15
  115.6 0.9 copy-start.16
  118.3 1.0 copy-start.14
  119.9 12.9 %copy-start.9 = (f32[512,64]{0,1:T(8,128)S(1)}, f32[512,64]{0,1:T(8,128)}, u32[]{:S(2)}) copy-start(f32[512,64]{0,1:T(8,128)} %fusion.55) | copy-start | bytes 393220
  119.9 12.9 %copy-start.10 = (f32[512,64]{0,1:T(8,128)S(1)}, f32[512,64]{0,1:T(8,128)}, u32[]{:S(2)}) copy-start(f32[512,64]{0,1:T(8,128)} %fusion.56) | copy-start | bytes 393220
  121.1 21.1 %all-to-all-start = ((bf16[16,8,1024]{2,1,0:T(8,128)(2,1)}), bf16[16,8,1024]{2,1,0:T(8,128)(2,1)S(1)}, u32[]{:S(2)}, u32[]{:S(2)}) async-start(bf16[16,8,1024]{2,1,0:T(8,128)(2,1)} %pad_maximum_fusion.7), calls=%async_computation | async-start | bytes 524288 | tf_op jit(solution)/shard_map/all_to_all | solution.py:175
  143.8 14.0 %all-to-all-start.1 = ((bf16[16,16,512]{2,1,0:T(8,128)(2,1)}), bf16[16,16,512]{2,1,0:T(8,128)(2,1)S(1)}, u32[]{:S(2)}, u32[]{:S(2)}) async-start(bf16[16,16,512]{2,1,0:T(8,128)(2,1)} %broadcast_in_dim.73), calls=%async_computation.1 | async-start | bytes 524288 | tf_op jit(solution)/shard_map/all_to_all | solution.py:191
Sparse Core Ops, SparseCore 0:
  34.5 40.7 all-gather.1

commit v5 on v4

--- a/solution.py
+++ b/solution.py
@@ -11,7 +11,7 @@
     return lax.ppermute(value, axis, [(i, (i + step) % size) for i in range(size)])
 
 
-def gathered(weight, piece, cot, early):
+def gathered(weight, piece, cot, own, row_index):
     barrier = lax.optimization_barrier
     n_z = lax.axis_size("z")
     z = lax.axis_index("z")
@@ -33,15 +33,28 @@
             result = lax.dynamic_update_slice(result, shard[None], ((z + offset) % n_z, 0, 0))
         return result.reshape(n_z * weight.shape[0], -1)
 
-    a1, b1, here, w0, cot, early = barrier(
-        (up(weight), down(weight), shift(piece, "yhi", 1), weight, cot, early)
-    )
+    here = shift(piece, "yhi", 1)
+    a1, b1, w0, own, cot = barrier((up(weight), down(weight), weight, own, cot))
+    a2, b2, o0, cot = barrier((up(a1), down(b1), across(w0), cot))
+    here, _ = barrier((here, a2))
     partner = lax.all_gather(here, ("x", "core"), axis=0, tiled=True)
-    a2, b2, o0, cot = barrier((up(a1), down(b1), across(w0), cot))
+    other_cot = shift(cot, "yhi", 1)
     a3, b3, oa2, o0, b2 = barrier((up(a2), down(b2), across(a2), o0, b2))
-    other_cot = shift(cot, "yhi", 1)
-    oa1, ob1, ob2, a4, b4, oa2, other_cot = barrier(
-        (up(o0), down(o0), across(b2), up(a3[:half]), down(b3[half:]), oa2, other_cot)
+    this_row = placed(
+        ((0, w0), (n_z - 1, a1), (1, b1), (n_z - 2, a2), (2, b2), (n_z - 3, a3), (3, b3))
+    )
+    own_sum = this_product(own, this_row, row_index)
+    oa1, ob1, ob2, a4, b4, oa2, own_sum, other_cot = barrier(
+        (
+            up(o0),
+            down(o0),
+            across(b2),
+            up(a3[:half]),
+            down(b3[half:]),
+            oa2,
+            own_sum,
+            other_cot,
+        )
     )
     a4 = jnp.concatenate((a4, b4), axis=0)
     last = (
@@ -49,20 +62,14 @@
         (up(oa2), (z + n_z - 3) % n_z),
         (down(ob2), (z + 3) % n_z),
     )
-    this_row = placed(
-        (
-            (0, w0),
-            (n_z - 1, a1),
-            (1, b1),
-            (n_z - 2, a2),
-            (2, b2),
-            (n_z - 3, a3),
-            (3, b3),
-            (n_z // 2, a4),
-        )
-    )
     other_row = placed(((0, o0), (n_z - 1, oa1), (1, ob1), (n_z - 2, oa2), (2, ob2)))
-    return this_row, other_row, last, other_cot, partner, early
+    return this_row, own_sum, (a4, far_z), other_row, last, other_cot, partner, own
+
+
+def this_product(rows, this_row, row_index):
+    depth = this_row.shape[0]
+    this = lax.dynamic_slice_in_dim(rows, row_index * depth, depth, 1)
+    return jnp.dot(this, this_row, preferred_element_type=F32)
 
 
 def projected(pre, cotangent, gate_projection, up_projection):
@@ -118,16 +125,16 @@
         return lax.dynamic_slice_in_dim(value, index * cols, cols, value.ndim - 1)
 
     def cotangents(index):
-        joined = jnp.concatenate(
-            (columns(doc_cotangents, index), columns(query_cotangents, index)), axis=1
+        return jnp.concatenate(
+            (columns(doc_cotangents, index), columns(query_cotangents, index)), axis=0
         )
-        return joined.reshape(-1, cols)
-
-    own_cot = cotangents(half_index)
+
     weight = jnp.concatenate((gate_weight, up_weight), axis=1)
-    this_row, other_row, last, other_cot, other, (own, own_cot) = gathered(
-        weight, piece, cotangents(1 - half_index), (own, own_cot)
-    )
+    own = own.reshape(-1, width)
+    this_row, own_sum, far, other_row, last, other_cot, partner, own = gathered(
+        weight, piece, cotangents(1 - half_index), own, row_index
+    )
+    partner = partner.reshape(own.shape)
     gate_proj = columns(gate_projection, half_index)
     up_proj = columns(up_projection, half_index)
 
@@ -136,31 +143,27 @@
     pres = []
     factors = []
     chunks = []
-    for rows in (own, other):
-        flat = rows.reshape(-1, width)
-        this_flat = lax.dynamic_slice_in_dim(flat, row_index * depth, depth, 1)
-        other_flat = lax.dynamic_slice_in_dim(flat, (1 - row_index) * depth, depth, 1)
-        pre = jnp.dot(this_flat, this_row, preferred_element_type=F32)
-        pres.append(pre + jnp.dot(other_flat, other_row, preferred_element_type=F32))
+    for rows, pre in ((own, own_sum), (partner, None)):
+        other_flat = lax.dynamic_slice_in_dim(rows, (1 - row_index) * depth, depth, 1)
+
+        def chunk(side, place):
+            return lax.dynamic_slice_in_dim(
+                rows, side * depth + place * shard_depth, shard_depth, 1
+            )
+
+        if pre is None:
+            pre = this_product(rows, this_row, row_index)
+        pre = pre + jnp.dot(other_flat, other_row, preferred_element_type=F32)
+        pre = pre + jnp.dot(chunk(row_index, far[1]), far[0], preferred_element_type=F32)
+        pres.append(pre)
         factors.append(
             lax.dot_general(
-                flat, input_projection, (((1,), (1,)), ((), ())), preferred_element_type=F32
+                rows, input_projection, (((1,), (1,)), ((), ())), preferred_element_type=F32
             )
         )
-        chunks.append(
-            [
-                lax.dynamic_slice_in_dim(other_flat, place * shard_depth, shard_depth, 1)
-                for _, place in last
-            ]
-        )
+        chunks.append([chunk(1 - row_index, place) for _, place in last])
     shards = [shard for shard, _ in last]
     pres, factors, chunks, shards = lax.optimization_barrier((pres, factors, chunks, shards))
-    parts = []
-    for pre, pieces, rows_cot in zip(pres, chunks, (own_cot, other_cot)):
-        for chunk, shard in zip(pieces, shards):
-            pre = pre + jnp.dot(chunk, shard, preferred_element_type=F32)
-        parts.append(projected(pre, rows_cot, gate_proj, up_proj))
-
     first = half_index == 0
 
     def ordered(pair, axis):
@@ -168,29 +171,53 @@
         b = jnp.where(first, pair[1], pair[0])
         return jnp.concatenate((a, b), axis=axis)
 
-    part = ordered(parts, 1).astype(BF16)
-    in_factor = ordered(factors, 0)
-    ranks = part.shape[0] // n_dq
-    part = part.reshape(n_dq, ranks, -1)
-    swapped = lax.all_to_all(part, dq, 0, 0, tiled=True)
-    out_sum = jnp.sum(swapped.astype(F32), axis=0)
+    totals = []
+    for pre, pieces in zip(pres, chunks):
+        for piece_of_rows, shard in zip(pieces, shards):
+            pre = pre + jnp.dot(piece_of_rows, shard, preferred_element_type=F32)
+        totals.append(pre.reshape(count, 2, length, -1))
+    own_cots = (columns(doc_cotangents, half_index), columns(query_cotangents, half_index))
+    other_cots = other_cot.reshape((2,) + own_cots[0].shape)
+
+    def sent(kind, totals):
+        parts = [
+            projected(
+                pre[:, kind].reshape(count * length, -1),
+                cots[kind].reshape(count * length, -1),
+                gate_proj,
+                up_proj,
+            )
+            for pre, cots in zip(totals, (own_cots, other_cots))
+        ]
+        part = ordered(parts, 1).astype(BF16)
+        return part.reshape(n_dq, part.shape[0] // n_dq, -1)
+
+    def scattered(part):
+        return lax.all_to_all(part, dq, 0, 0, tiled=True)
 
     pairs = 2 * count
-    factor = jnp.einsum(
-        "kel,elr->ekr",
-        out_sum.reshape(ranks, 2 * pairs, length),
-        in_factor.reshape(2 * pairs, length, rank),
-        precision=lax.Precision.HIGHEST,
-    ).reshape(pairs, 2, ranks * rank)
-    docs = factor[:, 0]
-    queries = factor[:, 1]
-    doc_squares = jnp.sum(docs * docs, axis=1)
-    docs = docs.astype(BF16)
-    queries = queries.astype(BF16)
-
+
+    def factored(kind, swapped):
+        out_sum = jnp.sum(swapped.astype(F32), axis=0)
+        in_factor = ordered([f.reshape(count, 2, length, rank)[:, kind] for f in factors], 0)
+        return jnp.einsum(
+            "kel,elr->ekr",
+            out_sum.reshape(-1, pairs, length),
+            in_factor,
+            precision=lax.Precision.HIGHEST,
+        ).reshape(pairs, -1)
+
+    query_sent = sent(1, totals)
+    query_sent, totals = lax.optimization_barrier((query_sent, totals))
+    query_part = scattered(query_sent)
+    doc_part = scattered(sent(0, totals))
+    queries = factored(1, query_part).astype(BF16)
     everyone = lax.all_to_all(
         jnp.broadcast_to(queries[None], (n_fsdp,) + queries.shape), fsdp, 0, 0, tiled=True
     ).reshape(n_fsdp * pairs, -1)
+    docs = factored(0, doc_part)
+    doc_squares = jnp.sum(docs * docs, axis=1)
+    docs = docs.astype(BF16)
     wide = everyone.astype(F32)
     query_squares = jnp.sum(wide * wide, axis=1)
     scores = lax.dot_general(

time: 180 us -> 199 us (1.11)
  matrix products: 28 us -> 36.1 us
  waiting for transfers between devices: 51.1 us -> 57.2 us
  local copies, waits for them, and re-layouts: 17.5 us -> 20.5 us
  other arithmetic: 9.47 us -> 11.5 us
    dot_general x13 -> x16, matrix products: 25.5 us -> 34.2 us  [the longest x6 11 us: body(): pre = pre + jnp.dot(piece_of_rows, shard, preferred_element_type=F32)]
    all_to_all x1 -> x2, waiting for transfers between devices: 9.1 us -> 14.9 us  [scattered(): return lax.all_to_all(part, dq, 0, 0, tiled=True)]
    optimization_barrier x0 -> x2, local copies, waits for them, and re-layouts: none -> 2.8 us  [body(): lax.optimization_barrier((pres, factors, chunks, shards))]
    dynamic_update_slice x13 -> x12, local copies, waits for them, and re-layouts: 7.8 us -> 6.52 us  [placed(): lax.dynamic_update_slice(result, shard[None], ((z + offset) % n_z, 0, 0))]
    all_to_all x1 -> x2, starting transfers between devices: 11.7 us -> 11.9 us  [scattered(): return lax.all_to_all(part, dq, 0, 0, tiled=True)]
  transfers between devices with their start and end apart: 21 -> 22, of which waited for: 11 -> 10; matrix products, arithmetic and copies ran while one was open for 23% -> 23% of each run, Pallas kernels for 0% -> 0%
where the time goes in v5:
time: 199 us; the launch traced here: 198 us
  waiting for transfers between devices  57.2 us (29%)
  starting transfers between devices  45.8 us (23%)
  matrix products  36.1 us (18%)
  local copies, waits for them, and re-layouts  20.5 us (10%)
  between operations  14.8 us (7%)
  blocking collectives  12.5 us (6%)
  other arithmetic  11.5 us (6%)
    ppermute x18, waiting for transfers between devices, shift(): lax.ppermute(value, axis, [(i, (i + step) % size) for i in range(size)])  34.4 us
    ppermute x18, starting transfers between devices, shift(): lax.ppermute(value, axis, [(i, (i + step) % size) for i in range(size)])  28 us
    all_to_all x2, waiting for transfers between devices, scattered(): return lax.all_to_all(part, dq, 0, 0, tiled=True)  14.9 us
    all_to_all x1, blocking collectives, body(): received = lax.all_to_all(payload, dq, 0, 0, tiled=True)  12.5 us
    all_to_all x2, starting transfers between devices, scattered(): return lax.all_to_all(part, dq, 0, 0, tiled=True)  11.9 us
    dot_general x6, matrix products, body(): pre = pre + jnp.dot(piece_of_rows, shard, preferred_element_type=F32)  11 us
    dot_general x2, matrix products, this_product(): return jnp.dot(this, this_row, preferred_element_type=F32)  8.97 us
    all_to_all x1, waiting for transfers between devices, body(): lax.all_to_all(jnp.broadcast_to(queries[None], (n_fsdp,) + queries.shape)...  7.92 us
  transfers between devices with their start and end apart: 22, of which 10 were waited for; matrix products, arithmetic and copies ran while one was open for 23% of the time, Pallas kernels for 0%

profile of v5, /device:TPU:1, one launch (start us, length us, event | category | flops | bytes accessed | tf_op | source)
XLA Modules:
  0.0 198.4 jit_solution(1112102393436284377)
XLA Ops:
  6.5 2.2 %pad_maximum_fusion.2 = bf16[320,896]{1,0:T(8,128)(2,1)} fusion(bf16[320,448]{1,0:T(8,128)(2,1)} %param.14, bf16[320,448]{1,0:T(8,128)(2,1)} %param.13), kind=kLoop, calls=%fused_computation.24 | loop fusion | flops 1146880 | bytes 1146880 | tf_op jit(solution)/shard_map/concatenate | solution.py:132
  8.8 2.5 %collective-permute-start = (bf16[320,896]{1,0:T(8,128)(2,1)}, bf16[320,896]{1,0:T(8,128)(2,1)}, u32[]{:S(2)}, u32[]{:S(2)}) collective-permute-start(bf16[320,896]{1,0:T(8,128)(2,1)} %pad_maximum_fusion.2), channel_id=1, source_target_pairs={{0,16},{16,32},{32,48},{48,64},{64,80},{80,96},{96,112},{112,0},{1... | collective-permute-start | bytes 1720328 | tf_op jit(solution)/shard_map/ppermute | solution.py:11
  11.2 3.9 %collective-permute-start.1 = (bf16[320,896]{1,0:T(8,128)(2,1)}, bf16[320,896]{1,0:T(8,128)(2,1)}, u32[]{:S(2)}, u32[]{:S(2)}) collective-permute-start(bf16[320,896]{1,0:T(8,128)(2,1)} %pad_maximum_fusion.2), channel_id=1, source_target_pairs={{0,112},{16,0},{32,16},{48,32},{64,48},{80,64},{96,80},{112,96},{1... | collective-permute-start | bytes 1720328 | tf_op jit(solution)/shard_map/ppermute | solution.py:11
  15.2 1.1 constant_dynamic-slice_fusion.6
  17.2 2.9 %collective-permute-start.14 = (bf16[1,64,5120]{2,1,0:T(8,128)(2,1)}, bf16[1,64,5120]{2,1,0:T(8,128)(2,1)}, u32[]{:S(2)}, u32[]{:S(2)}) collective-permute-start(bf16[1,64,5120]{2,1,0:T(8,128)(2,1)} %pad_maximum_fusion.1), channel_id=1, source_target_pairs={{0,1},{1,0},{2,3},{3,2},{4,5},{5,4},{6,7},{7,6},{8,9},{9,8},{10,11... | collective-permute-start | bytes 1966088 | tf_op jit(solution)/shard_map/ppermute | solution.py:11
  20.1 2.5 %constant_dynamic-slice_fusion.10 = (bf16[8,32,448]{2,1,0:T(8,128)(2,1)}, bf16[8,32,448]{2,1,0:T(8,128)(2,1)S(1)}, bf16[8,32,448]{2,1,0:T(8,128)(2,1)S(1)}, bf16[8,32,448]{2,1,0:T(8,128)(2,1)}) fusion(bf16[8,32,896]{2,1,0:T(8,128)(2,1)} %param.12, s32[]{:T(128)S(6)} %select_n.182, s32[]{:T(128)S(6)} %select_n.183, bf16[8,32,896]{2,1,0:T(8,128)(2,1)} %param.10), kind=kLoop, calls=%fused_computation.140 | loop fusion | bytes 1835016 | tf_op jit(solution)/shard_map/dynamic_slice | solution.py:125
  22.6 4.6 %pad_maximum_fusion = bf16[8,64,5120]{2,1,0:T(8,128)(2,1)} fusion(bf16[8,32,5120]{2,1,0:T(8,128)(2,1)S(1)} %copy-done.7, bf16[8,32,5120]{2,1,0:T(8,128)(2,1)} %param.9), kind=kLoop, calls=%fused_computation | loop fusion | flops 10485760 | bytes 10485760 | tf_op jit(solution)/shard_map/concatenate | solution.py:122
  28.2 2.7 %collective-permute-start.3 = (bf16[320,896]{1,0:T(8,128)(2,1)}, bf16[320,896]{1,0:T(8,128)(2,1)S(1)}, u32[]{:S(2)}, u32[]{:S(2)}) collective-permute-start(bf16[320,896]{1,0:T(8,128)(2,1)} %collective-permute-done.1), channel_id=1, source_target_pairs={{0,112},{16,0},{32,16},{48,32},{64,48},{80,64},{96,80},{112,96},{1... | collective-permute-start | bytes 1720328 | tf_op jit(solution)/shard_map/ppermute | solution.py:11
  30.9 1.3 collective-permute-start.4
  32.2 10.7 %collective-permute-done.2 = bf16[320,896]{1,0:T(8,128)(2,1)S(1)} collective-permute-done((bf16[320,896]{1,0:T(8,128)(2,1)}, bf16[320,896]{1,0:T(8,128)(2,1)S(1)}, u32[]{:S(2)}, u32[]{:S(2)}) %collective-permute-start.2) | collective-permute-done | bytes 573472 | tf_op jit(solution)/shard_map/ppermute | solution.py:11
  42.9 3.9 %collective-permute-done.4 = bf16[320,896]{1,0:T(8,128)(2,1)S(1)} collective-permute-done((bf16[320,896]{1,0:T(8,128)(2,1)}, bf16[320,896]{1,0:T(8,128)(2,1)S(1)}, u32[]{:S(2)}, u32[]{:S(2)}) %collective-permute-start.4) | collective-permute-done | bytes 573472 | tf_op jit(solution)/shard_map/ppermute | solution.py:11
  47.6 1.4 bitcast_dynamic-update-slice_fusion.11
  49.0 1.1 bitcast_dynamic-update-slice_fusion.10
  50.1 2.4 %fusion.80 = f32[512,64]{0,1:T(8,128)} fusion(bf16[512,5120]{1,0:T(8,128)(2,1)S(1)} %bitcast.134, bf16[64,5120]{1,0:T(8,128)(2,1)S(1)} %copy-done), kind=kOutput, calls=%fused_computation.150 | convolution fusion | flops 335544320 | bytes 6029312 | tf_op jit(solution)/shard_map/dot_general | solution.py:160
  53.6 2.7 %collective-permute-start.6 = (bf16[320,896]{1,0:T(8,128)(2,1)S(1)}, bf16[320,896]{1,0:T(8,128)(2,1)S(1)}, u32[]{:S(2)}, u32[]{:S(2)}) collective-permute-start(bf16[320,896]{1,0:T(8,128)(2,1)S(1)} %collective-permute-done.3), channel_id=1, source_target_pairs={{0,112},{16,0},{32,16},{48,32},{64,48},{80,64},{96,80},{112,96},{1... | collective-permute-start | bytes 1720328 | tf_op jit(solution)/shard_map/ppermute | solution.py:11
  56.3 1.4 constant_dynamic-slice_fusion.3
  57.7 1.2 bitcast_dynamic-update-slice_fusion.9
  59.5 7.0 %collective-permute-done.5 = bf16[320,896]{1,0:T(8,128)(2,1)S(1)} collective-permute-done((bf16[320,896]{1,0:T(8,128)(2,1)S(1)}, bf16[320,896]{1,0:T(8,128)(2,1)S(1)}, u32[]{:S(2)}, u32[]{:S(2)}) %collective-permute-start.5) | collective-permute-done | bytes 573472 | tf_op jit(solution)/shard_map/ppermute | solution.py:11
  66.5 3.2 %collective-permute-start.9 = (bf16[320,896]{1,0:T(8,128)(2,1)S(1)}, bf16[320,896]{1,0:T(8,128)(2,1)S(1)}, u32[]{:S(2)}, u32[]{:S(2)}) collective-permute-start(bf16[320,896]{1,0:T(8,128)(2,1)S(1)} %collective-permute-done.4), channel_id=1, source_target_pairs={{0,112},{16,0},{32,16},{48,32},{64,48},{80,64},{96,80},{112,96},{1... | collective-permute-start | bytes 1720328 | tf_op jit(solution)/shard_map/ppermute | solution.py:11
  70.6 5.3 %collective-permute-done.13 = bf16[16,32,448]{2,1,0:T(8,128)(2,1)S(1)} collective-permute-done((bf16[16,32,448]{2,1,0:T(8,128)(2,1)S(1)}, bf16[16,32,448]{2,1,0:T(8,128)(2,1)S(1)}, u32[]{:S(2)}, u32[]{:S(2)}) %collective-permute-start.13) | collective-permute-done | bytes 458784 | tf_op jit(solution)/shard_map/ppermute | solution.py:11
  75.9 2.8 %collective-permute-start.12 = (bf16[160,896]{1,0:T(8,128)(2,1)S(1)}, bf16[160,896]{1,0:T(8,128)(2,1)S(1)}, u32[]{:S(2)}, u32[]{:S(2)}) collective-permute-start(bf16[160,896]{1,0:T(8,128)(2,1)S(1)} %slice.72), channel_id=1, source_target_pairs={{0,112},{16,0},{32,16},{48,32},{64,48},{80,64},{96,80},{112,96},{1... | collective-permute-start | bytes 860168 | tf_op jit(solution)/shard_map/ppermute | solution.py:11
  78.7 2.9 %fusion.6 = f32[512,896]{1,0:T(8,128)S(1)} fusion(bf16[2560,896]{1,0:T(8,128)(2,1)S(1)} %bitcast.150, bf16[512,5120]{1,0:T(8,128)(2,1)S(1)} %bitcast.136, s32[]{:T(128)S(6)} %select_n.184), kind=kOutput, calls=%fused_computation.7 | convolution fusion | flops 2348810240 | bytes 9043972 | tf_op jit(solution)/shard_map/dot_general | solution.py:72
  82.2 3.1 %collective-permute-done.11 = bf16[160,896]{1,0:T(8,128)(2,1)S(1)} collective-permute-done((bf16[160,896]{1,0:T(8,128)(2,1)S(1)}, bf16[160,896]{1,0:T(8,128)(2,1)S(1)}, u32[]{:S(2)}, u32[]{:S(2)}) %collective-permute-start.11) | collective-permute-done | bytes 286752 | tf_op jit(solution)/shard_map/ppermute | solution.py:11
  85.4 3.4 %collective-permute-done.10 = bf16[320,896]{1,0:T(8,128)(2,1)} collective-permute-done((bf16[320,896]{1,0:T(8,128)(2,1)S(1)}, bf16[320,896]{1,0:T(8,128)(2,1)}, u32[]{:S(2)}, u32[]{:S(2)}) %collective-permute-start.10) | collective-permute-done | bytes 573472 | tf_op jit(solution)/shard_map/ppermute | solution.py:11
  88.8 1.2 collective-permute-start.15
  90.0 2.7 %collective-permute-start.17 = (bf16[320,896]{1,0:T(8,128)(2,1)}, bf16[320,896]{1,0:T(8,128)(2,1)}, u32[]{:S(2)}, u32[]{:S(2)}) collective-permute-start(bf16[320,896]{1,0:T(8,128)(2,1)} %collective-permute-done.10), channel_id=1, source_target_pairs={{0,112},{16,0},{32,16},{48,32},{64,48},{80,64},{96,80},{112,96},{1... | collective-permute-start | bytes 1720328 | tf_op jit(solution)/shard_map/ppermute | solution.py:11
  93.7 1.1 bitcast_dynamic-update-slice_fusion.1
  94.8 1.1 bitcast_dynamic-update-slice_fusion
  96.0 2.9 %fusion.4 = f32[512,896]{1,0:T(8,128)S(1)} fusion(bf16[2560,896]{1,0:T(8,128)(2,1)S(1)} %bitcast.148, bf16[512,5120]{1,0:T(8,128)(2,1)S(1)} %bitcast.137, s32[]{:T(128)S(6)} %select_n.199), kind=kOutput, calls=%fused_computation.5 | convolution fusion | flops 2348810240 | bytes 9043972 | tf_op jit(solution)/shard_map/dot_general | solution.py:156
  99.7 6.1 %fusion.2 = f32[512,896]{1,0:T(8,128)S(1)} fusion(bf16[2560,896]{1,0:T(8,128)(2,1)} %bitcast.151, bf16[512,5120]{1,0:T(8,128)(2,1)} %bitcast.139, s32[]{:T(128)S(6)} %select_n.184), kind=kOutput, calls=%fused_computation.3 | convolution fusion | flops 2348810240 | bytes 9043972 | tf_op jit(solution)/shard_map/dot_general | solution.py:72
  105.8 2.9 %fusion = f32[512,896]{1,0:T(8,128)S(1)} fusion(bf16[2560,896]{1,0:T(8,128)(2,1)S(1)} %bitcast.149, bf16[512,5120]{1,0:T(8,128)(2,1)S(1)} %bitcast.140, s32[]{:T(128)S(6)} %select_n.199), kind=kOutput, calls=%fused_computation.1 | convolution fusion | flops 2348810240 | bytes 9043972 | tf_op jit(solution)/shard_map/dot_general | solution.py:156
  108.7 2.0 %add_add_fusion.2 = f32[512,896]{1,0:T(8,128)} fusion(f32[512,896]{1,0:T(8,128)S(1)} %fusion.2, f32[512,896]{1,0:T(8,128)S(1)} %fusion, bf16[320,896]{1,0:T(8,128)(2,1)S(1)} %constant_dynamic-update-slice_fusion, bf16[512,5120]{1,0:T(8,128)(2,1)S(1)} %bitcast.141, s32[]{:T(128)S(6)} %select_n.201), kind=kOutput, calls=%fused_computation.11 | convolution fusion | flops 294518784 | bytes 6471684 | tf_op jit(solution)/shard_map/dot_general | solution.py:157
  110.8 1.5 constant_dynamic-slice_fusion
  112.3 2.4 %fusion.81 = f32[512,64]{0,1:T(8,128)} fusion(bf16[512,5120]{1,0:T(8,128)(2,1)S(1)} %bitcast.143, bf16[64,5120]{1,0:T(8,128)(2,1)S(1)} %copy-done), kind=kOutput, calls=%fused_computation.151 | convolution fusion | flops 335544320 | bytes 6029312 | tf_op jit(solution)/shard_map/dot_general | solution.py:160
  115.8 1.7 copy.27
  117.5 2.0 fusion.85
  119.5 1.8 fusion.84
  121.4 1.8 add_add_fusion
  123.3 1.7 fusion.83
  125.0 1.7 fusion.82
  126.8 1.9 add_add_fusion.1
  133.1 8.2 %all-to-all-start.1 = ((bf16[16,8,512]{2,1,0:T(8,128)(2,1)}), bf16[16,8,512]{2,1,0:T(8,128)(2,1)S(1)}, u32[]{:S(2)}, u32[]{:S(2)}) async-start(bf16[16,8,512]{2,1,0:T(8,128)(2,1)} %pad_maximum_fusion.6), calls=%async_computation.1 | async-start | bytes 262144 | tf_op jit(solution)/shard_map/all_to_all | solution.py:196
  142.0 7.3 %all-to-all-done.1 = bf16[16,8,512]{2,1,0:T(8,128)(2,1)S(1)} async-done(((bf16[16,8,512]{2,1,0:T(8,128)(2,1)}), bf16[16,8,512]{2,1,0:T(8,128)(2,1)S(1)}, u32[]{:S(2)}, u32[]{:S(2)}) %all-to-all-start.1) | async-done | bytes 131104 | tf_op jit(solution)/shard_map/all_to_all | solution.py:196
  149.3 3.7 %all-to-all-start = ((bf16[16,8,512]{2,1,0:T(8,128)(2,1)}), bf16[16,8,512]{2,1,0:T(8,128)(2,1)S(1)}, u32[]{:S(2)}, u32[]{:S(2)}) async-start(bf16[16,8,512]{2,1,0:T(8,128)(2,1)} %pad_maximum_fusion.9), calls=%async_computation | async-start | bytes 262144 | tf_op jit(solution)/shard_map/all_to_all | solution.py:196
  153.5 7.5 %all-to-all-done = bf16[16,8,512]{2,1,0:T(8,128)(2,1)S(1)} async-done(((bf16[16,8,512]{2,1,0:T(8,128)(2,1)}), bf16[16,8,512]{2,1,0:T(8,128)(2,1)S(1)}, u32[]{:S(2)}, u32[]{:S(2)}) %all-to-all-start) | async-done | bytes 131104 | tf_op jit(solution)/shard_map/all_to_all | solution.py:196
  161.8 5.9 %all-to-all-start.2 = ((bf16[16,16,512]{2,1,0:T(8,128)(2,1)}), bf16[16,16,512]{2,1,0:T(8,128)(2,1)S(1)}, u32[]{:S(2)}, u32[]{:S(2)}) async-start(bf16[16,16,512]{2,1,0:T(8,128)(2,1)} %broadcast_in_dim.69), calls=%async_computation.2 | async-start | bytes 524288 | tf_op jit(solution)/shard_map/all_to_all | solution.py:215
  168.7 7.9 %all-to-all-done.2 = bf16[16,16,512]{2,1,0:T(8,128)(2,1)S(1)} async-done(((bf16[16,16,512]{2,1,0:T(8,128)(2,1)}), bf16[16,16,512]{2,1,0:T(8,128)(2,1)S(1)}, u32[]{:S(2)}, u32[]{:S(2)}) %all-to-all-start.2) | async-done | bytes 262176 | tf_op jit(solution)/shard_map/all_to_all | solution.py:215
  177.2 12.5 %all_to_all.24 = f32[16,1,640]{2,1,0:T(1,128)S(1)} all-to-all(f32[16,1,640]{2,1,0:T(1,128)S(1)} %copy.35), channel_id=1, replica_groups=mesh['ylo'=2,'z'=8,'x'=4,'core'=2,'yhi'=2] {'x','core','yhi'}, dimensions={0} | all-to-all | bytes 81920 | tf_op jit(solution)/shard_map/all_to_all | solution.py:239
  (122 shorter events, 17.7 us)
Async XLA Ops:
  6.5 43.6 %copy-start = (bf16[64,5120]{1,0:T(8,128)(2,1)S(1)}, bf16[64,5120]{1,0:T(8,128)(2,1)}, u32[]{:S(2)}) copy-start(bf16[64,5120]{1,0:T(8,128)(2,1)} %param.15) | copy-start | bytes 1966084
  6.5 16.1 %copy-start.7 = (bf16[8,32,5120]{2,1,0:T(8,128)(2,1)S(1)}, bf16[8,32,5120]{2,1,0:T(8,128)(2,1)}, u32[]{:S(2)}) copy-start(bf16[8,32,5120]{2,1,0:T(8,128)(2,1)} %param.11) | copy-start | bytes 7864324
  6.5 93.1 %all-gather.2.cloned.1.call-start = ((), (), s32[]{:S(2)}) async-start(), calls=%async_computation.4 | async-start | bytes 5898240 | tf_op jit(solution)/shard_map/all_gather | solution.py:40
  8.8 19.4 %collective-permute-start = (bf16[320,896]{1,0:T(8,128)(2,1)}, bf16[320,896]{1,0:T(8,128)(2,1)}, u32[]{:S(2)}, u32[]{:S(2)}) collective-permute-start(bf16[320,896]{1,0:T(8,128)(2,1)} %pad_maximum_fusion.2), channel_id=1, source_target_pairs={{0,16},{16,32},{32,48},{48,64},{64,80},{80,96},{96,112},{112,0},{1... | collective-permute-start | bytes 1720328 | tf_op jit(solution)/shard_map/ppermute | solution.py:11
  11.2 17.0 %collective-permute-start.1 = (bf16[320,896]{1,0:T(8,128)(2,1)}, bf16[320,896]{1,0:T(8,128)(2,1)}, u32[]{:S(2)}, u32[]{:S(2)}) collective-permute-start(bf16[320,896]{1,0:T(8,128)(2,1)} %pad_maximum_fusion.2), channel_id=1, source_target_pairs={{0,112},{16,0},{32,16},{48,32},{64,48},{80,64},{96,80},{112,96},{1... | collective-permute-start | bytes 1720328 | tf_op jit(solution)/shard_map/ppermute | solution.py:11
  17.2 29.6 %collective-permute-start.14 = (bf16[1,64,5120]{2,1,0:T(8,128)(2,1)}, bf16[1,64,5120]{2,1,0:T(8,128)(2,1)}, u32[]{:S(2)}, u32[]{:S(2)}) collective-permute-start(bf16[1,64,5120]{2,1,0:T(8,128)(2,1)} %pad_maximum_fusion.1), channel_id=1, source_target_pairs={{0,1},{1,0},{2,3},{3,2},{4,5},{5,4},{6,7},{7,6},{8,9},{9,8},{10,11... | collective-permute-start | bytes 1966088 | tf_op jit(solution)/shard_map/ppermute | solution.py:11
  28.2 14.7 %collective-permute-start.2 = (bf16[320,896]{1,0:T(8,128)(2,1)}, bf16[320,896]{1,0:T(8,128)(2,1)S(1)}, u32[]{:S(2)}, u32[]{:S(2)}) collective-permute-start(bf16[320,896]{1,0:T(8,128)(2,1)} %collective-permute-done), channel_id=1, source_target_pairs={{0,16},{16,32},{32,48},{48,64},{64,80},{80,96},{96,112},{112,0},{1... | collective-permute-start | bytes 1720328 | tf_op jit(solution)/shard_map/ppermute | solution.py:11
  28.2 14.7 %collective-permute-start.3 = (bf16[320,896]{1,0:T(8,128)(2,1)}, bf16[320,896]{1,0:T(8,128)(2,1)S(1)}, u32[]{:S(2)}, u32[]{:S(2)}) collective-permute-start(bf16[320,896]{1,0:T(8,128)(2,1)} %collective-permute-done.1), channel_id=1, source_target_pairs={{0,112},{16,0},{32,16},{48,32},{64,48},{80,64},{96,80},{112,96},{1... | collective-permute-start | bytes 1720328 | tf_op jit(solution)/shard_map/ppermute | solution.py:11
  30.9 15.9 %collective-permute-start.4 = (bf16[320,896]{1,0:T(8,128)(2,1)}, bf16[320,896]{1,0:T(8,128)(2,1)S(1)}, u32[]{:S(2)}, u32[]{:S(2)}) collective-permute-start(bf16[320,896]{1,0:T(8,128)(2,1)} %pad_maximum_fusion.2), channel_id=1, source_target_pairs={{0,128},{128,0},{1,129},{129,1},{2,130},{130,2},{3,131},{131,3},{4... | collective-permute-start | bytes 1720328 | tf_op jit(solution)/shard_map/ppermute | solution.py:11
  47.0 3.2 %copy-start.1 = (bf16[8,64,5120]{2,1,0:T(8,128)(2,1)S(1)}, bf16[8,64,5120]{2,1,0:T(8,128)(2,1)}, u32[]{:S(2)}) copy-start(bf16[8,64,5120]{2,1,0:T(8,128)(2,1)} %pad_maximum_fusion) | copy-start | bytes 15728644
  52.5 13.9 %collective-permute-start.5 = (bf16[320,896]{1,0:T(8,128)(2,1)S(1)}, bf16[320,896]{1,0:T(8,128)(2,1)S(1)}, u32[]{:S(2)}, u32[]{:S(2)}) collective-permute-start(bf16[320,896]{1,0:T(8,128)(2,1)S(1)} %collective-permute-done.2), channel_id=1, source_target_pairs={{0,16},{16,32},{32,48},{48,64},{64,80},{80,96},{96,112},{112,0},{1... | collective-permute-start | bytes 1720328 | tf_op jit(solution)/shard_map/ppermute | solution.py:11
  52.5 13.9 %collective-permute-start.7 = (bf16[320,896]{1,0:T(8,128)(2,1)S(1)}, bf16[320,896]{1,0:T(8,128)(2,1)}, u32[]{:S(2)}, u32[]{:S(2)}) collective-permute-start(bf16[320,896]{1,0:T(8,128)(2,1)S(1)} %collective-permute-done.2), channel_id=1, source_target_pairs={{0,128},{128,0},{1,129},{129,1},{2,130},{130,2},{3,131},{131,3},{4... | collective-permute-start | bytes 1720328 | tf_op jit(solution)/shard_map/ppermute | solution.py:11
  53.6 12.9 %collective-permute-start.6 = (bf16[320,896]{1,0:T(8,128)(2,1)S(1)}, bf16[320,896]{1,0:T(8,128)(2,1)S(1)}, u32[]{:S(2)}, u32[]{:S(2)}) collective-permute-start(bf16[320,896]{1,0:T(8,128)(2,1)S(1)} %collective-permute-done.3), channel_id=1, source_target_pairs={{0,112},{16,0},{32,16},{48,32},{64,48},{80,64},{96,80},{112,96},{1... | collective-permute-start | bytes 1720328 | tf_op jit(solution)/shard_map/ppermute | solution.py:11
  58.9 17.1 %collective-permute-start.13 = (bf16[16,32,448]{2,1,0:T(8,128)(2,1)S(1)}, bf16[16,32,448]{2,1,0:T(8,128)(2,1)S(1)}, u32[]{:S(2)}, u32[]{:S(2)}) collective-permute-start(bf16[16,32,448]{2,1,0:T(8,128)(2,1)S(1)} %pad_maximum_fusion.3), channel_id=1, source_target_pairs={{0,1},{1,0},{2,3},{3,2},{4,5},{5,4},{6,7},{7,6},{8,9},{9,8},{10,11... | collective-permute-start | bytes 1376264 | tf_op jit(solution)/shard_map/ppermute | solution.py:11
  66.5 18.9 %collective-permute-start.8 = (bf16[320,896]{1,0:T(8,128)(2,1)S(1)}, bf16[320,896]{1,0:T(8,128)(2,1)S(1)}, u32[]{:S(2)}, u32[]{:S(2)}) collective-permute-start(bf16[320,896]{1,0:T(8,128)(2,1)S(1)} %collective-permute-done.4), channel_id=1, source_target_pairs={{0,16},{16,32},{32,48},{48,64},{64,80},{80,96},{96,112},{112,0},{1... | collective-permute-start | bytes 1720328 | tf_op jit(solution)/shard_map/ppermute | solution.py:11
  66.5 18.9 %collective-permute-start.9 = (bf16[320,896]{1,0:T(8,128)(2,1)S(1)}, bf16[320,896]{1,0:T(8,128)(2,1)S(1)}, u32[]{:S(2)}, u32[]{:S(2)}) collective-permute-start(bf16[320,896]{1,0:T(8,128)(2,1)S(1)} %collective-permute-done.4), channel_id=1, source_target_pairs={{0,112},{16,0},{32,16},{48,32},{64,48},{80,64},{96,80},{112,96},{1... | collective-permute-start | bytes 1720328 | tf_op jit(solution)/shard_map/ppermute | solution.py:11
  69.6 19.1 %collective-permute-start.10 = (bf16[320,896]{1,0:T(8,128)(2,1)S(1)}, bf16[320,896]{1,0:T(8,128)(2,1)}, u32[]{:S(2)}, u32[]{:S(2)}) collective-permute-start(bf16[320,896]{1,0:T(8,128)(2,1)S(1)} %collective-permute-done.3), channel_id=1, source_target_pairs={{0,128},{128,0},{1,129},{129,1},{2,130},{130,2},{3,131},{131,3},{4... | collective-permute-start | bytes 1720328 | tf_op jit(solution)/shard_map/ppermute | solution.py:11
  70.2 15.1 %collective-permute-start.11 = (bf16[160,896]{1,0:T(8,128)(2,1)S(1)}, bf16[160,896]{1,0:T(8,128)(2,1)S(1)}, u32[]{:S(2)}, u32[]{:S(2)}) collective-permute-start(bf16[160,896]{1,0:T(8,128)(2,1)S(1)} %slice.71), channel_id=1, source_target_pairs={{0,16},{16,32},{32,48},{48,64},{64,80},{80,96},{96,112},{112,0},{1... | collective-permute-start | bytes 860168 | tf_op jit(solution)/shard_map/ppermute | solution.py:11
  70.6 8.1 %copy-start.6 = (bf16[8,320,896]{2,1,0:T(8,128)(2,1)}, bf16[8,320,896]{2,1,0:T(8,128)(2,1)S(1)}, u32[]{:S(2)}) copy-start(bf16[8,320,896]{2,1,0:T(8,128)(2,1)S(1)} %bitcast_dynamic-update-slice_fusion.5) | copy-start | bytes 13762564
  75.9 9.5 %collective-permute-start.12 = (bf16[160,896]{1,0:T(8,128)(2,1)S(1)}, bf16[160,896]{1,0:T(8,128)(2,1)S(1)}, u32[]{:S(2)}, u32[]{:S(2)}) collective-permute-start(bf16[160,896]{1,0:T(8,128)(2,1)S(1)} %slice.72), channel_id=1, source_target_pairs={{0,112},{16,0},{32,16},{48,32},{64,48},{80,64},{96,80},{112,96},{1... | collective-permute-start | bytes 860168 | tf_op jit(solution)/shard_map/ppermute | solution.py:11
  88.8 25.8 %collective-permute-start.15 = (bf16[320,896]{1,0:T(8,128)(2,1)S(1)}, bf16[320,896]{1,0:T(8,128)(2,1)}, u32[]{:S(2)}, u32[]{:S(2)}) collective-permute-start(bf16[320,896]{1,0:T(8,128)(2,1)S(1)} %constant_dynamic-update-slice_fusion), channel_id=1, source_target_pairs={{0,128},{128,0},{1,129},{129,1},{2,130},{130,2},{3,131},{131,3},{4... | collective-permute-start | bytes 1720328 | tf_op jit(solution)/shard_map/ppermute | solution.py:11
  90.0 24.7 %collective-permute-start.16 = (bf16[320,896]{1,0:T(8,128)(2,1)}, bf16[320,896]{1,0:T(8,128)(2,1)}, u32[]{:S(2)}, u32[]{:S(2)}) collective-permute-start(bf16[320,896]{1,0:T(8,128)(2,1)} %collective-permute-done.7), channel_id=1, source_target_pairs={{0,16},{16,32},{32,48},{48,64},{64,80},{80,96},{96,112},{112,0},{1... | collective-permute-start | bytes 1720328 | tf_op jit(solution)/shard_map/ppermute | solution.py:11
  90.0 24.7 %collective-permute-start.17 = (bf16[320,896]{1,0:T(8,128)(2,1)}, bf16[320,896]{1,0:T(8,128)(2,1)}, u32[]{:S(2)}, u32[]{:S(2)}) collective-permute-start(bf16[320,896]{1,0:T(8,128)(2,1)} %collective-permute-done.10), channel_id=1, source_target_pairs={{0,112},{16,0},{32,16},{48,32},{64,48},{80,64},{96,80},{112,96},{1... | collective-permute-start | bytes 1720328 | tf_op jit(solution)/shard_map/ppermute | solution.py:11
  95.9 2.9 %copy-start.4 = (bf16[8,320,896]{2,1,0:T(8,128)(2,1)}, bf16[8,320,896]{2,1,0:T(8,128)(2,1)S(1)}, u32[]{:S(2)}) copy-start(bf16[8,320,896]{2,1,0:T(8,128)(2,1)S(1)} %bitcast_dynamic-update-slice_fusion) | copy-start | bytes 13762564
  99.7 6.1 %copy-start.2 = (bf16[8,64,5120]{2,1,0:T(8,128)(2,1)S(1)}, bf16[8,64,5120]{2,1,0:T(8,128)(2,1)}, u32[]{:S(2)}) copy-start(bf16[8,64,5120]{2,1,0:T(8,128)(2,1)} %all-gather.2.cloned.1.call-done) | copy-start | bytes 15728644
  99.7 6.1 %copy-start.5 = (bf16[8,320,896]{2,1,0:T(8,128)(2,1)S(1)}, bf16[8,320,896]{2,1,0:T(8,128)(2,1)}, u32[]{:S(2)}) copy-start(bf16[8,320,896]{2,1,0:T(8,128)(2,1)} %copy-done.4) | copy-start | bytes 13762564
  114.7 6.6 %copy-start.8 = (bf16[512,320]{1,0:T(8,128)(2,1)S(1)}, bf16[512,320]{1,0:T(8,128)(2,1)}, u32[]{:S(2)}) copy-start(bf16[512,320]{1,0:T(8,128)(2,1)} %get-tuple-element.77) | copy-start | bytes 983044
  117.5 3.8 %copy-start.3 = (f32[512,896]{1,0:T(8,128)S(1)}, f32[512,896]{1,0:T(8,128)}, u32[]{:S(2)}) copy-start(f32[512,896]{1,0:T(8,128)} %add_add_fusion.2) | copy-start | bytes 5505028
  121.3 1.9 copy-start.10
  121.3 3.7 %copy-start.9 = (bf16[512,320]{1,0:T(8,128)(2,1)S(1)}, bf16[512,320]{1,0:T(8,128)(2,1)}, u32[]{:S(2)}) copy-start(bf16[512,320]{1,0:T(8,128)(2,1)} %get-tuple-element.67) | copy-start | bytes 983044
  126.7 2.0 %copy-start.12 = (bf16[8,32,448]{2,1,0:T(8,128)(2,1)S(1)}, bf16[8,32,448]{2,1,0:T(8,128)(2,1)}, u32[]{:S(2)}) copy-start(bf16[8,32,448]{2,1,0:T(8,128)(2,1)} %get-tuple-element.102) | copy-start | bytes 688132
  126.8 2.6 %copy-start.16 = (bf16[64,896]{1,0:T(8,128)(2,1)S(1)}, bf16[64,896]{1,0:T(8,128)(2,1)}, u32[]{:S(2)}) copy-start(bf16[64,896]{1,0:T(8,128)(2,1)} %param.17) | copy-start | bytes 344068
  126.8 2.9 %copy-start.15 = (bf16[8,32,448]{2,1,0:T(8,128)(2,1)S(1)}, bf16[8,32,448]{2,1,0:T(8,128)(2,1)}, u32[]{:S(2)}) copy-start(bf16[8,32,448]{2,1,0:T(8,128)(2,1)} %get-tuple-element.105) | copy-start | bytes 688132
  128.7 1.5 copy-start.17
  128.7 2.7 %copy-start.11 = (bf16[8,32,448]{2,1,0:T(8,128)(2,1)S(1)}, bf16[8,32,448]{2,1,0:T(8,128)(2,1)}, u32[]{:S(2)}) copy-start(bf16[8,32,448]{2,1,0:T(8,128)(2,1)} %get-tuple-element.101) | copy-start | bytes 688132
  129.6 2.7 %copy-start.14 = (bf16[8,32,448]{2,1,0:T(8,128)(2,1)S(1)}, bf16[8,32,448]{2,1,0:T(8,128)(2,1)}, u32[]{:S(2)}) copy-start(bf16[8,32,448]{2,1,0:T(8,128)(2,1)} %get-tuple-element.114) | copy-start | bytes 688132
  131.3 9.9 %copy-start.13 = (f32[512,64]{1,0:T(8,128)S(1)}, f32[512,64]{1,0:T(8,128)}, u32[]{:S(2)}) copy-start(f32[512,64]{1,0:T(8,128)} %copy.27) | copy-start | bytes 393220
  133.1 16.2 %all-to-all-start.1 = ((bf16[16,8,512]{2,1,0:T(8,128)(2,1)}), bf16[16,8,512]{2,1,0:T(8,128)(2,1)S(1)}, u32[]{:S(2)}, u32[]{:S(2)}) async-start(bf16[16,8,512]{2,1,0:T(8,128)(2,1)} %pad_maximum_fusion.6), calls=%async_computation.1 | async-start | bytes 262144 | tf_op jit(solution)/shard_map/all_to_all | solution.py:196
  149.3 11.8 %all-to-all-start = ((bf16[16,8,512]{2,1,0:T(8,128)(2,1)}), bf16[16,8,512]{2,1,0:T(8,128)(2,1)S(1)}, u32[]{:S(2)}, u32[]{:S(2)}) async-start(bf16[16,8,512]{2,1,0:T(8,128)(2,1)} %pad_maximum_fusion.9), calls=%async_computation | async-start | bytes 262144 | tf_op jit(solution)/shard_map/all_to_all | solution.py:196
  161.8 14.9 %all-to-all-start.2 = ((bf16[16,16,512]{2,1,0:T(8,128)(2,1)}), bf16[16,16,512]{2,1,0:T(8,128)(2,1)S(1)}, u32[]{:S(2)}, u32[]{:S(2)}) async-start(bf16[16,16,512]{2,1,0:T(8,128)(2,1)} %broadcast_in_dim.69), calls=%async_computation.2 | async-start | bytes 524288 | tf_op jit(solution)/shard_map/all_to_all | solution.py:215
Sparse Core Ops, SparseCore 0:
  46.9 39.3 all-gather.1

commit v6 on v4

--- a/solution.py
+++ b/solution.py
@@ -11,7 +11,7 @@
     return lax.ppermute(value, axis, [(i, (i + step) % size) for i in range(size)])
 
 
-def gathered(weight, piece, cot, early):
+def gathered(weight, piece, cot, early, this_product):
     barrier = lax.optimization_barrier
     n_z = lax.axis_size("z")
     z = lax.axis_index("z")
@@ -40,8 +40,21 @@
     a2, b2, o0, cot = barrier((up(a1), down(b1), across(w0), cot))
     a3, b3, oa2, o0, b2 = barrier((up(a2), down(b2), across(a2), o0, b2))
     other_cot = shift(cot, "yhi", 1)
-    oa1, ob1, ob2, a4, b4, oa2, other_cot = barrier(
-        (up(o0), down(o0), across(b2), up(a3[:half]), down(b3[half:]), oa2, other_cot)
+    this_row = placed(
+        ((0, w0), (n_z - 1, a1), (1, b1), (n_z - 2, a2), (2, b2), (n_z - 3, a3), (3, b3))
+    )
+    own_sum = this_product(early[0], this_row)
+    oa1, ob1, ob2, a4, b4, oa2, other_cot, own_sum = barrier(
+        (
+            up(o0),
+            down(o0),
+            across(b2),
+            up(a3[:half]),
+            down(b3[half:]),
+            oa2,
+            other_cot,
+            own_sum,
+        )
     )
     a4 = jnp.concatenate((a4, b4), axis=0)
     last = (
@@ -49,20 +62,9 @@
         (up(oa2), (z + n_z - 3) % n_z),
         (down(ob2), (z + 3) % n_z),
     )
-    this_row = placed(
-        (
-            (0, w0),
-            (n_z - 1, a1),
-            (1, b1),
-            (n_z - 2, a2),
-            (2, b2),
-            (n_z - 3, a3),
-            (3, b3),
-            (n_z // 2, a4),
-        )
-    )
     other_row = placed(((0, o0), (n_z - 1, oa1), (1, ob1), (n_z - 2, oa2), (2, ob2)))
-    return this_row, other_row, last, other_cot, partner, early
+    sums = (own_sum, this_product(partner, this_row))
+    return sums, (a4, far_z), other_row, last, other_cot, partner, early
 
 
 def projected(pre, cotangent, gate_projection, up_projection):
@@ -125,36 +127,50 @@
 
     own_cot = cotangents(half_index)
     weight = jnp.concatenate((gate_weight, up_weight), axis=1)
-    this_row, other_row, last, other_cot, other, (own, own_cot) = gathered(
-        weight, piece, cotangents(1 - half_index), (own, own_cot)
+
+    def half_of(rows, side, depth):
+        return lax.dynamic_slice_in_dim(rows.reshape(-1, width), side * depth, depth, 1)
+
+    def this_product(rows, this_row):
+        flat = half_of(rows, row_index, this_row.shape[0])
+        return jnp.dot(flat, this_row, preferred_element_type=F32)
+
+    sums, far, other_row, last, other_cot, other, (own, own_cot) = gathered(
+        weight, piece, cotangents(1 - half_index), (own, own_cot), this_product
     )
     gate_proj = columns(gate_projection, half_index)
     up_proj = columns(up_projection, half_index)
 
-    depth = this_row.shape[0]
+    def inner_factor(rows):
+        return lax.dot_general(
+            rows.reshape(-1, width),
+            input_projection,
+            (((1,), (1,)), ((), ())),
+            preferred_element_type=F32,
+        )
+
+    depth = other_row.shape[0]
     shard_depth = weight.shape[0]
     pres = []
-    factors = []
     chunks = []
-    for rows in (own, other):
+    for rows, pre in zip((own, other), sums):
         flat = rows.reshape(-1, width)
-        this_flat = lax.dynamic_slice_in_dim(flat, row_index * depth, depth, 1)
-        other_flat = lax.dynamic_slice_in_dim(flat, (1 - row_index) * depth, depth, 1)
-        pre = jnp.dot(this_flat, this_row, preferred_element_type=F32)
-        pres.append(pre + jnp.dot(other_flat, other_row, preferred_element_type=F32))
-        factors.append(
-            lax.dot_general(
-                flat, input_projection, (((1,), (1,)), ((), ())), preferred_element_type=F32
+
+        def chunk(side, place):
+            return lax.dynamic_slice_in_dim(
+                flat, side * depth + place * shard_depth, shard_depth, 1
             )
-        )
-        chunks.append(
-            [
-                lax.dynamic_slice_in_dim(other_flat, place * shard_depth, shard_depth, 1)
-                for _, place in last
-            ]
-        )
+
+        other_flat = half_of(rows, 1 - row_index, depth)
+        pre = pre + jnp.dot(other_flat, other_row, preferred_element_type=F32)
+        pres.append(pre + jnp.dot(chunk(row_index, far[1]), far[0], preferred_element_type=F32))
+        chunks.append([chunk(1 - row_index, place) for _, place in last])
     shards = [shard for shard, _ in last]
-    pres, factors, chunks, shards = lax.optimization_barrier((pres, factors, chunks, shards))
+    own_factor = inner_factor(own)
+    pres, chunks, shards, own_factor, other = lax.optimization_barrier(
+        (pres, chunks, shards, own_factor, other)
+    )
+    factors = (own_factor, inner_factor(other))
     parts = []
     for pre, pieces, rows_cot in zip(pres, chunks, (own_cot, other_cot)):
         for chunk, shard in zip(pieces, shards):

time: 180 us -> 182 us (1.011)
  matrix products: 28 us -> 34.2 us
  waiting for transfers between devices: 51.1 us -> 46.9 us
  local copies, waits for them, and re-layouts: 17.5 us -> 15.5 us
    dot_general x6, matrix products: 4.18 us -> 10.7 us  [body(): pre = pre + jnp.dot(chunk, shard, preferred_element_type=F32)]
    ppermute x18, waiting for transfers between devices: 33.5 us -> 29.3 us  [shift(): lax.ppermute(value, axis, [(i, (i + step) % size) for i in range(size)])]
    dynamic_update_slice x13 -> x12, local copies, waits for them, and re-layouts: 7.8 us -> 6.2 us  [placed(): lax.dynamic_update_slice(result, shard[None], ((z + offset) % n_z, 0, 0))]
    dot_general x6 -> x8, matrix products: 20.7 us -> 20.4 us  [the longest x2 8.97 us: this_product(): return jnp.dot(flat, this_row, preferred_element_type=F32)]
  transfers between devices with their start and end apart: 21 -> 21, of which waited for: 11 -> 10; matrix products, arithmetic and copies ran while one was open for 23% -> 21% of each run, Pallas kernels for 0% -> 0%
where the time goes in v6:
time: 182 us; the launch traced here: 181 us
  starting transfers between devices  47.9 us (26%)
  waiting for transfers between devices  46.9 us (26%)
  matrix products  34.2 us (19%)
  local copies, waits for them, and re-layouts  15.5 us (9%)
  between operations  14.8 us (8%)
  blocking collectives  12.1 us (7%)
  other arithmetic  9.41 us (5%)
    ppermute x18, starting transfers between devices, shift(): lax.ppermute(value, axis, [(i, (i + step) % size) for i in range(size)])  30.1 us
    ppermute x18, waiting for transfers between devices, shift(): lax.ppermute(value, axis, [(i, (i + step) % size) for i in range(size)])  29.3 us
    all_to_all x1, starting transfers between devices, body(): swapped = lax.all_to_all(part, dq, 0, 0, tiled=True)  12.5 us
    all_to_all x1, blocking collectives, body(): received = lax.all_to_all(payload, dq, 0, 0, tiled=True)  12.1 us
    dot_general x6, matrix products, body(): pre = pre + jnp.dot(chunk, shard, preferred_element_type=F32)  10.7 us
    all_to_all x1, waiting for transfers between devices, body(): swapped = lax.all_to_all(part, dq, 0, 0, tiled=True)  9.11 us
    dot_general x2, matrix products, this_product(): return jnp.dot(flat, this_row, preferred_element_type=F32)  8.97 us
    all_to_all x1, waiting for transfers between devices, body(): lax.all_to_all(jnp.broadcast_to(queries[None], (n_fsdp,) + queries.shape)...  8.5 us
  transfers between devices with their start and end apart: 21, of which 10 were waited for; matrix products, arithmetic and copies ran while one was open for 21% of the time, Pallas kernels for 0%

profile of v6, /device:TPU:1, one launch (start us, length us, event | category | flops | bytes accessed | tf_op | source)
XLA Modules:
  0.0 180.9 jit_solution(10568915593245310228)
XLA Ops:
  6.5 2.2 %pad_maximum_fusion.2 = bf16[320,896]{1,0:T(8,128)(2,1)} fusion(bf16[320,448]{1,0:T(8,128)(2,1)} %param.14, bf16[320,448]{1,0:T(8,128)(2,1)} %param.13), kind=kLoop, calls=%fused_computation.31 | loop fusion | flops 1146880 | bytes 1146880 | tf_op jit(solution)/shard_map/concatenate | solution.py:129
  8.8 2.5 %collective-permute-start = (bf16[320,896]{1,0:T(8,128)(2,1)}, bf16[320,896]{1,0:T(8,128)(2,1)}, u32[]{:S(2)}, u32[]{:S(2)}) collective-permute-start(bf16[320,896]{1,0:T(8,128)(2,1)} %pad_maximum_fusion.2), channel_id=1, source_target_pairs={{0,16},{16,32},{32,48},{48,64},{64,80},{80,96},{96,112},{112,0},{1... | collective-permute-start | bytes 1720328 | tf_op jit(solution)/shard_map/ppermute | solution.py:11
  11.2 3.9 %collective-permute-start.1 = (bf16[320,896]{1,0:T(8,128)(2,1)}, bf16[320,896]{1,0:T(8,128)(2,1)}, u32[]{:S(2)}, u32[]{:S(2)}) collective-permute-start(bf16[320,896]{1,0:T(8,128)(2,1)} %pad_maximum_fusion.2), channel_id=1, source_target_pairs={{0,112},{16,0},{32,16},{48,32},{64,48},{80,64},{96,80},{112,96},{1... | collective-permute-start | bytes 1720328 | tf_op jit(solution)/shard_map/ppermute | solution.py:11
  15.2 1.1 constant_dynamic-slice_fusion.10
  17.2 2.9 %collective-permute-start.2 = (bf16[1,64,5120]{2,1,0:T(8,128)(2,1)}, bf16[1,64,5120]{2,1,0:T(8,128)(2,1)}, u32[]{:S(2)}, u32[]{:S(2)}) collective-permute-start(bf16[1,64,5120]{2,1,0:T(8,128)(2,1)} %pad_maximum_fusion.1), channel_id=1, source_target_pairs={{0,1},{1,0},{2,3},{3,2},{4,5},{5,4},{6,7},{7,6},{8,9},{9,8},{10,11... | collective-permute-start | bytes 1966088 | tf_op jit(solution)/shard_map/ppermute | solution.py:11
  20.1 1.8 %constant_dynamic-slice_fusion.6 = (bf16[8,32,448]{2,1,0:T(8,128)(2,1)S(1)}, bf16[8,32,448]{2,1,0:T(8,128)(2,1)S(1)}, bf16[8,32,448]{2,1,0:T(8,128)(2,1)S(1)}, bf16[8,32,448]{2,1,0:T(8,128)(2,1)S(1)}) fusion(bf16[8,32,896]{2,1,0:T(8,128)(2,1)} %param.12, s32[]{:T(128)S(6)} %select_n.146, s32[]{:T(128)S(6)} %select_n.148, bf16[8,32,896]{2,1,0:T(8,128)(2,1)} %param.10), kind=kLoop, calls=%fused_computation.92 | loop fusion | bytes 1835016 | tf_op jit(solution)/shard_map/dynamic_slice | solution.py:120
  23.7 2.9 %pad_maximum_fusion = bf16[8,64,5120]{2,1,0:T(8,128)(2,1)} fusion(bf16[8,32,5120]{2,1,0:T(8,128)(2,1)S(1)} %copy-done.6, bf16[8,32,5120]{2,1,0:T(8,128)(2,1)S(1)} %copy-done.7), kind=kLoop, calls=%fused_computation | loop fusion | flops 10485760 | bytes 10485760 | tf_op jit(solution)/shard_map/concatenate | solution.py:117
  26.5 1.7 collective-permute-done
  28.2 6.1 %collective-permute-done.2 = bf16[1,64,5120]{2,1,0:T(8,128)(2,1)} collective-permute-done((bf16[1,64,5120]{2,1,0:T(8,128)(2,1)}, bf16[1,64,5120]{2,1,0:T(8,128)(2,1)}, u32[]{:S(2)}, u32[]{:S(2)}) %collective-permute-start.2) | collective-permute-done | bytes 655392 | tf_op jit(solution)/shard_map/ppermute | solution.py:11
  34.6 2.7 %collective-permute-start.4 = (bf16[320,896]{1,0:T(8,128)(2,1)}, bf16[320,896]{1,0:T(8,128)(2,1)S(1)}, u32[]{:S(2)}, u32[]{:S(2)}) collective-permute-start(bf16[320,896]{1,0:T(8,128)(2,1)} %collective-permute-done.1), channel_id=1, source_target_pairs={{0,112},{16,0},{32,16},{48,32},{64,48},{80,64},{96,80},{112,96},{1... | collective-permute-start | bytes 1720328 | tf_op jit(solution)/shard_map/ppermute | solution.py:11
  37.2 1.3 collective-permute-start.5
  39.1 1.1 bitcast_dynamic-update-slice_fusion.11
  40.2 1.1 bitcast_dynamic-update-slice_fusion.10
  41.4 2.4 %fusion.56 = f32[512,64]{0,1:T(8,128)} fusion(bf16[512,5120]{1,0:T(8,128)(2,1)S(1)} %bitcast.76, bf16[64,5120]{1,0:T(8,128)(2,1)S(1)} %copy-done), kind=kOutput, calls=%fused_computation.106 | convolution fusion | flops 335544320 | bytes 6029312 | tf_op jit(solution)/shard_map/dot_general | solution.py:145
  43.8 4.8 %collective-permute-done.3 = bf16[320,896]{1,0:T(8,128)(2,1)S(1)} collective-permute-done((bf16[320,896]{1,0:T(8,128)(2,1)}, bf16[320,896]{1,0:T(8,128)(2,1)S(1)}, u32[]{:S(2)}, u32[]{:S(2)}) %collective-permute-start.3) | collective-permute-done | bytes 573472 | tf_op jit(solution)/shard_map/ppermute | solution.py:11
  48.6 0.9 collective-permute-done.5
  49.5 1.3 collective-permute-start.8
  50.8 2.7 %collective-permute-start.7 = (bf16[320,896]{1,0:T(8,128)(2,1)S(1)}, bf16[320,896]{1,0:T(8,128)(2,1)S(1)}, u32[]{:S(2)}, u32[]{:S(2)}) collective-permute-start(bf16[320,896]{1,0:T(8,128)(2,1)S(1)} %collective-permute-done.4), channel_id=1, source_target_pairs={{0,112},{16,0},{32,16},{48,32},{64,48},{80,64},{96,80},{112,96},{1... | collective-permute-start | bytes 1720328 | tf_op jit(solution)/shard_map/ppermute | solution.py:11
  53.5 1.5 constant_dynamic-slice_fusion.3
  54.9 1.1 bitcast_dynamic-update-slice_fusion.9
  56.1 2.7 %collective-permute-start.14 = (bf16[512,448]{1,0:T(8,128)(2,1)S(1)}, bf16[512,448]{1,0:T(8,128)(2,1)S(1)}, u32[]{:S(2)}, u32[]{:S(2)}) collective-permute-start(bf16[512,448]{1,0:T(8,128)(2,1)S(1)} %bitcast.94), channel_id=1, source_target_pairs={{0,1},{1,0},{2,3},{3,2},{4,5},{5,4},{6,7},{7,6},{8,9},{9,8},{10,11... | collective-permute-start | bytes 1376264 | tf_op jit(solution)/shard_map/ppermute | solution.py:11
  58.8 2.9 %collective-permute-done.6 = bf16[320,896]{1,0:T(8,128)(2,1)S(1)} collective-permute-done((bf16[320,896]{1,0:T(8,128)(2,1)S(1)}, bf16[320,896]{1,0:T(8,128)(2,1)S(1)}, u32[]{:S(2)}, u32[]{:S(2)}) %collective-permute-start.6) | collective-permute-done | bytes 573472 | tf_op jit(solution)/shard_map/ppermute | solution.py:11
  61.8 1.6 collective-permute-start.9
  63.3 1.8 %collective-permute-start.10 = (bf16[320,896]{1,0:T(8,128)(2,1)S(1)}, bf16[320,896]{1,0:T(8,128)(2,1)S(1)}, u32[]{:S(2)}, u32[]{:S(2)}) collective-permute-start(bf16[320,896]{1,0:T(8,128)(2,1)S(1)} %collective-permute-done.5), channel_id=1, source_target_pairs={{0,112},{16,0},{32,16},{48,32},{64,48},{80,64},{96,80},{112,96},{1... | collective-permute-start | bytes 1720328 | tf_op jit(solution)/shard_map/ppermute | solution.py:11
  66.1 8.5 %collective-permute-done.14 = bf16[512,448]{1,0:T(8,128)(2,1)S(1)} collective-permute-done((bf16[512,448]{1,0:T(8,128)(2,1)S(1)}, bf16[512,448]{1,0:T(8,128)(2,1)S(1)}, u32[]{:S(2)}, u32[]{:S(2)}) %collective-permute-start.14) | collective-permute-done | bytes 458784 | tf_op jit(solution)/shard_map/ppermute | solution.py:11
  74.6 1.9 %collective-permute-start.13 = (bf16[160,896]{1,0:T(8,128)(2,1)S(1)}, bf16[160,896]{1,0:T(8,128)(2,1)S(1)}, u32[]{:S(2)}, u32[]{:S(2)}) collective-permute-start(bf16[160,896]{1,0:T(8,128)(2,1)S(1)} %slice.35), channel_id=1, source_target_pairs={{0,112},{16,0},{32,16},{48,32},{64,48},{80,64},{96,80},{112,96},{1... | collective-permute-start | bytes 860168 | tf_op jit(solution)/shard_map/ppermute | solution.py:11
  76.5 2.9 %fusion.6 = f32[512,896]{1,0:T(8,128)S(1)} fusion(bf16[2560,896]{1,0:T(8,128)(2,1)S(1)} %bitcast.88, bf16[512,5120]{1,0:T(8,128)(2,1)S(1)} %bitcast.78, s32[]{:T(128)S(6)} %select_n.149), kind=kOutput, calls=%fused_computation.7 | convolution fusion | flops 2348810240 | bytes 9043972 | tf_op jit(solution)/shard_map/dot_general | solution.py:136
  80.1 3.2 %collective-permute-done.13 = bf16[160,896]{1,0:T(8,128)(2,1)S(1)} collective-permute-done((bf16[160,896]{1,0:T(8,128)(2,1)S(1)}, bf16[160,896]{1,0:T(8,128)(2,1)S(1)}, u32[]{:S(2)}, u32[]{:S(2)}) %collective-permute-start.13) | collective-permute-done | bytes 286752 | tf_op jit(solution)/shard_map/ppermute | solution.py:11
  83.3 1.3 collective-permute-done.11
  84.6 1.4 collective-permute-start.15
  86.4 2.3 %collective-permute-start.17 = (bf16[320,896]{1,0:T(8,128)(2,1)}, bf16[320,896]{1,0:T(8,128)(2,1)}, u32[]{:S(2)}, u32[]{:S(2)}) collective-permute-start(bf16[320,896]{1,0:T(8,128)(2,1)} %collective-permute-done.11), channel_id=1, source_target_pairs={{0,112},{16,0},{32,16},{48,32},{64,48},{80,64},{96,80},{112,96},{1... | collective-permute-start | bytes 1720328 | tf_op jit(solution)/shard_map/ppermute | solution.py:11
  88.8 1.1 bitcast_dynamic-update-slice_fusion.1
  90.0 1.1 bitcast_dynamic-update-slice_fusion
  91.1 2.9 %fusion.4 = f32[512,896]{1,0:T(8,128)S(1)} fusion(bf16[2560,896]{1,0:T(8,128)(2,1)S(1)} %bitcast.86, bf16[512,5120]{1,0:T(8,128)(2,1)S(1)} %bitcast.79, s32[]{:T(128)S(6)} %select_n.164), kind=kOutput, calls=%fused_computation.5 | convolution fusion | flops 2348810240 | bytes 9043972 | tf_op jit(solution)/shard_map/dot_general | solution.py:165
  94.9 6.1 %fusion.2 = f32[512,896]{1,0:T(8,128)S(1)} fusion(bf16[2560,896]{1,0:T(8,128)(2,1)} %bitcast.89, bf16[512,5120]{1,0:T(8,128)(2,1)} %bitcast.81, s32[]{:T(128)S(6)} %select_n.149), kind=kOutput, calls=%fused_computation.3 | convolution fusion | flops 2348810240 | bytes 9043972 | tf_op jit(solution)/shard_map/dot_general | solution.py:136
  101.0 2.9 %fusion = f32[512,896]{1,0:T(8,128)S(1)} fusion(bf16[2560,896]{1,0:T(8,128)(2,1)S(1)} %bitcast.87, bf16[512,5120]{1,0:T(8,128)(2,1)S(1)} %bitcast.82, s32[]{:T(128)S(6)} %select_n.164), kind=kOutput, calls=%fused_computation.1 | convolution fusion | flops 2348810240 | bytes 9043972 | tf_op jit(solution)/shard_map/dot_general | solution.py:165
  105.3 1.7 fusion.60
  107.0 1.7 fusion.59
  108.7 1.9 %add_add_fusion = f32[512,896]{1,0:T(8,128)S(1)} fusion(f32[512,896]{1,0:T(8,128)S(1)} %fusion.60, f32[512,896]{1,0:T(8,128)S(1)} %add_add_fusion.2, f32[512,896]{1,0:T(8,128)S(1)} %fusion.59, bf16[512,320]{1,0:T(8,128)(2,1)S(1)} %get-tuple-element.76, bf16[320,896]{1,0:T(8,128)(2,1)} %collective-permute-done.17), kind=kOutput, calls=%fused_computation.9 | convolution fusion | flops 294977536 | bytes 8241152 | tf_op jit(solution)/shard_map/dot_general | solution.py:177
  112.6 1.7 fusion.58
  114.3 1.7 fusion.57
  116.0 1.9 %add_add_fusion.1 = f32[512,896]{1,0:T(8,128)S(1)} fusion(f32[512,896]{1,0:T(8,128)S(1)} %fusion.58, f32[512,896]{1,0:T(8,128)S(1)} %add_add_fusion.3, f32[512,896]{1,0:T(8,128)S(1)} %fusion.57, bf16[512,320]{1,0:T(8,128)(2,1)S(1)} %get-tuple-element.70, bf16[320,896]{1,0:T(8,128)(2,1)} %collective-permute-done.17), kind=kOutput, calls=%fused_computation.10 | convolution fusion | flops 294977536 | bytes 8241152 | tf_op jit(solution)/shard_map/dot_general | solution.py:177
  119.3 1.7 fusion.61
  121.8 12.5 %all-to-all-start = ((bf16[16,8,1024]{2,1,0:T(8,128)(2,1)}), bf16[16,8,1024]{2,1,0:T(8,128)(2,1)S(1)}, u32[]{:S(2)}, u32[]{:S(2)}) async-start(bf16[16,8,1024]{2,1,0:T(8,128)(2,1)} %pad_maximum_fusion.7), calls=%async_computation | async-start | bytes 524288 | tf_op jit(solution)/shard_map/all_to_all | solution.py:191
  134.5 9.1 %all-to-all-done = bf16[16,8,1024]{2,1,0:T(8,128)(2,1)S(1)} async-done(((bf16[16,8,1024]{2,1,0:T(8,128)(2,1)}), bf16[16,8,1024]{2,1,0:T(8,128)(2,1)S(1)}, u32[]{:S(2)}, u32[]{:S(2)}) %all-to-all-start) | async-done | bytes 262176 | tf_op jit(solution)/shard_map/all_to_all | solution.py:191
  145.2 5.4 %all-to-all-start.1 = ((bf16[16,16,512]{2,1,0:T(8,128)(2,1)}), bf16[16,16,512]{2,1,0:T(8,128)(2,1)S(1)}, u32[]{:S(2)}, u32[]{:S(2)}) async-start(bf16[16,16,512]{2,1,0:T(8,128)(2,1)} %broadcast_in_dim.69), calls=%async_computation.1 | async-start | bytes 524288 | tf_op jit(solution)/shard_map/all_to_all | solution.py:207
  151.0 8.5 %all-to-all-done.1 = bf16[16,16,512]{2,1,0:T(8,128)(2,1)S(1)} async-done(((bf16[16,16,512]{2,1,0:T(8,128)(2,1)}), bf16[16,16,512]{2,1,0:T(8,128)(2,1)S(1)}, u32[]{:S(2)}, u32[]{:S(2)}) %all-to-all-start.1) | async-done | bytes 262176 | tf_op jit(solution)/shard_map/all_to_all | solution.py:207
  160.1 12.1 %all_to_all.19 = f32[16,1,640]{2,1,0:T(1,128)S(1)} all-to-all(f32[16,1,640]{2,1,0:T(1,128)S(1)} %copy.24), channel_id=1, replica_groups=mesh['ylo'=2,'z'=8,'x'=4,'core'=2,'yhi'=2] {'x','core','yhi'}, dimensions={0} | all-to-all | bytes 81920 | tf_op jit(solution)/shard_map/all_to_all | solution.py:228
  (104 shorter events, 15.6 us)
Async XLA Ops:
  6.5 34.9 %copy-start = (bf16[64,5120]{1,0:T(8,128)(2,1)S(1)}, bf16[64,5120]{1,0:T(8,128)(2,1)}, u32[]{:S(2)}) copy-start(bf16[64,5120]{1,0:T(8,128)(2,1)} %param.15) | copy-start | bytes 1966084
  6.5 17.1 %copy-start.6 = (bf16[8,32,5120]{2,1,0:T(8,128)(2,1)S(1)}, bf16[8,32,5120]{2,1,0:T(8,128)(2,1)}, u32[]{:S(2)}) copy-start(bf16[8,32,5120]{2,1,0:T(8,128)(2,1)} %param.11) | copy-start | bytes 7864324
  6.5 88.3 %all-gather.2.cloned.1.call-start = ((), (), s32[]{:S(2)}) async-start(), calls=%async_computation.3 | async-start | bytes 5898240 | tf_op jit(solution)/shard_map/all_gather | solution.py:39
  8.8 19.4 %collective-permute-start = (bf16[320,896]{1,0:T(8,128)(2,1)}, bf16[320,896]{1,0:T(8,128)(2,1)}, u32[]{:S(2)}, u32[]{:S(2)}) collective-permute-start(bf16[320,896]{1,0:T(8,128)(2,1)} %pad_maximum_fusion.2), channel_id=1, source_target_pairs={{0,16},{16,32},{32,48},{48,64},{64,80},{80,96},{96,112},{112,0},{1... | collective-permute-start | bytes 1720328 | tf_op jit(solution)/shard_map/ppermute | solution.py:11
  11.2 17.0 %collective-permute-start.1 = (bf16[320,896]{1,0:T(8,128)(2,1)}, bf16[320,896]{1,0:T(8,128)(2,1)}, u32[]{:S(2)}, u32[]{:S(2)}) collective-permute-start(bf16[320,896]{1,0:T(8,128)(2,1)} %pad_maximum_fusion.2), channel_id=1, source_target_pairs={{0,112},{16,0},{32,16},{48,32},{64,48},{80,64},{96,80},{112,96},{1... | collective-permute-start | bytes 1720328 | tf_op jit(solution)/shard_map/ppermute | solution.py:11
  17.2 17.1 %collective-permute-start.2 = (bf16[1,64,5120]{2,1,0:T(8,128)(2,1)}, bf16[1,64,5120]{2,1,0:T(8,128)(2,1)}, u32[]{:S(2)}, u32[]{:S(2)}) collective-permute-start(bf16[1,64,5120]{2,1,0:T(8,128)(2,1)} %pad_maximum_fusion.1), channel_id=1, source_target_pairs={{0,1},{1,0},{2,3},{3,2},{4,5},{5,4},{6,7},{7,6},{8,9},{9,8},{10,11... | collective-permute-start | bytes 1966088 | tf_op jit(solution)/shard_map/ppermute | solution.py:11
  20.1 3.6 %copy-start.7 = (bf16[8,32,5120]{2,1,0:T(8,128)(2,1)S(1)}, bf16[8,32,5120]{2,1,0:T(8,128)(2,1)}, u32[]{:S(2)}) copy-start(bf16[8,32,5120]{2,1,0:T(8,128)(2,1)} %param.9) | copy-start | bytes 7864324
  34.5 6.9 %copy-start.1 = (bf16[8,64,5120]{2,1,0:T(8,128)(2,1)S(1)}, bf16[8,64,5120]{2,1,0:T(8,128)(2,1)}, u32[]{:S(2)}) copy-start(bf16[8,64,5120]{2,1,0:T(8,128)(2,1)} %pad_maximum_fusion) | copy-start | bytes 15728644
  34.5 14.1 %collective-permute-start.3 = (bf16[320,896]{1,0:T(8,128)(2,1)}, bf16[320,896]{1,0:T(8,128)(2,1)S(1)}, u32[]{:S(2)}, u32[]{:S(2)}) collective-permute-start(bf16[320,896]{1,0:T(8,128)(2,1)} %collective-permute-done), channel_id=1, source_target_pairs={{0,16},{16,32},{32,48},{48,64},{64,80},{80,96},{96,112},{112,0},{1... | collective-permute-start | bytes 1720328 | tf_op jit(solution)/shard_map/ppermute | solution.py:11
  34.6 14.0 %collective-permute-start.4 = (bf16[320,896]{1,0:T(8,128)(2,1)}, bf16[320,896]{1,0:T(8,128)(2,1)S(1)}, u32[]{:S(2)}, u32[]{:S(2)}) collective-permute-start(bf16[320,896]{1,0:T(8,128)(2,1)} %collective-permute-done.1), channel_id=1, source_target_pairs={{0,112},{16,0},{32,16},{48,32},{64,48},{80,64},{96,80},{112,96},{1... | collective-permute-start | bytes 1720328 | tf_op jit(solution)/shard_map/ppermute | solution.py:11
  37.2 12.3 %collective-permute-start.5 = (bf16[320,896]{1,0:T(8,128)(2,1)}, bf16[320,896]{1,0:T(8,128)(2,1)S(1)}, u32[]{:S(2)}, u32[]{:S(2)}) collective-permute-start(bf16[320,896]{1,0:T(8,128)(2,1)} %pad_maximum_fusion.2), channel_id=1, source_target_pairs={{0,128},{128,0},{1,129},{129,1},{2,130},{130,2},{3,131},{131,3},{4... | collective-permute-start | bytes 1720328 | tf_op jit(solution)/shard_map/ppermute | solution.py:11
  41.4 14.6 %copy-start.12 = (bf16[8,64,448]{2,1,0:T(8,128)(2,1)S(1)}, bf16[8,64,448]{2,1,0:T(8,128)(2,1)}, u32[]{:S(2)}) copy-start(bf16[8,64,448]{2,1,0:T(8,128)(2,1)} %pad_maximum_fusion.3) | copy-start | bytes 1376260
  49.5 12.3 %collective-permute-start.6 = (bf16[320,896]{1,0:T(8,128)(2,1)S(1)}, bf16[320,896]{1,0:T(8,128)(2,1)S(1)}, u32[]{:S(2)}, u32[]{:S(2)}) collective-permute-start(bf16[320,896]{1,0:T(8,128)(2,1)S(1)} %collective-permute-done.3), channel_id=1, source_target_pairs={{0,16},{16,32},{32,48},{48,64},{64,80},{80,96},{96,112},{112,0},{1... | collective-permute-start | bytes 1720328 | tf_op jit(solution)/shard_map/ppermute | solution.py:11
  49.5 12.3 %collective-permute-start.8 = (bf16[320,896]{1,0:T(8,128)(2,1)S(1)}, bf16[320,896]{1,0:T(8,128)(2,1)}, u32[]{:S(2)}, u32[]{:S(2)}) collective-permute-start(bf16[320,896]{1,0:T(8,128)(2,1)S(1)} %collective-permute-done.3), channel_id=1, source_target_pairs={{0,128},{128,0},{1,129},{129,1},{2,130},{130,2},{3,131},{131,3},{4... | collective-permute-start | bytes 1720328 | tf_op jit(solution)/shard_map/ppermute | solution.py:11
  50.8 11.0 %collective-permute-start.7 = (bf16[320,896]{1,0:T(8,128)(2,1)S(1)}, bf16[320,896]{1,0:T(8,128)(2,1)S(1)}, u32[]{:S(2)}, u32[]{:S(2)}) collective-permute-start(bf16[320,896]{1,0:T(8,128)(2,1)S(1)} %collective-permute-done.4), channel_id=1, source_target_pairs={{0,112},{16,0},{32,16},{48,32},{64,48},{80,64},{96,80},{112,96},{1... | collective-permute-start | bytes 1720328 | tf_op jit(solution)/shard_map/ppermute | solution.py:11
  56.1 18.5 %collective-permute-start.14 = (bf16[512,448]{1,0:T(8,128)(2,1)S(1)}, bf16[512,448]{1,0:T(8,128)(2,1)S(1)}, u32[]{:S(2)}, u32[]{:S(2)}) collective-permute-start(bf16[512,448]{1,0:T(8,128)(2,1)S(1)} %bitcast.94), channel_id=1, source_target_pairs={{0,1},{1,0},{2,3},{3,2},{4,5},{5,4},{6,7},{7,6},{8,9},{9,8},{10,11... | collective-permute-start | bytes 1376264 | tf_op jit(solution)/shard_map/ppermute | solution.py:11
  61.8 21.5 %collective-permute-start.9 = (bf16[320,896]{1,0:T(8,128)(2,1)S(1)}, bf16[320,896]{1,0:T(8,128)(2,1)S(1)}, u32[]{:S(2)}, u32[]{:S(2)}) collective-permute-start(bf16[320,896]{1,0:T(8,128)(2,1)S(1)} %collective-permute-done.5), channel_id=1, source_target_pairs={{0,16},{16,32},{32,48},{48,64},{64,80},{80,96},{96,112},{112,0},{1... | collective-permute-start | bytes 1720328 | tf_op jit(solution)/shard_map/ppermute | solution.py:11
  63.3 19.9 %collective-permute-start.10 = (bf16[320,896]{1,0:T(8,128)(2,1)S(1)}, bf16[320,896]{1,0:T(8,128)(2,1)S(1)}, u32[]{:S(2)}, u32[]{:S(2)}) collective-permute-start(bf16[320,896]{1,0:T(8,128)(2,1)S(1)} %collective-permute-done.5), channel_id=1, source_target_pairs={{0,112},{16,0},{32,16},{48,32},{64,48},{80,64},{96,80},{112,96},{1... | collective-permute-start | bytes 1720328 | tf_op jit(solution)/shard_map/ppermute | solution.py:11
  65.2 19.4 %collective-permute-start.11 = (bf16[320,896]{1,0:T(8,128)(2,1)S(1)}, bf16[320,896]{1,0:T(8,128)(2,1)}, u32[]{:S(2)}, u32[]{:S(2)}) collective-permute-start(bf16[320,896]{1,0:T(8,128)(2,1)S(1)} %collective-permute-done.4), channel_id=1, source_target_pairs={{0,128},{128,0},{1,129},{129,1},{2,130},{130,2},{3,131},{131,3},{4... | collective-permute-start | bytes 1720328 | tf_op jit(solution)/shard_map/ppermute | solution.py:11
  65.8 14.3 %collective-permute-start.12 = (bf16[160,896]{1,0:T(8,128)(2,1)S(1)}, bf16[160,896]{1,0:T(8,128)(2,1)S(1)}, u32[]{:S(2)}, u32[]{:S(2)}) collective-permute-start(bf16[160,896]{1,0:T(8,128)(2,1)S(1)} %slice.34), channel_id=1, source_target_pairs={{0,16},{16,32},{32,48},{48,64},{64,80},{80,96},{96,112},{112,0},{1... | collective-permute-start | bytes 860168 | tf_op jit(solution)/shard_map/ppermute | solution.py:11
  66.1 10.4 %copy-start.5 = (bf16[8,320,896]{2,1,0:T(8,128)(2,1)}, bf16[8,320,896]{2,1,0:T(8,128)(2,1)S(1)}, u32[]{:S(2)}) copy-start(bf16[8,320,896]{2,1,0:T(8,128)(2,1)S(1)} %bitcast_dynamic-update-slice_fusion.5) | copy-start | bytes 13762564
  74.6 1.9 %copy-start.13 = (bf16[512,448]{1,0:T(8,128)(2,1)}, bf16[512,448]{1,0:T(8,128)(2,1)S(1)}, u32[]{:S(2)}) copy-start(bf16[512,448]{1,0:T(8,128)(2,1)S(1)} %collective-permute-done.14) | copy-start | bytes 1376260
  74.6 8.7 %collective-permute-start.13 = (bf16[160,896]{1,0:T(8,128)(2,1)S(1)}, bf16[160,896]{1,0:T(8,128)(2,1)S(1)}, u32[]{:S(2)}, u32[]{:S(2)}) collective-permute-start(bf16[160,896]{1,0:T(8,128)(2,1)S(1)} %slice.35), channel_id=1, source_target_pairs={{0,112},{16,0},{32,16},{48,32},{64,48},{80,64},{96,80},{112,96},{1... | collective-permute-start | bytes 860168 | tf_op jit(solution)/shard_map/ppermute | solution.py:11
  84.6 20.6 %collective-permute-start.15 = (bf16[320,896]{1,0:T(8,128)(2,1)S(1)}, bf16[320,896]{1,0:T(8,128)(2,1)}, u32[]{:S(2)}, u32[]{:S(2)}) collective-permute-start(bf16[320,896]{1,0:T(8,128)(2,1)S(1)} %constant_dynamic-update-slice_fusion), channel_id=1, source_target_pairs={{0,128},{128,0},{1,129},{129,1},{2,130},{130,2},{3,131},{131,3},{4... | collective-permute-start | bytes 1720328 | tf_op jit(solution)/shard_map/ppermute | solution.py:11
  86.0 19.3 %collective-permute-start.16 = (bf16[320,896]{1,0:T(8,128)(2,1)}, bf16[320,896]{1,0:T(8,128)(2,1)}, u32[]{:S(2)}, u32[]{:S(2)}) collective-permute-start(bf16[320,896]{1,0:T(8,128)(2,1)} %collective-permute-done.8), channel_id=1, source_target_pairs={{0,16},{16,32},{32,48},{48,64},{64,80},{80,96},{96,112},{112,0},{1... | collective-permute-start | bytes 1720328 | tf_op jit(solution)/shard_map/ppermute | solution.py:11
  86.4 18.9 %collective-permute-start.17 = (bf16[320,896]{1,0:T(8,128)(2,1)}, bf16[320,896]{1,0:T(8,128)(2,1)}, u32[]{:S(2)}, u32[]{:S(2)}) collective-permute-start(bf16[320,896]{1,0:T(8,128)(2,1)} %collective-permute-done.11), channel_id=1, source_target_pairs={{0,112},{16,0},{32,16},{48,32},{64,48},{80,64},{96,80},{112,96},{1... | collective-permute-start | bytes 1720328 | tf_op jit(solution)/shard_map/ppermute | solution.py:11
  91.1 2.9 %copy-start.3 = (bf16[8,320,896]{2,1,0:T(8,128)(2,1)}, bf16[8,320,896]{2,1,0:T(8,128)(2,1)S(1)}, u32[]{:S(2)}) copy-start(bf16[8,320,896]{2,1,0:T(8,128)(2,1)S(1)} %bitcast_dynamic-update-slice_fusion) | copy-start | bytes 13762564
  94.9 6.1 %copy-start.2 = (bf16[8,64,5120]{2,1,0:T(8,128)(2,1)S(1)}, bf16[8,64,5120]{2,1,0:T(8,128)(2,1)}, u32[]{:S(2)}) copy-start(bf16[8,64,5120]{2,1,0:T(8,128)(2,1)} %all-gather.2.cloned.1.call-done) | copy-start | bytes 15728644
  94.9 6.1 %copy-start.4 = (bf16[8,320,896]{2,1,0:T(8,128)(2,1)S(1)}, bf16[8,320,896]{2,1,0:T(8,128)(2,1)}, u32[]{:S(2)}) copy-start(bf16[8,320,896]{2,1,0:T(8,128)(2,1)} %copy-done.3) | copy-start | bytes 13762564
  108.7 1.9 %copy-start.14 = (bf16[512,448]{1,0:T(8,128)(2,1)S(1)}, bf16[512,448]{1,0:T(8,128)(2,1)}, u32[]{:S(2)}) copy-start(bf16[512,448]{1,0:T(8,128)(2,1)} %copy-done.13) | copy-start | bytes 1376260
  108.7 1.9 %copy-start.15 = (bf16[64,896]{1,0:T(8,128)(2,1)S(1)}, bf16[64,896]{1,0:T(8,128)(2,1)}, u32[]{:S(2)}) copy-start(bf16[64,896]{1,0:T(8,128)(2,1)} %param.17) | copy-start | bytes 344068
  110.7 0.9 copy-start.16
  111.6 1.0 copy-start.9
  111.6 2.7 %copy-start.8 = (bf16[512,320]{1,0:T(8,128)(2,1)S(1)}, bf16[512,320]{1,0:T(8,128)(2,1)}, u32[]{:S(2)}) copy-start(bf16[512,320]{1,0:T(8,128)(2,1)} %get-tuple-element.66) | copy-start | bytes 983044
  116.0 2.0 %copy-start.11 = (bf16[8,64,448]{2,1,0:T(8,128)(2,1)S(1)}, bf16[8,64,448]{2,1,0:T(8,128)(2,1)}, u32[]{:S(2)}) copy-start(bf16[8,64,448]{2,1,0:T(8,128)(2,1)} %pad_maximum_fusion.4) | copy-start | bytes 1376260
  119.3 15.0 %copy-start.10 = (f32[512,64]{0,1:T(8,128)S(1)}, f32[512,64]{0,1:T(8,128)}, u32[]{:S(2)}) copy-start(f32[512,64]{0,1:T(8,128)} %fusion.56) | copy-start | bytes 393220
  121.8 21.8 %all-to-all-start = ((bf16[16,8,1024]{2,1,0:T(8,128)(2,1)}), bf16[16,8,1024]{2,1,0:T(8,128)(2,1)S(1)}, u32[]{:S(2)}, u32[]{:S(2)}) async-start(bf16[16,8,1024]{2,1,0:T(8,128)(2,1)} %pad_maximum_fusion.7), calls=%async_computation | async-start | bytes 524288 | tf_op jit(solution)/shard_map/all_to_all | solution.py:191
  145.2 14.3 %all-to-all-start.1 = ((bf16[16,16,512]{2,1,0:T(8,128)(2,1)}), bf16[16,16,512]{2,1,0:T(8,128)(2,1)S(1)}, u32[]{:S(2)}, u32[]{:S(2)}) async-start(bf16[16,16,512]{2,1,0:T(8,128)(2,1)} %broadcast_in_dim.69), calls=%async_computation.1 | async-start | bytes 524288 | tf_op jit(solution)/shard_map/all_to_all | solution.py:207
Sparse Core Ops, SparseCore 0:
  34.4 40.7 all-gather.1

commit v7 on v6

--- a/solution.py
+++ b/solution.py
@@ -1,6 +1,8 @@
 import jax
 import jax.numpy as jnp
 from jax import lax
+from jax.experimental import pallas as pl
+from jax.experimental.pallas import tpu as pltpu
 from jax.sharding import PartitionSpec as P
 
 F32 = jnp.float32
@@ -63,26 +65,91 @@
         (down(ob2), (z + 3) % n_z),
     )
     other_row = placed(((0, o0), (n_z - 1, oa1), (1, ob1), (n_z - 2, oa2), (2, ob2)))
-    sums = (own_sum, this_product(partner, this_row))
-    return sums, (a4, far_z), other_row, last, other_cot, partner, early
-
-
-def projected(pre, cotangent, gate_projection, up_projection):
-    cols = pre.shape[1] // 2
-    gate = pre[:, :cols]
-    up = pre[:, cols:]
+    return this_row, own_sum, (a4, far_z), other_row, last, other_cot, partner, early
+
+
+VMEM_LIMIT = 28 * 2**20
+ROWS = 256
+WHOLE = pl.BlockSpec(memory_space=pltpu.VMEM)
+
+
+def halves_kernel(side_ref, this_x, other_x, this_row, other_row, out):
+    del side_ref
+    out[...] = jnp.dot(
+        this_x[...], this_row[...], preferred_element_type=F32
+    ) + jnp.dot(other_x[...], other_row[...], preferred_element_type=F32)
+
+
+def halves_product(rows, this_row, other_row, row_index):
+    count, width = rows.shape
+    depth, cols = this_row.shape
+    return pl.pallas_call(
+        halves_kernel,
+        out_shape=jax.ShapeDtypeStruct((count, cols), F32),
+        grid_spec=pltpu.PrefetchScalarGridSpec(
+            num_scalar_prefetch=1,
+            grid=(count // ROWS,),
+            in_specs=[
+                pl.BlockSpec((ROWS, depth), lambda i, side: (i, side[0])),
+                pl.BlockSpec((ROWS, depth), lambda i, side: (i, 1 - side[0])),
+                WHOLE,
+                WHOLE,
+            ],
+            out_specs=pl.BlockSpec((ROWS, cols), lambda i, side: (i, 0)),
+        ),
+        compiler_params=pltpu.CompilerParams(vmem_limit_bytes=VMEM_LIMIT),
+        cost_estimate=pl.CostEstimate(
+            flops=2 * count * width * cols,
+            bytes_accessed=2 * count * width + 4 * count * cols,
+            transcendentals=0,
+        ),
+        name="halves_product",
+    )(row_index.astype(jnp.int32).reshape(1), rows, rows, this_row, other_row)
+
+
+def finish_kernel(n, *refs):
+    sums, cot, projection = refs[0], refs[1], refs[2]
+    chunks, shards, out = refs[3 : 3 + n], refs[3 + n : 3 + 2 * n], refs[3 + 2 * n]
+    total = sums[...]
+    for chunk, shard in zip(chunks, shards):
+        total += jnp.dot(chunk[...], shard[...], preferred_element_type=F32)
+    half = total.shape[1] // 2
+    turned = pltpu.roll(total, half, 1)
+    low = lax.broadcasted_iota(jnp.int32, total.shape, 1) < half
+    gate = jnp.where(low, total, turned)
     sigma = jax.nn.sigmoid(gate)
-    upstream = cotangent.astype(F32)
-    gate_grad = (upstream * up * sigma * (1.0 + gate * (1.0 - sigma))).astype(BF16)
-    up_grad = (upstream * gate * sigma).astype(BF16)
-    dims = (((1,), (1,)), ((), ()))
-    return jnp.concatenate(
-        (
-            lax.dot_general(gate_projection, gate_grad, dims, preferred_element_type=F32),
-            lax.dot_general(up_projection, up_grad, dims, preferred_element_type=F32),
-        ),
-        axis=0,
-    )
+    slope = jnp.where(low, turned * (1.0 + gate * (1.0 - sigma)), gate)
+    grad = (cot[...].astype(F32) * sigma * slope).astype(BF16)
+    out[...] = lax.dot_general(
+        projection[...], grad, (((1,), (1,)), ((), ())), preferred_element_type=F32
+    ).astype(BF16)
+
+
+def finished(sums, cot, projection, chunks, shards):
+    count, cols = sums.shape
+    depth = shards[0].shape[0]
+    out_rows = projection.shape[0]
+    n = len(shards)
+    return pl.pallas_call(
+        lambda *refs: finish_kernel(n, *refs),
+        out_shape=jax.ShapeDtypeStruct((out_rows, count), BF16),
+        grid=(count // ROWS,),
+        in_specs=[
+            pl.BlockSpec((ROWS, cols), lambda i: (i, 0)),
+            pl.BlockSpec((ROWS, cols), lambda i: (i, 0)),
+            WHOLE,
+        ]
+        + [pl.BlockSpec((ROWS, depth), lambda i: (i, 0))] * n
+        + [WHOLE] * n,
+        out_specs=pl.BlockSpec((out_rows, ROWS), lambda i: (0, i)),
+        compiler_params=pltpu.CompilerParams(vmem_limit_bytes=VMEM_LIMIT),
+        cost_estimate=pl.CostEstimate(
+            flops=2 * count * cols * (n * depth + out_rows),
+            bytes_accessed=6 * count * cols + 2 * n * depth * (count + cols),
+            transcendentals=count * cols,
+        ),
+        name="finished",
+    )(sums, cot, projection, *chunks, *shards)
 
 
 def body(
@@ -135,11 +202,18 @@
         flat = half_of(rows, row_index, this_row.shape[0])
         return jnp.dot(flat, this_row, preferred_element_type=F32)
 
-    sums, far, other_row, last, other_cot, other, (own, own_cot) = gathered(
+    this_row, own_sum, far, other_row, last, other_cot, other, (own, own_cot) = gathered(
         weight, piece, cotangents(1 - half_index), (own, own_cot), this_product
     )
     gate_proj = columns(gate_projection, half_index)
     up_proj = columns(up_projection, half_index)
+    projection = jnp.concatenate(
+        (
+            jnp.pad(gate_proj, ((0, 0), (0, cols))),
+            jnp.pad(up_proj, ((0, 0), (cols, 0))),
+        ),
+        axis=0,
+    )
 
     def inner_factor(rows):
         return lax.dot_general(
@@ -151,9 +225,8 @@
 
     depth = other_row.shape[0]
     shard_depth = weight.shape[0]
-    pres = []
     chunks = []
-    for rows, pre in zip((own, other), sums):
+    for rows in (own, other):
         flat = rows.reshape(-1, width)
 
         def chunk(side, place):
@@ -161,21 +234,26 @@
                 flat, side * depth + place * shard_depth, shard_depth, 1
             )
 
-        other_flat = half_of(rows, 1 - row_index, depth)
-        pre = pre + jnp.dot(other_flat, other_row, preferred_element_type=F32)
-        pres.append(pre + jnp.dot(chunk(row_index, far[1]), far[0], preferred_element_type=F32))
-        chunks.append([chunk(1 - row_index, place) for _, place in last])
-    shards = [shard for shard, _ in last]
+        chunks.append(
+            [chunk(row_index, far[1])] + [chunk(1 - row_index, place) for _, place in last]
+        )
+    own_sum = own_sum + jnp.dot(
+        half_of(own, 1 - row_index, depth), other_row, preferred_element_type=F32
+    )
+    other_sum = halves_product(other.reshape(-1, width), this_row, other_row, row_index)
+    twice = [jnp.concatenate((cot, cot), axis=1) for cot in (own_cot, other_cot)]
     own_factor = inner_factor(own)
-    pres, chunks, shards, own_factor, other = lax.optimization_barrier(
-        (pres, chunks, shards, own_factor, other)
+    shards = [far[0]] + [shard for shard, _ in last]
+    own_sum, other_sum, twice, projection, chunks, shards, own_factor, other = (
+        lax.optimization_barrier(
+            (own_sum, other_sum, twice, projection, chunks, shards, own_factor, other)
+        )
     )
     factors = (own_factor, inner_factor(other))
-    parts = []
-    for pre, pieces, rows_cot in zip(pres, chunks, (own_cot, other_cot)):
-        for chunk, shard in zip(pieces, shards):
-            pre = pre + jnp.dot(chunk, shard, preferred_element_type=F32)
-        parts.append(projected(pre, rows_cot, gate_proj, up_proj))
+    parts = [
+        finished(sums, cot, projection, pieces, shards)
+        for sums, cot, pieces in zip((own_sum, other_sum), twice, chunks)
+    ]
 
     first = half_index == 0
 
@@ -184,7 +262,7 @@
         b = jnp.where(first, pair[1], pair[0])
         return jnp.concatenate((a, b), axis=axis)
 
-    part = ordered(parts, 1).astype(BF16)
+    part = ordered(parts, 1)
     in_factor = ordered(factors, 0)
     ranks = part.shape[0] // n_dq
     part = part.reshape(n_dq, ranks, -1)

time: 182 us -> 186 us (1.022)
  matrix products: 34.2 us -> 10.6 us
  Pallas kernels: 0 us -> 16.3 us
  local copies, waits for them, and re-layouts: 15.5 us -> 27.7 us
  other arithmetic: 9.41 us -> 11.9 us
  waiting for transfers between devices: 46.9 us -> 44.7 us
    dot_general x14 -> x1, matrix products: 20.4 us -> 2.89 us  [body(): jnp.dot(half_of(own, 1 - row_index, depth), other_row, preferred_element_...]
    pallas_call x0 -> x3, Pallas kernels: none -> 16.3 us  [the longest x2 10.2 us: finished(): pl.pallas_call(lambda *refs: finish_kernel(n, *refs), out_shape=jax.Shape...]
    unnamed x36 -> x42, local copies, waits for them, and re-layouts: 0.93 us -> 10 us
    dot_general x2 -> x1, matrix products: 8.97 us -> 2.86 us  [this_product(): return jnp.dot(flat, this_row, preferred_element_type=F32)]
    concatenate x0 -> x3, other arithmetic: none -> 2.32 us  [the longest x2 1.53 us: body(): jnp.concatenate((cot, cot), axis=1)]
    ppermute x18, waiting for transfers between devices: 29.3 us -> 27.1 us  [shift(): lax.ppermute(value, axis, [(i, (i + step) % size) for i in range(size)])]
    dynamic_slice x2, local copies, waits for them, and re-layouts: 2.01 us -> 4.24 us  [chunk(): lax.dynamic_slice_in_dim(flat, side * depth + place * shard_depth, shard_...]
  transfers between devices with their start and end apart: 21 -> 21, of which waited for: 10 -> 10; matrix products, arithmetic and copies ran while one was open for 21% -> 17% of each run, Pallas kernels for 0% -> 3%
where the time goes in v7:
time: 186 us
  starting transfers between devices  47.3 us (25%)
  waiting for transfers between devices  44.7 us (24%)
  local copies, waits for them, and re-layouts  27.7 us (15%)
  Pallas kernels  16.3 us (9%)
  between operations  14.7 us (8%)
  blocking collectives  12.5 us (7%)
  other arithmetic  11.9 us (6%)
  matrix products  10.6 us (6%)
    ppermute x18, starting transfers between devices, shift(): lax.ppermute(value, axis, [(i, (i + step) % size) for i in range(size)])  29.9 us
    ppermute x18, waiting for transfers between devices, shift(): lax.ppermute(value, axis, [(i, (i + step) % size) for i in range(size)])  27.1 us
    all_to_all x1, blocking collectives, body(): received = lax.all_to_all(payload, dq, 0, 0, tiled=True)  12.5 us
    all_to_all x1, starting transfers between devices, body(): swapped = lax.all_to_all(part, dq, 0, 0, tiled=True)  11.7 us
    pallas_call x2, Pallas kernels, finished(): pl.pallas_call(lambda *refs: finish_kernel(n, *refs), out_shape=jax.Shape...  10.2 us
    unnamed x42, local copies, waits for them, and re-layouts  10 us
    all_to_all x1, waiting for transfers between devices, body(): swapped = lax.all_to_all(part, dq, 0, 0, tiled=True)  9.11 us
    all_to_all x1, waiting for transfers between devices, body(): lax.all_to_all(jnp.broadcast_to(queries[None], (n_fsdp,) + queries.shape)...  8.5 us
  transfers between devices with their start and end apart: 21, of which 10 were waited for; matrix products, arithmetic and copies ran while one was open for 17% of the time, Pallas kernels for 3%

profile of v7, /device:TPU:1, one launch (start us, length us, event | category | flops | bytes accessed | tf_op | source)
XLA Modules:
  0.0 185.7 jit_solution(12407494358662007985)
XLA Ops:
  6.5 2.3 %pad_maximum_fusion.4 = bf16[320,896]{1,0:T(8,128)(2,1)} fusion(bf16[320,448]{1,0:T(8,128)(2,1)} %param.14, bf16[320,448]{1,0:T(8,128)(2,1)} %param.13), kind=kLoop, calls=%fused_computation.9 | loop fusion | flops 1146880 | bytes 1146880 | tf_op jit(solution)/shard_map/concatenate | solution.py:196
  8.8 2.5 %collective-permute-start = (bf16[320,896]{1,0:T(8,128)(2,1)}, bf16[320,896]{1,0:T(8,128)(2,1)}, u32[]{:S(2)}, u32[]{:S(2)}) collective-permute-start(bf16[320,896]{1,0:T(8,128)(2,1)} %pad_maximum_fusion.4), channel_id=1, source_target_pairs={{0,16},{16,32},{32,48},{48,64},{64,80},{80,96},{96,112},{112,0},{1... | collective-permute-start | bytes 1720328 | tf_op jit(solution)/shard_map/ppermute | solution.py:13
  11.3 3.9 %collective-permute-start.1 = (bf16[320,896]{1,0:T(8,128)(2,1)}, bf16[320,896]{1,0:T(8,128)(2,1)}, u32[]{:S(2)}, u32[]{:S(2)}) collective-permute-start(bf16[320,896]{1,0:T(8,128)(2,1)} %pad_maximum_fusion.4), channel_id=1, source_target_pairs={{0,112},{16,0},{32,16},{48,32},{64,48},{80,64},{96,80},{112,96},{1... | collective-permute-start | bytes 1720328 | tf_op jit(solution)/shard_map/ppermute | solution.py:13
  15.2 1.1 constant_dynamic-slice_fusion.14
  17.2 2.9 %collective-permute-start.2 = (bf16[1,64,5120]{2,1,0:T(8,128)(2,1)}, bf16[1,64,5120]{2,1,0:T(8,128)(2,1)}, u32[]{:S(2)}, u32[]{:S(2)}) collective-permute-start(bf16[1,64,5120]{2,1,0:T(8,128)(2,1)} %pad_maximum_fusion.3), channel_id=1, source_target_pairs={{0,1},{1,0},{2,3},{3,2},{4,5},{5,4},{6,7},{7,6},{8,9},{9,8},{10,11... | collective-permute-start | bytes 1966088 | tf_op jit(solution)/shard_map/ppermute | solution.py:13
  20.1 1.8 constant_dynamic-slice_fusion.10
  23.7 2.9 %pad_maximum_fusion = bf16[8,64,5120]{2,1,0:T(8,128)(2,1)} fusion(bf16[8,32,5120]{2,1,0:T(8,128)(2,1)S(1)} %copy-done.13, bf16[8,32,5120]{2,1,0:T(8,128)(2,1)S(1)} %copy-done.14), kind=kLoop, calls=%fused_computation | loop fusion | flops 10485760 | bytes 10485760 | tf_op jit(solution)/shard_map/concatenate | solution.py:184
  26.6 1.6 collective-permute-done
  28.2 6.1 %collective-permute-done.2 = bf16[1,64,5120]{2,1,0:T(8,128)(2,1)} collective-permute-done((bf16[1,64,5120]{2,1,0:T(8,128)(2,1)}, bf16[1,64,5120]{2,1,0:T(8,128)(2,1)}, u32[]{:S(2)}, u32[]{:S(2)}) %collective-permute-start.2) | collective-permute-done | bytes 655392 | tf_op jit(solution)/shard_map/ppermute | solution.py:13
  35.4 2.7 %collective-permute-start.4 = (bf16[320,896]{1,0:T(8,128)(2,1)}, bf16[320,896]{1,0:T(8,128)(2,1)S(1)}, u32[]{:S(2)}, u32[]{:S(2)}) collective-permute-start(bf16[320,896]{1,0:T(8,128)(2,1)} %collective-permute-done.1), channel_id=1, source_target_pairs={{0,112},{16,0},{32,16},{48,32},{64,48},{80,64},{96,80},{112,96},{1... | collective-permute-start | bytes 1720328 | tf_op jit(solution)/shard_map/ppermute | solution.py:13
  38.1 1.3 collective-permute-start.5
  40.0 1.1 bitcast_dynamic-update-slice_fusion.11
  41.1 1.1 bitcast_dynamic-update-slice_fusion.10
  42.3 1.9 %constant_dynamic-slice_fusion.4 = (bf16[512,320]{1,0:T(8,128)(2,1)}, bf16[512,320]{1,0:T(8,128)(2,1)}, bf16[512,320]{1,0:T(8,128)(2,1)}, bf16[512,320]{1,0:T(8,128)(2,1)}) fusion(bf16[512,5120]{1,0:T(8,128)(2,1)S(1)} %bitcast.67, s32[]{:T(128)S(6)} %select_n.159, s32[]{:T(128)S(6)} %select_n.158, s32[]{:T(128)S(6)} %select_n.157, s32[]{:T(128)S(6)} %select_n.156), kind=kLoop, calls=%fused_computation.49 | loop fusion | bytes 2621456 | tf_op jit(solution)/shard_map/dynamic_slice | solution.py:233
  44.2 1.7 fusion.14
  45.9 3.6 %collective-permute-done.3 = bf16[320,896]{1,0:T(8,128)(2,1)S(1)} collective-permute-done((bf16[320,896]{1,0:T(8,128)(2,1)}, bf16[320,896]{1,0:T(8,128)(2,1)S(1)}, u32[]{:S(2)}, u32[]{:S(2)}) %collective-permute-start.3) | collective-permute-done | bytes 573472 | tf_op jit(solution)/shard_map/ppermute | solution.py:13
  50.3 1.3 collective-permute-start.8
  51.6 2.7 %collective-permute-start.7 = (bf16[320,896]{1,0:T(8,128)(2,1)S(1)}, bf16[320,896]{1,0:T(8,128)(2,1)S(1)}, u32[]{:S(2)}, u32[]{:S(2)}) collective-permute-start(bf16[320,896]{1,0:T(8,128)(2,1)S(1)} %collective-permute-done.4), channel_id=1, source_target_pairs={{0,112},{16,0},{32,16},{48,32},{64,48},{80,64},{96,80},{112,96},{1... | collective-permute-start | bytes 1720328 | tf_op jit(solution)/shard_map/ppermute | solution.py:13
  54.6 1.1 bitcast_dynamic-update-slice_fusion.9
  55.8 2.7 %collective-permute-start.14 = (bf16[512,448]{1,0:T(8,128)(2,1)S(1)}, bf16[512,448]{1,0:T(8,128)(2,1)S(1)}, u32[]{:S(2)}, u32[]{:S(2)}) collective-permute-start(bf16[512,448]{1,0:T(8,128)(2,1)S(1)} %bitcast.74), channel_id=1, source_target_pairs={{0,1},{1,0},{2,3},{3,2},{4,5},{5,4},{6,7},{7,6},{8,9},{9,8},{10,11... | collective-permute-start | bytes 1376264 | tf_op jit(solution)/shard_map/ppermute | solution.py:13
  58.6 4.1 %collective-permute-done.6 = bf16[320,896]{1,0:T(8,128)(2,1)S(1)} collective-permute-done((bf16[320,896]{1,0:T(8,128)(2,1)S(1)}, bf16[320,896]{1,0:T(8,128)(2,1)S(1)}, u32[]{:S(2)}, u32[]{:S(2)}) %collective-permute-start.6) | collective-permute-done | bytes 573472 | tf_op jit(solution)/shard_map/ppermute | solution.py:13
  62.6 1.6 collective-permute-start.9
  64.2 1.8 collective-permute-start.10
  67.0 8.5 %collective-permute-done.14 = bf16[512,448]{1,0:T(8,128)(2,1)S(1)} collective-permute-done((bf16[512,448]{1,0:T(8,128)(2,1)S(1)}, bf16[512,448]{1,0:T(8,128)(2,1)S(1)}, u32[]{:S(2)}, u32[]{:S(2)}) %collective-permute-start.14) | collective-permute-done | bytes 458784 | tf_op jit(solution)/shard_map/ppermute | solution.py:13
  75.5 1.9 %collective-permute-start.13 = (bf16[160,896]{1,0:T(8,128)(2,1)S(1)}, bf16[160,896]{1,0:T(8,128)(2,1)S(1)}, u32[]{:S(2)}, u32[]{:S(2)}) collective-permute-start(bf16[160,896]{1,0:T(8,128)(2,1)S(1)} %slice.23), channel_id=1, source_target_pairs={{0,112},{16,0},{32,16},{48,32},{64,48},{80,64},{96,80},{112,96},{1... | collective-permute-start | bytes 860168 | tf_op jit(solution)/shard_map/ppermute | solution.py:13
  77.4 2.9 %fusion.2 = f32[512,896]{1,0:T(8,128)S(1)} fusion(bf16[2560,896]{1,0:T(8,128)(2,1)S(1)} %bitcast.65, bf16[512,5120]{1,0:T(8,128)(2,1)S(1)} %bitcast.69, s32[]{:T(128)S(6)} %select_n.139), kind=kOutput, calls=%fused_computation.3 | convolution fusion | flops 2348810240 | bytes 9043972 | tf_op jit(solution)/shard_map/dot_general | solution.py:203
  80.3 2.1 %copy-done.4 = bf16[8,320,896]{2,1,0:T(8,128)(2,1)} copy-done((bf16[8,320,896]{2,1,0:T(8,128)(2,1)}, bf16[8,320,896]{2,1,0:T(8,128)(2,1)S(1)}, u32[]{:S(2)}) %copy-start.4) | copy-done | bytes 4587544
  83.1 1.0 collective-permute-done.13
  84.1 1.3 collective-permute-done.11
  86.9 1.3 collective-permute-start.15
  88.5 2.3 %collective-permute-start.17 = (bf16[320,896]{1,0:T(8,128)(2,1)}, bf16[320,896]{1,0:T(8,128)(2,1)}, u32[]{:S(2)}, u32[]{:S(2)}) collective-permute-start(bf16[320,896]{1,0:T(8,128)(2,1)} %collective-permute-done.11), channel_id=1, source_target_pairs={{0,112},{16,0},{32,16},{48,32},{64,48},{80,64},{96,80},{112,96},{1... | collective-permute-start | bytes 1720328 | tf_op jit(solution)/shard_map/ppermute | solution.py:13
  91.0 1.1 bitcast_dynamic-update-slice_fusion.1
  92.1 1.1 bitcast_dynamic-update-slice_fusion
  93.3 2.9 %fusion = f32[512,896]{1,0:T(8,128)S(1)} fusion(bf16[2560,896]{1,0:T(8,128)(2,1)S(1)} %bitcast.63, bf16[512,5120]{1,0:T(8,128)(2,1)S(1)} %bitcast.70, s32[]{:T(128)S(6)} %select_n.154), kind=kOutput, calls=%fused_computation.1 | convolution fusion | flops 2348810240 | bytes 9043972 | tf_op jit(solution)/shard_map/dot_general | solution.py:240
  96.4 1.2 pad_maximum_fusion.2.refs_1_
  97.6 2.3 %constant_dynamic-slice_fusion = (bf16[512,320]{1,0:T(8,128)(2,1)S(1)}, bf16[512,320]{1,0:T(8,128)(2,1)S(1)}, bf16[512,320]{1,0:T(8,128)(2,1)S(1)}, bf16[512,320]{1,0:T(8,128)(2,1)S(1)}) fusion(bf16[512,5120]{1,0:T(8,128)(2,1)} %bitcast.59, s32[]{:T(128)S(6)} %select_n.159, s32[]{:T(128)S(6)} %select_n.158, s32[]{:T(128)S(6)} %select_n.157, s32[]{:T(128)S(6)} %select_n.156), kind=kLoop, calls=%fused_computation.45 | loop fusion | bytes 2621456 | tf_op jit(solution)/shard_map/dynamic_slice | solution.py:233
  100.0 2.5 %copy-done.1 = bf16[8,64,5120]{2,1,0:T(8,128)(2,1)S(1)} copy-done((bf16[8,64,5120]{2,1,0:T(8,128)(2,1)S(1)}, bf16[8,64,5120]{2,1,0:T(8,128)(2,1)}, u32[]{:S(2)}) %copy-start.1) | copy-done | bytes 5242904
  102.5 2.3 %copy-done.3 = bf16[8,320,896]{2,1,0:T(8,128)(2,1)S(1)} copy-done((bf16[8,320,896]{2,1,0:T(8,128)(2,1)S(1)}, bf16[8,320,896]{2,1,0:T(8,128)(2,1)}, u32[]{:S(2)}) %copy-start.3) | copy-done | bytes 4587544
  104.8 2.3 %copy-done.5 = bf16[8,320,896]{2,1,0:T(8,128)(2,1)S(1)} copy-done((bf16[8,320,896]{2,1,0:T(8,128)(2,1)S(1)}, bf16[8,320,896]{2,1,0:T(8,128)(2,1)}, u32[]{:S(2)}) %copy-start.5) | copy-done | bytes 4587544
  107.1 6.2 %halves_product.1.refs_0_ = f32[512,896]{1,0:T(8,128)S(1)} custom-call(s32[1]{0:T(128)} %bitcast.17.side_ref, bf16[512,5120]{1,0:T(8,128)(2,1)S(1)} %bitcast.60, bf16[512,5120]{1,0:T(8,128)(2,1)S(1)} %bitcast.61, bf16[2560,896]{1,0:T(8,128)(2,1)S(1)} %bitcast.66, bf16[2560,896]{1,0:T(8,128)(2,1)S(1)} %bitcast.64), custom_call_target="tpu_custom_call" | custom-call | flops 4697620480 | bytes 7077888 | tf_op jit(solution)/shard_map/halves_product/pallas_call | solution.py:86
  113.3 2.4 %fusion.15 = f32[512,64]{0,1:T(8,128)} fusion(bf16[512,5120]{1,0:T(8,128)(2,1)S(1)} %bitcast.62, bf16[64,5120]{1,0:T(8,128)(2,1)S(1)} %copy-done), kind=kOutput, calls=%fused_computation.67 | convolution fusion | flops 335544320 | bytes 6029312 | tf_op jit(solution)/shard_map/dot_general | solution.py:219
  115.7 5.1 %finished.2 = bf16[128,512]{1,0:T(8,128)(2,1)S(1)} custom-call(f32[512,896]{1,0:T(8,128)S(1)} %add.186.refs_0_, bf16[512,896]{1,0:T(8,128)(2,1)S(1)} %pad_maximum_fusion.1.refs_1_, bf16[128,896]{1,0:T(8,128)(2,1)S(1)} %copy-done.7, bf16[512,320]{1,0:T(8,128)(2,1)S(1)} %copy-done.11, bf16[512,320]{1,0:T(8,128)(2,1)S(1)} %copy-done.10, ...), custom_call_target="tpu_custom_call" | custom-call | flops 1291845632 | bytes 6356992 | tf_op jit(solution)/shard_map/finished/pallas_call | solution.py:133
  120.9 5.1 %finished.3 = bf16[128,512]{1,0:T(8,128)(2,1)S(1)} custom-call(f32[512,896]{1,0:T(8,128)S(1)} %halves_product.1.refs_0_, bf16[512,896]{1,0:T(8,128)(2,1)S(1)} %copy-done.6, bf16[128,896]{1,0:T(8,128)(2,1)S(1)} %copy-done.7, bf16[512,320]{1,0:T(8,128)(2,1)S(1)} %get-tuple-element.85.refs_3_, bf16[512,320]{1,0:T(8,128)(2,1)S(1)} %get-tuple-element.86.refs_4_, ...), custom_call_target="tpu_custom_call" | custom-call | flops 1291845632 | bytes 6356992 | tf_op jit(solution)/shard_map/finished/pallas_call | solution.py:133
  126.7 11.7 %all-to-all-start = ((bf16[16,8,1024]{2,1,0:T(8,128)(2,1)}), bf16[16,8,1024]{2,1,0:T(8,128)(2,1)S(1)}, u32[]{:S(2)}, u32[]{:S(2)}) async-start(bf16[16,8,1024]{2,1,0:T(8,128)(2,1)} %maximum_bitcast_fusion), calls=%async_computation | async-start | bytes 524288 | tf_op jit(solution)/shard_map/all_to_all | solution.py:269
  138.7 9.1 %all-to-all-done = bf16[16,8,1024]{2,1,0:T(8,128)(2,1)S(1)} async-done(((bf16[16,8,1024]{2,1,0:T(8,128)(2,1)}), bf16[16,8,1024]{2,1,0:T(8,128)(2,1)S(1)}, u32[]{:S(2)}, u32[]{:S(2)}) %all-to-all-start) | async-done | bytes 262176 | tf_op jit(solution)/shard_map/all_to_all | solution.py:269
  149.5 5.6 %all-to-all-start.1 = ((bf16[16,16,512]{2,1,0:T(8,128)(2,1)}), bf16[16,16,512]{2,1,0:T(8,128)(2,1)S(1)}, u32[]{:S(2)}, u32[]{:S(2)}) async-start(bf16[16,16,512]{2,1,0:T(8,128)(2,1)} %broadcast_in_dim.69), calls=%async_computation.1 | async-start | bytes 524288 | tf_op jit(solution)/shard_map/all_to_all | solution.py:285
  155.5 8.5 %all-to-all-done.1 = bf16[16,16,512]{2,1,0:T(8,128)(2,1)S(1)} async-done(((bf16[16,16,512]{2,1,0:T(8,128)(2,1)}), bf16[16,16,512]{2,1,0:T(8,128)(2,1)S(1)}, u32[]{:S(2)}, u32[]{:S(2)}) %all-to-all-start.1) | async-done | bytes 262176 | tf_op jit(solution)/shard_map/all_to_all | solution.py:285
  164.6 12.5 %all_to_all.19 = f32[16,1,640]{2,1,0:T(1,128)S(1)} all-to-all(f32[16,1,640]{2,1,0:T(1,128)S(1)} %copy.24), channel_id=1, replica_groups=mesh['ylo'=2,'z'=8,'x'=4,'core'=2,'yhi'=2] {'x','core','yhi'}, dimensions={0} | all-to-all | bytes 81920 | tf_op jit(solution)/shard_map/all_to_all | solution.py:306
  (104 shorter events, 13.9 us)
Async XLA Ops:
  6.5 37.6 %copy-start = (bf16[64,5120]{1,0:T(8,128)(2,1)S(1)}, bf16[64,5120]{1,0:T(8,128)(2,1)}, u32[]{:S(2)}) copy-start(bf16[64,5120]{1,0:T(8,128)(2,1)} %param.15) | copy-start | bytes 1966084
  6.5 17.2 %copy-start.13 = (bf16[8,32,5120]{2,1,0:T(8,128)(2,1)S(1)}, bf16[8,32,5120]{2,1,0:T(8,128)(2,1)}, u32[]{:S(2)}) copy-start(bf16[8,32,5120]{2,1,0:T(8,128)(2,1)} %param.11) | copy-start | bytes 7864324
  6.5 91.1 %all-gather.2.cloned.1.call-start = ((), (), s32[]{:S(2)}) async-start(), calls=%async_computation.3 | async-start | bytes 5898240 | tf_op jit(solution)/shard_map/all_gather | solution.py:41
  8.8 19.4 %collective-permute-start = (bf16[320,896]{1,0:T(8,128)(2,1)}, bf16[320,896]{1,0:T(8,128)(2,1)}, u32[]{:S(2)}, u32[]{:S(2)}) collective-permute-start(bf16[320,896]{1,0:T(8,128)(2,1)} %pad_maximum_fusion.4), channel_id=1, source_target_pairs={{0,16},{16,32},{32,48},{48,64},{64,80},{80,96},{96,112},{112,0},{1... | collective-permute-start | bytes 1720328 | tf_op jit(solution)/shard_map/ppermute | solution.py:13
  11.3 17.0 %collective-permute-start.1 = (bf16[320,896]{1,0:T(8,128)(2,1)}, bf16[320,896]{1,0:T(8,128)(2,1)}, u32[]{:S(2)}, u32[]{:S(2)}) collective-permute-start(bf16[320,896]{1,0:T(8,128)(2,1)} %pad_maximum_fusion.4), channel_id=1, source_target_pairs={{0,112},{16,0},{32,16},{48,32},{64,48},{80,64},{96,80},{112,96},{1... | collective-permute-start | bytes 1720328 | tf_op jit(solution)/shard_map/ppermute | solution.py:13
  17.2 17.1 %collective-permute-start.2 = (bf16[1,64,5120]{2,1,0:T(8,128)(2,1)}, bf16[1,64,5120]{2,1,0:T(8,128)(2,1)}, u32[]{:S(2)}, u32[]{:S(2)}) collective-permute-start(bf16[1,64,5120]{2,1,0:T(8,128)(2,1)} %pad_maximum_fusion.3), channel_id=1, source_target_pairs={{0,1},{1,0},{2,3},{3,2},{4,5},{5,4},{6,7},{7,6},{8,9},{9,8},{10,11... | collective-permute-start | bytes 1966088 | tf_op jit(solution)/shard_map/ppermute | solution.py:13
  20.1 3.6 %copy-start.14 = (bf16[8,32,5120]{2,1,0:T(8,128)(2,1)S(1)}, bf16[8,32,5120]{2,1,0:T(8,128)(2,1)}, u32[]{:S(2)}) copy-start(bf16[8,32,5120]{2,1,0:T(8,128)(2,1)} %param.9) | copy-start | bytes 7864324
  23.7 10.8 %copy-start.18 = (bf16[64,896]{1,0:T(8,128)(2,1)S(1)}, bf16[64,896]{1,0:T(8,128)(2,1)}, u32[]{:S(2)}) copy-start(bf16[64,896]{1,0:T(8,128)(2,1)} %param.17) | copy-start | bytes 344068
  23.7 10.8 %copy-start.19 = (bf16[64,896]{1,0:T(8,128)(2,1)S(1)}, bf16[64,896]{1,0:T(8,128)(2,1)}, u32[]{:S(2)}) copy-start(bf16[64,896]{1,0:T(8,128)(2,1)} %param.16) | copy-start | bytes 344068
  34.5 7.8 %copy-start.12 = (bf16[8,64,5120]{2,1,0:T(8,128)(2,1)S(1)}, bf16[8,64,5120]{2,1,0:T(8,128)(2,1)}, u32[]{:S(2)}) copy-start(bf16[8,64,5120]{2,1,0:T(8,128)(2,1)} %pad_maximum_fusion) | copy-start | bytes 15728644
  35.4 14.0 %collective-permute-start.3 = (bf16[320,896]{1,0:T(8,128)(2,1)}, bf16[320,896]{1,0:T(8,128)(2,1)S(1)}, u32[]{:S(2)}, u32[]{:S(2)}) collective-permute-start(bf16[320,896]{1,0:T(8,128)(2,1)} %collective-permute-done), channel_id=1, source_target_pairs={{0,16},{16,32},{32,48},{48,64},{64,80},{80,96},{96,112},{112,0},{1... | collective-permute-start | bytes 1720328 | tf_op jit(solution)/shard_map/ppermute | solution.py:13
  35.4 14.0 %collective-permute-start.4 = (bf16[320,896]{1,0:T(8,128)(2,1)}, bf16[320,896]{1,0:T(8,128)(2,1)S(1)}, u32[]{:S(2)}, u32[]{:S(2)}) collective-permute-start(bf16[320,896]{1,0:T(8,128)(2,1)} %collective-permute-done.1), channel_id=1, source_target_pairs={{0,112},{16,0},{32,16},{48,32},{64,48},{80,64},{96,80},{112,96},{1... | collective-permute-start | bytes 1720328 | tf_op jit(solution)/shard_map/ppermute | solution.py:13
  38.1 12.3 %collective-permute-start.5 = (bf16[320,896]{1,0:T(8,128)(2,1)}, bf16[320,896]{1,0:T(8,128)(2,1)S(1)}, u32[]{:S(2)}, u32[]{:S(2)}) collective-permute-start(bf16[320,896]{1,0:T(8,128)(2,1)} %pad_maximum_fusion.4), channel_id=1, source_target_pairs={{0,128},{128,0},{1,129},{129,1},{2,130},{130,2},{3,131},{131,3},{4... | collective-permute-start | bytes 1720328 | tf_op jit(solution)/shard_map/ppermute | solution.py:13
  42.3 12.1 %copy-start.15 = (bf16[8,64,448]{2,1,0:T(8,128)(2,1)S(1)}, bf16[8,64,448]{2,1,0:T(8,128)(2,1)}, u32[]{:S(2)}) copy-start(bf16[8,64,448]{2,1,0:T(8,128)(2,1)} %pad_maximum_fusion.6) | copy-start | bytes 1376260
  44.2 11.6 %copy-start.17 = (bf16[8,64,448]{2,1,0:T(8,128)(2,1)S(1)}, bf16[8,64,448]{2,1,0:T(8,128)(2,1)}, u32[]{:S(2)}) copy-start(bf16[8,64,448]{2,1,0:T(8,128)(2,1)} %pad_maximum_fusion.5) | copy-start | bytes 1376260
  50.3 12.3 %collective-permute-start.6 = (bf16[320,896]{1,0:T(8,128)(2,1)S(1)}, bf16[320,896]{1,0:T(8,128)(2,1)S(1)}, u32[]{:S(2)}, u32[]{:S(2)}) collective-permute-start(bf16[320,896]{1,0:T(8,128)(2,1)S(1)} %collective-permute-done.3), channel_id=1, source_target_pairs={{0,16},{16,32},{32,48},{48,64},{64,80},{80,96},{96,112},{112,0},{1... | collective-permute-start | bytes 1720328 | tf_op jit(solution)/shard_map/ppermute | solution.py:13
  50.3 12.3 %collective-permute-start.8 = (bf16[320,896]{1,0:T(8,128)(2,1)S(1)}, bf16[320,896]{1,0:T(8,128)(2,1)}, u32[]{:S(2)}, u32[]{:S(2)}) collective-permute-start(bf16[320,896]{1,0:T(8,128)(2,1)S(1)} %collective-permute-done.3), channel_id=1, source_target_pairs={{0,128},{128,0},{1,129},{129,1},{2,130},{130,2},{3,131},{131,3},{4... | collective-permute-start | bytes 1720328 | tf_op jit(solution)/shard_map/ppermute | solution.py:13
  51.6 11.0 %collective-permute-start.7 = (bf16[320,896]{1,0:T(8,128)(2,1)S(1)}, bf16[320,896]{1,0:T(8,128)(2,1)S(1)}, u32[]{:S(2)}, u32[]{:S(2)}) collective-permute-start(bf16[320,896]{1,0:T(8,128)(2,1)S(1)} %collective-permute-done.4), channel_id=1, source_target_pairs={{0,112},{16,0},{32,16},{48,32},{64,48},{80,64},{96,80},{112,96},{1... | collective-permute-start | bytes 1720328 | tf_op jit(solution)/shard_map/ppermute | solution.py:13
  55.8 19.7 %collective-permute-start.14 = (bf16[512,448]{1,0:T(8,128)(2,1)S(1)}, bf16[512,448]{1,0:T(8,128)(2,1)S(1)}, u32[]{:S(2)}, u32[]{:S(2)}) collective-permute-start(bf16[512,448]{1,0:T(8,128)(2,1)S(1)} %bitcast.74), channel_id=1, source_target_pairs={{0,1},{1,0},{2,3},{3,2},{4,5},{5,4},{6,7},{7,6},{8,9},{9,8},{10,11... | collective-permute-start | bytes 1376264 | tf_op jit(solution)/shard_map/ppermute | solution.py:13
  62.6 21.5 %collective-permute-start.9 = (bf16[320,896]{1,0:T(8,128)(2,1)S(1)}, bf16[320,896]{1,0:T(8,128)(2,1)S(1)}, u32[]{:S(2)}, u32[]{:S(2)}) collective-permute-start(bf16[320,896]{1,0:T(8,128)(2,1)S(1)} %collective-permute-done.5), channel_id=1, source_target_pairs={{0,16},{16,32},{32,48},{48,64},{64,80},{80,96},{96,112},{112,0},{1... | collective-permute-start | bytes 1720328 | tf_op jit(solution)/shard_map/ppermute | solution.py:13
  64.2 19.9 %collective-permute-start.10 = (bf16[320,896]{1,0:T(8,128)(2,1)S(1)}, bf16[320,896]{1,0:T(8,128)(2,1)S(1)}, u32[]{:S(2)}, u32[]{:S(2)}) collective-permute-start(bf16[320,896]{1,0:T(8,128)(2,1)S(1)} %collective-permute-done.5), channel_id=1, source_target_pairs={{0,112},{16,0},{32,16},{48,32},{64,48},{80,64},{96,80},{112,96},{1... | collective-permute-start | bytes 1720328 | tf_op jit(solution)/shard_map/ppermute | solution.py:13
  66.0 19.4 %collective-permute-start.11 = (bf16[320,896]{1,0:T(8,128)(2,1)S(1)}, bf16[320,896]{1,0:T(8,128)(2,1)}, u32[]{:S(2)}, u32[]{:S(2)}) collective-permute-start(bf16[320,896]{1,0:T(8,128)(2,1)S(1)} %collective-permute-done.4), channel_id=1, source_target_pairs={{0,128},{128,0},{1,129},{129,1},{2,130},{130,2},{3,131},{131,3},{4... | collective-permute-start | bytes 1720328 | tf_op jit(solution)/shard_map/ppermute | solution.py:13
  66.6 16.4 %collective-permute-start.12 = (bf16[160,896]{1,0:T(8,128)(2,1)S(1)}, bf16[160,896]{1,0:T(8,128)(2,1)S(1)}, u32[]{:S(2)}, u32[]{:S(2)}) collective-permute-start(bf16[160,896]{1,0:T(8,128)(2,1)S(1)} %slice.22), channel_id=1, source_target_pairs={{0,16},{16,32},{32,48},{48,64},{64,80},{80,96},{96,112},{112,0},{1... | collective-permute-start | bytes 860168 | tf_op jit(solution)/shard_map/ppermute | solution.py:13
  75.5 8.7 %collective-permute-start.13 = (bf16[160,896]{1,0:T(8,128)(2,1)S(1)}, bf16[160,896]{1,0:T(8,128)(2,1)S(1)}, u32[]{:S(2)}, u32[]{:S(2)}) collective-permute-start(bf16[160,896]{1,0:T(8,128)(2,1)S(1)} %slice.23), channel_id=1, source_target_pairs={{0,112},{16,0},{32,16},{48,32},{64,48},{80,64},{96,80},{112,96},{1... | collective-permute-start | bytes 860168 | tf_op jit(solution)/shard_map/ppermute | solution.py:13
  80.2 2.2 %copy-start.4 = (bf16[8,320,896]{2,1,0:T(8,128)(2,1)}, bf16[8,320,896]{2,1,0:T(8,128)(2,1)S(1)}, u32[]{:S(2)}) copy-start(bf16[8,320,896]{2,1,0:T(8,128)(2,1)S(1)} %bitcast_dynamic-update-slice_fusion.5) | copy-start | bytes 13762564
  86.9 26.4 %collective-permute-start.15 = (bf16[320,896]{1,0:T(8,128)(2,1)}, bf16[320,896]{1,0:T(8,128)(2,1)}, u32[]{:S(2)}, u32[]{:S(2)}) collective-permute-start(bf16[320,896]{1,0:T(8,128)(2,1)} %constant_dynamic-update-slice_fusion.refs_7_), channel_id=1, source_target_pairs={{0,128},{128,0},{1,129},{129,1},{2,130},{130,2},{3,131},{131,3},{4... | collective-permute-start | bytes 1720328 | tf_op jit(solution)/shard_map/ppermute | solution.py:13
  88.2 25.1 %collective-permute-start.16 = (bf16[320,896]{1,0:T(8,128)(2,1)}, bf16[320,896]{1,0:T(8,128)(2,1)}, u32[]{:S(2)}, u32[]{:S(2)}) collective-permute-start(bf16[320,896]{1,0:T(8,128)(2,1)} %collective-permute-done.8), channel_id=1, source_target_pairs={{0,16},{16,32},{32,48},{48,64},{64,80},{80,96},{96,112},{112,0},{1... | collective-permute-start | bytes 1720328 | tf_op jit(solution)/shard_map/ppermute | solution.py:13
  88.5 24.8 %collective-permute-start.17 = (bf16[320,896]{1,0:T(8,128)(2,1)}, bf16[320,896]{1,0:T(8,128)(2,1)}, u32[]{:S(2)}, u32[]{:S(2)}) collective-permute-start(bf16[320,896]{1,0:T(8,128)(2,1)} %collective-permute-done.11), channel_id=1, source_target_pairs={{0,112},{16,0},{32,16},{48,32},{64,48},{80,64},{96,80},{112,96},{1... | collective-permute-start | bytes 1720328 | tf_op jit(solution)/shard_map/ppermute | solution.py:13
  93.3 2.9 %copy-start.2 = (bf16[8,320,896]{2,1,0:T(8,128)(2,1)}, bf16[8,320,896]{2,1,0:T(8,128)(2,1)S(1)}, u32[]{:S(2)}) copy-start(bf16[8,320,896]{2,1,0:T(8,128)(2,1)S(1)} %bitcast_dynamic-update-slice_fusion) | copy-start | bytes 13762564
  100.0 2.5 %copy-start.1 = (bf16[8,64,5120]{2,1,0:T(8,128)(2,1)S(1)}, bf16[8,64,5120]{2,1,0:T(8,128)(2,1)}, u32[]{:S(2)}) copy-start(bf16[8,64,5120]{2,1,0:T(8,128)(2,1)} %all-gather.2.cloned.1.call-done) | copy-start | bytes 15728644
  102.5 2.3 %copy-start.3 = (bf16[8,320,896]{2,1,0:T(8,128)(2,1)S(1)}, bf16[8,320,896]{2,1,0:T(8,128)(2,1)}, u32[]{:S(2)}) copy-start(bf16[8,320,896]{2,1,0:T(8,128)(2,1)} %copy-done.2) | copy-start | bytes 13762564
  104.8 2.3 %copy-start.5 = (bf16[8,320,896]{2,1,0:T(8,128)(2,1)S(1)}, bf16[8,320,896]{2,1,0:T(8,128)(2,1)}, u32[]{:S(2)}) copy-start(bf16[8,320,896]{2,1,0:T(8,128)(2,1)} %copy-done.4) | copy-start | bytes 13762564
  113.2 2.5 %copy-start.7 = (bf16[128,896]{1,0:T(8,128)(2,1)S(1)}, bf16[128,896]{1,0:T(8,128)(2,1)}, u32[]{:S(2)}) copy-start(bf16[128,896]{1,0:T(8,128)(2,1)} %fusion.6.refs_2_) | copy-start | bytes 688132
  113.2 2.4 %copy-start.8 = (bf16[512,320]{1,0:T(8,128)(2,1)S(1)}, bf16[512,320]{1,0:T(8,128)(2,1)}, u32[]{:S(2)}) copy-start(bf16[512,320]{1,0:T(8,128)(2,1)} %get-tuple-element.78.refs_6_) | copy-start | bytes 983044
  113.3 2.4 %copy-start.9 = (bf16[512,320]{1,0:T(8,128)(2,1)S(1)}, bf16[512,320]{1,0:T(8,128)(2,1)}, u32[]{:S(2)}) copy-start(bf16[512,320]{1,0:T(8,128)(2,1)} %get-tuple-element.77.refs_5_) | copy-start | bytes 983044
  113.3 2.4 %copy-start.10 = (bf16[512,320]{1,0:T(8,128)(2,1)S(1)}, bf16[512,320]{1,0:T(8,128)(2,1)}, u32[]{:S(2)}) copy-start(bf16[512,320]{1,0:T(8,128)(2,1)} %get-tuple-element.76.refs_4_) | copy-start | bytes 983044
  113.3 2.4 %copy-start.11 = (bf16[512,320]{1,0:T(8,128)(2,1)S(1)}, bf16[512,320]{1,0:T(8,128)(2,1)}, u32[]{:S(2)}) copy-start(bf16[512,320]{1,0:T(8,128)(2,1)} %get-tuple-element.75.refs_3_) | copy-start | bytes 983044
  115.7 5.1 %copy-start.6 = (bf16[512,896]{1,0:T(8,128)(2,1)S(1)}, bf16[512,896]{1,0:T(8,128)(2,1)}, u32[]{:S(2)}) copy-start(bf16[512,896]{1,0:T(8,128)(2,1)} %pad_maximum_fusion.2.refs_1_) | copy-start | bytes 2752516
  120.8 17.6 %copy-start.16 = (f32[512,64]{0,1:T(8,128)S(1)}, f32[512,64]{0,1:T(8,128)}, u32[]{:S(2)}) copy-start(f32[512,64]{0,1:T(8,128)} %fusion.15) | copy-start | bytes 393220
  126.7 21.1 %all-to-all-start = ((bf16[16,8,1024]{2,1,0:T(8,128)(2,1)}), bf16[16,8,1024]{2,1,0:T(8,128)(2,1)S(1)}, u32[]{:S(2)}, u32[]{:S(2)}) async-start(bf16[16,8,1024]{2,1,0:T(8,128)(2,1)} %maximum_bitcast_fusion), calls=%async_computation | async-start | bytes 524288 | tf_op jit(solution)/shard_map/all_to_all | solution.py:269
  149.5 14.5 %all-to-all-start.1 = ((bf16[16,16,512]{2,1,0:T(8,128)(2,1)}), bf16[16,16,512]{2,1,0:T(8,128)(2,1)S(1)}, u32[]{:S(2)}, u32[]{:S(2)}) async-start(bf16[16,16,512]{2,1,0:T(8,128)(2,1)} %broadcast_in_dim.69), calls=%async_computation.1 | async-start | bytes 524288 | tf_op jit(solution)/shard_map/all_to_all | solution.py:285
Sparse Core Ops, SparseCore 0:
  34.4 40.6 all-gather.1

commit v8 on v4

--- a/solution.py
+++ b/solution.py
@@ -11,12 +11,13 @@
     return lax.ppermute(value, axis, [(i, (i + step) % size) for i in range(size)])
 
 
-def gathered(weight, piece, cot, early):
+def gathered(weight, piece, cot, early, start):
     barrier = lax.optimization_barrier
     n_z = lax.axis_size("z")
     z = lax.axis_index("z")
     half = weight.shape[0] // 2
-    far_z = (z + n_z // 2) % n_z
+    this = lax.axis_index("ylo") * n_z
+    other = n_z - this
 
     def up(value):
         return shift(value, "z", 1)
@@ -26,12 +27,6 @@
 
     def across(value):
         return shift(value, "ylo", 1)
-
-    def placed(by_offset):
-        result = jnp.zeros((n_z,) + weight.shape, weight.dtype)
-        for offset, shard in by_offset:
-            result = lax.dynamic_update_slice(result, shard[None], ((z + offset) % n_z, 0, 0))
-        return result.reshape(n_z * weight.shape[0], -1)
 
     a1, b1, here, w0, cot, early = barrier(
         (up(weight), down(weight), shift(piece, "yhi", 1), weight, cot, early)
@@ -45,24 +40,41 @@
     )
     a4 = jnp.concatenate((a4, b4), axis=0)
     last = (
-        (across(a4), far_z),
-        (up(oa2), (z + n_z - 3) % n_z),
-        (down(ob2), (z + 3) % n_z),
-    )
-    this_row = placed(
-        (
-            (0, w0),
-            (n_z - 1, a1),
-            (1, b1),
-            (n_z - 2, a2),
-            (2, b2),
-            (n_z - 3, a3),
-            (3, b3),
-            (n_z // 2, a4),
-        )
-    )
-    other_row = placed(((0, o0), (n_z - 1, oa1), (1, ob1), (n_z - 2, oa2), (2, ob2)))
-    return this_row, other_row, last, other_cot, partner, early
+        (across(a4), other + (z + n_z // 2) % n_z),
+        (up(oa2), other + (z + n_z - 3) % n_z),
+        (down(ob2), other + (z + 3) % n_z),
+    )
+    def placed(joined, shards):
+        for side, offset, shard in shards:
+            at = side + (z + offset) % n_z
+            joined = lax.dynamic_update_slice(joined, shard[None], (at, 0, 0))
+        return joined
+
+    joined = placed(
+        start.reshape(2 * n_z, weight.shape[0], -1),
+        (
+            (this, 0, w0),
+            (this, n_z - 1, a1),
+            (this, 1, b1),
+            (this, n_z - 2, a2),
+            (this, 2, b2),
+            (other, 0, o0),
+            (this, n_z - 3, a3),
+            (this, 3, b3),
+            (other, n_z - 2, oa2),
+        ),
+    )
+    joined, partner, early = barrier((joined, partner, early))
+    joined = placed(
+        joined,
+        (
+            (this, n_z // 2, a4),
+            (other, n_z - 1, oa1),
+            (other, 1, ob1),
+            (other, 2, ob2),
+        ),
+    )
+    return joined.reshape(start.shape), last, other_cot, partner, early
 
 
 def projected(pre, cotangent, gate_projection, up_projection):
@@ -124,39 +136,29 @@
         return joined.reshape(-1, cols)
 
     own_cot = cotangents(half_index)
+    piece, gate_weight, up_weight = lax.optimization_barrier((piece, gate_weight, up_weight))
     weight = jnp.concatenate((gate_weight, up_weight), axis=1)
-    this_row, other_row, last, other_cot, other, (own, own_cot) = gathered(
-        weight, piece, cotangents(1 - half_index), (own, own_cot)
+    wide = weight.shape[1]
+    start = jnp.pad(input_projection.T, ((0, 0), (wide, 0)))
+    joined, last, other_cot, other, (own, own_cot) = gathered(
+        weight, piece, cotangents(1 - half_index), (own, own_cot), start
     )
     gate_proj = columns(gate_projection, half_index)
     up_proj = columns(up_projection, half_index)
 
-    depth = this_row.shape[0]
-    shard_depth = weight.shape[0]
-    pres = []
-    factors = []
+    depth = weight.shape[0]
+    products = []
     chunks = []
     for rows in (own, other):
         flat = rows.reshape(-1, width)
-        this_flat = lax.dynamic_slice_in_dim(flat, row_index * depth, depth, 1)
-        other_flat = lax.dynamic_slice_in_dim(flat, (1 - row_index) * depth, depth, 1)
-        pre = jnp.dot(this_flat, this_row, preferred_element_type=F32)
-        pres.append(pre + jnp.dot(other_flat, other_row, preferred_element_type=F32))
-        factors.append(
-            lax.dot_general(
-                flat, input_projection, (((1,), (1,)), ((), ())), preferred_element_type=F32
-            )
-        )
-        chunks.append(
-            [
-                lax.dynamic_slice_in_dim(other_flat, place * shard_depth, shard_depth, 1)
-                for _, place in last
-            ]
-        )
+        products.append(jnp.dot(flat, joined, preferred_element_type=F32))
+        chunks.append([lax.dynamic_slice_in_dim(flat, at * depth, depth, 1) for _, at in last])
     shards = [shard for shard, _ in last]
-    pres, factors, chunks, shards = lax.optimization_barrier((pres, factors, chunks, shards))
+    products, chunks, shards = lax.optimization_barrier((products, chunks, shards))
     parts = []
-    for pre, pieces, rows_cot in zip(pres, chunks, (own_cot, other_cot)):
+    factors = [product[:, wide:] for product in products]
+    for product, pieces, rows_cot in zip(products, chunks, (own_cot, other_cot)):
+        pre = product[:, :wide]
         for chunk, shard in zip(pieces, shards):
             pre = pre + jnp.dot(chunk, shard, preferred_element_type=F32)
         parts.append(projected(pre, rows_cot, gate_proj, up_proj))

time: 180 us -> 196 us (1.089)
  local copies, waits for them, and re-layouts: 17.5 us -> 41.6 us
  waiting for transfers between devices: 51.1 us -> 39.2 us
  matrix products: 28 us -> 34.3 us
  starting transfers between devices: 46.4 us -> 44.3 us
    dynamic_update_slice x13, local copies, waits for them, and re-layouts: 7.8 us -> 19.8 us  [placed(): joined = lax.dynamic_update_slice(joined, shard[None], (at, 0, 0))]
    ppermute x18, waiting for transfers between devices: 33.5 us -> 22.5 us  [shift(): lax.ppermute(value, axis, [(i, (i + step) % size) for i in range(size)])]
    pad x0 -> x1, local copies, waits for them, and re-layouts: none -> 5.5 us  [body(): start = jnp.pad(input_projection.T, ((0, 0), (wide, 0)))]
    dot_general x6 -> x2, matrix products: 20.7 us -> 25.4 us  [body(): products.append(jnp.dot(flat, joined, preferred_element_type=F32))]
    dynamic_slice x2, local copies, waits for them, and re-layouts: 1.12 us -> 5.51 us  [body(): lax.dynamic_slice_in_dim(flat, at * depth, depth, 1)]
    dot_general x6, matrix products: 4.18 us -> 6.31 us  [body(): pre = pre + jnp.dot(chunk, shard, preferred_element_type=F32)]
  transfers between devices with their start and end apart: 21 -> 21, of which waited for: 11 -> 10; matrix products, arithmetic and copies ran while one was open for 23% -> 35% of each run, Pallas kernels for 0% -> 0%
where the time goes in v8:
time: 196 us; the launch traced here: 195 us
  starting transfers between devices  44.3 us (23%)
  local copies, waits for them, and re-layouts  41.6 us (21%)
  waiting for transfers between devices  39.2 us (20%)
  matrix products  34.3 us (17%)
  between operations  14.5 us (7%)
  blocking collectives  12.1 us (6%)
  other arithmetic  9.44 us (5%)
    ppermute x18, starting transfers between devices, shift(): lax.ppermute(value, axis, [(i, (i + step) % size) for i in range(size)])  29 us
    dot_general x2, matrix products, body(): products.append(jnp.dot(flat, joined, preferred_element_type=F32))  25.4 us
    ppermute x18, waiting for transfers between devices, shift(): lax.ppermute(value, axis, [(i, (i + step) % size) for i in range(size)])  22.5 us
    dynamic_update_slice x13, local copies, waits for them, and re-layouts, placed(): joined = lax.dynamic_update_slice(joined, shard[None], (at, 0, 0))  19.8 us
    all_to_all x1, blocking collectives, body(): received = lax.all_to_all(payload, dq, 0, 0, tiled=True)  12.1 us
    all_to_all x1, starting transfers between devices, body(): swapped = lax.all_to_all(part, dq, 0, 0, tiled=True)  10.6 us
    all_to_all x1, waiting for transfers between devices, body(): lax.all_to_all(jnp.broadcast_to(queries[None], (n_fsdp,) + queries.shape)...  8.5 us
    all_to_all x1, waiting for transfers between devices, body(): swapped = lax.all_to_all(part, dq, 0, 0, tiled=True)  8.15 us
  transfers between devices with their start and end apart: 21, of which 10 were waited for; matrix products, arithmetic and copies ran while one was open for 35% of the time, Pallas kernels for 0%

profile of v8, /device:TPU:1, one launch (start us, length us, event | category | flops | bytes accessed | tf_op | source)
XLA Modules:
  0.0 195.5 jit_solution(7291236587268328850)
XLA Ops:
  6.5 1.3 constant_dynamic-slice_fusion.10
  8.7 1.3 pad_maximum_fusion.2
  10.0 2.5 %collective-permute-start = (bf16[320,896]{1,0:T(8,128)(2,1)S(1)}, bf16[320,896]{1,0:T(8,128)(2,1)}, u32[]{:S(2)}, u32[]{:S(2)}) collective-permute-start(bf16[320,896]{1,0:T(8,128)(2,1)S(1)} %pad_maximum_fusion.2), channel_id=1, source_target_pairs={{0,16},{16,32},{32,48},{48,64},{64,80},{80,96},{96,112},{112,0},{1... | collective-permute-start | bytes 1720328 | tf_op jit(solution)/shard_map/ppermute | solution.py:11
  12.5 4.0 %collective-permute-start.1 = (bf16[320,896]{1,0:T(8,128)(2,1)S(1)}, bf16[320,896]{1,0:T(8,128)(2,1)}, u32[]{:S(2)}, u32[]{:S(2)}) collective-permute-start(bf16[320,896]{1,0:T(8,128)(2,1)S(1)} %pad_maximum_fusion.2), channel_id=1, source_target_pairs={{0,112},{16,0},{32,16},{48,32},{64,48},{80,64},{96,80},{112,96},{1... | collective-permute-start | bytes 1720328 | tf_op jit(solution)/shard_map/ppermute | solution.py:11
  16.5 2.9 %collective-permute-start.2 = (bf16[1,64,5120]{2,1,0:T(8,128)(2,1)}, bf16[1,64,5120]{2,1,0:T(8,128)(2,1)}, u32[]{:S(2)}, u32[]{:S(2)}) collective-permute-start(bf16[1,64,5120]{2,1,0:T(8,128)(2,1)} %pad_maximum_fusion.1), channel_id=1, source_target_pairs={{0,1},{1,0},{2,3},{3,2},{4,5},{5,4},{6,7},{7,6},{8,9},{9,8},{10,11... | collective-permute-start | bytes 1966088 | tf_op jit(solution)/shard_map/ppermute | solution.py:11
  19.5 1.8 constant_dynamic-slice_fusion.6
  21.3 0.9 pad_maximum_fusion.3
  23.1 2.8 %pad_maximum_fusion = bf16[8,64,5120]{2,1,0:T(8,128)(2,1)} fusion(bf16[8,32,5120]{2,1,0:T(8,128)(2,1)S(1)} %copy-done.2, bf16[8,32,5120]{2,1,0:T(8,128)(2,1)S(1)} %copy-done.3), kind=kLoop, calls=%fused_computation | loop fusion | flops 10485760 | bytes 10485760 | tf_op jit(solution)/shard_map/concatenate | solution.py:127
  25.9 3.4 %collective-permute-done = bf16[320,896]{1,0:T(8,128)(2,1)} collective-permute-done((bf16[320,896]{1,0:T(8,128)(2,1)S(1)}, bf16[320,896]{1,0:T(8,128)(2,1)}, u32[]{:S(2)}, u32[]{:S(2)}) %collective-permute-start) | collective-permute-done | bytes 573472 | tf_op jit(solution)/shard_map/ppermute | solution.py:11
  29.3 4.4 %collective-permute-done.2 = bf16[1,64,5120]{2,1,0:T(8,128)(2,1)} collective-permute-done((bf16[1,64,5120]{2,1,0:T(8,128)(2,1)}, bf16[1,64,5120]{2,1,0:T(8,128)(2,1)}, u32[]{:S(2)}, u32[]{:S(2)}) %collective-permute-start.2) | collective-permute-done | bytes 655392 | tf_op jit(solution)/shard_map/ppermute | solution.py:11
  33.8 2.7 %collective-permute-start.4 = (bf16[320,896]{1,0:T(8,128)(2,1)}, bf16[320,896]{1,0:T(8,128)(2,1)S(1)}, u32[]{:S(2)}, u32[]{:S(2)}) collective-permute-start(bf16[320,896]{1,0:T(8,128)(2,1)} %collective-permute-done.1), channel_id=1, source_target_pairs={{0,112},{16,0},{32,16},{48,32},{64,48},{80,64},{96,80},{112,96},{1... | collective-permute-start | bytes 1720328 | tf_op jit(solution)/shard_map/ppermute | solution.py:11
  36.4 1.3 collective-permute-start.5
  37.7 1.7 copy.48
  39.4 5.5 %pad.4 = bf16[5120,960]{1,0:T(8,128)(2,1)} pad(bf16[5120,64]{1,0:T(8,128)(2,1)S(1)} %bitcast.77, bf16[]{:T(256)} %constant.102.clone.1), padding=0_0x896_0 | pad | bytes 10485762 | tf_op jit(solution)/shard_map/jit(_pad)/pad | solution.py:142
  45.8 2.1 %collective-permute-done.3 = bf16[320,896]{1,0:T(8,128)(2,1)} collective-permute-done((bf16[320,896]{1,0:T(8,128)(2,1)}, bf16[320,896]{1,0:T(8,128)(2,1)}, u32[]{:S(2)}, u32[]{:S(2)}) %collective-permute-start.3) | collective-permute-done | bytes 573472 | tf_op jit(solution)/shard_map/ppermute | solution.py:11
  48.6 1.3 collective-permute-start.8
  49.9 2.7 %collective-permute-start.7 = (bf16[320,896]{1,0:T(8,128)(2,1)S(1)}, bf16[320,896]{1,0:T(8,128)(2,1)S(1)}, u32[]{:S(2)}, u32[]{:S(2)}) collective-permute-start(bf16[320,896]{1,0:T(8,128)(2,1)S(1)} %collective-permute-done.4), channel_id=1, source_target_pairs={{0,112},{16,0},{32,16},{48,32},{64,48},{80,64},{96,80},{112,96},{1... | collective-permute-start | bytes 1720328 | tf_op jit(solution)/shard_map/ppermute | solution.py:11
  52.5 1.9 bitcast_dynamic-update-slice_fusion.11
  54.5 1.9 bitcast_dynamic-update-slice_fusion.10
  56.4 1.0 copy.49
  57.4 2.6 %collective-permute-start.14 = (bf16[512,448]{0,1:T(8,128)(2,1)}, bf16[512,448]{0,1:T(8,128)(2,1)S(1)}, u32[]{:S(2)}, u32[]{:S(2)}) collective-permute-start(bf16[512,448]{0,1:T(8,128)(2,1)} %copy.49), channel_id=1, source_target_pairs={{0,1},{1,0},{2,3},{3,2},{4,5},{5,4},{6,7},{7,6},{8,9},{9,8},{10,11... | collective-permute-start | bytes 1376264 | tf_op jit(solution)/shard_map/ppermute | solution.py:11
  60.0 1.9 bitcast_dynamic-update-slice_fusion.9
  62.0 2.5 %collective-permute-start.10 = (bf16[320,896]{1,0:T(8,128)(2,1)}, bf16[320,896]{1,0:T(8,128)(2,1)S(1)}, u32[]{:S(2)}, u32[]{:S(2)}) collective-permute-start(bf16[320,896]{1,0:T(8,128)(2,1)} %collective-permute-done.5), channel_id=1, source_target_pairs={{0,112},{16,0},{32,16},{48,32},{64,48},{80,64},{96,80},{112,96},{1... | collective-permute-start | bytes 1720328 | tf_op jit(solution)/shard_map/ppermute | solution.py:11
  65.6 2.0 bitcast_dynamic-update-slice_fusion.7
  67.6 4.6 %collective-permute-done.14 = bf16[512,448]{0,1:T(8,128)(2,1)S(1)} collective-permute-done((bf16[512,448]{0,1:T(8,128)(2,1)}, bf16[512,448]{0,1:T(8,128)(2,1)S(1)}, u32[]{:S(2)}, u32[]{:S(2)}) %collective-permute-start.14) | collective-permute-done | bytes 458784 | tf_op jit(solution)/shard_map/ppermute | solution.py:11
  72.2 2.4 %collective-permute-start.13 = (bf16[160,896]{1,0:T(8,128)(2,1)S(1)}, bf16[160,896]{1,0:T(8,128)(2,1)S(1)}, u32[]{:S(2)}, u32[]{:S(2)}) collective-permute-start(bf16[160,896]{1,0:T(8,128)(2,1)S(1)} %slice.47), channel_id=1, source_target_pairs={{0,112},{16,0},{32,16},{48,32},{64,48},{80,64},{96,80},{112,96},{1... | collective-permute-start | bytes 860168 | tf_op jit(solution)/shard_map/ppermute | solution.py:11
  76.3 3.2 %collective-permute-done.12 = bf16[160,896]{1,0:T(8,128)(2,1)S(1)} collective-permute-done((bf16[160,896]{1,0:T(8,128)(2,1)S(1)}, bf16[160,896]{1,0:T(8,128)(2,1)S(1)}, u32[]{:S(2)}, u32[]{:S(2)}) %collective-permute-start.12) | collective-permute-done | bytes 286752 | tf_op jit(solution)/shard_map/ppermute | solution.py:11
  79.5 1.8 collective-permute-done.13
  81.3 2.3 %collective-permute-done.11 = bf16[320,896]{1,0:T(8,128)(2,1)} collective-permute-done((bf16[320,896]{1,0:T(8,128)(2,1)S(1)}, bf16[320,896]{1,0:T(8,128)(2,1)}, u32[]{:S(2)}, u32[]{:S(2)}) %collective-permute-start.11) | collective-permute-done | bytes 573472 | tf_op jit(solution)/shard_map/ppermute | solution.py:11
  85.4 1.1 collective-permute-start.15
  86.4 2.7 %collective-permute-start.17 = (bf16[320,896]{1,0:T(8,128)(2,1)}, bf16[320,896]{1,0:T(8,128)(2,1)S(1)}, u32[]{:S(2)}, u32[]{:S(2)}) collective-permute-start(bf16[320,896]{1,0:T(8,128)(2,1)} %collective-permute-done.11), channel_id=1, source_target_pairs={{0,112},{16,0},{32,16},{48,32},{64,48},{80,64},{96,80},{112,96},{1... | collective-permute-start | bytes 1720328 | tf_op jit(solution)/shard_map/ppermute | solution.py:11
  89.1 1.9 bitcast_dynamic-update-slice_fusion.4
  91.0 1.9 bitcast_dynamic-update-slice_fusion.3
  93.0 2.0 %bitcast_dynamic-update-slice_fusion.2 = bf16[16,320,960]{2,1,0:T(8,128)(2,1)} fusion(bf16[16,320,960]{2,1,0:T(8,128)(2,1)} %bitcast_dynamic-update-slice_fusion.3, s32[]{:T(128)S(6)} %select_n.170, bf16[320,896]{1,0:T(8,128)(2,1)} %copy-done.10), kind=kLoop, calls=%fused_computation.24 | loop fusion | bytes 1146884 | tf_op jit(solution)/shard_map/dynamic_update_slice | solution.py:50
  95.8 1.9 bitcast_dynamic-update-slice_fusion
  97.7 14.5 %fusion.38 = f32[512,960]{0,1:T(8,128)} fusion(bf16[512,5120]{1,0:T(8,128)(2,1)} %bitcast.82, bf16[5120,960]{1,0:T(8,128)(2,1)} %bitcast.73), kind=kOutput, calls=%fused_computation.89 | convolution fusion | flops 5033164800 | bytes 17039360 | tf_op jit(solution)/shard_map/dot_general | solution.py:154
  112.2 11.0 %fusion.37 = f32[512,960]{0,1:T(8,128)} fusion(bf16[512,5120]{1,0:T(8,128)(2,1)} %bitcast.75, bf16[5120,960]{1,0:T(8,128)(2,1)S(1)} %bitcast.74), kind=kOutput, calls=%fused_computation.88 | convolution fusion | flops 5033164800 | bytes 17039360 | tf_op jit(solution)/shard_map/dot_general | solution.py:154
  123.2 2.8 %constant_dynamic-slice_fusion = (bf16[512,320]{1,0:T(8,128)(2,1)S(1)}, bf16[512,320]{1,0:T(8,128)(2,1)}, bf16[512,320]{1,0:T(8,128)(2,1)}) fusion(bf16[512,5120]{1,0:T(8,128)(2,1)} %bitcast.83, s32[]{:T(128)S(6)} %select_n.175, s32[]{:T(128)S(6)} %select_n.174, s32[]{:T(128)S(6)} %select_n.173), kind=kLoop, calls=%fused_computation.68 | loop fusion | bytes 1966092 | tf_op jit(solution)/shard_map/dynamic_slice | solution.py:155
  125.9 2.8 %constant_dynamic-slice_fusion.3 = (bf16[512,320]{1,0:T(8,128)(2,1)S(1)}, bf16[512,320]{1,0:T(8,128)(2,1)}, bf16[512,320]{1,0:T(8,128)(2,1)}) fusion(bf16[512,5120]{1,0:T(8,128)(2,1)} %bitcast.76, s32[]{:T(128)S(6)} %select_n.175, s32[]{:T(128)S(6)} %select_n.174, s32[]{:T(128)S(6)} %select_n.173), kind=kLoop, calls=%fused_computation.71 | loop fusion | bytes 1966092 | tf_op jit(solution)/shard_map/dynamic_slice | solution.py:155
  128.7 1.0 copy.50
  129.7 1.8 fusion.39
  131.5 1.7 fusion.40
  138.9 10.6 %all-to-all-start = ((bf16[16,8,1024]{2,1,0:T(8,128)(2,1)}), bf16[16,8,1024]{2,1,0:T(8,128)(2,1)S(1)}, u32[]{:S(2)}, u32[]{:S(2)}) async-start(bf16[16,8,1024]{2,1,0:T(8,128)(2,1)} %pad_maximum_fusion.7), calls=%async_computation | async-start | bytes 524288 | tf_op jit(solution)/shard_map/all_to_all | solution.py:177
  149.4 1.0 slice_select_fusion.1
  150.7 8.2 %all-to-all-done = bf16[16,8,1024]{2,1,0:T(8,128)(2,1)S(1)} async-done(((bf16[16,8,1024]{2,1,0:T(8,128)(2,1)}), bf16[16,8,1024]{2,1,0:T(8,128)(2,1)S(1)}, u32[]{:S(2)}, u32[]{:S(2)}) %all-to-all-start) | async-done | bytes 262176 | tf_op jit(solution)/shard_map/all_to_all | solution.py:177
  160.4 4.7 %all-to-all-start.1 = ((bf16[16,16,512]{2,1,0:T(8,128)(2,1)}), bf16[16,16,512]{2,1,0:T(8,128)(2,1)S(1)}, u32[]{:S(2)}, u32[]{:S(2)}) async-start(bf16[16,16,512]{2,1,0:T(8,128)(2,1)} %broadcast_in_dim.73), calls=%async_computation.1 | async-start | bytes 524288 | tf_op jit(solution)/shard_map/all_to_all | solution.py:193
  165.6 8.5 %all-to-all-done.1 = bf16[16,16,512]{2,1,0:T(8,128)(2,1)S(1)} async-done(((bf16[16,16,512]{2,1,0:T(8,128)(2,1)}), bf16[16,16,512]{2,1,0:T(8,128)(2,1)S(1)}, u32[]{:S(2)}, u32[]{:S(2)}) %all-to-all-start.1) | async-done | bytes 262176 | tf_op jit(solution)/shard_map/all_to_all | solution.py:193
  174.7 12.1 %all_to_all.19 = f32[16,1,640]{2,1,0:T(1,128)S(1)} all-to-all(f32[16,1,640]{2,1,0:T(1,128)S(1)} %copy.63), channel_id=1, replica_groups=mesh['ylo'=2,'z'=8,'x'=4,'core'=2,'yhi'=2] {'x','core','yhi'}, dimensions={0} | all-to-all | bytes 81920 | tf_op jit(solution)/shard_map/all_to_all | solution.py:214
  (97 shorter events, 18.4 us)
Async XLA Ops:
  6.5 127.5 %copy-start = (bf16[64,896]{1,0:T(8,128)(2,1)S(1)}, bf16[64,896]{1,0:T(8,128)(2,1)}, u32[]{:S(2)}) copy-start(bf16[64,896]{1,0:T(8,128)(2,1)} %param.16) | copy-start | bytes 344068
  6.5 16.6 %copy-start.2 = (bf16[8,32,5120]{2,1,0:T(8,128)(2,1)S(1)}, bf16[8,32,5120]{2,1,0:T(8,128)(2,1)}, u32[]{:S(2)}) copy-start(bf16[8,32,5120]{2,1,0:T(8,128)(2,1)} %param.11) | copy-start | bytes 7864324
  6.5 84.5 %all-gather.2.cloned.1.call-start = ((), (), s32[]{:S(2)}) async-start(), calls=%async_computation.3 | async-start | bytes 5898240 | tf_op jit(solution)/shard_map/all_gather | solution.py:34
  10.0 19.3 %collective-permute-start = (bf16[320,896]{1,0:T(8,128)(2,1)S(1)}, bf16[320,896]{1,0:T(8,128)(2,1)}, u32[]{:S(2)}, u32[]{:S(2)}) collective-permute-start(bf16[320,896]{1,0:T(8,128)(2,1)S(1)} %pad_maximum_fusion.2), channel_id=1, source_target_pairs={{0,16},{16,32},{32,48},{48,64},{64,80},{80,96},{96,112},{112,0},{1... | collective-permute-start | bytes 1720328 | tf_op jit(solution)/shard_map/ppermute | solution.py:11
  12.5 16.8 %collective-permute-start.1 = (bf16[320,896]{1,0:T(8,128)(2,1)S(1)}, bf16[320,896]{1,0:T(8,128)(2,1)}, u32[]{:S(2)}, u32[]{:S(2)}) collective-permute-start(bf16[320,896]{1,0:T(8,128)(2,1)S(1)} %pad_maximum_fusion.2), channel_id=1, source_target_pairs={{0,112},{16,0},{32,16},{48,32},{64,48},{80,64},{96,80},{112,96},{1... | collective-permute-start | bytes 1720328 | tf_op jit(solution)/shard_map/ppermute | solution.py:11
  16.5 17.1 %collective-permute-start.2 = (bf16[1,64,5120]{2,1,0:T(8,128)(2,1)}, bf16[1,64,5120]{2,1,0:T(8,128)(2,1)}, u32[]{:S(2)}, u32[]{:S(2)}) collective-permute-start(bf16[1,64,5120]{2,1,0:T(8,128)(2,1)} %pad_maximum_fusion.1), channel_id=1, source_target_pairs={{0,1},{1,0},{2,3},{3,2},{4,5},{5,4},{6,7},{7,6},{8,9},{9,8},{10,11... | collective-permute-start | bytes 1966088 | tf_op jit(solution)/shard_map/ppermute | solution.py:11
  19.5 3.7 %copy-start.3 = (bf16[8,32,5120]{2,1,0:T(8,128)(2,1)S(1)}, bf16[8,32,5120]{2,1,0:T(8,128)(2,1)}, u32[]{:S(2)}) copy-start(bf16[8,32,5120]{2,1,0:T(8,128)(2,1)} %param.9) | copy-start | bytes 7864324
  33.7 14.2 %collective-permute-start.3 = (bf16[320,896]{1,0:T(8,128)(2,1)}, bf16[320,896]{1,0:T(8,128)(2,1)}, u32[]{:S(2)}, u32[]{:S(2)}) collective-permute-start(bf16[320,896]{1,0:T(8,128)(2,1)} %collective-permute-done), channel_id=1, source_target_pairs={{0,16},{16,32},{32,48},{48,64},{64,80},{80,96},{96,112},{112,0},{1... | collective-permute-start | bytes 1720328 | tf_op jit(solution)/shard_map/ppermute | solution.py:11
  33.8 14.1 %collective-permute-start.4 = (bf16[320,896]{1,0:T(8,128)(2,1)}, bf16[320,896]{1,0:T(8,128)(2,1)S(1)}, u32[]{:S(2)}, u32[]{:S(2)}) collective-permute-start(bf16[320,896]{1,0:T(8,128)(2,1)} %collective-permute-done.1), channel_id=1, source_target_pairs={{0,112},{16,0},{32,16},{48,32},{64,48},{80,64},{96,80},{112,96},{1... | collective-permute-start | bytes 1720328 | tf_op jit(solution)/shard_map/ppermute | solution.py:11
  36.4 12.2 %collective-permute-start.5 = (bf16[320,896]{1,0:T(8,128)(2,1)S(1)}, bf16[320,896]{1,0:T(8,128)(2,1)}, u32[]{:S(2)}, u32[]{:S(2)}) collective-permute-start(bf16[320,896]{1,0:T(8,128)(2,1)S(1)} %pad_maximum_fusion.2), channel_id=1, source_target_pairs={{0,128},{128,0},{1,129},{129,1},{2,130},{130,2},{3,131},{131,3},{4... | collective-permute-start | bytes 1720328 | tf_op jit(solution)/shard_map/ppermute | solution.py:11
  39.4 17.0 %copy-start.5 = (bf16[8,64,448]{2,1,0:T(8,128)(2,1)S(1)}, bf16[8,64,448]{2,1,0:T(8,128)(2,1)}, u32[]{:S(2)}) copy-start(bf16[8,64,448]{2,1,0:T(8,128)(2,1)} %pad_maximum_fusion.3) | copy-start | bytes 1376260
  48.6 13.4 %collective-permute-start.6 = (bf16[320,896]{1,0:T(8,128)(2,1)}, bf16[320,896]{1,0:T(8,128)(2,1)S(1)}, u32[]{:S(2)}, u32[]{:S(2)}) collective-permute-start(bf16[320,896]{1,0:T(8,128)(2,1)} %collective-permute-done.3), channel_id=1, source_target_pairs={{0,16},{16,32},{32,48},{48,64},{64,80},{80,96},{96,112},{112,0},{1... | collective-permute-start | bytes 1720328 | tf_op jit(solution)/shard_map/ppermute | solution.py:11
  48.6 13.4 %collective-permute-start.8 = (bf16[320,896]{1,0:T(8,128)(2,1)}, bf16[320,896]{1,0:T(8,128)(2,1)}, u32[]{:S(2)}, u32[]{:S(2)}) collective-permute-start(bf16[320,896]{1,0:T(8,128)(2,1)} %collective-permute-done.3), channel_id=1, source_target_pairs={{0,128},{128,0},{1,129},{129,1},{2,130},{130,2},{3,131},{131,3},{4... | collective-permute-start | bytes 1720328 | tf_op jit(solution)/shard_map/ppermute | solution.py:11
  49.9 12.1 %collective-permute-start.7 = (bf16[320,896]{1,0:T(8,128)(2,1)S(1)}, bf16[320,896]{1,0:T(8,128)(2,1)S(1)}, u32[]{:S(2)}, u32[]{:S(2)}) collective-permute-start(bf16[320,896]{1,0:T(8,128)(2,1)S(1)} %collective-permute-done.4), channel_id=1, source_target_pairs={{0,112},{16,0},{32,16},{48,32},{64,48},{80,64},{96,80},{112,96},{1... | collective-permute-start | bytes 1720328 | tf_op jit(solution)/shard_map/ppermute | solution.py:11
  57.4 14.8 %collective-permute-start.14 = (bf16[512,448]{0,1:T(8,128)(2,1)}, bf16[512,448]{0,1:T(8,128)(2,1)S(1)}, u32[]{:S(2)}, u32[]{:S(2)}) collective-permute-start(bf16[512,448]{0,1:T(8,128)(2,1)} %copy.49), channel_id=1, source_target_pairs={{0,1},{1,0},{2,3},{3,2},{4,5},{5,4},{6,7},{7,6},{8,9},{9,8},{10,11... | collective-permute-start | bytes 1376264 | tf_op jit(solution)/shard_map/ppermute | solution.py:11
  62.0 19.3 %collective-permute-start.10 = (bf16[320,896]{1,0:T(8,128)(2,1)}, bf16[320,896]{1,0:T(8,128)(2,1)S(1)}, u32[]{:S(2)}, u32[]{:S(2)}) collective-permute-start(bf16[320,896]{1,0:T(8,128)(2,1)} %collective-permute-done.5), channel_id=1, source_target_pairs={{0,112},{16,0},{32,16},{48,32},{64,48},{80,64},{96,80},{112,96},{1... | collective-permute-start | bytes 1720328 | tf_op jit(solution)/shard_map/ppermute | solution.py:11
  64.4 19.2 %collective-permute-start.9 = (bf16[320,896]{1,0:T(8,128)(2,1)}, bf16[320,896]{1,0:T(8,128)(2,1)S(1)}, u32[]{:S(2)}, u32[]{:S(2)}) collective-permute-start(bf16[320,896]{1,0:T(8,128)(2,1)} %collective-permute-done.5), channel_id=1, source_target_pairs={{0,16},{16,32},{32,48},{48,64},{64,80},{80,96},{96,112},{112,0},{1... | collective-permute-start | bytes 1720328 | tf_op jit(solution)/shard_map/ppermute | solution.py:11
  64.4 19.2 %collective-permute-start.11 = (bf16[320,896]{1,0:T(8,128)(2,1)S(1)}, bf16[320,896]{1,0:T(8,128)(2,1)}, u32[]{:S(2)}, u32[]{:S(2)}) collective-permute-start(bf16[320,896]{1,0:T(8,128)(2,1)S(1)} %collective-permute-done.4), channel_id=1, source_target_pairs={{0,128},{128,0},{1,129},{129,1},{2,130},{130,2},{3,131},{131,3},{4... | collective-permute-start | bytes 1720328 | tf_op jit(solution)/shard_map/ppermute | solution.py:11
  64.6 14.9 %collective-permute-start.12 = (bf16[160,896]{1,0:T(8,128)(2,1)S(1)}, bf16[160,896]{1,0:T(8,128)(2,1)S(1)}, u32[]{:S(2)}, u32[]{:S(2)}) collective-permute-start(bf16[160,896]{1,0:T(8,128)(2,1)S(1)} %slice.46), channel_id=1, source_target_pairs={{0,16},{16,32},{32,48},{48,64},{64,80},{80,96},{96,112},{112,0},{1... | collective-permute-start | bytes 860168 | tf_op jit(solution)/shard_map/ppermute | solution.py:11
  72.2 14.2 %copy-start.12 = (bf16[512,448]{0,1:T(8,128)(2,1)}, bf16[512,448]{0,1:T(8,128)(2,1)S(1)}, u32[]{:S(2)}) copy-start(bf16[512,448]{0,1:T(8,128)(2,1)S(1)} %collective-permute-done.14) | copy-start | bytes 1376260
  72.2 9.1 %collective-permute-start.13 = (bf16[160,896]{1,0:T(8,128)(2,1)S(1)}, bf16[160,896]{1,0:T(8,128)(2,1)S(1)}, u32[]{:S(2)}, u32[]{:S(2)}) collective-permute-start(bf16[160,896]{1,0:T(8,128)(2,1)S(1)} %slice.47), channel_id=1, source_target_pairs={{0,112},{16,0},{32,16},{48,32},{64,48},{80,64},{96,80},{112,96},{1... | collective-permute-start | bytes 860168 | tf_op jit(solution)/shard_map/ppermute | solution.py:11
  83.7 0.9 copy-start.10
  85.4 43.3 %collective-permute-start.15 = (bf16[320,896]{1,0:T(8,128)(2,1)}, bf16[320,896]{1,0:T(8,128)(2,1)S(1)}, u32[]{:S(2)}, u32[]{:S(2)}) collective-permute-start(bf16[320,896]{1,0:T(8,128)(2,1)} %constant_dynamic-update-slice_fusion), channel_id=1, source_target_pairs={{0,128},{128,0},{1,129},{129,1},{2,130},{130,2},{3,131},{131,3},{4... | collective-permute-start | bytes 1720328 | tf_op jit(solution)/shard_map/ppermute | solution.py:11
  86.4 42.3 %collective-permute-start.16 = (bf16[320,896]{1,0:T(8,128)(2,1)}, bf16[320,896]{1,0:T(8,128)(2,1)S(1)}, u32[]{:S(2)}, u32[]{:S(2)}) collective-permute-start(bf16[320,896]{1,0:T(8,128)(2,1)} %collective-permute-done.8), channel_id=1, source_target_pairs={{0,16},{16,32},{32,48},{48,64},{64,80},{80,96},{96,112},{112,0},{1... | collective-permute-start | bytes 1720328 | tf_op jit(solution)/shard_map/ppermute | solution.py:11
  86.4 42.3 %collective-permute-start.17 = (bf16[320,896]{1,0:T(8,128)(2,1)}, bf16[320,896]{1,0:T(8,128)(2,1)S(1)}, u32[]{:S(2)}, u32[]{:S(2)}) collective-permute-start(bf16[320,896]{1,0:T(8,128)(2,1)} %collective-permute-done.11), channel_id=1, source_target_pairs={{0,112},{16,0},{32,16},{48,32},{64,48},{80,64},{96,80},{112,96},{1... | collective-permute-start | bytes 1720328 | tf_op jit(solution)/shard_map/ppermute | solution.py:11
  97.7 14.5 %copy-start.1 = (bf16[16,320,960]{2,1,0:T(8,128)(2,1)S(1)}, bf16[16,320,960]{2,1,0:T(8,128)(2,1)}, u32[]{:S(2)}) copy-start(bf16[16,320,960]{2,1,0:T(8,128)(2,1)} %bitcast_dynamic-update-slice_fusion) | copy-start | bytes 29491204
  112.2 16.5 %copy-start.4 = (bf16[8,64,448]{2,1,0:T(8,128)(2,1)S(1)}, bf16[8,64,448]{2,1,0:T(8,128)(2,1)}, u32[]{:S(2)}) copy-start(bf16[8,64,448]{2,1,0:T(8,128)(2,1)} %pad_maximum_fusion.4) | copy-start | bytes 1376260
  129.7 3.6 %copy-start.7 = (f32[512,960]{0,1:T(8,128)S(1)}, f32[512,960]{0,1:T(8,128)}, u32[]{:S(2)}) copy-start(f32[512,960]{0,1:T(8,128)} %fusion.37) | copy-start | bytes 5898244
  131.5 2.5 %copy-start.11 = (bf16[512,448]{0,1:T(8,128)(2,1)S(1)}, bf16[512,448]{0,1:T(8,128)(2,1)}, u32[]{:S(2)}) copy-start(bf16[512,448]{0,1:T(8,128)(2,1)} %copy.50) | copy-start | bytes 1376260
  133.3 1.3 copy-start.14
  134.0 1.0 copy-start.9
  134.0 1.7 copy-start.8
  134.5 1.9 copy-start.6
  135.7 1.4 copy-start.13
  138.9 19.9 %all-to-all-start = ((bf16[16,8,1024]{2,1,0:T(8,128)(2,1)}), bf16[16,8,1024]{2,1,0:T(8,128)(2,1)S(1)}, u32[]{:S(2)}, u32[]{:S(2)}) async-start(bf16[16,8,1024]{2,1,0:T(8,128)(2,1)} %pad_maximum_fusion.7), calls=%async_computation | async-start | bytes 524288 | tf_op jit(solution)/shard_map/all_to_all | solution.py:177
  160.4 13.7 %all-to-all-start.1 = ((bf16[16,16,512]{2,1,0:T(8,128)(2,1)}), bf16[16,16,512]{2,1,0:T(8,128)(2,1)S(1)}, u32[]{:S(2)}, u32[]{:S(2)}) async-start(bf16[16,16,512]{2,1,0:T(8,128)(2,1)} %broadcast_in_dim.73), calls=%async_computation.1 | async-start | bytes 524288 | tf_op jit(solution)/shard_map/all_to_all | solution.py:193
Sparse Core Ops, SparseCore 0:
  33.8 40.6 all-gather.1

commit v9 on v6

--- a/solution.py
+++ b/solution.py
@@ -27,24 +27,30 @@
     def across(value):
         return shift(value, "ylo", 1)
 
-    def placed(by_offset):
-        result = jnp.zeros((n_z,) + weight.shape, weight.dtype)
-        for offset, shard in by_offset:
-            result = lax.dynamic_update_slice(result, shard[None], ((z + offset) % n_z, 0, 0))
-        return result.reshape(n_z * weight.shape[0], -1)
-
-    a1, b1, here, w0, cot, early = barrier(
-        (up(weight), down(weight), shift(piece, "yhi", 1), weight, cot, early)
+    def placed(joined, *shards):
+        for offset, shard in shards:
+            at = (z + offset) % n_z
+            joined = lax.dynamic_update_slice(joined, shard[None], (at, 0, 0))
+        return joined
+
+    a1, b1, o0, w0, cot, piece, early = barrier(
+        (up(weight), down(weight), across(weight), weight, cot, piece, early)
+    )
+    empty = jnp.zeros((n_z,) + weight.shape, weight.dtype)
+    this_row = placed(empty, (0, w0), (n_z - 1, a1), (1, b1))
+    other_row = placed(empty, (0, o0))
+    a2, b2, here, cot, this_row, other_row = barrier(
+        (up(a1), down(b1), shift(piece, "yhi", 1), cot, this_row, other_row)
     )
     partner = lax.all_gather(here, ("x", "core"), axis=0, tiled=True)
-    a2, b2, o0, cot = barrier((up(a1), down(b1), across(w0), cot))
-    a3, b3, oa2, o0, b2 = barrier((up(a2), down(b2), across(a2), o0, b2))
     other_cot = shift(cot, "yhi", 1)
-    this_row = placed(
-        ((0, w0), (n_z - 1, a1), (1, b1), (n_z - 2, a2), (2, b2), (n_z - 3, a3), (3, b3))
-    )
+    this_row = placed(this_row, (n_z - 2, a2), (2, b2))
+    a3, b3, oa2, b2, o0, this_row = barrier((up(a2), down(b2), across(a2), b2, o0, this_row))
+    this_row = placed(this_row, (n_z - 3, a3), (3, b3))
+    this_row = this_row.reshape(n_z * weight.shape[0], -1)
     own_sum = this_product(early[0], this_row)
-    oa1, ob1, ob2, a4, b4, oa2, other_cot, own_sum = barrier(
+    other_row = placed(other_row, (n_z - 2, oa2))
+    oa1, ob1, ob2, a4, b4, oa2, other_cot, own_sum, other_row = barrier(
         (
             up(o0),
             down(o0),
@@ -54,6 +60,7 @@
             oa2,
             other_cot,
             own_sum,
+            other_row,
         )
     )
     a4 = jnp.concatenate((a4, b4), axis=0)
@@ -62,9 +69,10 @@
         (up(oa2), (z + n_z - 3) % n_z),
         (down(ob2), (z + 3) % n_z),
     )
-    other_row = placed(((0, o0), (n_z - 1, oa1), (1, ob1), (n_z - 2, oa2), (2, ob2)))
-    sums = (own_sum, this_product(partner, this_row))
-    return sums, (a4, far_z), other_row, last, other_cot, partner, early
+    other_row = placed(other_row, (n_z - 1, oa1), (1, ob1), (2, ob2))
+    other_row = other_row.reshape(this_row.shape)
+    own_sum, other_row, partner = barrier((own_sum, other_row, partner))
+    return this_row, own_sum, (a4, far_z), other_row, last, other_cot, partner, early
 
 
 def projected(pre, cotangent, gate_projection, up_projection):
@@ -135,7 +143,7 @@
         flat = half_of(rows, row_index, this_row.shape[0])
         return jnp.dot(flat, this_row, preferred_element_type=F32)
 
-    sums, far, other_row, last, other_cot, other, (own, own_cot) = gathered(
+    this_row, own_sum, far, other_row, last, other_cot, other, (own, own_cot) = gathered(
         weight, piece, cotangents(1 - half_index), (own, own_cot), this_product
     )
     gate_proj = columns(gate_projection, half_index)
@@ -151,26 +159,33 @@
 
     depth = other_row.shape[0]
     shard_depth = weight.shape[0]
-    pres = []
-    chunks = []
-    for rows, pre in zip((own, other), sums):
-        flat = rows.reshape(-1, width)
-
-        def chunk(side, place):
-            return lax.dynamic_slice_in_dim(
-                flat, side * depth + place * shard_depth, shard_depth, 1
-            )
-
-        other_flat = half_of(rows, 1 - row_index, depth)
-        pre = pre + jnp.dot(other_flat, other_row, preferred_element_type=F32)
-        pres.append(pre + jnp.dot(chunk(row_index, far[1]), far[0], preferred_element_type=F32))
-        chunks.append([chunk(1 - row_index, place) for _, place in last])
+
+    def chunk(rows, side, place):
+        return lax.dynamic_slice_in_dim(
+            rows.reshape(-1, width), side * depth + place * shard_depth, shard_depth, 1
+        )
+
+    def rest(rows, pre):
+        pre = pre + jnp.dot(
+            half_of(rows, 1 - row_index, depth), other_row, preferred_element_type=F32
+        )
+        return pre + jnp.dot(
+            chunk(rows, row_index, far[1]), far[0], preferred_element_type=F32
+        )
+
+    def last_chunks(rows):
+        return [chunk(rows, 1 - row_index, place) for _, place in last]
+
+    own_done = (rest(own, own_sum), last_chunks(own), inner_factor(own))
+    own_done, other = lax.optimization_barrier((own_done, other))
+    other_done = (
+        rest(other, this_product(other, this_row)),
+        last_chunks(other),
+        inner_factor(other),
+    )
     shards = [shard for shard, _ in last]
-    own_factor = inner_factor(own)
-    pres, chunks, shards, own_factor, other = lax.optimization_barrier(
-        (pres, chunks, shards, own_factor, other)
-    )
-    factors = (own_factor, inner_factor(other))
+    own_done, other_done, shards = lax.optimization_barrier((own_done, other_done, shards))
+    pres, chunks, factors = zip(own_done, other_done)
     parts = []
     for pre, pieces, rows_cot in zip(pres, chunks, (own_cot, other_cot)):
         for chunk, shard in zip(pieces, shards):

time: 182 us -> 188 us (1.033)
  waiting for transfers between devices: 46.9 us -> 30.1 us
  local copies, waits for them, and re-layouts: 15.5 us -> 30.6 us
  matrix products: 34.2 us -> 39.6 us
    ppermute x18, waiting for transfers between devices: 29.3 us -> 12.5 us  [shift(): lax.ppermute(value, axis, [(i, (i + step) % size) for i in range(size)])]
    dynamic_update_slice x12, local copies, waits for them, and re-layouts: 6.2 us -> 14.7 us  [placed(): joined = lax.dynamic_update_slice(joined, shard[None], (at, 0, 0))]
    dot_general x4, matrix products: 7.35 us -> 14 us  [the longest x2 11.3 us: rest(): jnp.dot(half_of(rows, 1 - row_index, depth), other_row, preferred_element...]
    dot_general x6, matrix products: 10.7 us -> 4.34 us  [body(): pre = pre + jnp.dot(chunk, shard, preferred_element_type=F32)]
    broadcast_in_dim x0 -> x2, local copies, waits for them, and re-layouts: none -> 5.41 us  [gathered(): empty = jnp.zeros((n_z,) + weight.shape, weight.dtype)]
    dot_general x2, matrix products: 8.97 us -> 11.7 us  [this_product(): return jnp.dot(flat, this_row, preferred_element_type=F32)]
    dot_general x2, matrix products: 4.07 us -> 6.72 us  [inner_factor(): lax.dot_general(rows.reshape(-1, width), input_projection, (((1,), (1,)),...]
    concatenate x1, other arithmetic: 2.86 us -> 5.27 us  [body(): own = jnp.concatenate((doc_inputs, query_inputs), axis=1)]
  transfers between devices with their start and end apart: 21 -> 21, of which waited for: 10 -> 7; matrix products, arithmetic and copies ran while one was open for 21% -> 35% of each run, Pallas kernels for 0% -> 0%
where the time goes in v9:
time: 188 us; the launch traced here: 187 us
  starting transfers between devices  49.2 us (26%)
  matrix products  39.6 us (21%)
  local copies, waits for them, and re-layouts  30.6 us (16%)
  waiting for transfers between devices  30.1 us (16%)
  between operations  14.7 us (8%)
  blocking collectives  12.5 us (7%)
  other arithmetic  10.1 us (5%)
    ppermute x18, starting transfers between devices, shift(): lax.ppermute(value, axis, [(i, (i + step) % size) for i in range(size)])  29.3 us
    dynamic_update_slice x12, local copies, waits for them, and re-layouts, placed(): joined = lax.dynamic_update_slice(joined, shard[None], (at, 0, 0))  14.7 us
    all_to_all x1, starting transfers between devices, body(): swapped = lax.all_to_all(part, dq, 0, 0, tiled=True)  14.4 us
    ppermute x18, waiting for transfers between devices, shift(): lax.ppermute(value, axis, [(i, (i + step) % size) for i in range(size)])  12.5 us
    all_to_all x1, blocking collectives, body(): received = lax.all_to_all(payload, dq, 0, 0, tiled=True)  12.5 us
    dot_general x2, matrix products, this_product(): return jnp.dot(flat, this_row, preferred_element_type=F32)  11.7 us
    dot_general x2, matrix products, rest(): jnp.dot(half_of(rows, 1 - row_index, depth), other_row, preferred_element...  11.3 us
    all_to_all x1, waiting for transfers between devices, body(): swapped = lax.all_to_all(part, dq, 0, 0, tiled=True)  9.11 us
  transfers between devices with their start and end apart: 21, of which 7 were waited for; matrix products, arithmetic and copies ran while one was open for 35% of the time, Pallas kernels for 0%

profile of v9, /device:TPU:1, one launch (start us, length us, event | category | flops | bytes accessed | tf_op | source)
XLA Modules:
  0.0 186.7 jit_solution(1699594868377099022)
XLA Ops:
  6.5 1.3 pad_maximum_fusion.2
  7.9 2.5 %collective-permute-start = (bf16[320,896]{1,0:T(8,128)(2,1)S(1)}, bf16[320,896]{1,0:T(8,128)(2,1)}, u32[]{:S(2)}, u32[]{:S(2)}) collective-permute-start(bf16[320,896]{1,0:T(8,128)(2,1)S(1)} %pad_maximum_fusion.2), channel_id=1, source_target_pairs={{0,16},{16,32},{32,48},{48,64},{64,80},{80,96},{96,112},{112,0},{1... | collective-permute-start | bytes 1720328 | tf_op jit(solution)/shard_map/ppermute | solution.py:11
  10.4 4.0 %collective-permute-start.1 = (bf16[320,896]{1,0:T(8,128)(2,1)S(1)}, bf16[320,896]{1,0:T(8,128)(2,1)}, u32[]{:S(2)}, u32[]{:S(2)}) collective-permute-start(bf16[320,896]{1,0:T(8,128)(2,1)S(1)} %pad_maximum_fusion.2), channel_id=1, source_target_pairs={{0,112},{16,0},{32,16},{48,32},{64,48},{80,64},{96,80},{112,96},{1... | collective-permute-start | bytes 1720328 | tf_op jit(solution)/shard_map/ppermute | solution.py:11
  14.4 1.3 collective-permute-start.2
  15.7 5.3 %pad_maximum_fusion = bf16[8,64,5120]{2,1,0:T(8,128)(2,1)} fusion(bf16[8,32,5120]{2,1,0:T(8,128)(2,1)} %param.11, bf16[8,32,5120]{2,1,0:T(8,128)(2,1)} %param.9), kind=kLoop, calls=%fused_computation | loop fusion | flops 10485760 | bytes 10485760 | tf_op jit(solution)/shard_map/concatenate | solution.py:125
  21.0 1.1 constant_dynamic-slice_fusion.8
  22.6 0.9 pad_maximum_fusion.3
  23.5 0.9 pad_maximum_fusion.4
  24.4 2.8 %collective-permute-done = bf16[320,896]{1,0:T(8,128)(2,1)} collective-permute-done((bf16[320,896]{1,0:T(8,128)(2,1)S(1)}, bf16[320,896]{1,0:T(8,128)(2,1)}, u32[]{:S(2)}, u32[]{:S(2)}) %collective-permute-start) | collective-permute-done | bytes 573472 | tf_op jit(solution)/shard_map/ppermute | solution.py:11
  28.0 2.7 %collective-permute-start.4 = (bf16[320,896]{1,0:T(8,128)(2,1)}, bf16[320,896]{1,0:T(8,128)(2,1)S(1)}, u32[]{:S(2)}, u32[]{:S(2)}) collective-permute-start(bf16[320,896]{1,0:T(8,128)(2,1)} %collective-permute-done.1), channel_id=1, source_target_pairs={{0,112},{16,0},{32,16},{48,32},{64,48},{80,64},{96,80},{112,96},{1... | collective-permute-start | bytes 1720328 | tf_op jit(solution)/shard_map/ppermute | solution.py:11
  30.7 2.9 %collective-permute-start.5 = (bf16[1,64,5120]{2,1,0:T(8,128)(2,1)S(1)}, bf16[1,64,5120]{2,1,0:T(8,128)(2,1)S(1)}, u32[]{:S(2)}, u32[]{:S(2)}) collective-permute-start(bf16[1,64,5120]{2,1,0:T(8,128)(2,1)S(1)} %pad_maximum_fusion.1), channel_id=1, source_target_pairs={{0,1},{1,0},{2,3},{3,2},{4,5},{5,4},{6,7},{7,6},{8,9},{9,8},{10,11... | collective-permute-start | bytes 1966088 | tf_op jit(solution)/shard_map/ppermute | solution.py:11
  33.6 2.8 %broadcast_in_dim.60.clone = bf16[8,320,896]{2,1,0:T(8,128)(2,1)} broadcast(bf16[]{:T(256)} %constant.105.clone.1), dimensions={} | broadcast | bytes 4587522 | tf_op jit(solution)/shard_map/broadcast_in_dim | solution.py:39
  36.4 0.9 bitcast_dynamic-update-slice_fusion.11
  37.2 2.0 %bitcast_dynamic-update-slice_fusion.10 = bf16[8,320,896]{2,1,0:T(8,128)(2,1)} fusion(bf16[8,320,896]{2,1,0:T(8,128)(2,1)} %bitcast_dynamic-update-slice_fusion.11, s32[]{:T(128)S(6)} %select_n.152, bf16[320,896]{1,0:T(8,128)(2,1)} %collective-permute-done), kind=kLoop, calls=%fused_computation.42 | loop fusion | bytes 1146884 | tf_op jit(solution)/shard_map/dynamic_update_slice | solution.py:33
  39.2 1.9 %bitcast_dynamic-update-slice_fusion.9 = bf16[8,320,896]{2,1,0:T(8,128)(2,1)} fusion(bf16[8,320,896]{2,1,0:T(8,128)(2,1)} %bitcast_dynamic-update-slice_fusion.10, s32[]{:T(128)S(6)} %select_n.154, bf16[320,896]{1,0:T(8,128)(2,1)} %collective-permute-done.1), kind=kLoop, calls=%fused_computation.41 | loop fusion | bytes 1146884 | tf_op jit(solution)/shard_map/dynamic_update_slice | solution.py:33
  41.1 2.6 %broadcast_in_dim.60.clone.1 = bf16[8,320,896]{2,1,0:T(8,128)(2,1)} broadcast(bf16[]{:T(256)} %constant.105.clone.1), dimensions={} | broadcast | bytes 4587522 | tf_op jit(solution)/shard_map/broadcast_in_dim | solution.py:39
  46.0 0.9 copy-done.5
  47.1 4.3 %fusion.53 = f32[512,64]{0,1:T(8,128)S(1)} fusion(bf16[512,5120]{1,0:T(8,128)(2,1)} %bitcast.75, bf16[64,5120]{1,0:T(8,128)(2,1)S(1)} %copy-done), kind=kOutput, calls=%fused_computation.105 | convolution fusion | flops 335544320 | bytes 6029312 | tf_op jit(solution)/shard_map/dot_general | solution.py:153
  51.5 1.4 collective-permute-start.8
  52.9 2.6 %collective-permute-start.7 = (bf16[320,896]{1,0:T(8,128)(2,1)S(1)}, bf16[320,896]{1,0:T(8,128)(2,1)S(1)}, u32[]{:S(2)}, u32[]{:S(2)}) collective-permute-start(bf16[320,896]{1,0:T(8,128)(2,1)S(1)} %collective-permute-done.4), channel_id=1, source_target_pairs={{0,112},{16,0},{32,16},{48,32},{64,48},{80,64},{96,80},{112,96},{1... | collective-permute-start | bytes 1720328 | tf_op jit(solution)/shard_map/ppermute | solution.py:11
  55.5 2.8 %constant_dynamic-slice_fusion.3 = (bf16[512,320]{1,0:T(8,128)(2,1)S(1)}, bf16[512,320]{1,0:T(8,128)(2,1)}, bf16[512,320]{1,0:T(8,128)(2,1)}) fusion(bf16[512,5120]{1,0:T(8,128)(2,1)} %bitcast.76, s32[]{:T(128)S(6)} %select_n.169, s32[]{:T(128)S(6)} %select_n.168, s32[]{:T(128)S(6)} %select_n.167), kind=kLoop, calls=%fused_computation.85 | loop fusion | bytes 1966092 | tf_op jit(solution)/shard_map/dynamic_slice | solution.py:164
  58.3 2.6 %collective-permute-start.14 = (bf16[512,448]{1,0:T(8,128)(2,1)S(1)}, bf16[512,448]{1,0:T(8,128)(2,1)S(1)}, u32[]{:S(2)}, u32[]{:S(2)}) collective-permute-start(bf16[512,448]{1,0:T(8,128)(2,1)S(1)} %bitcast.91), channel_id=1, source_target_pairs={{0,1},{1,0},{2,3},{3,2},{4,5},{5,4},{6,7},{7,6},{8,9},{9,8},{10,11... | collective-permute-start | bytes 1376264 | tf_op jit(solution)/shard_map/ppermute | solution.py:11
  60.9 0.9 bitcast_dynamic-update-slice_fusion.7
  61.8 0.9 bitcast_dynamic-update-slice_fusion.6
  62.6 1.2 collective-permute-done.6
  63.9 3.4 %collective-permute-start.10 = (bf16[320,896]{1,0:T(8,128)(2,1)S(1)}, bf16[320,896]{1,0:T(8,128)(2,1)S(1)}, u32[]{:S(2)}, u32[]{:S(2)}) collective-permute-start(bf16[320,896]{1,0:T(8,128)(2,1)S(1)} %copy-done.9), channel_id=1, source_target_pairs={{0,112},{16,0},{32,16},{48,32},{64,48},{80,64},{96,80},{112,96},{1... | collective-permute-start | bytes 1720328 | tf_op jit(solution)/shard_map/ppermute | solution.py:11
  67.6 0.9 bitcast_dynamic-update-slice_fusion.5
  68.5 0.9 bitcast_dynamic-update-slice_fusion.4
  69.4 7.0 %collective-permute-done.14 = bf16[512,448]{1,0:T(8,128)(2,1)S(1)} collective-permute-done((bf16[512,448]{1,0:T(8,128)(2,1)S(1)}, bf16[512,448]{1,0:T(8,128)(2,1)S(1)}, u32[]{:S(2)}, u32[]{:S(2)}) %collective-permute-start.14) | collective-permute-done | bytes 458784 | tf_op jit(solution)/shard_map/ppermute | solution.py:11
  76.4 2.3 %collective-permute-start.13 = (bf16[160,896]{1,0:T(8,128)(2,1)S(1)}, bf16[160,896]{1,0:T(8,128)(2,1)S(1)}, u32[]{:S(2)}, u32[]{:S(2)}) collective-permute-start(bf16[160,896]{1,0:T(8,128)(2,1)S(1)} %slice.35), channel_id=1, source_target_pairs={{0,112},{16,0},{32,16},{48,32},{64,48},{80,64},{96,80},{112,96},{1... | collective-permute-start | bytes 860168 | tf_op jit(solution)/shard_map/ppermute | solution.py:11
  78.7 6.5 %fusion.6 = f32[512,896]{1,0:T(8,128)} fusion(bf16[2560,896]{1,0:T(8,128)(2,1)} %bitcast.11, bf16[512,5120]{1,0:T(8,128)(2,1)S(1)} %bitcast.81, s32[]{:T(128)S(6)} %select_n.159), kind=kOutput, calls=%fused_computation.7 | convolution fusion | flops 2348810240 | bytes 9043972 | tf_op jit(solution)/shard_map/dot_general | solution.py:144
  85.2 1.9 %bitcast_dynamic-update-slice_fusion.3 = bf16[8,320,896]{2,1,0:T(8,128)(2,1)} fusion(bf16[8,320,896]{2,1,0:T(8,128)(2,1)} %bitcast_dynamic-update-slice_fusion.8, s32[]{:T(128)S(6)} %select_n.156, bf16[320,896]{1,0:T(8,128)(2,1)} %collective-permute-done.8), kind=kLoop, calls=%fused_computation.35 | loop fusion | bytes 1146884 | tf_op jit(solution)/shard_map/dynamic_update_slice | solution.py:33
  87.8 0.9 collective-permute-start.16
  88.7 1.8 collective-permute-start.17
  90.5 0.9 bitcast_dynamic-update-slice_fusion.2
  91.4 0.9 bitcast_dynamic-update-slice_fusion.1
  92.2 1.9 %bitcast_dynamic-update-slice_fusion = bf16[8,320,896]{2,1,0:T(8,128)(2,1)} fusion(bf16[8,320,896]{2,1,0:T(8,128)(2,1)} %bitcast_dynamic-update-slice_fusion.1, s32[]{:T(128)S(6)} %select_n.158, bf16[320,896]{1,0:T(8,128)(2,1)} %collective-permute-done.11), kind=kLoop, calls=%fused_computation.32 | loop fusion | bytes 1146884 | tf_op jit(solution)/shard_map/dynamic_update_slice | solution.py:33
  94.1 6.1 %fusion.4 = f32[512,896]{1,0:T(8,128)S(1)} fusion(bf16[2560,896]{1,0:T(8,128)(2,1)} %bitcast.16, bf16[512,5120]{1,0:T(8,128)(2,1)} %bitcast.77, s32[]{:T(128)S(6)} %select_n.164), kind=kOutput, calls=%fused_computation.5 | convolution fusion | flops 2348810240 | bytes 9043972 | tf_op jit(solution)/shard_map/dot_general | solution.py:169
  100.3 2.0 %add_add_fusion.3 = f32[512,896]{1,0:T(8,128)S(1)} fusion(f32[512,896]{1,0:T(8,128)S(1)} %copy-done.2, f32[512,896]{1,0:T(8,128)S(1)} %fusion.4, bf16[320,896]{1,0:T(8,128)(2,1)S(1)} %constant_dynamic-update-slice_fusion, bf16[512,5120]{1,0:T(8,128)(2,1)} %bitcast.78, s32[]{:T(128)S(6)} %select_n.166), kind=kOutput, calls=%fused_computation.12 | convolution fusion | flops 294518784 | bytes 6471684 | tf_op jit(solution)/shard_map/dot_general | solution.py:172
  102.9 5.2 %fusion = f32[512,896]{1,0:T(8,128)S(1)} fusion(bf16[2560,896]{1,0:T(8,128)(2,1)} %bitcast.16, bf16[512,5120]{1,0:T(8,128)(2,1)S(1)} %bitcast.82, s32[]{:T(128)S(6)} %select_n.164), kind=kOutput, calls=%fused_computation.1 | convolution fusion | flops 2348810240 | bytes 9043972 | tf_op jit(solution)/shard_map/dot_general | solution.py:169
  108.1 5.2 %fusion.2 = f32[512,896]{1,0:T(8,128)S(1)} fusion(bf16[2560,896]{1,0:T(8,128)(2,1)} %bitcast.11, bf16[512,5120]{1,0:T(8,128)(2,1)S(1)} %bitcast.83, s32[]{:T(128)S(6)} %select_n.159), kind=kOutput, calls=%fused_computation.3 | convolution fusion | flops 2348810240 | bytes 9043972 | tf_op jit(solution)/shard_map/dot_general | solution.py:144
  114.7 2.4 %fusion.54 = f32[512,64]{0,1:T(8,128)} fusion(bf16[512,5120]{1,0:T(8,128)(2,1)S(1)} %bitcast.86, bf16[64,5120]{1,0:T(8,128)(2,1)S(1)} %copy-done), kind=kOutput, calls=%fused_computation.106 | convolution fusion | flops 335544320 | bytes 6029312 | tf_op jit(solution)/shard_map/dot_general | solution.py:153
  120.8 0.9 fusion.57
  125.2 14.4 %all-to-all-start = ((bf16[16,8,1024]{2,1,0:T(8,128)(2,1)}), bf16[16,8,1024]{2,1,0:T(8,128)(2,1)S(1)}, u32[]{:S(2)}, u32[]{:S(2)}) async-start(bf16[16,8,1024]{2,1,0:T(8,128)(2,1)} %pad_maximum_fusion.7), calls=%async_computation | async-start | bytes 524288 | tf_op jit(solution)/shard_map/all_to_all | solution.py:206
  139.9 9.1 %all-to-all-done = bf16[16,8,1024]{2,1,0:T(8,128)(2,1)S(1)} async-done(((bf16[16,8,1024]{2,1,0:T(8,128)(2,1)}), bf16[16,8,1024]{2,1,0:T(8,128)(2,1)S(1)}, u32[]{:S(2)}, u32[]{:S(2)}) %all-to-all-start) | async-done | bytes 262176 | tf_op jit(solution)/shard_map/all_to_all | solution.py:206
  150.7 5.4 %all-to-all-start.1 = ((bf16[16,16,512]{2,1,0:T(8,128)(2,1)}), bf16[16,16,512]{2,1,0:T(8,128)(2,1)S(1)}, u32[]{:S(2)}, u32[]{:S(2)}) async-start(bf16[16,16,512]{2,1,0:T(8,128)(2,1)} %broadcast_in_dim.73), calls=%async_computation.1 | async-start | bytes 524288 | tf_op jit(solution)/shard_map/all_to_all | solution.py:222
  156.5 8.5 %all-to-all-done.1 = bf16[16,16,512]{2,1,0:T(8,128)(2,1)S(1)} async-done(((bf16[16,16,512]{2,1,0:T(8,128)(2,1)}), bf16[16,16,512]{2,1,0:T(8,128)(2,1)S(1)}, u32[]{:S(2)}, u32[]{:S(2)}) %all-to-all-start.1) | async-done | bytes 262176 | tf_op jit(solution)/shard_map/all_to_all | solution.py:222
  165.6 12.5 %all_to_all.19 = f32[16,1,640]{2,1,0:T(1,128)S(1)} all-to-all(f32[16,1,640]{2,1,0:T(1,128)S(1)} %copy.24), channel_id=1, replica_groups=mesh['ylo'=2,'z'=8,'x'=4,'core'=2,'yhi'=2] {'x','core','yhi'}, dimensions={0} | all-to-all | bytes 81920 | tf_op jit(solution)/shard_map/all_to_all | solution.py:243
  (113 shorter events, 17.8 us)
Async XLA Ops:
  6.5 40.5 %copy-start = (bf16[64,5120]{1,0:T(8,128)(2,1)S(1)}, bf16[64,5120]{1,0:T(8,128)(2,1)}, u32[]{:S(2)}) copy-start(bf16[64,5120]{1,0:T(8,128)(2,1)} %param.15) | copy-start | bytes 1966084
  6.5 87.6 %all-gather.2.cloned.1.call-start = ((), (), s32[]{:S(2)}) async-start(), calls=%async_computation.3 | async-start | bytes 5898240 | tf_op jit(solution)/shard_map/all_gather | solution.py:45
  7.9 19.3 %collective-permute-start = (bf16[320,896]{1,0:T(8,128)(2,1)S(1)}, bf16[320,896]{1,0:T(8,128)(2,1)}, u32[]{:S(2)}, u32[]{:S(2)}) collective-permute-start(bf16[320,896]{1,0:T(8,128)(2,1)S(1)} %pad_maximum_fusion.2), channel_id=1, source_target_pairs={{0,16},{16,32},{32,48},{48,64},{64,80},{80,96},{96,112},{112,0},{1... | collective-permute-start | bytes 1720328 | tf_op jit(solution)/shard_map/ppermute | solution.py:11
  10.4 16.8 %collective-permute-start.1 = (bf16[320,896]{1,0:T(8,128)(2,1)S(1)}, bf16[320,896]{1,0:T(8,128)(2,1)}, u32[]{:S(2)}, u32[]{:S(2)}) collective-permute-start(bf16[320,896]{1,0:T(8,128)(2,1)S(1)} %pad_maximum_fusion.2), channel_id=1, source_target_pairs={{0,112},{16,0},{32,16},{48,32},{64,48},{80,64},{96,80},{112,96},{1... | collective-permute-start | bytes 1720328 | tf_op jit(solution)/shard_map/ppermute | solution.py:11
  14.4 13.6 %collective-permute-start.2 = (bf16[320,896]{1,0:T(8,128)(2,1)S(1)}, bf16[320,896]{1,0:T(8,128)(2,1)S(1)}, u32[]{:S(2)}, u32[]{:S(2)}) collective-permute-start(bf16[320,896]{1,0:T(8,128)(2,1)S(1)} %pad_maximum_fusion.2), channel_id=1, source_target_pairs={{0,128},{128,0},{1,129},{129,1},{2,130},{130,2},{3,131},{131,3},{4... | collective-permute-start | bytes 1720328 | tf_op jit(solution)/shard_map/ppermute | solution.py:11
  15.7 6.4 %copy-start.6 = (bf16[8,32,896]{2,1,0:T(8,128)(2,1)S(1)}, bf16[8,32,896]{2,1,0:T(8,128)(2,1)}, u32[]{:S(2)}) copy-start(bf16[8,32,896]{2,1,0:T(8,128)(2,1)} %param.12) | copy-start | bytes 1376260
  15.7 6.4 %copy-start.7 = (bf16[8,32,896]{2,1,0:T(8,128)(2,1)S(1)}, bf16[8,32,896]{2,1,0:T(8,128)(2,1)}, u32[]{:S(2)}) copy-start(bf16[8,32,896]{2,1,0:T(8,128)(2,1)} %param.10) | copy-start | bytes 1376260
  28.0 15.8 %copy-start.8 = (bf16[320,896]{1,0:T(8,128)(2,1)}, bf16[320,896]{1,0:T(8,128)(2,1)S(1)}, u32[]{:S(2)}) copy-start(bf16[320,896]{1,0:T(8,128)(2,1)S(1)} %collective-permute-done.2) | copy-start | bytes 1720324
  28.0 16.6 %collective-permute-start.3 = (bf16[320,896]{1,0:T(8,128)(2,1)}, bf16[320,896]{1,0:T(8,128)(2,1)S(1)}, u32[]{:S(2)}, u32[]{:S(2)}) collective-permute-start(bf16[320,896]{1,0:T(8,128)(2,1)} %collective-permute-done), channel_id=1, source_target_pairs={{0,16},{16,32},{32,48},{48,64},{64,80},{80,96},{96,112},{112,0},{1... | collective-permute-start | bytes 1720328 | tf_op jit(solution)/shard_map/ppermute | solution.py:11
  28.0 16.6 %collective-permute-start.4 = (bf16[320,896]{1,0:T(8,128)(2,1)}, bf16[320,896]{1,0:T(8,128)(2,1)S(1)}, u32[]{:S(2)}, u32[]{:S(2)}) collective-permute-start(bf16[320,896]{1,0:T(8,128)(2,1)} %collective-permute-done.1), channel_id=1, source_target_pairs={{0,112},{16,0},{32,16},{48,32},{64,48},{80,64},{96,80},{112,96},{1... | collective-permute-start | bytes 1720328 | tf_op jit(solution)/shard_map/ppermute | solution.py:11
  30.7 15.3 %collective-permute-start.5 = (bf16[1,64,5120]{2,1,0:T(8,128)(2,1)S(1)}, bf16[1,64,5120]{2,1,0:T(8,128)(2,1)S(1)}, u32[]{:S(2)}, u32[]{:S(2)}) collective-permute-start(bf16[1,64,5120]{2,1,0:T(8,128)(2,1)S(1)} %pad_maximum_fusion.1), channel_id=1, source_target_pairs={{0,1},{1,0},{2,3},{3,2},{4,5},{5,4},{6,7},{7,6},{8,9},{9,8},{10,11... | collective-permute-start | bytes 1966088 | tf_op jit(solution)/shard_map/ppermute | solution.py:11
  44.6 0.8 copy-start.10
  46.0 0.9 copy-start.5
  46.0 5.4 %copy-start.11 = (bf16[320,896]{1,0:T(8,128)(2,1)S(1)}, bf16[320,896]{1,0:T(8,128)(2,1)}, u32[]{:S(2)}) copy-start(bf16[320,896]{1,0:T(8,128)(2,1)} %copy-done.10) | copy-start | bytes 1720324
  46.9 11.4 %copy-start.14 = (bf16[8,64,448]{2,1,0:T(8,128)(2,1)S(1)}, bf16[8,64,448]{2,1,0:T(8,128)(2,1)}, u32[]{:S(2)}) copy-start(bf16[8,64,448]{2,1,0:T(8,128)(2,1)} %pad_maximum_fusion.3) | copy-start | bytes 1376260
  47.0 16.8 %copy-start.9 = (bf16[320,896]{1,0:T(8,128)(2,1)S(1)}, bf16[320,896]{1,0:T(8,128)(2,1)}, u32[]{:S(2)}) copy-start(bf16[320,896]{1,0:T(8,128)(2,1)} %copy-done.8) | copy-start | bytes 1720324
  47.0 31.7 %slice-start = ((s8[5242880]{0:T(1024)(128)(4,1)}), s8[4194304]{0:T(1024)(128)(4,1)S(1)}, s32[]{:S(2)}) async-start(s8[5242880]{0:T(1024)(128)(4,1)} %bitcast.79), calls=%async_computation.4 | async-start | bytes 8388608
  51.4 27.3 %slice-start.1 = ((s8[5242880]{0:T(1024)(128)(4,1)}), s8[1048576]{0:T(1024)(128)(4,1)S(1)}, s32[]{:S(2)}) async-start(s8[5242880]{0:T(1024)(128)(4,1)} %bitcast.79), calls=%async_computation.5 | async-start | bytes 2097152
  51.4 12.4 %collective-permute-start.6 = (bf16[320,896]{1,0:T(8,128)(2,1)S(1)}, bf16[320,896]{1,0:T(8,128)(2,1)S(1)}, u32[]{:S(2)}, u32[]{:S(2)}) collective-permute-start(bf16[320,896]{1,0:T(8,128)(2,1)S(1)} %copy-done.11), channel_id=1, source_target_pairs={{0,16},{16,32},{32,48},{48,64},{64,80},{80,96},{96,112},{112,0},{1... | collective-permute-start | bytes 1720328 | tf_op jit(solution)/shard_map/ppermute | solution.py:11
  51.5 12.4 %collective-permute-start.8 = (bf16[320,896]{1,0:T(8,128)(2,1)S(1)}, bf16[320,896]{1,0:T(8,128)(2,1)}, u32[]{:S(2)}, u32[]{:S(2)}) collective-permute-start(bf16[320,896]{1,0:T(8,128)(2,1)S(1)} %copy-done.11), channel_id=1, source_target_pairs={{0,128},{128,0},{1,129},{129,1},{2,130},{130,2},{3,131},{131,3},{4... | collective-permute-start | bytes 1720328 | tf_op jit(solution)/shard_map/ppermute | solution.py:11
  52.9 11.0 %collective-permute-start.7 = (bf16[320,896]{1,0:T(8,128)(2,1)S(1)}, bf16[320,896]{1,0:T(8,128)(2,1)S(1)}, u32[]{:S(2)}, u32[]{:S(2)}) collective-permute-start(bf16[320,896]{1,0:T(8,128)(2,1)S(1)} %collective-permute-done.4), channel_id=1, source_target_pairs={{0,112},{16,0},{32,16},{48,32},{64,48},{80,64},{96,80},{112,96},{1... | collective-permute-start | bytes 1720328 | tf_op jit(solution)/shard_map/ppermute | solution.py:11
  58.3 18.2 %collective-permute-start.14 = (bf16[512,448]{1,0:T(8,128)(2,1)S(1)}, bf16[512,448]{1,0:T(8,128)(2,1)S(1)}, u32[]{:S(2)}, u32[]{:S(2)}) collective-permute-start(bf16[512,448]{1,0:T(8,128)(2,1)S(1)} %bitcast.91), channel_id=1, source_target_pairs={{0,1},{1,0},{2,3},{3,2},{4,5},{5,4},{6,7},{7,6},{8,9},{9,8},{10,11... | collective-permute-start | bytes 1376264 | tf_op jit(solution)/shard_map/ppermute | solution.py:11
  63.9 23.3 %collective-permute-start.10 = (bf16[320,896]{1,0:T(8,128)(2,1)S(1)}, bf16[320,896]{1,0:T(8,128)(2,1)S(1)}, u32[]{:S(2)}, u32[]{:S(2)}) collective-permute-start(bf16[320,896]{1,0:T(8,128)(2,1)S(1)} %copy-done.9), channel_id=1, source_target_pairs={{0,112},{16,0},{32,16},{48,32},{64,48},{80,64},{96,80},{112,96},{1... | collective-permute-start | bytes 1720328 | tf_op jit(solution)/shard_map/ppermute | solution.py:11
  67.3 19.9 %collective-permute-start.9 = (bf16[320,896]{1,0:T(8,128)(2,1)S(1)}, bf16[320,896]{1,0:T(8,128)(2,1)S(1)}, u32[]{:S(2)}, u32[]{:S(2)}) collective-permute-start(bf16[320,896]{1,0:T(8,128)(2,1)S(1)} %copy-done.9), channel_id=1, source_target_pairs={{0,16},{16,32},{32,48},{48,64},{64,80},{80,96},{96,112},{112,0},{1... | collective-permute-start | bytes 1720328 | tf_op jit(solution)/shard_map/ppermute | solution.py:11
  67.3 19.9 %collective-permute-start.11 = (bf16[320,896]{1,0:T(8,128)(2,1)S(1)}, bf16[320,896]{1,0:T(8,128)(2,1)}, u32[]{:S(2)}, u32[]{:S(2)}) collective-permute-start(bf16[320,896]{1,0:T(8,128)(2,1)S(1)} %collective-permute-done.4), channel_id=1, source_target_pairs={{0,128},{128,0},{1,129},{129,1},{2,130},{130,2},{3,131},{131,3},{4... | collective-permute-start | bytes 1720328 | tf_op jit(solution)/shard_map/ppermute | solution.py:11
  67.5 19.7 %collective-permute-start.12 = (bf16[160,896]{1,0:T(8,128)(2,1)S(1)}, bf16[160,896]{1,0:T(8,128)(2,1)S(1)}, u32[]{:S(2)}, u32[]{:S(2)}) collective-permute-start(bf16[160,896]{1,0:T(8,128)(2,1)S(1)} %slice.34), channel_id=1, source_target_pairs={{0,16},{16,32},{32,48},{48,64},{64,80},{80,96},{96,112},{112,0},{1... | collective-permute-start | bytes 860168 | tf_op jit(solution)/shard_map/ppermute | solution.py:11
  76.4 2.3 %copy-start.15 = (bf16[512,448]{1,0:T(8,128)(2,1)}, bf16[512,448]{1,0:T(8,128)(2,1)S(1)}, u32[]{:S(2)}) copy-start(bf16[512,448]{1,0:T(8,128)(2,1)S(1)} %collective-permute-done.14) | copy-start | bytes 1376260
  76.4 10.7 %collective-permute-start.13 = (bf16[160,896]{1,0:T(8,128)(2,1)S(1)}, bf16[160,896]{1,0:T(8,128)(2,1)S(1)}, u32[]{:S(2)}, u32[]{:S(2)}) collective-permute-start(bf16[160,896]{1,0:T(8,128)(2,1)S(1)} %slice.35), channel_id=1, source_target_pairs={{0,112},{16,0},{32,16},{48,32},{64,48},{80,64},{96,80},{112,96},{1... | collective-permute-start | bytes 860168 | tf_op jit(solution)/shard_map/ppermute | solution.py:11
  87.2 29.8 %collective-permute-start.15 = (bf16[320,896]{1,0:T(8,128)(2,1)S(1)}, bf16[320,896]{1,0:T(8,128)(2,1)S(1)}, u32[]{:S(2)}, u32[]{:S(2)}) collective-permute-start(bf16[320,896]{1,0:T(8,128)(2,1)S(1)} %constant_dynamic-update-slice_fusion), channel_id=1, source_target_pairs={{0,128},{128,0},{1,129},{129,1},{2,130},{130,2},{3,131},{131,3},{4... | collective-permute-start | bytes 1720328 | tf_op jit(solution)/shard_map/ppermute | solution.py:11
  87.8 29.2 %collective-permute-start.16 = (bf16[320,896]{1,0:T(8,128)(2,1)}, bf16[320,896]{1,0:T(8,128)(2,1)S(1)}, u32[]{:S(2)}, u32[]{:S(2)}) collective-permute-start(bf16[320,896]{1,0:T(8,128)(2,1)} %collective-permute-done.8), channel_id=1, source_target_pairs={{0,16},{16,32},{32,48},{48,64},{64,80},{80,96},{96,112},{112,0},{1... | collective-permute-start | bytes 1720328 | tf_op jit(solution)/shard_map/ppermute | solution.py:11
  88.7 28.4 %collective-permute-start.17 = (bf16[320,896]{1,0:T(8,128)(2,1)}, bf16[320,896]{1,0:T(8,128)(2,1)S(1)}, u32[]{:S(2)}, u32[]{:S(2)}) collective-permute-start(bf16[320,896]{1,0:T(8,128)(2,1)} %collective-permute-done.11), channel_id=1, source_target_pairs={{0,112},{16,0},{32,16},{48,32},{64,48},{80,64},{96,80},{112,96},{1... | collective-permute-start | bytes 1720328 | tf_op jit(solution)/shard_map/ppermute | solution.py:11
  94.1 6.1 %copy-start.2 = (f32[512,896]{1,0:T(8,128)S(1)}, f32[512,896]{1,0:T(8,128)}, u32[]{:S(2)}) copy-start(f32[512,896]{1,0:T(8,128)} %fusion.6) | copy-start | bytes 5505028
  100.2 2.6 %copy-start.1 = (bf16[8,64,5120]{2,1,0:T(8,128)(2,1)S(1)}, bf16[8,64,5120]{2,1,0:T(8,128)(2,1)}, u32[]{:S(2)}) copy-start(bf16[8,64,5120]{2,1,0:T(8,128)(2,1)} %all-gather.2.cloned.1.call-done) | copy-start | bytes 15728644
  114.1 3.0 %copy-start.4 = (bf16[512,320]{1,0:T(8,128)(2,1)S(1)}, bf16[512,320]{1,0:T(8,128)(2,1)}, u32[]{:S(2)}) copy-start(bf16[512,320]{1,0:T(8,128)(2,1)} %get-tuple-element.94) | copy-start | bytes 983044
  114.6 3.1 %copy-start.3 = (bf16[512,320]{1,0:T(8,128)(2,1)S(1)}, bf16[512,320]{1,0:T(8,128)(2,1)}, u32[]{:S(2)}) copy-start(bf16[512,320]{1,0:T(8,128)(2,1)} %get-tuple-element.96) | copy-start | bytes 983044
  118.4 1.0 copy-start.13
  118.4 1.0 copy-start.17
  119.4 0.9 copy-start.18
  122.3 1.0 copy-start.16
  124.0 15.7 %copy-start.12 = (f32[512,64]{0,1:T(8,128)S(1)}, f32[512,64]{0,1:T(8,128)}, u32[]{:S(2)}) copy-start(f32[512,64]{0,1:T(8,128)} %fusion.54) | copy-start | bytes 393220
  125.2 23.8 %all-to-all-start = ((bf16[16,8,1024]{2,1,0:T(8,128)(2,1)}), bf16[16,8,1024]{2,1,0:T(8,128)(2,1)S(1)}, u32[]{:S(2)}, u32[]{:S(2)}) async-start(bf16[16,8,1024]{2,1,0:T(8,128)(2,1)} %pad_maximum_fusion.7), calls=%async_computation | async-start | bytes 524288 | tf_op jit(solution)/shard_map/all_to_all | solution.py:206
  150.7 14.3 %all-to-all-start.1 = ((bf16[16,16,512]{2,1,0:T(8,128)(2,1)}), bf16[16,16,512]{2,1,0:T(8,128)(2,1)S(1)}, u32[]{:S(2)}, u32[]{:S(2)}) async-start(bf16[16,16,512]{2,1,0:T(8,128)(2,1)} %broadcast_in_dim.73), calls=%async_computation.1 | async-start | bytes 524288 | tf_op jit(solution)/shard_map/all_to_all | solution.py:222
Sparse Core Ops, SparseCore 0:
  47.0 41.8 all-gather.1

commit v10 on v4

--- a/solution.py
+++ b/solution.py
@@ -11,7 +11,7 @@
     return lax.ppermute(value, axis, [(i, (i + step) % size) for i in range(size)])
 
 
-def gathered(weight, piece, cot, early):
+def gathered(weight, piece, cot, early, inner_factor):
     barrier = lax.optimization_barrier
     n_z = lax.axis_size("z")
     z = lax.axis_index("z")
@@ -27,17 +27,29 @@
     def across(value):
         return shift(value, "ylo", 1)
 
-    def placed(by_offset):
-        result = jnp.zeros((n_z,) + weight.shape, weight.dtype)
+    def placed(result, by_offset):
         for offset, shard in by_offset:
             result = lax.dynamic_update_slice(result, shard[None], ((z + offset) % n_z, 0, 0))
-        return result.reshape(n_z * weight.shape[0], -1)
-
-    a1, b1, here, w0, cot, early = barrier(
-        (up(weight), down(weight), shift(piece, "yhi", 1), weight, cot, early)
+        return result
+
+    a1, b1, o0, w0, cot, piece, early = barrier(
+        (up(weight), down(weight), across(weight), weight, cot, piece, early)
+    )
+    this_row = placed(
+        jnp.zeros((n_z,) + weight.shape, weight.dtype), ((0, w0), (n_z - 1, a1))
+    )
+    a2, b2, here, o0, cot, own_factor, this_row = barrier(
+        (
+            up(a1),
+            down(b1),
+            shift(piece, "yhi", 1),
+            o0,
+            cot,
+            inner_factor(early[0]),
+            this_row,
+        )
     )
     partner = lax.all_gather(here, ("x", "core"), axis=0, tiled=True)
-    a2, b2, o0, cot = barrier((up(a1), down(b1), across(w0), cot))
     a3, b3, oa2, o0, b2 = barrier((up(a2), down(b2), across(a2), o0, b2))
     other_cot = shift(cot, "yhi", 1)
     oa1, ob1, ob2, a4, b4, oa2, other_cot = barrier(
@@ -50,19 +62,15 @@
         (down(ob2), (z + 3) % n_z),
     )
     this_row = placed(
-        (
-            (0, w0),
-            (n_z - 1, a1),
-            (1, b1),
-            (n_z - 2, a2),
-            (2, b2),
-            (n_z - 3, a3),
-            (3, b3),
-            (n_z // 2, a4),
-        )
-    )
-    other_row = placed(((0, o0), (n_z - 1, oa1), (1, ob1), (n_z - 2, oa2), (2, ob2)))
-    return this_row, other_row, last, other_cot, partner, early
+        this_row,
+        ((1, b1), (n_z - 2, a2), (2, b2), (n_z - 3, a3), (3, b3), (n_z // 2, a4)),
+    )
+    other_row = placed(
+        jnp.zeros_like(this_row),
+        ((0, o0), (n_z - 1, oa1), (1, ob1), (n_z - 2, oa2), (2, ob2)),
+    )
+    flat = (n_z * weight.shape[0], -1)
+    return this_row.reshape(flat), other_row.reshape(flat), last, other_cot, partner, early, own_factor
 
 
 def projected(pre, cotangent, gate_projection, up_projection):
@@ -125,8 +133,17 @@
 
     own_cot = cotangents(half_index)
     weight = jnp.concatenate((gate_weight, up_weight), axis=1)
-    this_row, other_row, last, other_cot, other, (own, own_cot) = gathered(
-        weight, piece, cotangents(1 - half_index), (own, own_cot)
+
+    def inner_factor(rows):
+        return lax.dot_general(
+            rows.reshape(-1, width),
+            input_projection,
+            (((1,), (1,)), ((), ())),
+            preferred_element_type=F32,
+        )
+
+    this_row, other_row, last, other_cot, other, (own, own_cot), own_factor = gathered(
+        weight, piece, cotangents(1 - half_index), (own, own_cot), inner_factor
     )
     gate_proj = columns(gate_projection, half_index)
     up_proj = columns(up_projection, half_index)
@@ -134,7 +151,6 @@
     depth = this_row.shape[0]
     shard_depth = weight.shape[0]
     pres = []
-    factors = []
     chunks = []
     for rows in (own, other):
         flat = rows.reshape(-1, width)
@@ -142,17 +158,13 @@
         other_flat = lax.dynamic_slice_in_dim(flat, (1 - row_index) * depth, depth, 1)
         pre = jnp.dot(this_flat, this_row, preferred_element_type=F32)
         pres.append(pre + jnp.dot(other_flat, other_row, preferred_element_type=F32))
-        factors.append(
-            lax.dot_general(
-                flat, input_projection, (((1,), (1,)), ((), ())), preferred_element_type=F32
-            )
-        )
         chunks.append(
             [
                 lax.dynamic_slice_in_dim(other_flat, place * shard_depth, shard_depth, 1)
                 for _, place in last
             ]
         )
+    factors = (own_factor, inner_factor(other))
     shards = [shard for shard, _ in last]
     pres, factors, chunks, shards = lax.optimization_barrier((pres, factors, chunks, shards))
     parts = []

time: 180 us -> 178 us (0.989)
  waiting for transfers between devices: 51.1 us -> 43.7 us
  local copies, waits for them, and re-layouts: 17.5 us -> 21.3 us
    ppermute x18, waiting for transfers between devices: 33.5 us -> 26.1 us  [shift(): lax.ppermute(value, axis, [(i, (i + step) % size) for i in range(size)])]
    dynamic_update_slice x13, local copies, waits for them, and re-layouts: 7.8 us -> 10.4 us  [placed(): lax.dynamic_update_slice(result, shard[None], ((z + offset) % n_z, 0, 0))]
    concatenate x1, other arithmetic: 2.86 us -> 5.27 us  [body(): own = jnp.concatenate((doc_inputs, query_inputs), axis=1)]
  transfers between devices with their start and end apart: 21 -> 21, of which waited for: 11 -> 12; matrix products, arithmetic and copies ran while one was open for 23% -> 26% of each run, Pallas kernels for 0% -> 0%
where the time goes in v10:
time: 178 us; the launch traced here: 177 us
  starting transfers between devices  47.1 us (26%)
  waiting for transfers between devices  43.7 us (25%)
  matrix products  28 us (16%)
  local copies, waits for them, and re-layouts  21.3 us (12%)
  between operations  14.8 us (8%)
  blocking collectives  12.1 us (7%)
  other arithmetic  10.1 us (6%)
    ppermute x18, starting transfers between devices, shift(): lax.ppermute(value, axis, [(i, (i + step) % size) for i in range(size)])  30.5 us
    ppermute x18, waiting for transfers between devices, shift(): lax.ppermute(value, axis, [(i, (i + step) % size) for i in range(size)])  26.1 us
    all_to_all x1, blocking collectives, body(): received = lax.all_to_all(payload, dq, 0, 0, tiled=True)  12.1 us
    all_to_all x1, starting transfers between devices, body(): swapped = lax.all_to_all(part, dq, 0, 0, tiled=True)  11.7 us
    dynamic_update_slice x13, local copies, waits for them, and re-layouts, placed(): lax.dynamic_update_slice(result, shard[None], ((z + offset) % n_z, 0, 0))  10.4 us
    all_to_all x1, waiting for transfers between devices, body(): swapped = lax.all_to_all(part, dq, 0, 0, tiled=True)  9.1 us
    dot_general x2, matrix products, body(): jnp.dot(other_flat, other_row, preferred_element_type=F32)  8.98 us
    all_to_all x1, waiting for transfers between devices, body(): lax.all_to_all(jnp.broadcast_to(queries[None], (n_fsdp,) + queries.shape)...  8.5 us
  transfers between devices with their start and end apart: 21, of which 12 were waited for; matrix products, arithmetic and copies ran while one was open for 26% of the time, Pallas kernels for 0%

profile of v10, /device:TPU:1, one launch (start us, length us, event | category | flops | bytes accessed | tf_op | source)
XLA Modules:
  0.0 177.0 jit_solution(17533360686603226581)
XLA Ops:
  6.5 1.3 pad_maximum_fusion.2
  7.9 2.5 %collective-permute-start = (bf16[320,896]{1,0:T(8,128)(2,1)S(1)}, bf16[320,896]{1,0:T(8,128)(2,1)}, u32[]{:S(2)}, u32[]{:S(2)}) collective-permute-start(bf16[320,896]{1,0:T(8,128)(2,1)S(1)} %pad_maximum_fusion.2), channel_id=1, source_target_pairs={{0,16},{16,32},{32,48},{48,64},{64,80},{80,96},{96,112},{112,0},{1... | collective-permute-start | bytes 1720328 | tf_op jit(solution)/shard_map/ppermute | solution.py:11
  10.4 4.0 %collective-permute-start.1 = (bf16[320,896]{1,0:T(8,128)(2,1)S(1)}, bf16[320,896]{1,0:T(8,128)(2,1)}, u32[]{:S(2)}, u32[]{:S(2)}) collective-permute-start(bf16[320,896]{1,0:T(8,128)(2,1)S(1)} %pad_maximum_fusion.2), channel_id=1, source_target_pairs={{0,112},{16,0},{32,16},{48,32},{64,48},{80,64},{96,80},{112,96},{1... | collective-permute-start | bytes 1720328 | tf_op jit(solution)/shard_map/ppermute | solution.py:11
  14.4 1.3 collective-permute-start.2
  15.7 5.3 %pad_maximum_fusion = bf16[8,64,5120]{2,1,0:T(8,128)(2,1)} fusion(bf16[8,32,5120]{2,1,0:T(8,128)(2,1)} %param.11, bf16[8,32,5120]{2,1,0:T(8,128)(2,1)} %param.9), kind=kLoop, calls=%fused_computation | loop fusion | flops 10485760 | bytes 10485760 | tf_op jit(solution)/shard_map/concatenate | solution.py:123
  21.0 1.1 constant_dynamic-slice_fusion.8
  22.6 0.9 pad_maximum_fusion.3
  23.5 0.9 pad_maximum_fusion.4
  24.4 2.8 %collective-permute-done = bf16[320,896]{1,0:T(8,128)(2,1)} collective-permute-done((bf16[320,896]{1,0:T(8,128)(2,1)S(1)}, bf16[320,896]{1,0:T(8,128)(2,1)}, u32[]{:S(2)}, u32[]{:S(2)}) %collective-permute-start) | collective-permute-done | bytes 573472 | tf_op jit(solution)/shard_map/ppermute | solution.py:11
  27.2 0.8 collective-permute-done.2
  28.0 2.7 %collective-permute-start.4 = (bf16[320,896]{1,0:T(8,128)(2,1)}, bf16[320,896]{1,0:T(8,128)(2,1)}, u32[]{:S(2)}, u32[]{:S(2)}) collective-permute-start(bf16[320,896]{1,0:T(8,128)(2,1)} %collective-permute-done.1), channel_id=1, source_target_pairs={{0,112},{16,0},{32,16},{48,32},{64,48},{80,64},{96,80},{112,96},{1... | collective-permute-start | bytes 1720328 | tf_op jit(solution)/shard_map/ppermute | solution.py:11
  30.7 2.9 %collective-permute-start.5 = (bf16[1,64,5120]{2,1,0:T(8,128)(2,1)S(1)}, bf16[1,64,5120]{2,1,0:T(8,128)(2,1)S(1)}, u32[]{:S(2)}, u32[]{:S(2)}) collective-permute-start(bf16[1,64,5120]{2,1,0:T(8,128)(2,1)S(1)} %pad_maximum_fusion.1), channel_id=1, source_target_pairs={{0,1},{1,0},{2,3},{3,2},{4,5},{5,4},{6,7},{7,6},{8,9},{9,8},{10,11... | collective-permute-start | bytes 1966088 | tf_op jit(solution)/shard_map/ppermute | solution.py:11
  34.3 1.1 bitcast_dynamic-update-slice_fusion.11
  35.4 2.4 %fusion.55 = f32[512,64]{0,1:T(8,128)} fusion(bf16[512,5120]{1,0:T(8,128)(2,1)S(1)} %bitcast.76, bf16[64,5120]{1,0:T(8,128)(2,1)S(1)} %copy-done), kind=kOutput, calls=%fused_computation.102 | convolution fusion | flops 335544320 | bytes 6029312 | tf_op jit(solution)/shard_map/dot_general | solution.py:138
  37.8 4.4 %collective-permute-done.3 = bf16[320,896]{1,0:T(8,128)(2,1)} collective-permute-done((bf16[320,896]{1,0:T(8,128)(2,1)}, bf16[320,896]{1,0:T(8,128)(2,1)}, u32[]{:S(2)}, u32[]{:S(2)}) %collective-permute-start.3) | collective-permute-done | bytes 573472 | tf_op jit(solution)/shard_map/ppermute | solution.py:11
  42.2 3.8 %collective-permute-done.5 = bf16[1,64,5120]{2,1,0:T(8,128)(2,1)S(1)} collective-permute-done((bf16[1,64,5120]{2,1,0:T(8,128)(2,1)S(1)}, bf16[1,64,5120]{2,1,0:T(8,128)(2,1)S(1)}, u32[]{:S(2)}, u32[]{:S(2)}) %collective-permute-start.5) | collective-permute-done | bytes 655392 | tf_op jit(solution)/shard_map/ppermute | solution.py:11
  46.0 0.8 copy-done.9
  47.1 1.4 collective-permute-start.8
  48.5 2.6 %collective-permute-start.7 = (bf16[320,896]{1,0:T(8,128)(2,1)}, bf16[320,896]{1,0:T(8,128)(2,1)S(1)}, u32[]{:S(2)}, u32[]{:S(2)}) collective-permute-start(bf16[320,896]{1,0:T(8,128)(2,1)} %collective-permute-done.4), channel_id=1, source_target_pairs={{0,112},{16,0},{32,16},{48,32},{64,48},{80,64},{96,80},{112,96},{1... | collective-permute-start | bytes 1720328 | tf_op jit(solution)/shard_map/ppermute | solution.py:11
  51.0 1.9 %constant_dynamic-slice_fusion.3 = (bf16[512,320]{1,0:T(8,128)(2,1)S(1)}, bf16[512,320]{1,0:T(8,128)(2,1)S(1)}, bf16[512,320]{1,0:T(8,128)(2,1)S(1)}) fusion(bf16[512,5120]{1,0:T(8,128)(2,1)} %bitcast.75, s32[]{:T(128)S(6)} %dynamic_slice.81, s32[]{:T(128)S(6)} %dynamic_slice.79, s32[]{:T(128)S(6)} %dynamic_slice.77), kind=kLoop, calls=%fused_computation.81 | loop fusion | bytes 1966092 | tf_op jit(solution)/shard_map/dynamic_slice | solution.py:163
  52.9 2.7 %collective-permute-start.14 = (bf16[512,448]{1,0:T(8,128)(2,1)}, bf16[512,448]{1,0:T(8,128)(2,1)S(1)}, u32[]{:S(2)}, u32[]{:S(2)}) collective-permute-start(bf16[512,448]{1,0:T(8,128)(2,1)} %bitcast.93), channel_id=1, source_target_pairs={{0,1},{1,0},{2,3},{3,2},{4,5},{5,4},{6,7},{7,6},{8,9},{9,8},{10,11... | collective-permute-start | bytes 1376264 | tf_op jit(solution)/shard_map/ppermute | solution.py:11
  55.6 1.9 %bitcast_dynamic-update-slice_fusion.10 = bf16[8,320,896]{2,1,0:T(8,128)(2,1)} fusion(bf16[8,320,896]{2,1,0:T(8,128)(2,1)} %copy-done.4, s32[]{:T(128)S(6)} %select_n.164, bf16[320,896]{1,0:T(8,128)(2,1)} %collective-permute-done.1), kind=kLoop, calls=%fused_computation.42 | loop fusion | bytes 1146884 | tf_op jit(solution)/shard_map/dynamic_update_slice | solution.py:32
  57.5 1.9 %bitcast_dynamic-update-slice_fusion.9 = bf16[8,320,896]{2,1,0:T(8,128)(2,1)} fusion(bf16[8,320,896]{2,1,0:T(8,128)(2,1)} %bitcast_dynamic-update-slice_fusion.10, s32[]{:T(128)S(6)} %select_n.166, bf16[320,896]{1,0:T(8,128)(2,1)} %collective-permute-done.3), kind=kLoop, calls=%fused_computation.41 | loop fusion | bytes 1146884 | tf_op jit(solution)/shard_map/dynamic_update_slice | solution.py:32
  60.5 2.8 %collective-permute-start.10 = (bf16[320,896]{1,0:T(8,128)(2,1)S(1)}, bf16[320,896]{1,0:T(8,128)(2,1)S(1)}, u32[]{:S(2)}, u32[]{:S(2)}) collective-permute-start(bf16[320,896]{1,0:T(8,128)(2,1)S(1)} %copy-done.13), channel_id=1, source_target_pairs={{0,112},{16,0},{32,16},{48,32},{64,48},{80,64},{96,80},{112,96},{1... | collective-permute-start | bytes 1720328 | tf_op jit(solution)/shard_map/ppermute | solution.py:11
  64.5 1.1 bitcast_dynamic-update-slice_fusion.8
  65.7 6.5 %collective-permute-done.14 = bf16[512,448]{1,0:T(8,128)(2,1)S(1)} collective-permute-done((bf16[512,448]{1,0:T(8,128)(2,1)}, bf16[512,448]{1,0:T(8,128)(2,1)S(1)}, u32[]{:S(2)}, u32[]{:S(2)}) %collective-permute-start.14) | collective-permute-done | bytes 458784 | tf_op jit(solution)/shard_map/ppermute | solution.py:11
  72.2 2.3 %collective-permute-start.13 = (bf16[160,896]{1,0:T(8,128)(2,1)S(1)}, bf16[160,896]{1,0:T(8,128)(2,1)S(1)}, u32[]{:S(2)}, u32[]{:S(2)}) collective-permute-start(bf16[160,896]{1,0:T(8,128)(2,1)S(1)} %slice.35), channel_id=1, source_target_pairs={{0,112},{16,0},{32,16},{48,32},{64,48},{80,64},{96,80},{112,96},{1... | collective-permute-start | bytes 860168 | tf_op jit(solution)/shard_map/ppermute | solution.py:11
  74.7 1.3 collective-permute-done.12
  76.0 4.4 %collective-permute-done.13 = bf16[160,896]{1,0:T(8,128)(2,1)S(1)} collective-permute-done((bf16[160,896]{1,0:T(8,128)(2,1)S(1)}, bf16[160,896]{1,0:T(8,128)(2,1)S(1)}, u32[]{:S(2)}, u32[]{:S(2)}) %collective-permute-start.13) | collective-permute-done | bytes 286752 | tf_op jit(solution)/shard_map/ppermute | solution.py:11
  80.4 1.8 collective-permute-done.11
  83.7 1.3 collective-permute-start.15
  85.0 0.9 collective-permute-start.16
  85.8 1.8 %collective-permute-start.17 = (bf16[320,896]{1,0:T(8,128)(2,1)}, bf16[320,896]{1,0:T(8,128)(2,1)S(1)}, u32[]{:S(2)}, u32[]{:S(2)}) collective-permute-start(bf16[320,896]{1,0:T(8,128)(2,1)} %collective-permute-done.11), channel_id=1, source_target_pairs={{0,112},{16,0},{32,16},{48,32},{64,48},{80,64},{96,80},{112,96},{1... | collective-permute-start | bytes 1720328 | tf_op jit(solution)/shard_map/ppermute | solution.py:11
  87.8 1.1 bitcast_dynamic-update-slice_fusion.1
  88.9 1.1 bitcast_dynamic-update-slice_fusion
  90.1 1.6 bitcast_dynamic-update-slice_fusion.5
  91.7 2.9 %fusion.4 = f32[512,896]{1,0:T(8,128)S(1)} fusion(bf16[2560,896]{1,0:T(8,128)(2,1)S(1)} %bitcast.85, bf16[512,5120]{1,0:T(8,128)(2,1)S(1)} %bitcast.79, s32[]{:T(128)S(6)} %select_n.175), kind=kOutput, calls=%fused_computation.5 | convolution fusion | flops 2348810240 | bytes 9043972 | tf_op jit(solution)/shard_map/dot_general | solution.py:160
  94.6 4.2 %fusion.8 = f32[512,896]{1,0:T(8,128)} fusion(f32[512,896]{1,0:T(8,128)S(1)} %fusion.4, bf16[2560,896]{1,0:T(8,128)(2,1)S(1)} %bitcast.87, bf16[512,5120]{1,0:T(8,128)(2,1)S(1)} %bitcast.80, s32[]{:T(128)S(6)} %select_n.158), kind=kOutput, calls=%fused_computation.11 | convolution fusion | flops 2349268992 | bytes 10878980 | tf_op jit(solution)/shard_map/dot_general | solution.py:159
  98.8 6.1 %fusion = f32[512,896]{1,0:T(8,128)S(1)} fusion(bf16[2560,896]{1,0:T(8,128)(2,1)} %bitcast.86, bf16[512,5120]{1,0:T(8,128)(2,1)} %bitcast.81, s32[]{:T(128)S(6)} %select_n.175), kind=kOutput, calls=%fused_computation.1 | convolution fusion | flops 2348810240 | bytes 9043972 | tf_op jit(solution)/shard_map/dot_general | solution.py:160
  104.9 2.4 %fusion.56 = f32[512,64]{0,1:T(8,128)} fusion(bf16[512,5120]{1,0:T(8,128)(2,1)S(1)} %bitcast.82, bf16[64,5120]{1,0:T(8,128)(2,1)S(1)} %copy-done), kind=kOutput, calls=%fused_computation.103 | convolution fusion | flops 335544320 | bytes 6029312 | tf_op jit(solution)/shard_map/dot_general | solution.py:138
  107.8 2.9 %fusion.11 = f32[512,896]{1,0:T(8,128)S(1)} fusion(f32[512,896]{1,0:T(8,128)S(1)} %fusion, bf16[2560,896]{1,0:T(8,128)(2,1)S(1)} %bitcast.88, bf16[512,5120]{1,0:T(8,128)(2,1)S(1)} %bitcast.84, s32[]{:T(128)S(6)} %select_n.158), kind=kOutput, calls=%fused_computation.12 | convolution fusion | flops 2349268992 | bytes 10878980 | tf_op jit(solution)/shard_map/dot_general | solution.py:159
  112.1 0.8 add_add_fusion
  114.0 0.9 fusion.28
  119.1 11.7 %all-to-all-start = ((bf16[16,8,1024]{2,1,0:T(8,128)(2,1)}), bf16[16,8,1024]{2,1,0:T(8,128)(2,1)S(1)}, u32[]{:S(2)}, u32[]{:S(2)}) async-start(bf16[16,8,1024]{2,1,0:T(8,128)(2,1)} %pad_maximum_fusion.7), calls=%async_computation | async-start | bytes 524288 | tf_op jit(solution)/shard_map/all_to_all | solution.py:187
  131.2 9.1 %all-to-all-done = bf16[16,8,1024]{2,1,0:T(8,128)(2,1)S(1)} async-done(((bf16[16,8,1024]{2,1,0:T(8,128)(2,1)}), bf16[16,8,1024]{2,1,0:T(8,128)(2,1)S(1)}, u32[]{:S(2)}, u32[]{:S(2)}) %all-to-all-start) | async-done | bytes 262176 | tf_op jit(solution)/shard_map/all_to_all | solution.py:187
  141.9 4.9 %all-to-all-start.1 = ((bf16[16,16,512]{2,1,0:T(8,128)(2,1)}), bf16[16,16,512]{2,1,0:T(8,128)(2,1)S(1)}, u32[]{:S(2)}, u32[]{:S(2)}) async-start(bf16[16,16,512]{2,1,0:T(8,128)(2,1)} %broadcast_in_dim.73), calls=%async_computation.1 | async-start | bytes 524288 | tf_op jit(solution)/shard_map/all_to_all | solution.py:203
  147.2 8.5 %all-to-all-done.1 = bf16[16,16,512]{2,1,0:T(8,128)(2,1)S(1)} async-done(((bf16[16,16,512]{2,1,0:T(8,128)(2,1)}), bf16[16,16,512]{2,1,0:T(8,128)(2,1)S(1)}, u32[]{:S(2)}, u32[]{:S(2)}) %all-to-all-start.1) | async-done | bytes 262176 | tf_op jit(solution)/shard_map/all_to_all | solution.py:203
  156.3 12.1 %all_to_all.19 = f32[16,1,640]{2,1,0:T(1,128)S(1)} all-to-all(f32[16,1,640]{2,1,0:T(1,128)S(1)} %copy.24), channel_id=1, replica_groups=mesh['ylo'=2,'z'=8,'x'=4,'core'=2,'yhi'=2] {'x','core','yhi'}, dimensions={0} | all-to-all | bytes 81920 | tf_op jit(solution)/shard_map/all_to_all | solution.py:224
  (116 shorter events, 16.4 us)
Async XLA Ops:
  6.5 28.9 %copy-start = (bf16[64,5120]{1,0:T(8,128)(2,1)S(1)}, bf16[64,5120]{1,0:T(8,128)(2,1)}, u32[]{:S(2)}) copy-start(bf16[64,5120]{1,0:T(8,128)(2,1)} %param.15) | copy-start | bytes 1966084
  6.5 92.2 %all-gather.2.cloned.1.call-start = ((), (), s32[]{:S(2)}) async-start(), calls=%async_computation.3 | async-start | bytes 5898240 | tf_op jit(solution)/shard_map/all_gather | solution.py:52
  7.9 19.3 %collective-permute-start = (bf16[320,896]{1,0:T(8,128)(2,1)S(1)}, bf16[320,896]{1,0:T(8,128)(2,1)}, u32[]{:S(2)}, u32[]{:S(2)}) collective-permute-start(bf16[320,896]{1,0:T(8,128)(2,1)S(1)} %pad_maximum_fusion.2), channel_id=1, source_target_pairs={{0,16},{16,32},{32,48},{48,64},{64,80},{80,96},{96,112},{112,0},{1... | collective-permute-start | bytes 1720328 | tf_op jit(solution)/shard_map/ppermute | solution.py:11
  10.4 16.8 %collective-permute-start.1 = (bf16[320,896]{1,0:T(8,128)(2,1)S(1)}, bf16[320,896]{1,0:T(8,128)(2,1)}, u32[]{:S(2)}, u32[]{:S(2)}) collective-permute-start(bf16[320,896]{1,0:T(8,128)(2,1)S(1)} %pad_maximum_fusion.2), channel_id=1, source_target_pairs={{0,112},{16,0},{32,16},{48,32},{64,48},{80,64},{96,80},{112,96},{1... | collective-permute-start | bytes 1720328 | tf_op jit(solution)/shard_map/ppermute | solution.py:11
  14.4 13.6 %collective-permute-start.2 = (bf16[320,896]{1,0:T(8,128)(2,1)S(1)}, bf16[320,896]{1,0:T(8,128)(2,1)S(1)}, u32[]{:S(2)}, u32[]{:S(2)}) collective-permute-start(bf16[320,896]{1,0:T(8,128)(2,1)S(1)} %pad_maximum_fusion.2), channel_id=1, source_target_pairs={{0,128},{128,0},{1,129},{129,1},{2,130},{130,2},{3,131},{131,3},{4... | collective-permute-start | bytes 1720328 | tf_op jit(solution)/shard_map/ppermute | solution.py:11
  15.7 6.4 %copy-start.10 = (bf16[8,32,896]{2,1,0:T(8,128)(2,1)S(1)}, bf16[8,32,896]{2,1,0:T(8,128)(2,1)}, u32[]{:S(2)}) copy-start(bf16[8,32,896]{2,1,0:T(8,128)(2,1)} %param.12) | copy-start | bytes 1376260
  15.7 6.4 %copy-start.11 = (bf16[8,32,896]{2,1,0:T(8,128)(2,1)S(1)}, bf16[8,32,896]{2,1,0:T(8,128)(2,1)}, u32[]{:S(2)}) copy-start(bf16[8,32,896]{2,1,0:T(8,128)(2,1)} %param.10) | copy-start | bytes 1376260
  24.4 11.1 %copy-start.1 = (bf16[8,64,5120]{2,1,0:T(8,128)(2,1)S(1)}, bf16[8,64,5120]{2,1,0:T(8,128)(2,1)}, u32[]{:S(2)}) copy-start(bf16[8,64,5120]{2,1,0:T(8,128)(2,1)} %pad_maximum_fusion) | copy-start | bytes 15728644
  28.0 9.8 %copy-start.12 = (bf16[320,896]{1,0:T(8,128)(2,1)}, bf16[320,896]{1,0:T(8,128)(2,1)S(1)}, u32[]{:S(2)}) copy-start(bf16[320,896]{1,0:T(8,128)(2,1)S(1)} %collective-permute-done.2) | copy-start | bytes 1720324
  28.0 14.2 %collective-permute-start.3 = (bf16[320,896]{1,0:T(8,128)(2,1)}, bf16[320,896]{1,0:T(8,128)(2,1)}, u32[]{:S(2)}, u32[]{:S(2)}) collective-permute-start(bf16[320,896]{1,0:T(8,128)(2,1)} %collective-permute-done), channel_id=1, source_target_pairs={{0,16},{16,32},{32,48},{48,64},{64,80},{80,96},{96,112},{112,0},{1... | collective-permute-start | bytes 1720328 | tf_op jit(solution)/shard_map/ppermute | solution.py:11
  28.0 14.2 %collective-permute-start.4 = (bf16[320,896]{1,0:T(8,128)(2,1)}, bf16[320,896]{1,0:T(8,128)(2,1)}, u32[]{:S(2)}, u32[]{:S(2)}) collective-permute-start(bf16[320,896]{1,0:T(8,128)(2,1)} %collective-permute-done.1), channel_id=1, source_target_pairs={{0,112},{16,0},{32,16},{48,32},{64,48},{80,64},{96,80},{112,96},{1... | collective-permute-start | bytes 1720328 | tf_op jit(solution)/shard_map/ppermute | solution.py:11
  30.7 15.3 %collective-permute-start.5 = (bf16[1,64,5120]{2,1,0:T(8,128)(2,1)S(1)}, bf16[1,64,5120]{2,1,0:T(8,128)(2,1)S(1)}, u32[]{:S(2)}, u32[]{:S(2)}) collective-permute-start(bf16[1,64,5120]{2,1,0:T(8,128)(2,1)S(1)} %pad_maximum_fusion.1), channel_id=1, source_target_pairs={{0,1},{1,0},{2,3},{3,2},{4,5},{5,4},{6,7},{7,6},{8,9},{9,8},{10,11... | collective-permute-start | bytes 1966088 | tf_op jit(solution)/shard_map/ppermute | solution.py:11
  35.4 2.4 %copy-start.4 = (bf16[8,320,896]{2,1,0:T(8,128)(2,1)}, bf16[8,320,896]{2,1,0:T(8,128)(2,1)S(1)}, u32[]{:S(2)}) copy-start(bf16[8,320,896]{2,1,0:T(8,128)(2,1)S(1)} %bitcast_dynamic-update-slice_fusion.11) | copy-start | bytes 13762564
  42.2 17.6 %copy-start.13 = (bf16[320,896]{1,0:T(8,128)(2,1)S(1)}, bf16[320,896]{1,0:T(8,128)(2,1)}, u32[]{:S(2)}) copy-start(bf16[320,896]{1,0:T(8,128)(2,1)} %copy-done.12) | copy-start | bytes 1720324
  46.0 0.8 copy-start.9
  47.0 12.6 %collective-permute-start.6 = (bf16[320,896]{1,0:T(8,128)(2,1)}, bf16[320,896]{1,0:T(8,128)(2,1)S(1)}, u32[]{:S(2)}, u32[]{:S(2)}) collective-permute-start(bf16[320,896]{1,0:T(8,128)(2,1)} %collective-permute-done.3), channel_id=1, source_target_pairs={{0,16},{16,32},{32,48},{48,64},{64,80},{80,96},{96,112},{112,0},{1... | collective-permute-start | bytes 1720328 | tf_op jit(solution)/shard_map/ppermute | solution.py:11
  47.1 12.7 %collective-permute-start.8 = (bf16[320,896]{1,0:T(8,128)(2,1)}, bf16[320,896]{1,0:T(8,128)(2,1)}, u32[]{:S(2)}, u32[]{:S(2)}) collective-permute-start(bf16[320,896]{1,0:T(8,128)(2,1)} %collective-permute-done.3), channel_id=1, source_target_pairs={{0,128},{128,0},{1,129},{129,1},{2,130},{130,2},{3,131},{131,3},{4... | collective-permute-start | bytes 1720328 | tf_op jit(solution)/shard_map/ppermute | solution.py:11
  48.5 11.3 %collective-permute-start.7 = (bf16[320,896]{1,0:T(8,128)(2,1)}, bf16[320,896]{1,0:T(8,128)(2,1)S(1)}, u32[]{:S(2)}, u32[]{:S(2)}) collective-permute-start(bf16[320,896]{1,0:T(8,128)(2,1)} %collective-permute-done.4), channel_id=1, source_target_pairs={{0,112},{16,0},{32,16},{48,32},{64,48},{80,64},{96,80},{112,96},{1... | collective-permute-start | bytes 1720328 | tf_op jit(solution)/shard_map/ppermute | solution.py:11
  52.9 19.3 %collective-permute-start.14 = (bf16[512,448]{1,0:T(8,128)(2,1)}, bf16[512,448]{1,0:T(8,128)(2,1)S(1)}, u32[]{:S(2)}, u32[]{:S(2)}) collective-permute-start(bf16[512,448]{1,0:T(8,128)(2,1)} %bitcast.93), channel_id=1, source_target_pairs={{0,1},{1,0},{2,3},{3,2},{4,5},{5,4},{6,7},{7,6},{8,9},{9,8},{10,11... | collective-permute-start | bytes 1376264 | tf_op jit(solution)/shard_map/ppermute | solution.py:11
  59.5 5.0 %copy-start.5 = (bf16[8,320,896]{2,1,0:T(8,128)(2,1)S(1)}, bf16[8,320,896]{2,1,0:T(8,128)(2,1)}, u32[]{:S(2)}) copy-start(bf16[8,320,896]{2,1,0:T(8,128)(2,1)} %bitcast_dynamic-update-slice_fusion.9) | copy-start | bytes 13762564
  59.8 20.6 %collective-permute-start.9 = (bf16[320,896]{1,0:T(8,128)(2,1)S(1)}, bf16[320,896]{1,0:T(8,128)(2,1)S(1)}, u32[]{:S(2)}, u32[]{:S(2)}) collective-permute-start(bf16[320,896]{1,0:T(8,128)(2,1)S(1)} %copy-done.13), channel_id=1, source_target_pairs={{0,16},{16,32},{32,48},{48,64},{64,80},{80,96},{96,112},{112,0},{1... | collective-permute-start | bytes 1720328 | tf_op jit(solution)/shard_map/ppermute | solution.py:11
  60.5 19.9 %collective-permute-start.10 = (bf16[320,896]{1,0:T(8,128)(2,1)S(1)}, bf16[320,896]{1,0:T(8,128)(2,1)S(1)}, u32[]{:S(2)}, u32[]{:S(2)}) collective-permute-start(bf16[320,896]{1,0:T(8,128)(2,1)S(1)} %copy-done.13), channel_id=1, source_target_pairs={{0,112},{16,0},{32,16},{48,32},{64,48},{80,64},{96,80},{112,96},{1... | collective-permute-start | bytes 1720328 | tf_op jit(solution)/shard_map/ppermute | solution.py:11
  63.3 18.8 %collective-permute-start.11 = (bf16[320,896]{1,0:T(8,128)(2,1)}, bf16[320,896]{1,0:T(8,128)(2,1)}, u32[]{:S(2)}, u32[]{:S(2)}) collective-permute-start(bf16[320,896]{1,0:T(8,128)(2,1)} %collective-permute-done.4), channel_id=1, source_target_pairs={{0,128},{128,0},{1,129},{129,1},{2,130},{130,2},{3,131},{131,3},{4... | collective-permute-start | bytes 1720328 | tf_op jit(solution)/shard_map/ppermute | solution.py:11
  63.7 12.2 %collective-permute-start.12 = (bf16[160,896]{1,0:T(8,128)(2,1)S(1)}, bf16[160,896]{1,0:T(8,128)(2,1)S(1)}, u32[]{:S(2)}, u32[]{:S(2)}) collective-permute-start(bf16[160,896]{1,0:T(8,128)(2,1)S(1)} %slice.34), channel_id=1, source_target_pairs={{0,16},{16,32},{32,48},{48,64},{64,80},{80,96},{96,112},{112,0},{1... | collective-permute-start | bytes 860168 | tf_op jit(solution)/shard_map/ppermute | solution.py:11
  63.8 27.8 %slice-start = ((s8[5242880]{0:T(1024)(128)(4,1)}), s8[1048576]{0:T(1024)(128)(4,1)S(1)}, s32[]{:S(2)}) async-start(s8[5242880]{0:T(1024)(128)(4,1)} %bitcast.77), calls=%async_computation.4 | async-start | bytes 2097152
  65.7 26.0 %slice-start.1 = ((s8[5242880]{0:T(1024)(128)(4,1)}), s8[4194304]{0:T(1024)(128)(4,1)S(1)}, s32[]{:S(2)}) async-start(s8[5242880]{0:T(1024)(128)(4,1)} %bitcast.77), calls=%async_computation.5 | async-start | bytes 8388608
  72.2 19.4 %copy-start.17 = (bf16[512,448]{1,0:T(8,128)(2,1)}, bf16[512,448]{1,0:T(8,128)(2,1)S(1)}, u32[]{:S(2)}) copy-start(bf16[512,448]{1,0:T(8,128)(2,1)S(1)} %collective-permute-done.14) | copy-start | bytes 1376260
  72.2 8.2 %collective-permute-start.13 = (bf16[160,896]{1,0:T(8,128)(2,1)S(1)}, bf16[160,896]{1,0:T(8,128)(2,1)S(1)}, u32[]{:S(2)}, u32[]{:S(2)}) collective-permute-start(bf16[160,896]{1,0:T(8,128)(2,1)S(1)} %slice.35), channel_id=1, source_target_pairs={{0,112},{16,0},{32,16},{48,32},{64,48},{80,64},{96,80},{112,96},{1... | collective-permute-start | bytes 860168 | tf_op jit(solution)/shard_map/ppermute | solution.py:11
  83.7 27.1 %collective-permute-start.15 = (bf16[320,896]{1,0:T(8,128)(2,1)}, bf16[320,896]{1,0:T(8,128)(2,1)S(1)}, u32[]{:S(2)}, u32[]{:S(2)}) collective-permute-start(bf16[320,896]{1,0:T(8,128)(2,1)} %constant_dynamic-update-slice_fusion), channel_id=1, source_target_pairs={{0,128},{128,0},{1,129},{129,1},{2,130},{130,2},{3,131},{131,3},{4... | collective-permute-start | bytes 1720328 | tf_op jit(solution)/shard_map/ppermute | solution.py:11
  85.0 25.8 %collective-permute-start.16 = (bf16[320,896]{1,0:T(8,128)(2,1)}, bf16[320,896]{1,0:T(8,128)(2,1)S(1)}, u32[]{:S(2)}, u32[]{:S(2)}) collective-permute-start(bf16[320,896]{1,0:T(8,128)(2,1)} %collective-permute-done.8), channel_id=1, source_target_pairs={{0,16},{16,32},{32,48},{48,64},{64,80},{80,96},{96,112},{112,0},{1... | collective-permute-start | bytes 1720328 | tf_op jit(solution)/shard_map/ppermute | solution.py:11
  85.8 24.9 %collective-permute-start.17 = (bf16[320,896]{1,0:T(8,128)(2,1)}, bf16[320,896]{1,0:T(8,128)(2,1)S(1)}, u32[]{:S(2)}, u32[]{:S(2)}) collective-permute-start(bf16[320,896]{1,0:T(8,128)(2,1)} %collective-permute-done.11), channel_id=1, source_target_pairs={{0,112},{16,0},{32,16},{48,32},{64,48},{80,64},{96,80},{112,96},{1... | collective-permute-start | bytes 1720328 | tf_op jit(solution)/shard_map/ppermute | solution.py:11
  90.1 4.5 %copy-start.3 = (bf16[8,320,896]{2,1,0:T(8,128)(2,1)}, bf16[8,320,896]{2,1,0:T(8,128)(2,1)S(1)}, u32[]{:S(2)}) copy-start(bf16[8,320,896]{2,1,0:T(8,128)(2,1)S(1)} %bitcast_dynamic-update-slice_fusion) | copy-start | bytes 13762564
  91.7 2.9 %copy-start.6 = (bf16[8,320,896]{2,1,0:T(8,128)(2,1)}, bf16[8,320,896]{2,1,0:T(8,128)(2,1)S(1)}, u32[]{:S(2)}) copy-start(bf16[8,320,896]{2,1,0:T(8,128)(2,1)S(1)} %bitcast_dynamic-update-slice_fusion.5) | copy-start | bytes 13762564
  98.8 6.1 %copy-start.2 = (bf16[8,64,5120]{2,1,0:T(8,128)(2,1)S(1)}, bf16[8,64,5120]{2,1,0:T(8,128)(2,1)}, u32[]{:S(2)}) copy-start(bf16[8,64,5120]{2,1,0:T(8,128)(2,1)} %all-gather.2.cloned.1.call-done) | copy-start | bytes 15728644
  104.9 2.9 %copy-start.7 = (bf16[8,320,896]{2,1,0:T(8,128)(2,1)S(1)}, bf16[8,320,896]{2,1,0:T(8,128)(2,1)}, u32[]{:S(2)}) copy-start(bf16[8,320,896]{2,1,0:T(8,128)(2,1)} %copy-done.6) | copy-start | bytes 13762564
  112.1 1.0 copy-start.18
  112.1 1.0 copy-start.19
  113.1 0.9 copy-start.20
  114.0 2.2 %copy-start.8 = (f32[512,896]{1,0:T(8,128)S(1)}, f32[512,896]{1,0:T(8,128)}, u32[]{:S(2)}) copy-start(f32[512,896]{1,0:T(8,128)} %fusion.8) | copy-start | bytes 5505028
  116.2 1.0 copy-start.16
  117.7 13.2 %copy-start.14 = (f32[512,64]{0,1:T(8,128)S(1)}, f32[512,64]{0,1:T(8,128)}, u32[]{:S(2)}) copy-start(f32[512,64]{0,1:T(8,128)} %fusion.55) | copy-start | bytes 393220
  117.7 13.2 %copy-start.15 = (f32[512,64]{0,1:T(8,128)S(1)}, f32[512,64]{0,1:T(8,128)}, u32[]{:S(2)}) copy-start(f32[512,64]{0,1:T(8,128)} %fusion.56) | copy-start | bytes 393220
  119.1 21.1 %all-to-all-start = ((bf16[16,8,1024]{2,1,0:T(8,128)(2,1)}), bf16[16,8,1024]{2,1,0:T(8,128)(2,1)S(1)}, u32[]{:S(2)}, u32[]{:S(2)}) async-start(bf16[16,8,1024]{2,1,0:T(8,128)(2,1)} %pad_maximum_fusion.7), calls=%async_computation | async-start | bytes 524288 | tf_op jit(solution)/shard_map/all_to_all | solution.py:187
  141.9 13.8 %all-to-all-start.1 = ((bf16[16,16,512]{2,1,0:T(8,128)(2,1)}), bf16[16,16,512]{2,1,0:T(8,128)(2,1)S(1)}, u32[]{:S(2)}, u32[]{:S(2)}) async-start(bf16[16,16,512]{2,1,0:T(8,128)(2,1)} %broadcast_in_dim.73), calls=%async_computation.1 | async-start | bytes 524288 | tf_op jit(solution)/shard_map/all_to_all | solution.py:203
Sparse Core Ops, SparseCore 0:
  47.0 41.8 all-gather.1

commit v11 on v10

--- a/solution.py
+++ b/solution.py
@@ -11,7 +11,7 @@
     return lax.ppermute(value, axis, [(i, (i + step) % size) for i in range(size)])
 
 
-def gathered(weight, piece, cot, early, inner_factor):
+def gathered(weight, piece, cot, early, inner_factor, this_product):
     barrier = lax.optimization_barrier
     n_z = lax.axis_size("z")
     z = lax.axis_index("z")
@@ -52,8 +52,21 @@
     partner = lax.all_gather(here, ("x", "core"), axis=0, tiled=True)
     a3, b3, oa2, o0, b2 = barrier((up(a2), down(b2), across(a2), o0, b2))
     other_cot = shift(cot, "yhi", 1)
-    oa1, ob1, ob2, a4, b4, oa2, other_cot = barrier(
-        (up(o0), down(o0), across(b2), up(a3[:half]), down(b3[half:]), oa2, other_cot)
+    flat = (n_z * weight.shape[0], -1)
+    this_row = placed(this_row, ((1, b1), (n_z - 2, a2), (2, b2), (n_z - 3, a3), (3, b3)))
+    this_row = this_row.reshape(flat)
+    own_sum = this_product(early[0], this_row)
+    oa1, ob1, ob2, a4, b4, oa2, other_cot, own_sum = barrier(
+        (
+            up(o0),
+            down(o0),
+            across(b2),
+            up(a3[:half]),
+            down(b3[half:]),
+            oa2,
+            other_cot,
+            own_sum,
+        )
     )
     a4 = jnp.concatenate((a4, b4), axis=0)
     last = (
@@ -61,16 +74,13 @@
         (up(oa2), (z + n_z - 3) % n_z),
         (down(ob2), (z + 3) % n_z),
     )
-    this_row = placed(
-        this_row,
-        ((1, b1), (n_z - 2, a2), (2, b2), (n_z - 3, a3), (3, b3), (n_z // 2, a4)),
-    )
     other_row = placed(
-        jnp.zeros_like(this_row),
+        jnp.zeros((n_z,) + weight.shape, weight.dtype),
         ((0, o0), (n_z - 1, oa1), (1, ob1), (n_z - 2, oa2), (2, ob2)),
-    )
-    flat = (n_z * weight.shape[0], -1)
-    return this_row.reshape(flat), other_row.reshape(flat), last, other_cot, partner, early, own_factor
+    ).reshape(flat)
+    own_sum, other_row, partner = barrier((own_sum, other_row, partner))
+    this = (this_row, own_sum, (a4, far_z))
+    return this, other_row, last, other_cot, partner, early, own_factor
 
 
 def projected(pre, cotangent, gate_projection, up_projection):
@@ -142,28 +152,42 @@
             preferred_element_type=F32,
         )
 
-    this_row, other_row, last, other_cot, other, (own, own_cot), own_factor = gathered(
-        weight, piece, cotangents(1 - half_index), (own, own_cot), inner_factor
-    )
+    def half_of(rows, side, depth):
+        return lax.dynamic_slice_in_dim(rows.reshape(-1, width), side * depth, depth, 1)
+
+    def this_product(rows, this_row):
+        flat = half_of(rows, row_index, this_row.shape[0])
+        return jnp.dot(flat, this_row, preferred_element_type=F32)
+
+    this, other_row, last, other_cot, other, (own, own_cot), own_factor = gathered(
+        weight, piece, cotangents(1 - half_index), (own, own_cot), inner_factor, this_product
+    )
+    this_row, own_sum, far = this
     gate_proj = columns(gate_projection, half_index)
     up_proj = columns(up_projection, half_index)
 
     depth = this_row.shape[0]
     shard_depth = weight.shape[0]
-    pres = []
-    chunks = []
-    for rows in (own, other):
-        flat = rows.reshape(-1, width)
-        this_flat = lax.dynamic_slice_in_dim(flat, row_index * depth, depth, 1)
-        other_flat = lax.dynamic_slice_in_dim(flat, (1 - row_index) * depth, depth, 1)
-        pre = jnp.dot(this_flat, this_row, preferred_element_type=F32)
-        pres.append(pre + jnp.dot(other_flat, other_row, preferred_element_type=F32))
-        chunks.append(
-            [
-                lax.dynamic_slice_in_dim(other_flat, place * shard_depth, shard_depth, 1)
-                for _, place in last
-            ]
-        )
+
+    def chunk(rows, side, place):
+        return lax.dynamic_slice_in_dim(
+            rows.reshape(-1, width), side * depth + place * shard_depth, shard_depth, 1
+        )
+
+    def rest(rows, pre):
+        pre = pre + jnp.dot(
+            half_of(rows, 1 - row_index, depth), other_row, preferred_element_type=F32
+        )
+        return pre + jnp.dot(
+            chunk(rows, row_index, far[1]), far[0], preferred_element_type=F32
+        )
+
+    own_pre = rest(own, own_sum)
+    own_pre, other = lax.optimization_barrier((own_pre, other))
+    pres = (own_pre, rest(other, this_product(other, this_row)))
+    chunks = [[chunk(rows, 1 - row_index, at) for _, at in last] for rows in (own, other)]
+    factors = (own_factor, inner_factor(other))
+    shards = [shard for shard, _ in last]
     factors = (own_factor, inner_factor(other))
     shards = [shard for shard, _ in last]
     pres, factors, chunks, shards = lax.optimization_barrier((pres, factors, chunks, shards))

time: 178 us -> 184 us (1.034)
  waiting for transfers between devices: 43.7 us -> 34.9 us
  matrix products: 28 us -> 34.9 us
  local copies, waits for them, and re-layouts: 21.3 us -> 27.1 us
  starting transfers between devices: 47.1 us -> 49.1 us
    ppermute x18, waiting for transfers between devices: 26.1 us -> 17.2 us  [shift(): lax.ppermute(value, axis, [(i, (i + step) % size) for i in range(size)])]
    dot_general x4 -> x6, matrix products: 16 us -> 23.7 us  [the longest x2 11.5 us: rest(): jnp.dot(half_of(rows, 1 - row_index, depth), other_row, preferred_element...]
    dynamic_update_slice x13 -> x12, local copies, waits for them, and re-layouts: 10.4 us -> 14.1 us  [placed(): lax.dynamic_update_slice(result, shard[None], ((z + offset) % n_z, 0, 0))]
    all_to_all x1, starting transfers between devices: 11.7 us -> 14.8 us  [body(): swapped = lax.all_to_all(part, dq, 0, 0, tiled=True)]
    another operation x2, local copies, waits for them, and re-layouts: 1.16 us -> 3.23 us
  transfers between devices with their start and end apart: 21 -> 21, of which waited for: 12 -> 9; matrix products, arithmetic and copies ran while one was open for 26% -> 32% of each run, Pallas kernels for 0% -> 0%
where the time goes in v11:
time: 184 us; the launch traced here: 183 us
  starting transfers between devices  49.1 us (27%)
  waiting for transfers between devices  34.9 us (19%)
  matrix products  34.9 us (19%)
  local copies, waits for them, and re-layouts  27.1 us (15%)
  between operations  14.8 us (8%)
  blocking collectives  12.5 us (7%)
  other arithmetic  10.1 us (5%)
    ppermute x18, starting transfers between devices, shift(): lax.ppermute(value, axis, [(i, (i + step) % size) for i in range(size)])  28.8 us
    ppermute x18, waiting for transfers between devices, shift(): lax.ppermute(value, axis, [(i, (i + step) % size) for i in range(size)])  17.2 us
    all_to_all x1, starting transfers between devices, body(): swapped = lax.all_to_all(part, dq, 0, 0, tiled=True)  14.8 us
    dynamic_update_slice x12, local copies, waits for them, and re-layouts, placed(): lax.dynamic_update_slice(result, shard[None], ((z + offset) % n_z, 0, 0))  14.1 us
    all_to_all x1, blocking collectives, body(): received = lax.all_to_all(payload, dq, 0, 0, tiled=True)  12.5 us
    dot_general x2, matrix products, rest(): jnp.dot(half_of(rows, 1 - row_index, depth), other_row, preferred_element...  11.5 us
    dot_general x2, matrix products, this_product(): return jnp.dot(flat, this_row, preferred_element_type=F32)  9.41 us
    all_to_all x1, waiting for transfers between devices, body(): swapped = lax.all_to_all(part, dq, 0, 0, tiled=True)  9.11 us
  transfers between devices with their start and end apart: 21, of which 9 were waited for; matrix products, arithmetic and copies ran while one was open for 32% of the time, Pallas kernels for 0%

profile of v11, /device:TPU:1, one launch (start us, length us, event | category | flops | bytes accessed | tf_op | source)
XLA Modules:
  0.0 183.3 jit_solution(14142622141669299622)
XLA Ops:
  6.5 1.3 pad_maximum_fusion.2
  7.9 2.5 %collective-permute-start = (bf16[320,896]{1,0:T(8,128)(2,1)S(1)}, bf16[320,896]{1,0:T(8,128)(2,1)}, u32[]{:S(2)}, u32[]{:S(2)}) collective-permute-start(bf16[320,896]{1,0:T(8,128)(2,1)S(1)} %pad_maximum_fusion.2), channel_id=1, source_target_pairs={{0,16},{16,32},{32,48},{48,64},{64,80},{80,96},{96,112},{112,0},{1... | collective-permute-start | bytes 1720328 | tf_op jit(solution)/shard_map/ppermute | solution.py:11
  10.4 4.0 %collective-permute-start.1 = (bf16[320,896]{1,0:T(8,128)(2,1)S(1)}, bf16[320,896]{1,0:T(8,128)(2,1)}, u32[]{:S(2)}, u32[]{:S(2)}) collective-permute-start(bf16[320,896]{1,0:T(8,128)(2,1)S(1)} %pad_maximum_fusion.2), channel_id=1, source_target_pairs={{0,112},{16,0},{32,16},{48,32},{64,48},{80,64},{96,80},{112,96},{1... | collective-permute-start | bytes 1720328 | tf_op jit(solution)/shard_map/ppermute | solution.py:11
  14.4 1.3 collective-permute-start.2
  15.7 5.3 %pad_maximum_fusion = bf16[8,64,5120]{2,1,0:T(8,128)(2,1)} fusion(bf16[8,32,5120]{2,1,0:T(8,128)(2,1)} %param.11, bf16[8,32,5120]{2,1,0:T(8,128)(2,1)} %param.9), kind=kLoop, calls=%fused_computation | loop fusion | flops 10485760 | bytes 10485760 | tf_op jit(solution)/shard_map/concatenate | solution.py:133
  21.0 1.1 constant_dynamic-slice_fusion.8
  22.6 0.8 pad_maximum_fusion.3
  23.5 0.9 pad_maximum_fusion.4
  24.4 2.7 %collective-permute-done = bf16[320,896]{1,0:T(8,128)(2,1)} collective-permute-done((bf16[320,896]{1,0:T(8,128)(2,1)S(1)}, bf16[320,896]{1,0:T(8,128)(2,1)}, u32[]{:S(2)}, u32[]{:S(2)}) %collective-permute-start) | collective-permute-done | bytes 573472 | tf_op jit(solution)/shard_map/ppermute | solution.py:11
  27.2 0.8 collective-permute-done.2
  28.0 2.7 %collective-permute-start.4 = (bf16[320,896]{1,0:T(8,128)(2,1)}, bf16[320,896]{1,0:T(8,128)(2,1)}, u32[]{:S(2)}, u32[]{:S(2)}) collective-permute-start(bf16[320,896]{1,0:T(8,128)(2,1)} %collective-permute-done.1), channel_id=1, source_target_pairs={{0,112},{16,0},{32,16},{48,32},{64,48},{80,64},{96,80},{112,96},{1... | collective-permute-start | bytes 1720328 | tf_op jit(solution)/shard_map/ppermute | solution.py:11
  30.7 2.9 %collective-permute-start.5 = (bf16[1,64,5120]{2,1,0:T(8,128)(2,1)S(1)}, bf16[1,64,5120]{2,1,0:T(8,128)(2,1)S(1)}, u32[]{:S(2)}, u32[]{:S(2)}) collective-permute-start(bf16[1,64,5120]{2,1,0:T(8,128)(2,1)S(1)} %pad_maximum_fusion.1), channel_id=1, source_target_pairs={{0,1},{1,0},{2,3},{3,2},{4,5},{5,4},{6,7},{7,6},{8,9},{9,8},{10,11... | collective-permute-start | bytes 1966088 | tf_op jit(solution)/shard_map/ppermute | solution.py:11
  34.3 1.1 bitcast_dynamic-update-slice_fusion.10
  35.4 2.4 %fusion.53 = f32[512,64]{0,1:T(8,128)} fusion(bf16[512,5120]{1,0:T(8,128)(2,1)S(1)} %bitcast.78, bf16[64,5120]{1,0:T(8,128)(2,1)S(1)} %copy-done), kind=kOutput, calls=%fused_computation.105 | convolution fusion | flops 335544320 | bytes 6029312 | tf_op jit(solution)/shard_map/dot_general | solution.py:148
  37.8 4.2 %collective-permute-done.3 = bf16[320,896]{1,0:T(8,128)(2,1)S(1)} collective-permute-done((bf16[320,896]{1,0:T(8,128)(2,1)}, bf16[320,896]{1,0:T(8,128)(2,1)S(1)}, u32[]{:S(2)}, u32[]{:S(2)}) %collective-permute-start.3) | collective-permute-done | bytes 573472 | tf_op jit(solution)/shard_map/ppermute | solution.py:11
  42.1 4.0 %collective-permute-done.5 = bf16[1,64,5120]{2,1,0:T(8,128)(2,1)S(1)} collective-permute-done((bf16[1,64,5120]{2,1,0:T(8,128)(2,1)S(1)}, bf16[1,64,5120]{2,1,0:T(8,128)(2,1)S(1)}, u32[]{:S(2)}, u32[]{:S(2)}) %collective-permute-start.5) | collective-permute-done | bytes 655392 | tf_op jit(solution)/shard_map/ppermute | solution.py:11
  46.0 0.9 copy-done.7
  47.1 1.4 collective-permute-start.8
  48.5 2.6 %collective-permute-start.7 = (bf16[320,896]{1,0:T(8,128)(2,1)}, bf16[320,896]{1,0:T(8,128)(2,1)S(1)}, u32[]{:S(2)}, u32[]{:S(2)}) collective-permute-start(bf16[320,896]{1,0:T(8,128)(2,1)} %collective-permute-done.4), channel_id=1, source_target_pairs={{0,112},{16,0},{32,16},{48,32},{64,48},{80,64},{96,80},{112,96},{1... | collective-permute-start | bytes 1720328 | tf_op jit(solution)/shard_map/ppermute | solution.py:11
  51.1 2.7 %constant_dynamic-slice_fusion.3 = (bf16[512,320]{1,0:T(8,128)(2,1)S(1)}, bf16[512,320]{1,0:T(8,128)(2,1)}, bf16[512,320]{1,0:T(8,128)(2,1)}) fusion(bf16[512,5120]{1,0:T(8,128)(2,1)} %bitcast.75, s32[]{:T(128)S(6)} %select_n.169, s32[]{:T(128)S(6)} %select_n.168, s32[]{:T(128)S(6)} %select_n.167), kind=kLoop, calls=%fused_computation.82 | loop fusion | bytes 1966092 | tf_op jit(solution)/shard_map/dynamic_slice | solution.py:173
  53.8 2.6 %collective-permute-start.14 = (bf16[512,448]{1,0:T(8,128)(2,1)}, bf16[512,448]{1,0:T(8,128)(2,1)S(1)}, u32[]{:S(2)}, u32[]{:S(2)}) collective-permute-start(bf16[512,448]{1,0:T(8,128)(2,1)} %bitcast.95), channel_id=1, source_target_pairs={{0,1},{1,0},{2,3},{3,2},{4,5},{5,4},{6,7},{7,6},{8,9},{9,8},{10,11... | collective-permute-start | bytes 1376264 | tf_op jit(solution)/shard_map/ppermute | solution.py:11
  56.4 1.9 %bitcast_dynamic-update-slice_fusion.9 = bf16[8,320,896]{2,1,0:T(8,128)(2,1)} fusion(bf16[8,320,896]{2,1,0:T(8,128)(2,1)} %copy-done.3, s32[]{:T(128)S(6)} %select_n.155, bf16[320,896]{1,0:T(8,128)(2,1)} %collective-permute-done.1), kind=kLoop, calls=%fused_computation.41 | loop fusion | bytes 1146884 | tf_op jit(solution)/shard_map/dynamic_update_slice | solution.py:32
  58.4 0.9 bitcast_dynamic-update-slice_fusion.8
  59.8 3.3 %collective-permute-start.10 = (bf16[320,896]{1,0:T(8,128)(2,1)}, bf16[320,896]{1,0:T(8,128)(2,1)S(1)}, u32[]{:S(2)}, u32[]{:S(2)}) collective-permute-start(bf16[320,896]{1,0:T(8,128)(2,1)} %copy-done.10), channel_id=1, source_target_pairs={{0,112},{16,0},{32,16},{48,32},{64,48},{80,64},{96,80},{112,96},{1... | collective-permute-start | bytes 1720328 | tf_op jit(solution)/shard_map/ppermute | solution.py:11
  63.4 2.0 %bitcast_dynamic-update-slice_fusion.7 = bf16[8,320,896]{2,1,0:T(8,128)(2,1)} fusion(bf16[8,320,896]{2,1,0:T(8,128)(2,1)} %bitcast_dynamic-update-slice_fusion.8, s32[]{:T(128)S(6)} %select_n.159, bf16[320,896]{1,0:T(8,128)(2,1)} %collective-permute-done.4), kind=kLoop, calls=%fused_computation.39 | loop fusion | bytes 1146884 | tf_op jit(solution)/shard_map/dynamic_update_slice | solution.py:32
  65.4 0.9 bitcast_dynamic-update-slice_fusion.6
  66.2 0.9 bitcast_dynamic-update-slice_fusion.5
  67.2 4.9 %collective-permute-done.14 = bf16[512,448]{1,0:T(8,128)(2,1)S(1)} collective-permute-done((bf16[512,448]{1,0:T(8,128)(2,1)}, bf16[512,448]{1,0:T(8,128)(2,1)S(1)}, u32[]{:S(2)}, u32[]{:S(2)}) %collective-permute-start.14) | collective-permute-done | bytes 458784 | tf_op jit(solution)/shard_map/ppermute | solution.py:11
  72.1 2.3 %collective-permute-start.13 = (bf16[160,896]{1,0:T(8,128)(2,1)S(1)}, bf16[160,896]{1,0:T(8,128)(2,1)S(1)}, u32[]{:S(2)}, u32[]{:S(2)}) collective-permute-start(bf16[160,896]{1,0:T(8,128)(2,1)S(1)} %slice.35), channel_id=1, source_target_pairs={{0,112},{16,0},{32,16},{48,32},{64,48},{80,64},{96,80},{112,96},{1... | collective-permute-start | bytes 860168 | tf_op jit(solution)/shard_map/ppermute | solution.py:11
  74.4 6.5 %fusion.6 = f32[512,896]{1,0:T(8,128)} fusion(bf16[2560,896]{1,0:T(8,128)(2,1)} %bitcast.87, bf16[512,5120]{1,0:T(8,128)(2,1)S(1)} %bitcast.81, s32[]{:T(128)S(6)} %select_n.153), kind=kOutput, calls=%fused_computation.7 | convolution fusion | flops 2348810240 | bytes 9043972 | tf_op jit(solution)/shard_map/dot_general | solution.py:160
  80.9 2.6 %broadcast.20 = bf16[8,320,896]{2,1,0:T(8,128)(2,1)} broadcast(bf16[]{:T(256)} %constant.105.clone.1), dimensions={} | broadcast | bytes 4587522 | tf_op jit(solution)/shard_map/broadcast.3
  83.6 0.9 bitcast_dynamic-update-slice_fusion.4
  84.7 2.7 %collective-permute-start.17 = (bf16[320,896]{1,0:T(8,128)(2,1)}, bf16[320,896]{1,0:T(8,128)(2,1)S(1)}, u32[]{:S(2)}, u32[]{:S(2)}) collective-permute-start(bf16[320,896]{1,0:T(8,128)(2,1)} %collective-permute-done.11), channel_id=1, source_target_pairs={{0,112},{16,0},{32,16},{48,32},{64,48},{80,64},{96,80},{112,96},{1... | collective-permute-start | bytes 1720328 | tf_op jit(solution)/shard_map/ppermute | solution.py:11
  87.4 0.9 bitcast_dynamic-update-slice_fusion.3
  88.2 0.9 bitcast_dynamic-update-slice_fusion.2
  89.1 1.9 %bitcast_dynamic-update-slice_fusion.1 = bf16[8,320,896]{2,1,0:T(8,128)(2,1)} fusion(bf16[8,320,896]{2,1,0:T(8,128)(2,1)} %bitcast_dynamic-update-slice_fusion.2, s32[]{:T(128)S(6)} %select_n.157, bf16[320,896]{1,0:T(8,128)(2,1)} %collective-permute-done.8), kind=kLoop, calls=%fused_computation.33 | loop fusion | bytes 1146884 | tf_op jit(solution)/shard_map/dynamic_update_slice | solution.py:32
  91.0 1.9 %bitcast_dynamic-update-slice_fusion = bf16[8,320,896]{2,1,0:T(8,128)(2,1)} fusion(bf16[8,320,896]{2,1,0:T(8,128)(2,1)} %bitcast_dynamic-update-slice_fusion.1, s32[]{:T(128)S(6)} %select_n.159, bf16[320,896]{1,0:T(8,128)(2,1)} %collective-permute-done.11), kind=kLoop, calls=%fused_computation.32 | loop fusion | bytes 1146884 | tf_op jit(solution)/shard_map/dynamic_update_slice | solution.py:32
  92.9 6.1 %fusion.4 = f32[512,896]{1,0:T(8,128)S(1)} fusion(bf16[2560,896]{1,0:T(8,128)(2,1)} %bitcast.16, bf16[512,5120]{1,0:T(8,128)(2,1)} %bitcast.76, s32[]{:T(128)S(6)} %select_n.164), kind=kOutput, calls=%fused_computation.5 | convolution fusion | flops 2348810240 | bytes 9043972 | tf_op jit(solution)/shard_map/dot_general | solution.py:178
  99.1 2.0 %add_add_fusion.3 = f32[512,896]{1,0:T(8,128)S(1)} fusion(f32[512,896]{1,0:T(8,128)S(1)} %copy-done.4, f32[512,896]{1,0:T(8,128)S(1)} %fusion.4, bf16[320,896]{1,0:T(8,128)(2,1)S(1)} %constant_dynamic-update-slice_fusion, bf16[512,5120]{1,0:T(8,128)(2,1)} %bitcast.77, s32[]{:T(128)S(6)} %select_n.166), kind=kOutput, calls=%fused_computation.12 | convolution fusion | flops 294518784 | bytes 6471684 | tf_op jit(solution)/shard_map/dot_general | solution.py:181
  101.7 5.4 %fusion = f32[512,896]{1,0:T(8,128)S(1)} fusion(bf16[2560,896]{1,0:T(8,128)(2,1)} %bitcast.16, bf16[512,5120]{1,0:T(8,128)(2,1)S(1)} %bitcast.82, s32[]{:T(128)S(6)} %select_n.164), kind=kOutput, calls=%fused_computation.1 | convolution fusion | flops 2348810240 | bytes 9043972 | tf_op jit(solution)/shard_map/dot_general | solution.py:178
  107.2 2.9 %fusion.2 = f32[512,896]{1,0:T(8,128)S(1)} fusion(bf16[2560,896]{1,0:T(8,128)(2,1)S(1)} %bitcast.90, bf16[512,5120]{1,0:T(8,128)(2,1)S(1)} %bitcast.83, s32[]{:T(128)S(6)} %select_n.153), kind=kOutput, calls=%fused_computation.3 | convolution fusion | flops 2348810240 | bytes 9043972 | tf_op jit(solution)/shard_map/dot_general | solution.py:160
  111.4 1.7 fusion.54
  117.5 0.9 fusion.58
  121.4 14.8 %all-to-all-start = ((bf16[16,8,1024]{2,1,0:T(8,128)(2,1)}), bf16[16,8,1024]{2,1,0:T(8,128)(2,1)S(1)}, u32[]{:S(2)}, u32[]{:S(2)}) async-start(bf16[16,8,1024]{2,1,0:T(8,128)(2,1)} %pad_maximum_fusion.7), calls=%async_computation | async-start | bytes 524288 | tf_op jit(solution)/shard_map/all_to_all | solution.py:211
  136.4 9.1 %all-to-all-done = bf16[16,8,1024]{2,1,0:T(8,128)(2,1)S(1)} async-done(((bf16[16,8,1024]{2,1,0:T(8,128)(2,1)}), bf16[16,8,1024]{2,1,0:T(8,128)(2,1)S(1)}, u32[]{:S(2)}, u32[]{:S(2)}) %all-to-all-start) | async-done | bytes 262176 | tf_op jit(solution)/shard_map/all_to_all | solution.py:211
  147.2 5.5 %all-to-all-start.1 = ((bf16[16,16,512]{2,1,0:T(8,128)(2,1)}), bf16[16,16,512]{2,1,0:T(8,128)(2,1)S(1)}, u32[]{:S(2)}, u32[]{:S(2)}) async-start(bf16[16,16,512]{2,1,0:T(8,128)(2,1)} %broadcast_in_dim.69), calls=%async_computation.1 | async-start | bytes 524288 | tf_op jit(solution)/shard_map/all_to_all | solution.py:227
  153.1 8.5 %all-to-all-done.1 = bf16[16,16,512]{2,1,0:T(8,128)(2,1)S(1)} async-done(((bf16[16,16,512]{2,1,0:T(8,128)(2,1)}), bf16[16,16,512]{2,1,0:T(8,128)(2,1)S(1)}, u32[]{:S(2)}, u32[]{:S(2)}) %all-to-all-start.1) | async-done | bytes 262176 | tf_op jit(solution)/shard_map/all_to_all | solution.py:227
  162.2 12.5 %all_to_all.19 = f32[16,1,640]{2,1,0:T(1,128)S(1)} all-to-all(f32[16,1,640]{2,1,0:T(1,128)S(1)} %copy.24), channel_id=1, replica_groups=mesh['ylo'=2,'z'=8,'x'=4,'core'=2,'yhi'=2] {'x','core','yhi'}, dimensions={0} | all-to-all | bytes 81920 | tf_op jit(solution)/shard_map/all_to_all | solution.py:248
  (116 shorter events, 15.5 us)
Async XLA Ops:
  6.5 28.9 %copy-start = (bf16[64,5120]{1,0:T(8,128)(2,1)S(1)}, bf16[64,5120]{1,0:T(8,128)(2,1)}, u32[]{:S(2)}) copy-start(bf16[64,5120]{1,0:T(8,128)(2,1)} %param.15) | copy-start | bytes 1966084
  6.5 86.4 %all-gather.2.cloned.1.call-start = ((), (), s32[]{:S(2)}) async-start(), calls=%async_computation.3 | async-start | bytes 5898240 | tf_op jit(solution)/shard_map/all_gather | solution.py:52
  7.9 19.3 %collective-permute-start = (bf16[320,896]{1,0:T(8,128)(2,1)S(1)}, bf16[320,896]{1,0:T(8,128)(2,1)}, u32[]{:S(2)}, u32[]{:S(2)}) collective-permute-start(bf16[320,896]{1,0:T(8,128)(2,1)S(1)} %pad_maximum_fusion.2), channel_id=1, source_target_pairs={{0,16},{16,32},{32,48},{48,64},{64,80},{80,96},{96,112},{112,0},{1... | collective-permute-start | bytes 1720328 | tf_op jit(solution)/shard_map/ppermute | solution.py:11
  10.4 16.8 %collective-permute-start.1 = (bf16[320,896]{1,0:T(8,128)(2,1)S(1)}, bf16[320,896]{1,0:T(8,128)(2,1)}, u32[]{:S(2)}, u32[]{:S(2)}) collective-permute-start(bf16[320,896]{1,0:T(8,128)(2,1)S(1)} %pad_maximum_fusion.2), channel_id=1, source_target_pairs={{0,112},{16,0},{32,16},{48,32},{64,48},{80,64},{96,80},{112,96},{1... | collective-permute-start | bytes 1720328 | tf_op jit(solution)/shard_map/ppermute | solution.py:11
  14.4 13.6 %collective-permute-start.2 = (bf16[320,896]{1,0:T(8,128)(2,1)S(1)}, bf16[320,896]{1,0:T(8,128)(2,1)S(1)}, u32[]{:S(2)}, u32[]{:S(2)}) collective-permute-start(bf16[320,896]{1,0:T(8,128)(2,1)S(1)} %pad_maximum_fusion.2), channel_id=1, source_target_pairs={{0,128},{128,0},{1,129},{129,1},{2,130},{130,2},{3,131},{131,3},{4... | collective-permute-start | bytes 1720328 | tf_op jit(solution)/shard_map/ppermute | solution.py:11
  15.7 6.4 %copy-start.8 = (bf16[8,32,896]{2,1,0:T(8,128)(2,1)S(1)}, bf16[8,32,896]{2,1,0:T(8,128)(2,1)}, u32[]{:S(2)}) copy-start(bf16[8,32,896]{2,1,0:T(8,128)(2,1)} %param.12) | copy-start | bytes 1376260
  15.7 6.4 %copy-start.9 = (bf16[8,32,896]{2,1,0:T(8,128)(2,1)S(1)}, bf16[8,32,896]{2,1,0:T(8,128)(2,1)}, u32[]{:S(2)}) copy-start(bf16[8,32,896]{2,1,0:T(8,128)(2,1)} %param.10) | copy-start | bytes 1376260
  24.4 11.0 %copy-start.1 = (bf16[8,64,5120]{2,1,0:T(8,128)(2,1)S(1)}, bf16[8,64,5120]{2,1,0:T(8,128)(2,1)}, u32[]{:S(2)}) copy-start(bf16[8,64,5120]{2,1,0:T(8,128)(2,1)} %pad_maximum_fusion) | copy-start | bytes 15728644
  28.0 19.1 %copy-start.10 = (bf16[320,896]{1,0:T(8,128)(2,1)}, bf16[320,896]{1,0:T(8,128)(2,1)S(1)}, u32[]{:S(2)}) copy-start(bf16[320,896]{1,0:T(8,128)(2,1)S(1)} %collective-permute-done.2) | copy-start | bytes 1720324
  28.0 14.0 %collective-permute-start.3 = (bf16[320,896]{1,0:T(8,128)(2,1)}, bf16[320,896]{1,0:T(8,128)(2,1)S(1)}, u32[]{:S(2)}, u32[]{:S(2)}) collective-permute-start(bf16[320,896]{1,0:T(8,128)(2,1)} %collective-permute-done), channel_id=1, source_target_pairs={{0,16},{16,32},{32,48},{48,64},{64,80},{80,96},{96,112},{112,0},{1... | collective-permute-start | bytes 1720328 | tf_op jit(solution)/shard_map/ppermute | solution.py:11
  28.0 14.0 %collective-permute-start.4 = (bf16[320,896]{1,0:T(8,128)(2,1)}, bf16[320,896]{1,0:T(8,128)(2,1)}, u32[]{:S(2)}, u32[]{:S(2)}) collective-permute-start(bf16[320,896]{1,0:T(8,128)(2,1)} %collective-permute-done.1), channel_id=1, source_target_pairs={{0,112},{16,0},{32,16},{48,32},{64,48},{80,64},{96,80},{112,96},{1... | collective-permute-start | bytes 1720328 | tf_op jit(solution)/shard_map/ppermute | solution.py:11
  30.7 15.3 %collective-permute-start.5 = (bf16[1,64,5120]{2,1,0:T(8,128)(2,1)S(1)}, bf16[1,64,5120]{2,1,0:T(8,128)(2,1)S(1)}, u32[]{:S(2)}, u32[]{:S(2)}) collective-permute-start(bf16[1,64,5120]{2,1,0:T(8,128)(2,1)S(1)} %pad_maximum_fusion.1), channel_id=1, source_target_pairs={{0,1},{1,0},{2,3},{3,2},{4,5},{5,4},{6,7},{7,6},{8,9},{9,8},{10,11... | collective-permute-start | bytes 1966088 | tf_op jit(solution)/shard_map/ppermute | solution.py:11
  35.4 2.4 %copy-start.3 = (bf16[8,320,896]{2,1,0:T(8,128)(2,1)}, bf16[8,320,896]{2,1,0:T(8,128)(2,1)S(1)}, u32[]{:S(2)}) copy-start(bf16[8,320,896]{2,1,0:T(8,128)(2,1)S(1)} %bitcast_dynamic-update-slice_fusion.10) | copy-start | bytes 13762564
  35.4 38.9 %slice-start = ((s8[5242880]{0:T(1024)(128)(4,1)}), s8[1048576]{0:T(1024)(128)(4,1)S(1)}, s32[]{:S(2)}) async-start(s8[5242880]{0:T(1024)(128)(4,1)} %bitcast.79), calls=%async_computation.4 | async-start | bytes 2097152
  46.0 0.9 copy-start.7
  47.0 27.3 %slice-start.1 = ((s8[5242880]{0:T(1024)(128)(4,1)}), s8[4194304]{0:T(1024)(128)(4,1)S(1)}, s32[]{:S(2)}) async-start(s8[5242880]{0:T(1024)(128)(4,1)} %bitcast.79), calls=%async_computation.5 | async-start | bytes 8388608
  47.0 12.4 %collective-permute-start.6 = (bf16[320,896]{1,0:T(8,128)(2,1)S(1)}, bf16[320,896]{1,0:T(8,128)(2,1)S(1)}, u32[]{:S(2)}, u32[]{:S(2)}) collective-permute-start(bf16[320,896]{1,0:T(8,128)(2,1)S(1)} %collective-permute-done.3), channel_id=1, source_target_pairs={{0,16},{16,32},{32,48},{48,64},{64,80},{80,96},{96,112},{112,0},{1... | collective-permute-start | bytes 1720328 | tf_op jit(solution)/shard_map/ppermute | solution.py:11
  47.1 12.7 %collective-permute-start.8 = (bf16[320,896]{1,0:T(8,128)(2,1)S(1)}, bf16[320,896]{1,0:T(8,128)(2,1)}, u32[]{:S(2)}, u32[]{:S(2)}) collective-permute-start(bf16[320,896]{1,0:T(8,128)(2,1)S(1)} %collective-permute-done.3), channel_id=1, source_target_pairs={{0,128},{128,0},{1,129},{129,1},{2,130},{130,2},{3,131},{131,3},{4... | collective-permute-start | bytes 1720328 | tf_op jit(solution)/shard_map/ppermute | solution.py:11
  48.5 11.3 %collective-permute-start.7 = (bf16[320,896]{1,0:T(8,128)(2,1)}, bf16[320,896]{1,0:T(8,128)(2,1)S(1)}, u32[]{:S(2)}, u32[]{:S(2)}) collective-permute-start(bf16[320,896]{1,0:T(8,128)(2,1)} %collective-permute-done.4), channel_id=1, source_target_pairs={{0,112},{16,0},{32,16},{48,32},{64,48},{80,64},{96,80},{112,96},{1... | collective-permute-start | bytes 1720328 | tf_op jit(solution)/shard_map/ppermute | solution.py:11
  53.8 18.2 %collective-permute-start.14 = (bf16[512,448]{1,0:T(8,128)(2,1)}, bf16[512,448]{1,0:T(8,128)(2,1)S(1)}, u32[]{:S(2)}, u32[]{:S(2)}) collective-permute-start(bf16[512,448]{1,0:T(8,128)(2,1)} %bitcast.95), channel_id=1, source_target_pairs={{0,1},{1,0},{2,3},{3,2},{4,5},{5,4},{6,7},{7,6},{8,9},{9,8},{10,11... | collective-permute-start | bytes 1376264 | tf_op jit(solution)/shard_map/ppermute | solution.py:11
  59.8 24.6 %collective-permute-start.10 = (bf16[320,896]{1,0:T(8,128)(2,1)}, bf16[320,896]{1,0:T(8,128)(2,1)S(1)}, u32[]{:S(2)}, u32[]{:S(2)}) collective-permute-start(bf16[320,896]{1,0:T(8,128)(2,1)} %copy-done.10), channel_id=1, source_target_pairs={{0,112},{16,0},{32,16},{48,32},{64,48},{80,64},{96,80},{112,96},{1... | collective-permute-start | bytes 1720328 | tf_op jit(solution)/shard_map/ppermute | solution.py:11
  63.1 21.3 %collective-permute-start.9 = (bf16[320,896]{1,0:T(8,128)(2,1)}, bf16[320,896]{1,0:T(8,128)(2,1)S(1)}, u32[]{:S(2)}, u32[]{:S(2)}) collective-permute-start(bf16[320,896]{1,0:T(8,128)(2,1)} %copy-done.10), channel_id=1, source_target_pairs={{0,16},{16,32},{32,48},{48,64},{64,80},{80,96},{96,112},{112,0},{1... | collective-permute-start | bytes 1720328 | tf_op jit(solution)/shard_map/ppermute | solution.py:11
  63.1 21.3 %collective-permute-start.11 = (bf16[320,896]{1,0:T(8,128)(2,1)}, bf16[320,896]{1,0:T(8,128)(2,1)}, u32[]{:S(2)}, u32[]{:S(2)}) collective-permute-start(bf16[320,896]{1,0:T(8,128)(2,1)} %collective-permute-done.4), channel_id=1, source_target_pairs={{0,128},{128,0},{1,129},{129,1},{2,130},{130,2},{3,131},{131,3},{4... | collective-permute-start | bytes 1720328 | tf_op jit(solution)/shard_map/ppermute | solution.py:11
  63.3 21.1 %collective-permute-start.12 = (bf16[160,896]{1,0:T(8,128)(2,1)S(1)}, bf16[160,896]{1,0:T(8,128)(2,1)S(1)}, u32[]{:S(2)}, u32[]{:S(2)}) collective-permute-start(bf16[160,896]{1,0:T(8,128)(2,1)S(1)} %slice.34), channel_id=1, source_target_pairs={{0,16},{16,32},{32,48},{48,64},{64,80},{80,96},{96,112},{112,0},{1... | collective-permute-start | bytes 860168 | tf_op jit(solution)/shard_map/ppermute | solution.py:11
  72.1 2.3 %copy-start.14 = (bf16[512,448]{1,0:T(8,128)(2,1)}, bf16[512,448]{1,0:T(8,128)(2,1)S(1)}, u32[]{:S(2)}) copy-start(bf16[512,448]{1,0:T(8,128)(2,1)S(1)} %collective-permute-done.14) | copy-start | bytes 1376260
  72.1 12.4 %collective-permute-start.13 = (bf16[160,896]{1,0:T(8,128)(2,1)S(1)}, bf16[160,896]{1,0:T(8,128)(2,1)S(1)}, u32[]{:S(2)}, u32[]{:S(2)}) collective-permute-start(bf16[160,896]{1,0:T(8,128)(2,1)S(1)} %slice.35), channel_id=1, source_target_pairs={{0,112},{16,0},{32,16},{48,32},{64,48},{80,64},{96,80},{112,96},{1... | collective-permute-start | bytes 860168 | tf_op jit(solution)/shard_map/ppermute | solution.py:11
  80.9 2.7 %copy-start.11 = (bf16[320,896]{1,0:T(8,128)(2,1)S(1)}, bf16[320,896]{1,0:T(8,128)(2,1)}, u32[]{:S(2)}) copy-start(bf16[320,896]{1,0:T(8,128)(2,1)} %copy-done.10) | copy-start | bytes 1720324
  84.5 28.6 %collective-permute-start.15 = (bf16[320,896]{1,0:T(8,128)(2,1)S(1)}, bf16[320,896]{1,0:T(8,128)(2,1)S(1)}, u32[]{:S(2)}, u32[]{:S(2)}) collective-permute-start(bf16[320,896]{1,0:T(8,128)(2,1)S(1)} %constant_dynamic-update-slice_fusion), channel_id=1, source_target_pairs={{0,128},{128,0},{1,129},{129,1},{2,130},{130,2},{3,131},{131,3},{4... | collective-permute-start | bytes 1720328 | tf_op jit(solution)/shard_map/ppermute | solution.py:11
  84.6 28.5 %collective-permute-start.16 = (bf16[320,896]{1,0:T(8,128)(2,1)}, bf16[320,896]{1,0:T(8,128)(2,1)S(1)}, u32[]{:S(2)}, u32[]{:S(2)}) collective-permute-start(bf16[320,896]{1,0:T(8,128)(2,1)} %collective-permute-done.8), channel_id=1, source_target_pairs={{0,16},{16,32},{32,48},{48,64},{64,80},{80,96},{96,112},{112,0},{1... | collective-permute-start | bytes 1720328 | tf_op jit(solution)/shard_map/ppermute | solution.py:11
  84.7 28.4 %collective-permute-start.17 = (bf16[320,896]{1,0:T(8,128)(2,1)}, bf16[320,896]{1,0:T(8,128)(2,1)S(1)}, u32[]{:S(2)}, u32[]{:S(2)}) collective-permute-start(bf16[320,896]{1,0:T(8,128)(2,1)} %collective-permute-done.11), channel_id=1, source_target_pairs={{0,112},{16,0},{32,16},{48,32},{64,48},{80,64},{96,80},{112,96},{1... | collective-permute-start | bytes 1720328 | tf_op jit(solution)/shard_map/ppermute | solution.py:11
  92.9 6.1 %copy-start.4 = (f32[512,896]{1,0:T(8,128)S(1)}, f32[512,896]{1,0:T(8,128)}, u32[]{:S(2)}) copy-start(f32[512,896]{1,0:T(8,128)} %fusion.6) | copy-start | bytes 5505028
  99.0 2.6 %copy-start.2 = (bf16[8,64,5120]{2,1,0:T(8,128)(2,1)S(1)}, bf16[8,64,5120]{2,1,0:T(8,128)(2,1)}, u32[]{:S(2)}) copy-start(bf16[8,64,5120]{2,1,0:T(8,128)(2,1)} %all-gather.2.cloned.1.call-done) | copy-start | bytes 15728644
  99.0 8.1 %slice-start.2 = ((s8[4587520]{0:T(1024)(128)(4,1)}), s8[4194304]{0:T(1024)(128)(4,1)S(1)}, s32[]{:S(2)}) async-start(s8[4587520]{0:T(1024)(128)(4,1)} %bitcast.88), calls=%async_computation.6 | async-start | bytes 8388608
  101.7 5.5 %slice-start.3 = ((s8[4587520]{0:T(1024)(128)(4,1)}), s8[393216]{0:T(1024)(128)(4,1)S(1)}, s32[]{:S(2)}) async-start(s8[4587520]{0:T(1024)(128)(4,1)} %bitcast.88), calls=%async_computation.7 | async-start | bytes 786432
  110.8 2.3 %copy-start.6 = (bf16[512,320]{1,0:T(8,128)(2,1)S(1)}, bf16[512,320]{1,0:T(8,128)(2,1)}, u32[]{:S(2)}) copy-start(bf16[512,320]{1,0:T(8,128)(2,1)} %get-tuple-element.84) | copy-start | bytes 983044
  111.4 2.4 %copy-start.5 = (bf16[512,320]{1,0:T(8,128)(2,1)S(1)}, bf16[512,320]{1,0:T(8,128)(2,1)}, u32[]{:S(2)}) copy-start(bf16[512,320]{1,0:T(8,128)(2,1)} %get-tuple-element.86) | copy-start | bytes 983044
  114.5 1.0 copy-start.13
  114.5 1.0 copy-start.16
  115.5 0.9 copy-start.17
  118.5 1.0 copy-start.15
  120.2 16.0 %copy-start.12 = (f32[512,64]{0,1:T(8,128)S(1)}, f32[512,64]{0,1:T(8,128)}, u32[]{:S(2)}) copy-start(f32[512,64]{0,1:T(8,128)} %fusion.53) | copy-start | bytes 393220
  121.4 24.1 %all-to-all-start = ((bf16[16,8,1024]{2,1,0:T(8,128)(2,1)}), bf16[16,8,1024]{2,1,0:T(8,128)(2,1)S(1)}, u32[]{:S(2)}, u32[]{:S(2)}) async-start(bf16[16,8,1024]{2,1,0:T(8,128)(2,1)} %pad_maximum_fusion.7), calls=%async_computation | async-start | bytes 524288 | tf_op jit(solution)/shard_map/all_to_all | solution.py:211
  147.2 14.4 %all-to-all-start.1 = ((bf16[16,16,512]{2,1,0:T(8,128)(2,1)}), bf16[16,16,512]{2,1,0:T(8,128)(2,1)S(1)}, u32[]{:S(2)}, u32[]{:S(2)}) async-start(bf16[16,16,512]{2,1,0:T(8,128)(2,1)} %broadcast_in_dim.69), calls=%async_computation.1 | async-start | bytes 524288 | tf_op jit(solution)/shard_map/all_to_all | solution.py:227
Sparse Core Ops, SparseCore 0:
  47.0 41.8 all-gather.1

commit v12 on v11

--- a/solution.py
+++ b/solution.py
@@ -78,7 +78,6 @@
         jnp.zeros((n_z,) + weight.shape, weight.dtype),
         ((0, o0), (n_z - 1, oa1), (1, ob1), (n_z - 2, oa2), (2, ob2)),
     ).reshape(flat)
-    own_sum, other_row, partner = barrier((own_sum, other_row, partner))
     this = (this_row, own_sum, (a4, far_z))
     return this, other_row, last, other_cot, partner, early, own_factor
 
@@ -182,9 +181,7 @@
             chunk(rows, row_index, far[1]), far[0], preferred_element_type=F32
         )
 
-    own_pre = rest(own, own_sum)
-    own_pre, other = lax.optimization_barrier((own_pre, other))
-    pres = (own_pre, rest(other, this_product(other, this_row)))
+    pres = (rest(own, own_sum), rest(other, this_product(other, this_row)))
     chunks = [[chunk(rows, 1 - row_index, at) for _, at in last] for rows in (own, other)]
     factors = (own_factor, inner_factor(other))
     shards = [shard for shard, _ in last]

time: 184 us -> 183 us (level)
  local copies, waits for them, and re-layouts: 27.1 us -> 22.9 us
  matrix products: 34.9 us -> 38.7 us
  starting transfers between devices: 49.1 us -> 47 us
    dot_general x6, matrix products: 4.28 us -> 10.8 us  [body(): pre = pre + jnp.dot(chunk, shard, preferred_element_type=F32)]
    dot_general x2, matrix products: 11.5 us -> 5.77 us  [rest(): jnp.dot(half_of(rows, 1 - row_index, depth), other_row, preferred_element...]
    dynamic_update_slice x12, local copies, waits for them, and re-layouts: 14.1 us -> 11.3 us  [placed(): lax.dynamic_update_slice(result, shard[None], ((z + offset) % n_z, 0, 0))]
    all_to_all x1, starting transfers between devices: 14.8 us -> 11.9 us  [body(): swapped = lax.all_to_all(part, dq, 0, 0, tiled=True)]
    another operation x2, local copies, waits for them, and re-layouts: 3.23 us -> 1.16 us
    dot_general x2, matrix products: 9.41 us -> 11.4 us  [this_product(): return jnp.dot(flat, this_row, preferred_element_type=F32)]
  transfers between devices with their start and end apart: 21 -> 21, of which waited for: 9 -> 8; matrix products, arithmetic and copies ran while one was open for 32% -> 28% of each run, Pallas kernels for 0% -> 0%
where the time goes in v12:
time: 183 us; the launch traced here: 182 us
  starting transfers between devices  47 us (26%)
  matrix products  38.7 us (21%)
  waiting for transfers between devices  35.7 us (20%)
  local copies, waits for them, and re-layouts  22.9 us (13%)
  between operations  14.8 us (8%)
  blocking collectives  12.5 us (7%)
  other arithmetic  10.2 us (6%)
    ppermute x18, starting transfers between devices, shift(): lax.ppermute(value, axis, [(i, (i + step) % size) for i in range(size)])  29.7 us
    ppermute x18, waiting for transfers between devices, shift(): lax.ppermute(value, axis, [(i, (i + step) % size) for i in range(size)])  18.1 us
    all_to_all x1, blocking collectives, body(): received = lax.all_to_all(payload, dq, 0, 0, tiled=True)  12.5 us
    all_to_all x1, starting transfers between devices, body(): swapped = lax.all_to_all(part, dq, 0, 0, tiled=True)  11.9 us
    dot_general x2, matrix products, this_product(): return jnp.dot(flat, this_row, preferred_element_type=F32)  11.4 us
    dynamic_update_slice x12, local copies, waits for them, and re-layouts, placed(): lax.dynamic_update_slice(result, shard[None], ((z + offset) % n_z, 0, 0))  11.3 us
    dot_general x6, matrix products, body(): pre = pre + jnp.dot(chunk, shard, preferred_element_type=F32)  10.8 us
    all_to_all x1, waiting for transfers between devices, body(): swapped = lax.all_to_all(part, dq, 0, 0, tiled=True)  9.11 us
  transfers between devices with their start and end apart: 21, of which 8 were waited for; matrix products, arithmetic and copies ran while one was open for 28% of the time, Pallas kernels for 0%

profile of v12, /device:TPU:1, one launch (start us, length us, event | category | flops | bytes accessed | tf_op | source)
XLA Modules:
  0.0 181.8 jit_solution(2036098942196657450)
XLA Ops:
  6.5 1.3 pad_maximum_fusion.2
  7.9 2.5 %collective-permute-start = (bf16[320,896]{1,0:T(8,128)(2,1)S(1)}, bf16[320,896]{1,0:T(8,128)(2,1)}, u32[]{:S(2)}, u32[]{:S(2)}) collective-permute-start(bf16[320,896]{1,0:T(8,128)(2,1)S(1)} %pad_maximum_fusion.2), channel_id=1, source_target_pairs={{0,16},{16,32},{32,48},{48,64},{64,80},{80,96},{96,112},{112,0},{1... | collective-permute-start | bytes 1720328 | tf_op jit(solution)/shard_map/ppermute | solution.py:11
  10.4 4.0 %collective-permute-start.1 = (bf16[320,896]{1,0:T(8,128)(2,1)S(1)}, bf16[320,896]{1,0:T(8,128)(2,1)}, u32[]{:S(2)}, u32[]{:S(2)}) collective-permute-start(bf16[320,896]{1,0:T(8,128)(2,1)S(1)} %pad_maximum_fusion.2), channel_id=1, source_target_pairs={{0,112},{16,0},{32,16},{48,32},{64,48},{80,64},{96,80},{112,96},{1... | collective-permute-start | bytes 1720328 | tf_op jit(solution)/shard_map/ppermute | solution.py:11
  14.4 1.3 collective-permute-start.2
  15.7 5.3 %pad_maximum_fusion = bf16[8,64,5120]{2,1,0:T(8,128)(2,1)} fusion(bf16[8,32,5120]{2,1,0:T(8,128)(2,1)} %param.11, bf16[8,32,5120]{2,1,0:T(8,128)(2,1)} %param.9), kind=kLoop, calls=%fused_computation | loop fusion | flops 10485760 | bytes 10485760 | tf_op jit(solution)/shard_map/concatenate | solution.py:132
  21.1 1.1 constant_dynamic-slice_fusion.8
  24.5 2.7 %collective-permute-done = bf16[320,896]{1,0:T(8,128)(2,1)} collective-permute-done((bf16[320,896]{1,0:T(8,128)(2,1)S(1)}, bf16[320,896]{1,0:T(8,128)(2,1)}, u32[]{:S(2)}, u32[]{:S(2)}) %collective-permute-start) | collective-permute-done | bytes 573472 | tf_op jit(solution)/shard_map/ppermute | solution.py:11
  28.0 2.7 %collective-permute-start.4 = (bf16[320,896]{1,0:T(8,128)(2,1)}, bf16[320,896]{1,0:T(8,128)(2,1)}, u32[]{:S(2)}, u32[]{:S(2)}) collective-permute-start(bf16[320,896]{1,0:T(8,128)(2,1)} %collective-permute-done.1), channel_id=1, source_target_pairs={{0,112},{16,0},{32,16},{48,32},{64,48},{80,64},{96,80},{112,96},{1... | collective-permute-start | bytes 1720328 | tf_op jit(solution)/shard_map/ppermute | solution.py:11
  30.7 2.9 %collective-permute-start.5 = (bf16[1,64,5120]{2,1,0:T(8,128)(2,1)S(1)}, bf16[1,64,5120]{2,1,0:T(8,128)(2,1)S(1)}, u32[]{:S(2)}, u32[]{:S(2)}) collective-permute-start(bf16[1,64,5120]{2,1,0:T(8,128)(2,1)S(1)} %pad_maximum_fusion.1), channel_id=1, source_target_pairs={{0,1},{1,0},{2,3},{3,2},{4,5},{5,4},{6,7},{7,6},{8,9},{9,8},{10,11... | collective-permute-start | bytes 1966088 | tf_op jit(solution)/shard_map/ppermute | solution.py:11
  34.3 1.1 bitcast_dynamic-update-slice_fusion.10
  35.4 2.4 %fusion.56 = f32[512,64]{0,1:T(8,128)} fusion(bf16[512,5120]{1,0:T(8,128)(2,1)S(1)} %bitcast.76, bf16[64,5120]{1,0:T(8,128)(2,1)S(1)} %copy-done), kind=kOutput, calls=%fused_computation.106 | convolution fusion | flops 335544320 | bytes 6029312 | tf_op jit(solution)/shard_map/dot_general | solution.py:147
  37.8 4.3 %collective-permute-done.3 = bf16[320,896]{1,0:T(8,128)(2,1)} collective-permute-done((bf16[320,896]{1,0:T(8,128)(2,1)}, bf16[320,896]{1,0:T(8,128)(2,1)}, u32[]{:S(2)}, u32[]{:S(2)}) %collective-permute-start.3) | collective-permute-done | bytes 573472 | tf_op jit(solution)/shard_map/ppermute | solution.py:11
  42.2 3.8 %collective-permute-done.5 = bf16[1,64,5120]{2,1,0:T(8,128)(2,1)S(1)} collective-permute-done((bf16[1,64,5120]{2,1,0:T(8,128)(2,1)S(1)}, bf16[1,64,5120]{2,1,0:T(8,128)(2,1)S(1)}, u32[]{:S(2)}, u32[]{:S(2)}) %collective-permute-start.5) | collective-permute-done | bytes 655392 | tf_op jit(solution)/shard_map/ppermute | solution.py:11
  47.1 1.4 collective-permute-start.8
  48.5 2.6 %collective-permute-start.7 = (bf16[320,896]{1,0:T(8,128)(2,1)}, bf16[320,896]{1,0:T(8,128)(2,1)S(1)}, u32[]{:S(2)}, u32[]{:S(2)}) collective-permute-start(bf16[320,896]{1,0:T(8,128)(2,1)} %collective-permute-done.4), channel_id=1, source_target_pairs={{0,112},{16,0},{32,16},{48,32},{64,48},{80,64},{96,80},{112,96},{1... | collective-permute-start | bytes 1720328 | tf_op jit(solution)/shard_map/ppermute | solution.py:11
  51.0 2.9 %constant_dynamic-slice_fusion.3 = (bf16[512,320]{1,0:T(8,128)(2,1)}, bf16[512,320]{1,0:T(8,128)(2,1)}, bf16[512,320]{1,0:T(8,128)(2,1)}) fusion(bf16[512,5120]{1,0:T(8,128)(2,1)} %bitcast.75, s32[]{:T(128)S(6)} %select_n.169, s32[]{:T(128)S(6)} %select_n.168, s32[]{:T(128)S(6)} %select_n.167), kind=kLoop, calls=%fused_computation.83 | loop fusion | bytes 1966092 | tf_op jit(solution)/shard_map/dynamic_slice | solution.py:172
  53.9 2.6 %collective-permute-start.14 = (bf16[512,448]{1,0:T(8,128)(2,1)}, bf16[512,448]{1,0:T(8,128)(2,1)S(1)}, u32[]{:S(2)}, u32[]{:S(2)}) collective-permute-start(bf16[512,448]{1,0:T(8,128)(2,1)} %bitcast.95), channel_id=1, source_target_pairs={{0,1},{1,0},{2,3},{3,2},{4,5},{5,4},{6,7},{7,6},{8,9},{9,8},{10,11... | collective-permute-start | bytes 1376264 | tf_op jit(solution)/shard_map/ppermute | solution.py:11
  56.6 1.9 %bitcast_dynamic-update-slice_fusion.9 = bf16[8,320,896]{2,1,0:T(8,128)(2,1)} fusion(bf16[8,320,896]{2,1,0:T(8,128)(2,1)} %copy-done.5, s32[]{:T(128)S(6)} %select_n.155, bf16[320,896]{1,0:T(8,128)(2,1)} %collective-permute-done.1), kind=kLoop, calls=%fused_computation.41 | loop fusion | bytes 1146884 | tf_op jit(solution)/shard_map/dynamic_update_slice | solution.py:32
  58.5 1.9 %bitcast_dynamic-update-slice_fusion.8 = bf16[8,320,896]{2,1,0:T(8,128)(2,1)} fusion(bf16[8,320,896]{2,1,0:T(8,128)(2,1)} %bitcast_dynamic-update-slice_fusion.9, s32[]{:T(128)S(6)} %select_n.157, bf16[320,896]{1,0:T(8,128)(2,1)} %collective-permute-done.3), kind=kLoop, calls=%fused_computation.40 | loop fusion | bytes 1146884 | tf_op jit(solution)/shard_map/dynamic_update_slice | solution.py:32
  60.5 2.7 %collective-permute-start.10 = (bf16[320,896]{1,0:T(8,128)(2,1)S(1)}, bf16[320,896]{1,0:T(8,128)(2,1)S(1)}, u32[]{:S(2)}, u32[]{:S(2)}) collective-permute-start(bf16[320,896]{1,0:T(8,128)(2,1)S(1)} %collective-permute-done.2), channel_id=1, source_target_pairs={{0,112},{16,0},{32,16},{48,32},{64,48},{80,64},{96,80},{112,96},{1... | collective-permute-start | bytes 1720328 | tf_op jit(solution)/shard_map/ppermute | solution.py:11
  63.8 1.9 %bitcast_dynamic-update-slice_fusion.7 = bf16[8,320,896]{2,1,0:T(8,128)(2,1)} fusion(bf16[8,320,896]{2,1,0:T(8,128)(2,1)} %bitcast_dynamic-update-slice_fusion.8, s32[]{:T(128)S(6)} %select_n.159, bf16[320,896]{1,0:T(8,128)(2,1)} %collective-permute-done.4), kind=kLoop, calls=%fused_computation.39 | loop fusion | bytes 1146884 | tf_op jit(solution)/shard_map/dynamic_update_slice | solution.py:32
  65.7 0.9 bitcast_dynamic-update-slice_fusion.6
  66.6 0.9 bitcast_dynamic-update-slice_fusion.5
  67.5 4.7 %collective-permute-done.14 = bf16[512,448]{1,0:T(8,128)(2,1)S(1)} collective-permute-done((bf16[512,448]{1,0:T(8,128)(2,1)}, bf16[512,448]{1,0:T(8,128)(2,1)S(1)}, u32[]{:S(2)}, u32[]{:S(2)}) %collective-permute-start.14) | collective-permute-done | bytes 458784 | tf_op jit(solution)/shard_map/ppermute | solution.py:11
  72.2 2.3 %collective-permute-start.13 = (bf16[160,896]{1,0:T(8,128)(2,1)S(1)}, bf16[160,896]{1,0:T(8,128)(2,1)S(1)}, u32[]{:S(2)}, u32[]{:S(2)}) collective-permute-start(bf16[160,896]{1,0:T(8,128)(2,1)S(1)} %slice.35), channel_id=1, source_target_pairs={{0,112},{16,0},{32,16},{48,32},{64,48},{80,64},{96,80},{112,96},{1... | collective-permute-start | bytes 860168 | tf_op jit(solution)/shard_map/ppermute | solution.py:11
  74.5 5.3 %fusion.6 = f32[512,896]{1,0:T(8,128)S(1)} fusion(bf16[2560,896]{1,0:T(8,128)(2,1)} %bitcast.89, bf16[512,5120]{1,0:T(8,128)(2,1)S(1)} %bitcast.79, s32[]{:T(128)S(6)} %select_n.153), kind=kOutput, calls=%fused_computation.7 | convolution fusion | flops 2348810240 | bytes 9043972 | tf_op jit(solution)/shard_map/dot_general | solution.py:159
  80.5 1.6 collective-permute-done.11
  83.6 1.3 collective-permute-start.15
  85.8 1.8 %collective-permute-start.17 = (bf16[320,896]{1,0:T(8,128)(2,1)}, bf16[320,896]{1,0:T(8,128)(2,1)}, u32[]{:S(2)}, u32[]{:S(2)}) collective-permute-start(bf16[320,896]{1,0:T(8,128)(2,1)} %collective-permute-done.11), channel_id=1, source_target_pairs={{0,112},{16,0},{32,16},{48,32},{64,48},{80,64},{96,80},{112,96},{1... | collective-permute-start | bytes 1720328 | tf_op jit(solution)/shard_map/ppermute | solution.py:11
  87.8 1.1 bitcast_dynamic-update-slice_fusion.1
  88.9 1.1 bitcast_dynamic-update-slice_fusion
  90.0 2.9 %fusion.4 = f32[512,896]{1,0:T(8,128)S(1)} fusion(bf16[2560,896]{1,0:T(8,128)(2,1)S(1)} %bitcast.87, bf16[512,5120]{1,0:T(8,128)(2,1)S(1)} %bitcast.80, s32[]{:T(128)S(6)} %select_n.164), kind=kOutput, calls=%fused_computation.5 | convolution fusion | flops 2348810240 | bytes 9043972 | tf_op jit(solution)/shard_map/dot_general | solution.py:177
  92.9 1.9 %add_add_fusion.3 = f32[512,896]{1,0:T(8,128)S(1)} fusion(f32[512,896]{1,0:T(8,128)S(1)} %fusion.6, f32[512,896]{1,0:T(8,128)S(1)} %fusion.4, bf16[320,896]{1,0:T(8,128)(2,1)} %constant_dynamic-update-slice_fusion, bf16[512,5120]{1,0:T(8,128)(2,1)S(1)} %bitcast.81, s32[]{:T(128)S(6)} %select_n.166), kind=kOutput, calls=%fused_computation.12 | convolution fusion | flops 294518784 | bytes 6471684 | tf_op jit(solution)/shard_map/dot_general | solution.py:180
  94.9 6.1 %fusion.2 = f32[512,896]{1,0:T(8,128)S(1)} fusion(bf16[2560,896]{1,0:T(8,128)(2,1)} %bitcast.90, bf16[512,5120]{1,0:T(8,128)(2,1)} %bitcast.82, s32[]{:T(128)S(6)} %select_n.153), kind=kOutput, calls=%fused_computation.3 | convolution fusion | flops 2348810240 | bytes 9043972 | tf_op jit(solution)/shard_map/dot_general | solution.py:159
  101.0 2.9 %fusion = f32[512,896]{1,0:T(8,128)S(1)} fusion(bf16[2560,896]{1,0:T(8,128)(2,1)S(1)} %bitcast.88, bf16[512,5120]{1,0:T(8,128)(2,1)S(1)} %bitcast.83, s32[]{:T(128)S(6)} %select_n.164), kind=kOutput, calls=%fused_computation.1 | convolution fusion | flops 2348810240 | bytes 9043972 | tf_op jit(solution)/shard_map/dot_general | solution.py:177
  103.9 1.9 %add_add_fusion.2 = f32[512,896]{1,0:T(8,128)S(1)} fusion(f32[512,896]{1,0:T(8,128)S(1)} %fusion.2, f32[512,896]{1,0:T(8,128)S(1)} %fusion, bf16[320,896]{1,0:T(8,128)(2,1)} %constant_dynamic-update-slice_fusion, bf16[512,5120]{1,0:T(8,128)(2,1)S(1)} %bitcast.84, s32[]{:T(128)S(6)} %select_n.166), kind=kOutput, calls=%fused_computation.11 | convolution fusion | flops 294518784 | bytes 6471684 | tf_op jit(solution)/shard_map/dot_general | solution.py:180
  106.3 1.7 fusion.57
  108.1 1.7 fusion.61
  109.8 1.7 fusion.60
  111.5 1.8 %add_add_fusion = f32[512,896]{1,0:T(8,128)S(1)} fusion(f32[512,896]{1,0:T(8,128)S(1)} %fusion.61, f32[512,896]{1,0:T(8,128)S(1)} %add_add_fusion.2, f32[512,896]{1,0:T(8,128)S(1)} %fusion.60, bf16[512,320]{1,0:T(8,128)(2,1)S(1)} %get-tuple-element.84, bf16[320,896]{1,0:T(8,128)(2,1)} %collective-permute-done.17), kind=kOutput, calls=%fused_computation.9 | convolution fusion | flops 294977536 | bytes 8241152 | tf_op jit(solution)/shard_map/dot_general | solution.py:194
  115.3 1.7 fusion.59
  117.0 1.7 fusion.58
  118.7 2.2 %add_add_fusion.1 = f32[512,896]{1,0:T(8,128)S(1)} fusion(f32[512,896]{1,0:T(8,128)S(1)} %fusion.59, f32[512,896]{1,0:T(8,128)S(1)} %add_add_fusion.3, f32[512,896]{1,0:T(8,128)S(1)} %fusion.58, bf16[512,320]{1,0:T(8,128)(2,1)S(1)} %copy-done.6, bf16[320,896]{1,0:T(8,128)(2,1)} %collective-permute-done.17), kind=kOutput, calls=%fused_computation.10 | convolution fusion | flops 294977536 | bytes 8241152 | tf_op jit(solution)/shard_map/dot_general | solution.py:194
  122.8 11.9 %all-to-all-start = ((bf16[16,8,1024]{2,1,0:T(8,128)(2,1)}), bf16[16,8,1024]{2,1,0:T(8,128)(2,1)S(1)}, u32[]{:S(2)}, u32[]{:S(2)}) async-start(bf16[16,8,1024]{2,1,0:T(8,128)(2,1)} %pad_maximum_fusion.7), calls=%async_computation | async-start | bytes 524288 | tf_op jit(solution)/shard_map/all_to_all | solution.py:208
  135.0 9.1 %all-to-all-done = bf16[16,8,1024]{2,1,0:T(8,128)(2,1)S(1)} async-done(((bf16[16,8,1024]{2,1,0:T(8,128)(2,1)}), bf16[16,8,1024]{2,1,0:T(8,128)(2,1)S(1)}, u32[]{:S(2)}, u32[]{:S(2)}) %all-to-all-start) | async-done | bytes 262176 | tf_op jit(solution)/shard_map/all_to_all | solution.py:208
  145.7 5.4 %all-to-all-start.1 = ((bf16[16,16,512]{2,1,0:T(8,128)(2,1)}), bf16[16,16,512]{2,1,0:T(8,128)(2,1)S(1)}, u32[]{:S(2)}, u32[]{:S(2)}) async-start(bf16[16,16,512]{2,1,0:T(8,128)(2,1)} %broadcast_in_dim.69), calls=%async_computation.1 | async-start | bytes 524288 | tf_op jit(solution)/shard_map/all_to_all | solution.py:224
  151.5 8.5 %all-to-all-done.1 = bf16[16,16,512]{2,1,0:T(8,128)(2,1)S(1)} async-done(((bf16[16,16,512]{2,1,0:T(8,128)(2,1)}), bf16[16,16,512]{2,1,0:T(8,128)(2,1)S(1)}, u32[]{:S(2)}, u32[]{:S(2)}) %all-to-all-start.1) | async-done | bytes 262176 | tf_op jit(solution)/shard_map/all_to_all | solution.py:224
  160.6 12.5 %all_to_all.19 = f32[16,1,640]{2,1,0:T(1,128)S(1)} all-to-all(f32[16,1,640]{2,1,0:T(1,128)S(1)} %copy.24), channel_id=1, replica_groups=mesh['ylo'=2,'z'=8,'x'=4,'core'=2,'yhi'=2] {'x','core','yhi'}, dimensions={0} | all-to-all | bytes 81920 | tf_op jit(solution)/shard_map/all_to_all | solution.py:245
  (111 shorter events, 16.7 us)
Async XLA Ops:
  6.5 28.9 %copy-start = (bf16[64,5120]{1,0:T(8,128)(2,1)S(1)}, bf16[64,5120]{1,0:T(8,128)(2,1)}, u32[]{:S(2)}) copy-start(bf16[64,5120]{1,0:T(8,128)(2,1)} %param.15) | copy-start | bytes 1966084
  6.5 88.3 %all-gather.2.cloned.1.call-start = ((), (), s32[]{:S(2)}) async-start(), calls=%async_computation.3 | async-start | bytes 5898240 | tf_op jit(solution)/shard_map/all_gather | solution.py:52
  7.9 19.3 %collective-permute-start = (bf16[320,896]{1,0:T(8,128)(2,1)S(1)}, bf16[320,896]{1,0:T(8,128)(2,1)}, u32[]{:S(2)}, u32[]{:S(2)}) collective-permute-start(bf16[320,896]{1,0:T(8,128)(2,1)S(1)} %pad_maximum_fusion.2), channel_id=1, source_target_pairs={{0,16},{16,32},{32,48},{48,64},{64,80},{80,96},{96,112},{112,0},{1... | collective-permute-start | bytes 1720328 | tf_op jit(solution)/shard_map/ppermute | solution.py:11
  10.4 16.8 %collective-permute-start.1 = (bf16[320,896]{1,0:T(8,128)(2,1)S(1)}, bf16[320,896]{1,0:T(8,128)(2,1)}, u32[]{:S(2)}, u32[]{:S(2)}) collective-permute-start(bf16[320,896]{1,0:T(8,128)(2,1)S(1)} %pad_maximum_fusion.2), channel_id=1, source_target_pairs={{0,112},{16,0},{32,16},{48,32},{64,48},{80,64},{96,80},{112,96},{1... | collective-permute-start | bytes 1720328 | tf_op jit(solution)/shard_map/ppermute | solution.py:11
  14.4 13.6 %collective-permute-start.2 = (bf16[320,896]{1,0:T(8,128)(2,1)S(1)}, bf16[320,896]{1,0:T(8,128)(2,1)S(1)}, u32[]{:S(2)}, u32[]{:S(2)}) collective-permute-start(bf16[320,896]{1,0:T(8,128)(2,1)S(1)} %pad_maximum_fusion.2), channel_id=1, source_target_pairs={{0,128},{128,0},{1,129},{129,1},{2,130},{130,2},{3,131},{131,3},{4... | collective-permute-start | bytes 1720328 | tf_op jit(solution)/shard_map/ppermute | solution.py:11
  15.7 6.5 %copy-start.10 = (bf16[8,32,896]{2,1,0:T(8,128)(2,1)S(1)}, bf16[8,32,896]{2,1,0:T(8,128)(2,1)}, u32[]{:S(2)}) copy-start(bf16[8,32,896]{2,1,0:T(8,128)(2,1)} %param.12) | copy-start | bytes 1376260
  15.7 6.5 %copy-start.11 = (bf16[8,32,896]{2,1,0:T(8,128)(2,1)S(1)}, bf16[8,32,896]{2,1,0:T(8,128)(2,1)}, u32[]{:S(2)}) copy-start(bf16[8,32,896]{2,1,0:T(8,128)(2,1)} %param.10) | copy-start | bytes 1376260
  24.4 11.0 %copy-start.1 = (bf16[8,64,5120]{2,1,0:T(8,128)(2,1)S(1)}, bf16[8,64,5120]{2,1,0:T(8,128)(2,1)}, u32[]{:S(2)}) copy-start(bf16[8,64,5120]{2,1,0:T(8,128)(2,1)} %pad_maximum_fusion) | copy-start | bytes 15728644
  28.0 14.2 %collective-permute-start.3 = (bf16[320,896]{1,0:T(8,128)(2,1)}, bf16[320,896]{1,0:T(8,128)(2,1)}, u32[]{:S(2)}, u32[]{:S(2)}) collective-permute-start(bf16[320,896]{1,0:T(8,128)(2,1)} %collective-permute-done), channel_id=1, source_target_pairs={{0,16},{16,32},{32,48},{48,64},{64,80},{80,96},{96,112},{112,0},{1... | collective-permute-start | bytes 1720328 | tf_op jit(solution)/shard_map/ppermute | solution.py:11
  28.0 14.2 %collective-permute-start.4 = (bf16[320,896]{1,0:T(8,128)(2,1)}, bf16[320,896]{1,0:T(8,128)(2,1)}, u32[]{:S(2)}, u32[]{:S(2)}) collective-permute-start(bf16[320,896]{1,0:T(8,128)(2,1)} %collective-permute-done.1), channel_id=1, source_target_pairs={{0,112},{16,0},{32,16},{48,32},{64,48},{80,64},{96,80},{112,96},{1... | collective-permute-start | bytes 1720328 | tf_op jit(solution)/shard_map/ppermute | solution.py:11
  30.7 15.3 %collective-permute-start.5 = (bf16[1,64,5120]{2,1,0:T(8,128)(2,1)S(1)}, bf16[1,64,5120]{2,1,0:T(8,128)(2,1)S(1)}, u32[]{:S(2)}, u32[]{:S(2)}) collective-permute-start(bf16[1,64,5120]{2,1,0:T(8,128)(2,1)S(1)} %pad_maximum_fusion.1), channel_id=1, source_target_pairs={{0,1},{1,0},{2,3},{3,2},{4,5},{5,4},{6,7},{7,6},{8,9},{9,8},{10,11... | collective-permute-start | bytes 1966088 | tf_op jit(solution)/shard_map/ppermute | solution.py:11
  35.4 2.4 %copy-start.5 = (bf16[8,320,896]{2,1,0:T(8,128)(2,1)}, bf16[8,320,896]{2,1,0:T(8,128)(2,1)S(1)}, u32[]{:S(2)}) copy-start(bf16[8,320,896]{2,1,0:T(8,128)(2,1)S(1)} %bitcast_dynamic-update-slice_fusion.10) | copy-start | bytes 13762564
  35.4 39.1 %slice-start = ((s8[5242880]{0:T(1024)(128)(4,1)}), s8[1048576]{0:T(1024)(128)(4,1)S(1)}, s32[]{:S(2)}) async-start(s8[5242880]{0:T(1024)(128)(4,1)} %bitcast.77), calls=%async_computation.4 | async-start | bytes 2097152
  46.0 0.8 copy-start.9
  47.0 27.5 %slice-start.1 = ((s8[5242880]{0:T(1024)(128)(4,1)}), s8[4194304]{0:T(1024)(128)(4,1)S(1)}, s32[]{:S(2)}) async-start(s8[5242880]{0:T(1024)(128)(4,1)} %bitcast.77), calls=%async_computation.5 | async-start | bytes 8388608
  47.0 13.4 %collective-permute-start.6 = (bf16[320,896]{1,0:T(8,128)(2,1)}, bf16[320,896]{1,0:T(8,128)(2,1)S(1)}, u32[]{:S(2)}, u32[]{:S(2)}) collective-permute-start(bf16[320,896]{1,0:T(8,128)(2,1)} %collective-permute-done.3), channel_id=1, source_target_pairs={{0,16},{16,32},{32,48},{48,64},{64,80},{80,96},{96,112},{112,0},{1... | collective-permute-start | bytes 1720328 | tf_op jit(solution)/shard_map/ppermute | solution.py:11
  47.1 13.3 %collective-permute-start.8 = (bf16[320,896]{1,0:T(8,128)(2,1)}, bf16[320,896]{1,0:T(8,128)(2,1)}, u32[]{:S(2)}, u32[]{:S(2)}) collective-permute-start(bf16[320,896]{1,0:T(8,128)(2,1)} %collective-permute-done.3), channel_id=1, source_target_pairs={{0,128},{128,0},{1,129},{129,1},{2,130},{130,2},{3,131},{131,3},{4... | collective-permute-start | bytes 1720328 | tf_op jit(solution)/shard_map/ppermute | solution.py:11
  48.5 12.0 %collective-permute-start.7 = (bf16[320,896]{1,0:T(8,128)(2,1)}, bf16[320,896]{1,0:T(8,128)(2,1)S(1)}, u32[]{:S(2)}, u32[]{:S(2)}) collective-permute-start(bf16[320,896]{1,0:T(8,128)(2,1)} %collective-permute-done.4), channel_id=1, source_target_pairs={{0,112},{16,0},{32,16},{48,32},{64,48},{80,64},{96,80},{112,96},{1... | collective-permute-start | bytes 1720328 | tf_op jit(solution)/shard_map/ppermute | solution.py:11
  53.9 18.3 %collective-permute-start.14 = (bf16[512,448]{1,0:T(8,128)(2,1)}, bf16[512,448]{1,0:T(8,128)(2,1)S(1)}, u32[]{:S(2)}, u32[]{:S(2)}) collective-permute-start(bf16[512,448]{1,0:T(8,128)(2,1)} %bitcast.95), channel_id=1, source_target_pairs={{0,1},{1,0},{2,3},{3,2},{4,5},{5,4},{6,7},{7,6},{8,9},{9,8},{10,11... | collective-permute-start | bytes 1376264 | tf_op jit(solution)/shard_map/ppermute | solution.py:11
  60.4 20.1 %collective-permute-start.9 = (bf16[320,896]{1,0:T(8,128)(2,1)S(1)}, bf16[320,896]{1,0:T(8,128)(2,1)S(1)}, u32[]{:S(2)}, u32[]{:S(2)}) collective-permute-start(bf16[320,896]{1,0:T(8,128)(2,1)S(1)} %collective-permute-done.2), channel_id=1, source_target_pairs={{0,16},{16,32},{32,48},{48,64},{64,80},{80,96},{96,112},{112,0},{1... | collective-permute-start | bytes 1720328 | tf_op jit(solution)/shard_map/ppermute | solution.py:11
  60.5 20.0 %collective-permute-start.10 = (bf16[320,896]{1,0:T(8,128)(2,1)S(1)}, bf16[320,896]{1,0:T(8,128)(2,1)S(1)}, u32[]{:S(2)}, u32[]{:S(2)}) collective-permute-start(bf16[320,896]{1,0:T(8,128)(2,1)S(1)} %collective-permute-done.2), channel_id=1, source_target_pairs={{0,112},{16,0},{32,16},{48,32},{64,48},{80,64},{96,80},{112,96},{1... | collective-permute-start | bytes 1720328 | tf_op jit(solution)/shard_map/ppermute | solution.py:11
  63.2 19.0 %collective-permute-start.11 = (bf16[320,896]{1,0:T(8,128)(2,1)}, bf16[320,896]{1,0:T(8,128)(2,1)}, u32[]{:S(2)}, u32[]{:S(2)}) collective-permute-start(bf16[320,896]{1,0:T(8,128)(2,1)} %collective-permute-done.4), channel_id=1, source_target_pairs={{0,128},{128,0},{1,129},{129,1},{2,130},{130,2},{3,131},{131,3},{4... | collective-permute-start | bytes 1720328 | tf_op jit(solution)/shard_map/ppermute | solution.py:11
  63.7 16.8 %collective-permute-start.12 = (bf16[160,896]{1,0:T(8,128)(2,1)S(1)}, bf16[160,896]{1,0:T(8,128)(2,1)S(1)}, u32[]{:S(2)}, u32[]{:S(2)}) collective-permute-start(bf16[160,896]{1,0:T(8,128)(2,1)S(1)} %slice.34), channel_id=1, source_target_pairs={{0,16},{16,32},{32,48},{48,64},{64,80},{80,96},{96,112},{112,0},{1... | collective-permute-start | bytes 860168 | tf_op jit(solution)/shard_map/ppermute | solution.py:11
  72.2 2.3 %copy-start.14 = (bf16[512,448]{1,0:T(8,128)(2,1)}, bf16[512,448]{1,0:T(8,128)(2,1)S(1)}, u32[]{:S(2)}) copy-start(bf16[512,448]{1,0:T(8,128)(2,1)S(1)} %collective-permute-done.14) | copy-start | bytes 1376260
  72.2 8.3 %collective-permute-start.13 = (bf16[160,896]{1,0:T(8,128)(2,1)S(1)}, bf16[160,896]{1,0:T(8,128)(2,1)S(1)}, u32[]{:S(2)}, u32[]{:S(2)}) collective-permute-start(bf16[160,896]{1,0:T(8,128)(2,1)S(1)} %slice.35), channel_id=1, source_target_pairs={{0,112},{16,0},{32,16},{48,32},{64,48},{80,64},{96,80},{112,96},{1... | collective-permute-start | bytes 860168 | tf_op jit(solution)/shard_map/ppermute | solution.py:11
  83.6 24.4 %collective-permute-start.15 = (bf16[320,896]{1,0:T(8,128)(2,1)}, bf16[320,896]{1,0:T(8,128)(2,1)}, u32[]{:S(2)}, u32[]{:S(2)}) collective-permute-start(bf16[320,896]{1,0:T(8,128)(2,1)} %constant_dynamic-update-slice_fusion), channel_id=1, source_target_pairs={{0,128},{128,0},{1,129},{129,1},{2,130},{130,2},{3,131},{131,3},{4... | collective-permute-start | bytes 1720328 | tf_op jit(solution)/shard_map/ppermute | solution.py:11
  84.9 23.1 %collective-permute-start.16 = (bf16[320,896]{1,0:T(8,128)(2,1)}, bf16[320,896]{1,0:T(8,128)(2,1)}, u32[]{:S(2)}, u32[]{:S(2)}) collective-permute-start(bf16[320,896]{1,0:T(8,128)(2,1)} %collective-permute-done.8), channel_id=1, source_target_pairs={{0,16},{16,32},{32,48},{48,64},{64,80},{80,96},{96,112},{112,0},{1... | collective-permute-start | bytes 1720328 | tf_op jit(solution)/shard_map/ppermute | solution.py:11
  85.8 22.3 %collective-permute-start.17 = (bf16[320,896]{1,0:T(8,128)(2,1)}, bf16[320,896]{1,0:T(8,128)(2,1)}, u32[]{:S(2)}, u32[]{:S(2)}) collective-permute-start(bf16[320,896]{1,0:T(8,128)(2,1)} %collective-permute-done.11), channel_id=1, source_target_pairs={{0,112},{16,0},{32,16},{48,32},{64,48},{80,64},{96,80},{112,96},{1... | collective-permute-start | bytes 1720328 | tf_op jit(solution)/shard_map/ppermute | solution.py:11
  90.0 2.9 %copy-start.3 = (bf16[8,320,896]{2,1,0:T(8,128)(2,1)}, bf16[8,320,896]{2,1,0:T(8,128)(2,1)S(1)}, u32[]{:S(2)}) copy-start(bf16[8,320,896]{2,1,0:T(8,128)(2,1)S(1)} %bitcast_dynamic-update-slice_fusion) | copy-start | bytes 13762564
  94.8 6.1 %copy-start.2 = (bf16[8,64,5120]{2,1,0:T(8,128)(2,1)S(1)}, bf16[8,64,5120]{2,1,0:T(8,128)(2,1)}, u32[]{:S(2)}) copy-start(bf16[8,64,5120]{2,1,0:T(8,128)(2,1)} %all-gather.2.cloned.1.call-done) | copy-start | bytes 15728644
  94.9 6.1 %copy-start.4 = (bf16[8,320,896]{2,1,0:T(8,128)(2,1)S(1)}, bf16[8,320,896]{2,1,0:T(8,128)(2,1)}, u32[]{:S(2)}) copy-start(bf16[8,320,896]{2,1,0:T(8,128)(2,1)} %copy-done.3) | copy-start | bytes 13762564
  111.5 1.9 %copy-start.15 = (bf16[512,448]{1,0:T(8,128)(2,1)S(1)}, bf16[512,448]{1,0:T(8,128)(2,1)}, u32[]{:S(2)}) copy-start(bf16[512,448]{1,0:T(8,128)(2,1)} %copy-done.14) | copy-start | bytes 1376260
  111.5 1.9 %copy-start.16 = (bf16[64,896]{1,0:T(8,128)(2,1)S(1)}, bf16[64,896]{1,0:T(8,128)(2,1)}, u32[]{:S(2)}) copy-start(bf16[64,896]{1,0:T(8,128)(2,1)} %param.17) | copy-start | bytes 344068
  113.4 0.9 copy-start.17
  114.3 1.0 copy-start.8
  114.3 2.7 %copy-start.7 = (bf16[512,320]{1,0:T(8,128)(2,1)S(1)}, bf16[512,320]{1,0:T(8,128)(2,1)}, u32[]{:S(2)}) copy-start(bf16[512,320]{1,0:T(8,128)(2,1)} %get-tuple-element.74) | copy-start | bytes 983044
  114.3 4.4 %copy-start.6 = (bf16[512,320]{1,0:T(8,128)(2,1)S(1)}, bf16[512,320]{1,0:T(8,128)(2,1)}, u32[]{:S(2)}) copy-start(bf16[512,320]{1,0:T(8,128)(2,1)} %get-tuple-element.78) | copy-start | bytes 983044
  118.7 2.2 %copy-start.13 = (bf16[8,64,448]{2,1,0:T(8,128)(2,1)S(1)}, bf16[8,64,448]{2,1,0:T(8,128)(2,1)}, u32[]{:S(2)}) copy-start(bf16[8,64,448]{2,1,0:T(8,128)(2,1)} %pad_maximum_fusion.4) | copy-start | bytes 1376260
  121.4 13.4 %copy-start.12 = (f32[512,64]{0,1:T(8,128)S(1)}, f32[512,64]{0,1:T(8,128)}, u32[]{:S(2)}) copy-start(f32[512,64]{0,1:T(8,128)} %fusion.56) | copy-start | bytes 393220
  122.8 21.3 %all-to-all-start = ((bf16[16,8,1024]{2,1,0:T(8,128)(2,1)}), bf16[16,8,1024]{2,1,0:T(8,128)(2,1)S(1)}, u32[]{:S(2)}, u32[]{:S(2)}) async-start(bf16[16,8,1024]{2,1,0:T(8,128)(2,1)} %pad_maximum_fusion.7), calls=%async_computation | async-start | bytes 524288 | tf_op jit(solution)/shard_map/all_to_all | solution.py:208
  145.7 14.3 %all-to-all-start.1 = ((bf16[16,16,512]{2,1,0:T(8,128)(2,1)}), bf16[16,16,512]{2,1,0:T(8,128)(2,1)S(1)}, u32[]{:S(2)}, u32[]{:S(2)}) async-start(bf16[16,16,512]{2,1,0:T(8,128)(2,1)} %broadcast_in_dim.69), calls=%async_computation.1 | async-start | bytes 524288 | tf_op jit(solution)/shard_map/all_to_all | solution.py:224
Sparse Core Ops, SparseCore 0:
  47.0 41.8 all-gather.1

commit v13 on v10

--- a/solution.py
+++ b/solution.py
@@ -1,6 +1,8 @@
 import jax
 import jax.numpy as jnp
 from jax import lax
+from jax.experimental import pallas as pl
+from jax.experimental.pallas import tpu as pltpu
 from jax.sharding import PartitionSpec as P
 
 F32 = jnp.float32
@@ -71,6 +73,45 @@
     )
     flat = (n_z * weight.shape[0], -1)
     return this_row.reshape(flat), other_row.reshape(flat), last, other_cot, partner, early, own_factor
+
+
+VMEM_LIMIT = 14 * 2**20
+ROWS = 256
+WHOLE = pl.BlockSpec(memory_space=pltpu.VMEM)
+
+
+def halves_kernel(side_ref, this_x, other_x, this_row, other_row, out):
+    del side_ref
+    out[...] = jnp.dot(
+        this_x[...], this_row[...], preferred_element_type=F32
+    ) + jnp.dot(other_x[...], other_row[...], preferred_element_type=F32)
+
+
+def halves_product(rows, this_row, other_row, row_index):
+    count, width = rows.shape
+    depth, cols = this_row.shape
+    return pl.pallas_call(
+        halves_kernel,
+        out_shape=jax.ShapeDtypeStruct((count, cols), F32),
+        grid_spec=pltpu.PrefetchScalarGridSpec(
+            num_scalar_prefetch=1,
+            grid=(count // ROWS,),
+            in_specs=[
+                pl.BlockSpec((ROWS, depth), lambda i, side: (i, side[0])),
+                pl.BlockSpec((ROWS, depth), lambda i, side: (i, 1 - side[0])),
+                WHOLE,
+                WHOLE,
+            ],
+            out_specs=pl.BlockSpec((ROWS, cols), lambda i, side: (i, 0)),
+        ),
+        compiler_params=pltpu.CompilerParams(vmem_limit_bytes=VMEM_LIMIT),
+        cost_estimate=pl.CostEstimate(
+            flops=2 * count * width * cols,
+            bytes_accessed=2 * count * width + 4 * count * cols,
+            transcendentals=0,
+        ),
+        name="halves_product",
+    )(row_index.astype(jnp.int32).reshape(1), rows, rows, this_row, other_row)
 
 
 def projected(pre, cotangent, gate_projection, up_projection):
@@ -154,10 +195,14 @@
     chunks = []
     for rows in (own, other):
         flat = rows.reshape(-1, width)
-        this_flat = lax.dynamic_slice_in_dim(flat, row_index * depth, depth, 1)
         other_flat = lax.dynamic_slice_in_dim(flat, (1 - row_index) * depth, depth, 1)
-        pre = jnp.dot(this_flat, this_row, preferred_element_type=F32)
-        pres.append(pre + jnp.dot(other_flat, other_row, preferred_element_type=F32))
+        if rows is own:
+            this_flat = lax.dynamic_slice_in_dim(flat, row_index * depth, depth, 1)
+            pre = jnp.dot(this_flat, this_row, preferred_element_type=F32)
+            pre = pre + jnp.dot(other_flat, other_row, preferred_element_type=F32)
+        else:
+            pre = halves_product(flat, this_row, other_row, row_index)
+        pres.append(pre)
         chunks.append(
             [
                 lax.dynamic_slice_in_dim(other_flat, place * shard_depth, shard_depth, 1)
@@ -180,11 +225,15 @@
         b = jnp.where(first, pair[1], pair[0])
         return jnp.concatenate((a, b), axis=axis)
 
-    part = ordered(parts, 1).astype(BF16)
+    part = ordered(parts, 1)
     in_factor = ordered(factors, 0)
     ranks = part.shape[0] // n_dq
-    part = part.reshape(n_dq, ranks, -1)
-    swapped = lax.all_to_all(part, dq, 0, 0, tiled=True)
+    core = lax.axis_index("core")
+    part = part.reshape(2, n_dq // 2, ranks, -1)
+    mine = lax.dynamic_index_in_dim(part, core, 0, keepdims=False)
+    theirs = lax.dynamic_index_in_dim(part, 1 - core, 0, keepdims=False)
+    part = (mine + shift(theirs, "core", 1)).astype(BF16)
+    swapped = lax.all_to_all(part, ("x", "yhi"), 0, 0, tiled=True)
     out_sum = jnp.sum(swapped.astype(F32), axis=0)
 
     pairs = 2 * count

time: 178 us -> 184 us (1.034)
  local copies, waits for them, and re-layouts: 21.3 us -> 30.7 us
  Pallas kernels: 0 us -> 8.33 us
  waiting for transfers between devices: 43.7 us -> 36.4 us
  matrix products: 28 us -> 23.5 us
  blocking collectives: 12.1 us -> 14.1 us
    pallas_call x0 -> x1, Pallas kernels: none -> 8.33 us  [halves_product(): pl.pallas_call(halves_kernel, out_shape=jax.ShapeDtypeStruct((count, cols...]
    dot_general x2 -> x1, matrix products: 8.98 us -> 2.88 us  [body(): pre = pre + jnp.dot(other_flat, other_row, preferred_element_type=F32)]
    all_to_all x1, starting transfers between devices: 11.7 us -> 6.14 us  [body(): swapped = lax.all_to_all(part, ('x', 'yhi'), 0, 0, tiled=True)]
    dynamic_update_slice x13, local copies, waits for them, and re-layouts: 10.4 us -> 15.5 us  [placed(): lax.dynamic_update_slice(result, shard[None], ((z + offset) % n_z, 0, 0))]
    ppermute x18 -> x19, starting transfers between devices: 30.5 us -> 35.4 us  [shift(): lax.ppermute(value, axis, [(i, (i + step) % size) for i in range(size)])]
    ppermute x18 -> x19, waiting for transfers between devices: 26.1 us -> 22.3 us  [shift(): lax.ppermute(value, axis, [(i, (i + step) % size) for i in range(size)])]
    dot_general x2, matrix products: 4.72 us -> 7.35 us  [inner_factor(): lax.dot_general(rows.reshape(-1, width), input_projection, (((1,), (1,)),...]
    all_to_all x1, waiting for transfers between devices: 9.1 us -> 6.71 us  [body(): swapped = lax.all_to_all(part, ('x', 'yhi'), 0, 0, tiled=True)]
  transfers between devices with their start and end apart: 21 -> 22, of which waited for: 12 -> 13; matrix products, arithmetic and copies ran while one was open for 26% -> 26% of each run, Pallas kernels for 0% -> 5%
where the time goes in v13:
time: 184 us; the launch traced here: 183 us
  starting transfers between devices  46.4 us (25%)
  waiting for transfers between devices  36.4 us (20%)
  local copies, waits for them, and re-layouts  30.7 us (17%)
  matrix products  23.5 us (13%)
  between operations  14.7 us (8%)
  blocking collectives  14.1 us (8%)
  other arithmetic  9.22 us (5%)
  Pallas kernels  8.33 us (5%)
    ppermute x19, starting transfers between devices, shift(): lax.ppermute(value, axis, [(i, (i + step) % size) for i in range(size)])  35.4 us
    ppermute x19, waiting for transfers between devices, shift(): lax.ppermute(value, axis, [(i, (i + step) % size) for i in range(size)])  22.3 us
    dynamic_update_slice x13, local copies, waits for them, and re-layouts, placed(): lax.dynamic_update_slice(result, shard[None], ((z + offset) % n_z, 0, 0))  15.5 us
    all_to_all x1, blocking collectives, body(): received = lax.all_to_all(payload, dq, 0, 0, tiled=True)  14.1 us
    pallas_call x1, Pallas kernels, halves_product(): pl.pallas_call(halves_kernel, out_shape=jax.ShapeDtypeStruct((count, cols...  8.33 us
    all_to_all x1, waiting for transfers between devices, body(): lax.all_to_all(jnp.broadcast_to(queries[None], (n_fsdp,) + queries.shape)...  7.36 us
    dot_general x2, matrix products, inner_factor(): lax.dot_general(rows.reshape(-1, width), input_projection, (((1,), (1,)),...  7.35 us
    all_to_all x1, waiting for transfers between devices, body(): swapped = lax.all_to_all(part, ('x', 'yhi'), 0, 0, tiled=True)  6.71 us
  transfers between devices with their start and end apart: 22, of which 13 were waited for; matrix products, arithmetic and copies ran while one was open for 26% of the time, Pallas kernels for 5%

profile of v13, /device:TPU:1, one launch (start us, length us, event | category | flops | bytes accessed | tf_op | source)
XLA Modules:
  0.0 183.3 jit_solution(13063608829142986433)
XLA Ops:
  6.5 1.3 pad_maximum_fusion.2
  7.9 2.5 %collective-permute-start = (bf16[320,896]{1,0:T(8,128)(2,1)S(1)}, bf16[320,896]{1,0:T(8,128)(2,1)}, u32[]{:S(2)}, u32[]{:S(2)}) collective-permute-start(bf16[320,896]{1,0:T(8,128)(2,1)S(1)} %pad_maximum_fusion.2), channel_id=1, source_target_pairs={{0,16},{16,32},{32,48},{48,64},{64,80},{80,96},{96,112},{112,0},{1... | collective-permute-start | bytes 1720328 | tf_op jit(solution)/shard_map/ppermute | solution.py:13
  10.4 4.0 %collective-permute-start.1 = (bf16[320,896]{1,0:T(8,128)(2,1)S(1)}, bf16[320,896]{1,0:T(8,128)(2,1)}, u32[]{:S(2)}, u32[]{:S(2)}) collective-permute-start(bf16[320,896]{1,0:T(8,128)(2,1)S(1)} %pad_maximum_fusion.2), channel_id=1, source_target_pairs={{0,112},{16,0},{32,16},{48,32},{64,48},{80,64},{96,80},{112,96},{1... | collective-permute-start | bytes 1720328 | tf_op jit(solution)/shard_map/ppermute | solution.py:13
  14.4 1.3 collective-permute-start.2
  15.7 5.3 %pad_maximum_fusion = bf16[8,64,5120]{2,1,0:T(8,128)(2,1)} fusion(bf16[8,32,5120]{2,1,0:T(8,128)(2,1)} %param.11, bf16[8,32,5120]{2,1,0:T(8,128)(2,1)} %param.9), kind=kLoop, calls=%fused_computation | loop fusion | flops 10485760 | bytes 10485760 | tf_op jit(solution)/shard_map/concatenate | solution.py:164
  21.0 1.1 constant_dynamic-slice_fusion.8
  22.7 0.9 pad_maximum_fusion.4
  23.6 3.6 %collective-permute-done = bf16[320,896]{1,0:T(8,128)(2,1)} collective-permute-done((bf16[320,896]{1,0:T(8,128)(2,1)S(1)}, bf16[320,896]{1,0:T(8,128)(2,1)}, u32[]{:S(2)}, u32[]{:S(2)}) %collective-permute-start) | collective-permute-done | bytes 573472 | tf_op jit(solution)/shard_map/ppermute | solution.py:13
  28.0 2.7 %collective-permute-start.4 = (bf16[320,896]{1,0:T(8,128)(2,1)}, bf16[320,896]{1,0:T(8,128)(2,1)}, u32[]{:S(2)}, u32[]{:S(2)}) collective-permute-start(bf16[320,896]{1,0:T(8,128)(2,1)} %collective-permute-done.1), channel_id=1, source_target_pairs={{0,112},{16,0},{32,16},{48,32},{64,48},{80,64},{96,80},{112,96},{1... | collective-permute-start | bytes 1720328 | tf_op jit(solution)/shard_map/ppermute | solution.py:13
  30.7 2.9 %collective-permute-start.5 = (bf16[1,64,5120]{2,1,0:T(8,128)(2,1)S(1)}, bf16[1,64,5120]{2,1,0:T(8,128)(2,1)S(1)}, u32[]{:S(2)}, u32[]{:S(2)}) collective-permute-start(bf16[1,64,5120]{2,1,0:T(8,128)(2,1)S(1)} %pad_maximum_fusion.1), channel_id=1, source_target_pairs={{0,1},{1,0},{2,3},{3,2},{4,5},{5,4},{6,7},{7,6},{8,9},{9,8},{10,11... | collective-permute-start | bytes 1966088 | tf_op jit(solution)/shard_map/ppermute | solution.py:13
  33.6 2.6 %broadcast.20.clone = bf16[8,320,896]{2,1,0:T(8,128)(2,1)} broadcast(bf16[]{:T(256)} %constant.171.clone.1), dimensions={} | broadcast | bytes 4587522 | tf_op jit(solution)/shard_map/broadcast.3
  36.2 0.8 bitcast_dynamic-update-slice_fusion.12
  37.1 1.9 %bitcast_dynamic-update-slice_fusion.11 = bf16[8,320,896]{2,1,0:T(8,128)(2,1)} fusion(bf16[8,320,896]{2,1,0:T(8,128)(2,1)} %bitcast_dynamic-update-slice_fusion.12, s32[]{:T(128)S(6)} %select_n.168, bf16[320,896]{1,0:T(8,128)(2,1)} %collective-permute-done), kind=kLoop, calls=%fused_computation.42 | loop fusion | bytes 1146884 | tf_op jit(solution)/shard_map/dynamic_update_slice | solution.py:34
  39.0 2.3 %fusion.52 = f32[512,64]{0,1:T(8,128)} fusion(bf16[512,5120]{1,0:T(8,128)(2,1)S(1)} %bitcast.87, bf16[64,5120]{1,0:T(8,128)(2,1)S(1)} %copy-done), kind=kOutput, calls=%fused_computation.102 | convolution fusion | flops 335544320 | bytes 6029312 | tf_op jit(solution)/shard_map/dot_general | solution.py:179
  42.2 3.8 %collective-permute-done.5 = bf16[1,64,5120]{2,1,0:T(8,128)(2,1)S(1)} collective-permute-done((bf16[1,64,5120]{2,1,0:T(8,128)(2,1)S(1)}, bf16[1,64,5120]{2,1,0:T(8,128)(2,1)S(1)}, u32[]{:S(2)}, u32[]{:S(2)}) %collective-permute-start.5) | collective-permute-done | bytes 655392 | tf_op jit(solution)/shard_map/ppermute | solution.py:13
  47.1 1.4 collective-permute-start.8
  48.5 2.6 %collective-permute-start.7 = (bf16[320,896]{1,0:T(8,128)(2,1)}, bf16[320,896]{1,0:T(8,128)(2,1)S(1)}, u32[]{:S(2)}, u32[]{:S(2)}) collective-permute-start(bf16[320,896]{1,0:T(8,128)(2,1)} %collective-permute-done.4), channel_id=1, source_target_pairs={{0,112},{16,0},{32,16},{48,32},{64,48},{80,64},{96,80},{112,96},{1... | collective-permute-start | bytes 1720328 | tf_op jit(solution)/shard_map/ppermute | solution.py:13
  51.0 1.9 %constant_dynamic-slice_fusion.3 = (bf16[512,320]{1,0:T(8,128)(2,1)S(1)}, bf16[512,320]{1,0:T(8,128)(2,1)S(1)}, bf16[512,320]{1,0:T(8,128)(2,1)S(1)}) fusion(bf16[512,5120]{1,0:T(8,128)(2,1)} %bitcast.86, s32[]{:T(128)S(6)} %dynamic_slice.81, s32[]{:T(128)S(6)} %dynamic_slice.79, s32[]{:T(128)S(6)} %dynamic_slice.77), kind=kLoop, calls=%fused_computation.83 | loop fusion | bytes 1966092 | tf_op jit(solution)/shard_map/dynamic_slice | solution.py:208
  52.9 2.7 %collective-permute-start.14 = (bf16[512,448]{1,0:T(8,128)(2,1)S(1)}, bf16[512,448]{1,0:T(8,128)(2,1)S(1)}, u32[]{:S(2)}, u32[]{:S(2)}) collective-permute-start(bf16[512,448]{1,0:T(8,128)(2,1)S(1)} %bitcast.100), channel_id=1, source_target_pairs={{0,1},{1,0},{2,3},{3,2},{4,5},{5,4},{6,7},{7,6},{8,9},{9,8},{10,11... | collective-permute-start | bytes 1376264 | tf_op jit(solution)/shard_map/ppermute | solution.py:13
  55.6 1.9 %bitcast_dynamic-update-slice_fusion.10 = bf16[8,320,896]{2,1,0:T(8,128)(2,1)} fusion(bf16[8,320,896]{2,1,0:T(8,128)(2,1)} %bitcast_dynamic-update-slice_fusion.11, s32[]{:T(128)S(6)} %select_n.170, bf16[320,896]{1,0:T(8,128)(2,1)} %collective-permute-done.1), kind=kLoop, calls=%fused_computation.41 | loop fusion | bytes 1146884 | tf_op jit(solution)/shard_map/dynamic_update_slice | solution.py:34
  57.5 1.9 %bitcast_dynamic-update-slice_fusion.9 = bf16[8,320,896]{2,1,0:T(8,128)(2,1)} fusion(bf16[8,320,896]{2,1,0:T(8,128)(2,1)} %bitcast_dynamic-update-slice_fusion.10, s32[]{:T(128)S(6)} %select_n.172, bf16[320,896]{1,0:T(8,128)(2,1)} %collective-permute-done.3), kind=kLoop, calls=%fused_computation.40 | loop fusion | bytes 1146884 | tf_op jit(solution)/shard_map/dynamic_update_slice | solution.py:34
  59.8 3.3 %collective-permute-start.10 = (bf16[320,896]{1,0:T(8,128)(2,1)S(1)}, bf16[320,896]{1,0:T(8,128)(2,1)S(1)}, u32[]{:S(2)}, u32[]{:S(2)}) collective-permute-start(bf16[320,896]{1,0:T(8,128)(2,1)S(1)} %copy-done.10), channel_id=1, source_target_pairs={{0,112},{16,0},{32,16},{48,32},{64,48},{80,64},{96,80},{112,96},{1... | collective-permute-start | bytes 1720328 | tf_op jit(solution)/shard_map/ppermute | solution.py:13
  64.0 2.3 %bitcast_dynamic-update-slice_fusion.8 = bf16[8,320,896]{2,1,0:T(8,128)(2,1)} fusion(bf16[8,320,896]{2,1,0:T(8,128)(2,1)} %bitcast_dynamic-update-slice_fusion.9, s32[]{:T(128)S(6)} %select_n.174, bf16[320,896]{1,0:T(8,128)(2,1)} %collective-permute-done.4), kind=kLoop, calls=%fused_computation.39 | loop fusion | bytes 1146884 | tf_op jit(solution)/shard_map/dynamic_update_slice | solution.py:34
  66.3 5.9 %collective-permute-done.14 = bf16[512,448]{1,0:T(8,128)(2,1)S(1)} collective-permute-done((bf16[512,448]{1,0:T(8,128)(2,1)S(1)}, bf16[512,448]{1,0:T(8,128)(2,1)S(1)}, u32[]{:S(2)}, u32[]{:S(2)}) %collective-permute-start.14) | collective-permute-done | bytes 458784 | tf_op jit(solution)/shard_map/ppermute | solution.py:13
  72.2 2.3 %collective-permute-start.13 = (bf16[160,896]{1,0:T(8,128)(2,1)S(1)}, bf16[160,896]{1,0:T(8,128)(2,1)S(1)}, u32[]{:S(2)}, u32[]{:S(2)}) collective-permute-start(bf16[160,896]{1,0:T(8,128)(2,1)S(1)} %slice.35), channel_id=1, source_target_pairs={{0,112},{16,0},{32,16},{48,32},{64,48},{80,64},{96,80},{112,96},{1... | collective-permute-start | bytes 860168 | tf_op jit(solution)/shard_map/ppermute | solution.py:13
  74.5 0.9 bitcast_dynamic-update-slice_fusion.7
  75.4 0.9 bitcast_dynamic-update-slice_fusion.6
  76.2 1.9 %collective-permute-done.12 = bf16[160,896]{1,0:T(8,128)(2,1)S(1)} collective-permute-done((bf16[160,896]{1,0:T(8,128)(2,1)S(1)}, bf16[160,896]{1,0:T(8,128)(2,1)S(1)}, u32[]{:S(2)}, u32[]{:S(2)}) %collective-permute-start.12) | collective-permute-done | bytes 286752 | tf_op jit(solution)/shard_map/ppermute | solution.py:13
  78.2 1.6 collective-permute-done.13
  79.8 2.4 %collective-permute-done.11 = bf16[320,896]{1,0:T(8,128)(2,1)} collective-permute-done((bf16[320,896]{1,0:T(8,128)(2,1)}, bf16[320,896]{1,0:T(8,128)(2,1)}, u32[]{:S(2)}, u32[]{:S(2)}) %collective-permute-start.11) | collective-permute-done | bytes 573472 | tf_op jit(solution)/shard_map/ppermute | solution.py:13
  83.7 1.3 collective-permute-start.15
  85.0 0.9 collective-permute-start.16
  85.8 1.8 collective-permute-start.17
  87.8 1.1 bitcast_dynamic-update-slice_fusion.1
  88.9 1.1 bitcast_dynamic-update-slice_fusion
  90.1 2.4 %bitcast_dynamic-update-slice_fusion.5 = bf16[8,320,896]{2,1,0:T(8,128)(2,1)} fusion(bf16[8,320,896]{2,1,0:T(8,128)(2,1)} %bitcast_dynamic-update-slice_fusion.6, s32[]{:T(128)S(6)} %select_n.180, bf16[320,896]{1,0:T(8,128)(2,1)} %constant_dynamic-update-slice_fusion), kind=kLoop, calls=%fused_computation.36 | loop fusion | bytes 1146884 | tf_op jit(solution)/shard_map/dynamic_update_slice | solution.py:34
  92.5 2.9 %fusion = f32[512,896]{1,0:T(8,128)S(1)} fusion(bf16[2560,896]{1,0:T(8,128)(2,1)S(1)} %bitcast.84, bf16[512,5120]{1,0:T(8,128)(2,1)S(1)} %bitcast.90, s32[]{:T(128)S(6)} %select_n.181), kind=kOutput, calls=%fused_computation.1 | convolution fusion | flops 2348810240 | bytes 9043972 | tf_op jit(solution)/shard_map/dot_general | solution.py:202
  95.4 6.5 %fusion.4 = f32[512,896]{1,0:T(8,128)} fusion(f32[512,896]{1,0:T(8,128)S(1)} %fusion, bf16[2560,896]{1,0:T(8,128)(2,1)} %bitcast.11.this_row, bf16[512,5120]{1,0:T(8,128)(2,1)S(1)} %bitcast.91, s32[]{:T(128)S(6)} %select_n.164), kind=kOutput, calls=%fused_computation.7 | convolution fusion | flops 2349268992 | bytes 10878980 | tf_op jit(solution)/shard_map/dot_general | solution.py:201
  101.8 5.0 %fusion.53 = f32[512,64]{0,1:T(8,128)} fusion(bf16[512,5120]{1,0:T(8,128)(2,1)} %bitcast.80, bf16[64,5120]{1,0:T(8,128)(2,1)S(1)} %copy-done), kind=kOutput, calls=%fused_computation.103 | convolution fusion | flops 335544320 | bytes 6029312 | tf_op jit(solution)/shard_map/dot_general | solution.py:179
  107.4 2.3 %copy-done.3 = bf16[8,320,896]{2,1,0:T(8,128)(2,1)S(1)} copy-done((bf16[8,320,896]{2,1,0:T(8,128)(2,1)S(1)}, bf16[8,320,896]{2,1,0:T(8,128)(2,1)}, u32[]{:S(2)}) %copy-start.3) | copy-done | bytes 4587544
  109.7 8.3 %halves_product.1 = f32[512,896]{1,0:T(8,128)S(1)} custom-call(s32[1]{0:T(128)} %bitcast.18.side_ref, bf16[512,5120]{1,0:T(8,128)(2,1)S(1)} %bitcast.82, bf16[512,5120]{1,0:T(8,128)(2,1)S(1)} %bitcast.83, bf16[2560,896]{1,0:T(8,128)(2,1)} %bitcast.11.this_row, bf16[2560,896]{1,0:T(8,128)(2,1)S(1)} %bitcast.85), custom_call_target="tpu_custom_call" | custom-call | flops 4697620480 | bytes 7077888 | tf_op jit(solution)/shard_map/halves_product/pallas_call | solution.py:93
  125.4 5.4 %collective-permute-start.18 = (f32[8,8,1024]{2,1,0:T(8,128)S(1)}, f32[8,8,1024]{2,1,0:T(8,128)S(1)}, u32[]{:S(2)}, u32[]{:S(2)}) collective-permute-start(f32[8,8,1024]{2,1,0:T(8,128)S(1)} %fusion.26), channel_id=1, source_target_pairs={{0,2},{2,0},{1,3},{3,1},{4,6},{6,4},{5,7},{7,5},{8,10},{10,8},{9,1... | collective-permute-start | bytes 786440 | tf_op jit(solution)/shard_map/ppermute | solution.py:13
  130.9 1.1 collective-permute-done.18
  132.7 6.1 %all-to-all-start = ((bf16[8,8,1024]{2,1,0:T(8,128)(2,1)}), bf16[8,8,1024]{2,1,0:T(8,128)(2,1)S(1)}, u32[]{:S(2)}, u32[]{:S(2)}) async-start(bf16[8,8,1024]{2,1,0:T(8,128)(2,1)} %fusion.30), calls=%async_computation | async-start | bytes 262144 | tf_op jit(solution)/shard_map/all_to_all | solution.py:236
  139.0 6.7 %all-to-all-done = bf16[8,8,1024]{2,1,0:T(8,128)(2,1)S(1)} async-done(((bf16[8,8,1024]{2,1,0:T(8,128)(2,1)}), bf16[8,8,1024]{2,1,0:T(8,128)(2,1)S(1)}, u32[]{:S(2)}, u32[]{:S(2)}) %all-to-all-start) | async-done | bytes 131104 | tf_op jit(solution)/shard_map/all_to_all | solution.py:236
  147.4 4.8 %all-to-all-start.1 = ((bf16[16,16,512]{2,1,0:T(8,128)(2,1)}), bf16[16,16,512]{2,1,0:T(8,128)(2,1)S(1)}, u32[]{:S(2)}, u32[]{:S(2)}) async-start(bf16[16,16,512]{2,1,0:T(8,128)(2,1)} %broadcast_in_dim.73), calls=%async_computation.1 | async-start | bytes 524288 | tf_op jit(solution)/shard_map/all_to_all | solution.py:252
  152.6 7.4 %all-to-all-done.1 = bf16[16,16,512]{2,1,0:T(8,128)(2,1)S(1)} async-done(((bf16[16,16,512]{2,1,0:T(8,128)(2,1)}), bf16[16,16,512]{2,1,0:T(8,128)(2,1)S(1)}, u32[]{:S(2)}, u32[]{:S(2)}) %all-to-all-start.1) | async-done | bytes 262176 | tf_op jit(solution)/shard_map/all_to_all | solution.py:252
  160.5 14.1 %all_to_all.19 = f32[16,1,640]{2,1,0:T(1,128)S(1)} all-to-all(f32[16,1,640]{2,1,0:T(1,128)S(1)} %copy.24), channel_id=1, replica_groups=mesh['ylo'=2,'z'=8,'x'=4,'core'=2,'yhi'=2] {'x','core','yhi'}, dimensions={0} | all-to-all | bytes 81920 | tf_op jit(solution)/shard_map/all_to_all | solution.py:273
  (112 shorter events, 18.4 us)
Async XLA Ops:
  6.5 32.5 %copy-start = (bf16[64,5120]{1,0:T(8,128)(2,1)S(1)}, bf16[64,5120]{1,0:T(8,128)(2,1)}, u32[]{:S(2)}) copy-start(bf16[64,5120]{1,0:T(8,128)(2,1)} %param.15) | copy-start | bytes 1966084
  6.5 95.3 %all-gather.2.cloned.1.call-start = ((), (), s32[]{:S(2)}) async-start(), calls=%async_computation.3 | async-start | bytes 5898240 | tf_op jit(solution)/shard_map/all_gather | solution.py:54
  7.9 19.3 %collective-permute-start = (bf16[320,896]{1,0:T(8,128)(2,1)S(1)}, bf16[320,896]{1,0:T(8,128)(2,1)}, u32[]{:S(2)}, u32[]{:S(2)}) collective-permute-start(bf16[320,896]{1,0:T(8,128)(2,1)S(1)} %pad_maximum_fusion.2), channel_id=1, source_target_pairs={{0,16},{16,32},{32,48},{48,64},{64,80},{80,96},{96,112},{112,0},{1... | collective-permute-start | bytes 1720328 | tf_op jit(solution)/shard_map/ppermute | solution.py:13
  10.4 16.8 %collective-permute-start.1 = (bf16[320,896]{1,0:T(8,128)(2,1)S(1)}, bf16[320,896]{1,0:T(8,128)(2,1)}, u32[]{:S(2)}, u32[]{:S(2)}) collective-permute-start(bf16[320,896]{1,0:T(8,128)(2,1)S(1)} %pad_maximum_fusion.2), channel_id=1, source_target_pairs={{0,112},{16,0},{32,16},{48,32},{64,48},{80,64},{96,80},{112,96},{1... | collective-permute-start | bytes 1720328 | tf_op jit(solution)/shard_map/ppermute | solution.py:13
  14.4 13.6 %collective-permute-start.2 = (bf16[320,896]{1,0:T(8,128)(2,1)S(1)}, bf16[320,896]{1,0:T(8,128)(2,1)S(1)}, u32[]{:S(2)}, u32[]{:S(2)}) collective-permute-start(bf16[320,896]{1,0:T(8,128)(2,1)S(1)} %pad_maximum_fusion.2), channel_id=1, source_target_pairs={{0,128},{128,0},{1,129},{129,1},{2,130},{130,2},{3,131},{131,3},{4... | collective-permute-start | bytes 1720328 | tf_op jit(solution)/shard_map/ppermute | solution.py:13
  15.7 6.4 %copy-start.7 = (bf16[8,32,896]{2,1,0:T(8,128)(2,1)S(1)}, bf16[8,32,896]{2,1,0:T(8,128)(2,1)}, u32[]{:S(2)}) copy-start(bf16[8,32,896]{2,1,0:T(8,128)(2,1)} %param.12) | copy-start | bytes 1376260
  15.7 6.4 %copy-start.8 = (bf16[8,32,896]{2,1,0:T(8,128)(2,1)S(1)}, bf16[8,32,896]{2,1,0:T(8,128)(2,1)}, u32[]{:S(2)}) copy-start(bf16[8,32,896]{2,1,0:T(8,128)(2,1)} %param.10) | copy-start | bytes 1376260
  23.5 15.5 %copy-start.4 = (bf16[8,64,5120]{2,1,0:T(8,128)(2,1)S(1)}, bf16[8,64,5120]{2,1,0:T(8,128)(2,1)}, u32[]{:S(2)}) copy-start(bf16[8,64,5120]{2,1,0:T(8,128)(2,1)} %pad_maximum_fusion) | copy-start | bytes 15728644
  28.0 13.4 %copy-start.9 = (bf16[320,896]{1,0:T(8,128)(2,1)}, bf16[320,896]{1,0:T(8,128)(2,1)S(1)}, u32[]{:S(2)}) copy-start(bf16[320,896]{1,0:T(8,128)(2,1)S(1)} %collective-permute-done.2) | copy-start | bytes 1720324
  28.0 14.2 %collective-permute-start.3 = (bf16[320,896]{1,0:T(8,128)(2,1)}, bf16[320,896]{1,0:T(8,128)(2,1)}, u32[]{:S(2)}, u32[]{:S(2)}) collective-permute-start(bf16[320,896]{1,0:T(8,128)(2,1)} %collective-permute-done), channel_id=1, source_target_pairs={{0,16},{16,32},{32,48},{48,64},{64,80},{80,96},{96,112},{112,0},{1... | collective-permute-start | bytes 1720328 | tf_op jit(solution)/shard_map/ppermute | solution.py:13
  28.0 14.2 %collective-permute-start.4 = (bf16[320,896]{1,0:T(8,128)(2,1)}, bf16[320,896]{1,0:T(8,128)(2,1)}, u32[]{:S(2)}, u32[]{:S(2)}) collective-permute-start(bf16[320,896]{1,0:T(8,128)(2,1)} %collective-permute-done.1), channel_id=1, source_target_pairs={{0,112},{16,0},{32,16},{48,32},{64,48},{80,64},{96,80},{112,96},{1... | collective-permute-start | bytes 1720328 | tf_op jit(solution)/shard_map/ppermute | solution.py:13
  30.7 15.3 %collective-permute-start.5 = (bf16[1,64,5120]{2,1,0:T(8,128)(2,1)S(1)}, bf16[1,64,5120]{2,1,0:T(8,128)(2,1)S(1)}, u32[]{:S(2)}, u32[]{:S(2)}) collective-permute-start(bf16[1,64,5120]{2,1,0:T(8,128)(2,1)S(1)} %pad_maximum_fusion.1), channel_id=1, source_target_pairs={{0,1},{1,0},{2,3},{3,2},{4,5},{5,4},{6,7},{7,6},{8,9},{9,8},{10,11... | collective-permute-start | bytes 1966088 | tf_op jit(solution)/shard_map/ppermute | solution.py:13
  42.2 17.6 %copy-start.10 = (bf16[320,896]{1,0:T(8,128)(2,1)S(1)}, bf16[320,896]{1,0:T(8,128)(2,1)}, u32[]{:S(2)}) copy-start(bf16[320,896]{1,0:T(8,128)(2,1)} %copy-done.9) | copy-start | bytes 1720324
  46.0 0.8 copy-start.6
  47.0 12.6 %collective-permute-start.6 = (bf16[320,896]{1,0:T(8,128)(2,1)}, bf16[320,896]{1,0:T(8,128)(2,1)S(1)}, u32[]{:S(2)}, u32[]{:S(2)}) collective-permute-start(bf16[320,896]{1,0:T(8,128)(2,1)} %collective-permute-done.3), channel_id=1, source_target_pairs={{0,16},{16,32},{32,48},{48,64},{64,80},{80,96},{96,112},{112,0},{1... | collective-permute-start | bytes 1720328 | tf_op jit(solution)/shard_map/ppermute | solution.py:13
  47.1 12.7 %collective-permute-start.8 = (bf16[320,896]{1,0:T(8,128)(2,1)}, bf16[320,896]{1,0:T(8,128)(2,1)}, u32[]{:S(2)}, u32[]{:S(2)}) collective-permute-start(bf16[320,896]{1,0:T(8,128)(2,1)} %collective-permute-done.3), channel_id=1, source_target_pairs={{0,128},{128,0},{1,129},{129,1},{2,130},{130,2},{3,131},{131,3},{4... | collective-permute-start | bytes 1720328 | tf_op jit(solution)/shard_map/ppermute | solution.py:13
  48.5 11.3 %collective-permute-start.7 = (bf16[320,896]{1,0:T(8,128)(2,1)}, bf16[320,896]{1,0:T(8,128)(2,1)S(1)}, u32[]{:S(2)}, u32[]{:S(2)}) collective-permute-start(bf16[320,896]{1,0:T(8,128)(2,1)} %collective-permute-done.4), channel_id=1, source_target_pairs={{0,112},{16,0},{32,16},{48,32},{64,48},{80,64},{96,80},{112,96},{1... | collective-permute-start | bytes 1720328 | tf_op jit(solution)/shard_map/ppermute | solution.py:13
  52.9 19.3 %collective-permute-start.14 = (bf16[512,448]{1,0:T(8,128)(2,1)S(1)}, bf16[512,448]{1,0:T(8,128)(2,1)S(1)}, u32[]{:S(2)}, u32[]{:S(2)}) collective-permute-start(bf16[512,448]{1,0:T(8,128)(2,1)S(1)} %bitcast.100), channel_id=1, source_target_pairs={{0,1},{1,0},{2,3},{3,2},{4,5},{5,4},{6,7},{7,6},{8,9},{9,8},{10,11... | collective-permute-start | bytes 1376264 | tf_op jit(solution)/shard_map/ppermute | solution.py:13
  59.8 20.0 %collective-permute-start.10 = (bf16[320,896]{1,0:T(8,128)(2,1)S(1)}, bf16[320,896]{1,0:T(8,128)(2,1)S(1)}, u32[]{:S(2)}, u32[]{:S(2)}) collective-permute-start(bf16[320,896]{1,0:T(8,128)(2,1)S(1)} %copy-done.10), channel_id=1, source_target_pairs={{0,112},{16,0},{32,16},{48,32},{64,48},{80,64},{96,80},{112,96},{1... | collective-permute-start | bytes 1720328 | tf_op jit(solution)/shard_map/ppermute | solution.py:13
  63.1 19.1 %collective-permute-start.9 = (bf16[320,896]{1,0:T(8,128)(2,1)S(1)}, bf16[320,896]{1,0:T(8,128)(2,1)S(1)}, u32[]{:S(2)}, u32[]{:S(2)}) collective-permute-start(bf16[320,896]{1,0:T(8,128)(2,1)S(1)} %copy-done.10), channel_id=1, source_target_pairs={{0,16},{16,32},{32,48},{48,64},{64,80},{80,96},{96,112},{112,0},{1... | collective-permute-start | bytes 1720328 | tf_op jit(solution)/shard_map/ppermute | solution.py:13
  63.1 19.1 %collective-permute-start.11 = (bf16[320,896]{1,0:T(8,128)(2,1)}, bf16[320,896]{1,0:T(8,128)(2,1)}, u32[]{:S(2)}, u32[]{:S(2)}) collective-permute-start(bf16[320,896]{1,0:T(8,128)(2,1)} %collective-permute-done.4), channel_id=1, source_target_pairs={{0,128},{128,0},{1,129},{129,1},{2,130},{130,2},{3,131},{131,3},{4... | collective-permute-start | bytes 1720328 | tf_op jit(solution)/shard_map/ppermute | solution.py:13
  63.3 14.9 %collective-permute-start.12 = (bf16[160,896]{1,0:T(8,128)(2,1)S(1)}, bf16[160,896]{1,0:T(8,128)(2,1)S(1)}, u32[]{:S(2)}, u32[]{:S(2)}) collective-permute-start(bf16[160,896]{1,0:T(8,128)(2,1)S(1)} %slice.34), channel_id=1, source_target_pairs={{0,16},{16,32},{32,48},{48,64},{64,80},{80,96},{96,112},{112,0},{1... | collective-permute-start | bytes 860168 | tf_op jit(solution)/shard_map/ppermute | solution.py:13
  63.4 29.1 %slice-start = ((s8[5242880]{0:T(1024)(128)(4,1)}), s8[4194304]{0:T(1024)(128)(4,1)S(1)}, s32[]{:S(2)}) async-start(s8[5242880]{0:T(1024)(128)(4,1)} %bitcast.88), calls=%async_computation.4 | async-start | bytes 8388608
  66.3 26.1 %slice-start.1 = ((s8[5242880]{0:T(1024)(128)(4,1)}), s8[1048576]{0:T(1024)(128)(4,1)S(1)}, s32[]{:S(2)}) async-start(s8[5242880]{0:T(1024)(128)(4,1)} %bitcast.88), calls=%async_computation.5 | async-start | bytes 2097152
  72.2 20.2 %copy-start.14 = (bf16[512,448]{1,0:T(8,128)(2,1)}, bf16[512,448]{1,0:T(8,128)(2,1)S(1)}, u32[]{:S(2)}) copy-start(bf16[512,448]{1,0:T(8,128)(2,1)S(1)} %collective-permute-done.14) | copy-start | bytes 1376260
  72.2 7.6 %collective-permute-start.13 = (bf16[160,896]{1,0:T(8,128)(2,1)S(1)}, bf16[160,896]{1,0:T(8,128)(2,1)S(1)}, u32[]{:S(2)}, u32[]{:S(2)}) collective-permute-start(bf16[160,896]{1,0:T(8,128)(2,1)S(1)} %slice.35), channel_id=1, source_target_pairs={{0,112},{16,0},{32,16},{48,32},{64,48},{80,64},{96,80},{112,96},{1... | collective-permute-start | bytes 860168 | tf_op jit(solution)/shard_map/ppermute | solution.py:13
  83.7 34.4 %collective-permute-start.15 = (bf16[320,896]{1,0:T(8,128)(2,1)}, bf16[320,896]{1,0:T(8,128)(2,1)S(1)}, u32[]{:S(2)}, u32[]{:S(2)}) collective-permute-start(bf16[320,896]{1,0:T(8,128)(2,1)} %constant_dynamic-update-slice_fusion), channel_id=1, source_target_pairs={{0,128},{128,0},{1,129},{129,1},{2,130},{130,2},{3,131},{131,3},{4... | collective-permute-start | bytes 1720328 | tf_op jit(solution)/shard_map/ppermute | solution.py:13
  85.0 33.1 %collective-permute-start.16 = (bf16[320,896]{1,0:T(8,128)(2,1)}, bf16[320,896]{1,0:T(8,128)(2,1)S(1)}, u32[]{:S(2)}, u32[]{:S(2)}) collective-permute-start(bf16[320,896]{1,0:T(8,128)(2,1)} %collective-permute-done.8), channel_id=1, source_target_pairs={{0,16},{16,32},{32,48},{48,64},{64,80},{80,96},{96,112},{112,0},{1... | collective-permute-start | bytes 1720328 | tf_op jit(solution)/shard_map/ppermute | solution.py:13
  85.8 32.3 %collective-permute-start.17 = (bf16[320,896]{1,0:T(8,128)(2,1)}, bf16[320,896]{1,0:T(8,128)(2,1)S(1)}, u32[]{:S(2)}, u32[]{:S(2)}) collective-permute-start(bf16[320,896]{1,0:T(8,128)(2,1)} %collective-permute-done.11), channel_id=1, source_target_pairs={{0,112},{16,0},{32,16},{48,32},{64,48},{80,64},{96,80},{112,96},{1... | collective-permute-start | bytes 1720328 | tf_op jit(solution)/shard_map/ppermute | solution.py:13
  90.1 5.3 %copy-start.2 = (bf16[8,320,896]{2,1,0:T(8,128)(2,1)}, bf16[8,320,896]{2,1,0:T(8,128)(2,1)S(1)}, u32[]{:S(2)}) copy-start(bf16[8,320,896]{2,1,0:T(8,128)(2,1)S(1)} %bitcast_dynamic-update-slice_fusion) | copy-start | bytes 13762564
  101.8 5.0 %copy-start.1 = (bf16[8,64,5120]{2,1,0:T(8,128)(2,1)S(1)}, bf16[8,64,5120]{2,1,0:T(8,128)(2,1)}, u32[]{:S(2)}) copy-start(bf16[8,64,5120]{2,1,0:T(8,128)(2,1)} %all-gather.2.cloned.1.call-done) | copy-start | bytes 15728644
  107.4 2.3 %copy-start.3 = (bf16[8,320,896]{2,1,0:T(8,128)(2,1)S(1)}, bf16[8,320,896]{2,1,0:T(8,128)(2,1)}, u32[]{:S(2)}) copy-start(bf16[8,320,896]{2,1,0:T(8,128)(2,1)} %copy-done.2) | copy-start | bytes 13762564
  118.0 1.5 copy-start.5
  119.5 1.0 copy-start.13
  119.5 1.1 copy-start.16
  120.6 0.9 copy-start.17
  123.2 1.0 copy-start.15
  124.9 5.9 %copy-start.11 = (f32[512,64]{0,1:T(8,128)S(1)}, f32[512,64]{0,1:T(8,128)}, u32[]{:S(2)}) copy-start(f32[512,64]{0,1:T(8,128)} %fusion.52) | copy-start | bytes 393220
  124.9 5.9 %copy-start.12 = (f32[512,64]{0,1:T(8,128)S(1)}, f32[512,64]{0,1:T(8,128)}, u32[]{:S(2)}) copy-start(f32[512,64]{0,1:T(8,128)} %fusion.53) | copy-start | bytes 393220
  125.4 6.6 %collective-permute-start.18 = (f32[8,8,1024]{2,1,0:T(8,128)S(1)}, f32[8,8,1024]{2,1,0:T(8,128)S(1)}, u32[]{:S(2)}, u32[]{:S(2)}) collective-permute-start(f32[8,8,1024]{2,1,0:T(8,128)S(1)} %fusion.26), channel_id=1, source_target_pairs={{0,2},{2,0},{1,3},{3,1},{4,6},{6,4},{5,7},{7,5},{8,10},{10,8},{9,1... | collective-permute-start | bytes 786440 | tf_op jit(solution)/shard_map/ppermute | solution.py:13
  132.7 13.1 %all-to-all-start = ((bf16[8,8,1024]{2,1,0:T(8,128)(2,1)}), bf16[8,8,1024]{2,1,0:T(8,128)(2,1)S(1)}, u32[]{:S(2)}, u32[]{:S(2)}) async-start(bf16[8,8,1024]{2,1,0:T(8,128)(2,1)} %fusion.30), calls=%async_computation | async-start | bytes 262144 | tf_op jit(solution)/shard_map/all_to_all | solution.py:236
  147.4 12.6 %all-to-all-start.1 = ((bf16[16,16,512]{2,1,0:T(8,128)(2,1)}), bf16[16,16,512]{2,1,0:T(8,128)(2,1)S(1)}, u32[]{:S(2)}, u32[]{:S(2)}) async-start(bf16[16,16,512]{2,1,0:T(8,128)(2,1)} %broadcast_in_dim.73), calls=%async_computation.1 | async-start | bytes 524288 | tf_op jit(solution)/shard_map/all_to_all | solution.py:252
Sparse Core Ops, SparseCore 0:
  47.0 41.8 all-gather.1

commit v14 on v10

--- a/solution.py
+++ b/solution.py
@@ -16,7 +16,6 @@
     n_z = lax.axis_size("z")
     z = lax.axis_index("z")
     half = weight.shape[0] // 2
-    far_z = (z + n_z // 2) % n_z
 
     def up(value):
         return shift(value, "z", 1)
@@ -27,18 +26,22 @@
     def across(value):
         return shift(value, "ylo", 1)
 
+    this = lax.axis_index("ylo") * n_z
+    other = n_z - this
+
     def placed(result, by_offset):
-        for offset, shard in by_offset:
-            result = lax.dynamic_update_slice(result, shard[None], ((z + offset) % n_z, 0, 0))
+        for side, offset, shard in by_offset:
+            at = side + (z + offset) % n_z
+            result = lax.dynamic_update_slice(result, shard[None], (at, 0, 0))
         return result
 
     a1, b1, o0, w0, cot, piece, early = barrier(
         (up(weight), down(weight), across(weight), weight, cot, piece, early)
     )
-    this_row = placed(
-        jnp.zeros((n_z,) + weight.shape, weight.dtype), ((0, w0), (n_z - 1, a1))
-    )
-    a2, b2, here, o0, cot, own_factor, this_row = barrier(
+    joined = placed(
+        jnp.zeros((2 * n_z,) + weight.shape, weight.dtype), ((this, 0, w0), (this, n_z - 1, a1))
+    )
+    a2, b2, here, o0, cot, own_factor, joined = barrier(
         (
             up(a1),
             down(b1),
@@ -46,7 +49,7 @@
             o0,
             cot,
             inner_factor(early[0]),
-            this_row,
+            joined,
         )
     )
     partner = lax.all_gather(here, ("x", "core"), axis=0, tiled=True)
@@ -57,20 +60,28 @@
     )
     a4 = jnp.concatenate((a4, b4), axis=0)
     last = (
-        (across(a4), far_z),
-        (up(oa2), (z + n_z - 3) % n_z),
-        (down(ob2), (z + 3) % n_z),
-    )
-    this_row = placed(
-        this_row,
-        ((1, b1), (n_z - 2, a2), (2, b2), (n_z - 3, a3), (3, b3), (n_z // 2, a4)),
-    )
-    other_row = placed(
-        jnp.zeros_like(this_row),
-        ((0, o0), (n_z - 1, oa1), (1, ob1), (n_z - 2, oa2), (2, ob2)),
-    )
-    flat = (n_z * weight.shape[0], -1)
-    return this_row.reshape(flat), other_row.reshape(flat), last, other_cot, partner, early, own_factor
+        (across(a4), other + (z + n_z // 2) % n_z),
+        (up(oa2), other + (z + n_z - 3) % n_z),
+        (down(ob2), other + (z + 3) % n_z),
+    )
+    joined = placed(
+        joined,
+        (
+            (this, 1, b1),
+            (other, 0, o0),
+            (this, n_z - 2, a2),
+            (this, 2, b2),
+            (this, n_z - 3, a3),
+            (this, 3, b3),
+            (other, n_z - 2, oa2),
+            (this, n_z // 2, a4),
+            (other, n_z - 1, oa1),
+            (other, 1, ob1),
+            (other, 2, ob2),
+        ),
+    )
+    joined = joined.reshape(2 * n_z * weight.shape[0], -1)
+    return joined, last, other_cot, partner, early, own_factor
 
 
 def projected(pre, cotangent, gate_projection, up_projection):
@@ -104,7 +115,6 @@
 ):
     count, length, width = doc_inputs.shape
     half_index = lax.axis_index("yhi")
-    row_index = lax.axis_index("ylo")
     dq = ("x", "core", "yhi")
     fsdp = ("ylo", "z")
     n_dq = lax.axis_size(dq)
@@ -142,28 +152,19 @@
             preferred_element_type=F32,
         )
 
-    this_row, other_row, last, other_cot, other, (own, own_cot), own_factor = gathered(
+    joined, last, other_cot, other, (own, own_cot), own_factor = gathered(
         weight, piece, cotangents(1 - half_index), (own, own_cot), inner_factor
     )
     gate_proj = columns(gate_projection, half_index)
     up_proj = columns(up_projection, half_index)
 
-    depth = this_row.shape[0]
-    shard_depth = weight.shape[0]
+    depth = weight.shape[0]
     pres = []
     chunks = []
     for rows in (own, other):
         flat = rows.reshape(-1, width)
-        this_flat = lax.dynamic_slice_in_dim(flat, row_index * depth, depth, 1)
-        other_flat = lax.dynamic_slice_in_dim(flat, (1 - row_index) * depth, depth, 1)
-        pre = jnp.dot(this_flat, this_row, preferred_element_type=F32)
-        pres.append(pre + jnp.dot(other_flat, other_row, preferred_element_type=F32))
-        chunks.append(
-            [
-                lax.dynamic_slice_in_dim(other_flat, place * shard_depth, shard_depth, 1)
-                for _, place in last
-            ]
-        )
+        pres.append(jnp.dot(flat, joined, preferred_element_type=F32))
+        chunks.append([lax.dynamic_slice_in_dim(flat, at * depth, depth, 1) for _, at in last])
     factors = (own_factor, inner_factor(other))
     shards = [shard for shard, _ in last]
     pres, factors, chunks, shards = lax.optimization_barrier((pres, factors, chunks, shards))

time: 178 us -> 188 us (1.056)
  local copies, waits for them, and re-layouts: 21.3 us -> 28 us
  matrix products: 28 us -> 34.1 us
    dynamic_update_slice x13, local copies, waits for them, and re-layouts: 10.4 us -> 17.3 us  [placed(): result = lax.dynamic_update_slice(result, shard[None], (at, 0, 0))]
    dot_general x4 -> x2, matrix products: 16 us -> 22 us  [body(): pres.append(jnp.dot(flat, joined, preferred_element_type=F32))]
    ppermute x18, starting transfers between devices: 30.5 us -> 28.5 us  [shift(): lax.ppermute(value, axis, [(i, (i + step) % size) for i in range(size)])]
  transfers between devices with their start and end apart: 21 -> 21, of which waited for: 12 -> 11; matrix products, arithmetic and copies ran while one was open for 26% -> 32% of each run, Pallas kernels for 0% -> 0%
where the time goes in v14:
time: 188 us
  starting transfers between devices  45.8 us (24%)
  waiting for transfers between devices  42.9 us (23%)
  matrix products  34.1 us (18%)
  local copies, waits for them, and re-layouts  28 us (15%)
  between operations  14.5 us (8%)
  blocking collectives  12.1 us (6%)
  other arithmetic  10.2 us (5%)
    ppermute x18, starting transfers between devices, shift(): lax.ppermute(value, axis, [(i, (i + step) % size) for i in range(size)])  28.5 us
    ppermute x18, waiting for transfers between devices, shift(): lax.ppermute(value, axis, [(i, (i + step) % size) for i in range(size)])  25.3 us
    dot_general x2, matrix products, body(): pres.append(jnp.dot(flat, joined, preferred_element_type=F32))  22 us
    dynamic_update_slice x13, local copies, waits for them, and re-layouts, placed(): result = lax.dynamic_update_slice(result, shard[None], (at, 0, 0))  17.3 us
    all_to_all x1, starting transfers between devices, body(): swapped = lax.all_to_all(part, dq, 0, 0, tiled=True)  12.3 us
    all_to_all x1, blocking collectives, body(): received = lax.all_to_all(payload, dq, 0, 0, tiled=True)  12.1 us
    all_to_all x1, waiting for transfers between devices, body(): swapped = lax.all_to_all(part, dq, 0, 0, tiled=True)  9.1 us
    all_to_all x1, waiting for transfers between devices, body(): lax.all_to_all(jnp.broadcast_to(queries[None], (n_fsdp,) + queries.shape)...  8.5 us
  transfers between devices with their start and end apart: 21, of which 11 were waited for; matrix products, arithmetic and copies ran while one was open for 32% of the time, Pallas kernels for 0%

profile of v14, /device:TPU:1, one launch (start us, length us, event | category | flops | bytes accessed | tf_op | source)
XLA Modules:
  0.0 187.7 jit_solution(12028967450680428420)
XLA Ops:
  6.5 1.3 pad_maximum_fusion.2
  7.9 2.5 %collective-permute-start = (bf16[320,896]{1,0:T(8,128)(2,1)S(1)}, bf16[320,896]{1,0:T(8,128)(2,1)}, u32[]{:S(2)}, u32[]{:S(2)}) collective-permute-start(bf16[320,896]{1,0:T(8,128)(2,1)S(1)} %pad_maximum_fusion.2), channel_id=1, source_target_pairs={{0,16},{16,32},{32,48},{48,64},{64,80},{80,96},{96,112},{112,0},{1... | collective-permute-start | bytes 1720328 | tf_op jit(solution)/shard_map/ppermute | solution.py:11
  10.4 4.0 %collective-permute-start.1 = (bf16[320,896]{1,0:T(8,128)(2,1)S(1)}, bf16[320,896]{1,0:T(8,128)(2,1)}, u32[]{:S(2)}, u32[]{:S(2)}) collective-permute-start(bf16[320,896]{1,0:T(8,128)(2,1)S(1)} %pad_maximum_fusion.2), channel_id=1, source_target_pairs={{0,112},{16,0},{32,16},{48,32},{64,48},{80,64},{96,80},{112,96},{1... | collective-permute-start | bytes 1720328 | tf_op jit(solution)/shard_map/ppermute | solution.py:11
  14.4 1.3 collective-permute-start.2
  15.7 5.3 %pad_maximum_fusion = bf16[8,64,5120]{2,1,0:T(8,128)(2,1)} fusion(bf16[8,32,5120]{2,1,0:T(8,128)(2,1)} %param.11, bf16[8,32,5120]{2,1,0:T(8,128)(2,1)} %param.9), kind=kLoop, calls=%fused_computation | loop fusion | flops 10485760 | bytes 10485760 | tf_op jit(solution)/shard_map/concatenate | solution.py:133
  21.1 1.1 constant_dynamic-slice_fusion.8
  22.7 0.9 pad_maximum_fusion.3
  23.5 0.9 pad_maximum_fusion.4
  24.4 2.7 %collective-permute-done = bf16[320,896]{1,0:T(8,128)(2,1)} collective-permute-done((bf16[320,896]{1,0:T(8,128)(2,1)S(1)}, bf16[320,896]{1,0:T(8,128)(2,1)}, u32[]{:S(2)}, u32[]{:S(2)}) %collective-permute-start) | collective-permute-done | bytes 573472 | tf_op jit(solution)/shard_map/ppermute | solution.py:11
  28.0 2.7 %collective-permute-start.4 = (bf16[320,896]{1,0:T(8,128)(2,1)}, bf16[320,896]{1,0:T(8,128)(2,1)}, u32[]{:S(2)}, u32[]{:S(2)}) collective-permute-start(bf16[320,896]{1,0:T(8,128)(2,1)} %collective-permute-done.1), channel_id=1, source_target_pairs={{0,112},{16,0},{32,16},{48,32},{64,48},{80,64},{96,80},{112,96},{1... | collective-permute-start | bytes 1720328 | tf_op jit(solution)/shard_map/ppermute | solution.py:11
  30.7 2.9 %collective-permute-start.5 = (bf16[1,64,5120]{2,1,0:T(8,128)(2,1)S(1)}, bf16[1,64,5120]{2,1,0:T(8,128)(2,1)S(1)}, u32[]{:S(2)}, u32[]{:S(2)}) collective-permute-start(bf16[1,64,5120]{2,1,0:T(8,128)(2,1)S(1)} %pad_maximum_fusion.1), channel_id=1, source_target_pairs={{0,1},{1,0},{2,3},{3,2},{4,5},{5,4},{6,7},{7,6},{8,9},{9,8},{10,11... | collective-permute-start | bytes 1966088 | tf_op jit(solution)/shard_map/ppermute | solution.py:11
  33.6 1.3 broadcast_in_dim.63
  34.9 1.1 bitcast_dynamic-update-slice_fusion.11
  36.1 2.9 %fusion.37 = f32[512,64]{0,1:T(8,128)} fusion(bf16[512,5120]{1,0:T(8,128)(2,1)S(1)} %bitcast.77, bf16[64,5120]{1,0:T(8,128)(2,1)S(1)} %copy-done), kind=kOutput, calls=%fused_computation.88 | convolution fusion | flops 335544320 | bytes 6029312 | tf_op jit(solution)/shard_map/dot_general | solution.py:148
  39.7 2.4 %collective-permute-done.3 = bf16[320,896]{1,0:T(8,128)(2,1)} collective-permute-done((bf16[320,896]{1,0:T(8,128)(2,1)}, bf16[320,896]{1,0:T(8,128)(2,1)}, u32[]{:S(2)}, u32[]{:S(2)}) %collective-permute-start.3) | collective-permute-done | bytes 573472 | tf_op jit(solution)/shard_map/ppermute | solution.py:11
  42.2 3.8 %collective-permute-done.5 = bf16[1,64,5120]{2,1,0:T(8,128)(2,1)S(1)} collective-permute-done((bf16[1,64,5120]{2,1,0:T(8,128)(2,1)S(1)}, bf16[1,64,5120]{2,1,0:T(8,128)(2,1)S(1)}, u32[]{:S(2)}, u32[]{:S(2)}) %collective-permute-start.5) | collective-permute-done | bytes 655392 | tf_op jit(solution)/shard_map/ppermute | solution.py:11
  47.0 2.7 %collective-permute-start.7 = (bf16[320,896]{1,0:T(8,128)(2,1)}, bf16[320,896]{1,0:T(8,128)(2,1)S(1)}, u32[]{:S(2)}, u32[]{:S(2)}) collective-permute-start(bf16[320,896]{1,0:T(8,128)(2,1)} %collective-permute-done.4), channel_id=1, source_target_pairs={{0,112},{16,0},{32,16},{48,32},{64,48},{80,64},{96,80},{112,96},{1... | collective-permute-start | bytes 1720328 | tf_op jit(solution)/shard_map/ppermute | solution.py:11
  49.6 1.3 collective-permute-start.8
  50.9 2.0 %constant_dynamic-slice_fusion.3 = (bf16[512,320]{1,0:T(8,128)(2,1)S(1)}, bf16[512,320]{1,0:T(8,128)(2,1)S(1)}, bf16[512,320]{1,0:T(8,128)(2,1)S(1)}) fusion(bf16[512,5120]{1,0:T(8,128)(2,1)} %bitcast.74, s32[]{:T(128)S(6)} %select_n.175, s32[]{:T(128)S(6)} %select_n.174, s32[]{:T(128)S(6)} %select_n.173), kind=kLoop, calls=%fused_computation.71 | loop fusion | bytes 1966092 | tf_op jit(solution)/shard_map/dynamic_slice | solution.py:167
  52.9 2.7 %collective-permute-start.14 = (bf16[512,448]{1,0:T(8,128)(2,1)}, bf16[512,448]{1,0:T(8,128)(2,1)S(1)}, u32[]{:S(2)}, u32[]{:S(2)}) collective-permute-start(bf16[512,448]{1,0:T(8,128)(2,1)} %bitcast.90), channel_id=1, source_target_pairs={{0,1},{1,0},{2,3},{3,2},{4,5},{5,4},{6,7},{7,6},{8,9},{9,8},{10,11... | collective-permute-start | bytes 1376264 | tf_op jit(solution)/shard_map/ppermute | solution.py:11
  55.6 2.1 %bitcast_dynamic-update-slice_fusion.10 = bf16[16,320,896]{2,1,0:T(8,128)(2,1)} fusion(bf16[16,320,896]{2,1,0:T(8,128)(2,1)} %copy-done.1, s32[]{:T(128)S(6)} %select_n.157, bf16[320,896]{1,0:T(8,128)(2,1)} %collective-permute-done.1), kind=kLoop, calls=%fused_computation.32 | loop fusion | bytes 1146884 | tf_op jit(solution)/shard_map/dynamic_update_slice | solution.py:35
  57.7 1.8 collective-permute-done.6
  59.5 1.0 collective-permute-done.8
  60.5 2.7 %collective-permute-start.10 = (bf16[320,896]{1,0:T(8,128)(2,1)S(1)}, bf16[320,896]{1,0:T(8,128)(2,1)S(1)}, u32[]{:S(2)}, u32[]{:S(2)}) collective-permute-start(bf16[320,896]{1,0:T(8,128)(2,1)S(1)} %collective-permute-done.2), channel_id=1, source_target_pairs={{0,112},{16,0},{32,16},{48,32},{64,48},{80,64},{96,80},{112,96},{1... | collective-permute-start | bytes 1720328 | tf_op jit(solution)/shard_map/ppermute | solution.py:11
  63.2 1.3 collective-permute-start.11
  64.6 0.9 bitcast_dynamic-update-slice_fusion.9
  65.5 1.9 %bitcast_dynamic-update-slice_fusion.8 = bf16[16,320,896]{2,1,0:T(8,128)(2,1)} fusion(bf16[16,320,896]{2,1,0:T(8,128)(2,1)} %bitcast_dynamic-update-slice_fusion.9, s32[]{:T(128)S(6)} %select_n.160, bf16[320,896]{1,0:T(8,128)(2,1)} %collective-permute-done.3), kind=kLoop, calls=%fused_computation.30 | loop fusion | bytes 1146884 | tf_op jit(solution)/shard_map/dynamic_update_slice | solution.py:35
  67.4 1.9 %bitcast_dynamic-update-slice_fusion.7 = bf16[16,320,896]{2,1,0:T(8,128)(2,1)} fusion(bf16[16,320,896]{2,1,0:T(8,128)(2,1)} %bitcast_dynamic-update-slice_fusion.8, s32[]{:T(128)S(6)} %select_n.162, bf16[320,896]{1,0:T(8,128)(2,1)} %collective-permute-done.4), kind=kLoop, calls=%fused_computation.29 | loop fusion | bytes 1146884 | tf_op jit(solution)/shard_map/dynamic_update_slice | solution.py:35
  69.4 4.7 %collective-permute-done.14 = bf16[512,448]{1,0:T(8,128)(2,1)S(1)} collective-permute-done((bf16[512,448]{1,0:T(8,128)(2,1)}, bf16[512,448]{1,0:T(8,128)(2,1)S(1)}, u32[]{:S(2)}, u32[]{:S(2)}) %collective-permute-start.14) | collective-permute-done | bytes 458784 | tf_op jit(solution)/shard_map/ppermute | solution.py:11
  74.4 0.9 bitcast_dynamic-update-slice_fusion.6
  75.3 0.8 bitcast_dynamic-update-slice_fusion.5
  76.1 6.1 %collective-permute-done.13 = bf16[160,896]{1,0:T(8,128)(2,1)S(1)} collective-permute-done((bf16[160,896]{1,0:T(8,128)(2,1)S(1)}, bf16[160,896]{1,0:T(8,128)(2,1)S(1)}, u32[]{:S(2)}, u32[]{:S(2)}) %collective-permute-start.13) | collective-permute-done | bytes 286752 | tf_op jit(solution)/shard_map/ppermute | solution.py:11
  82.2 1.8 collective-permute-done.11
  85.6 1.3 collective-permute-start.15
  86.9 2.7 %collective-permute-start.17 = (bf16[320,896]{1,0:T(8,128)(2,1)}, bf16[320,896]{1,0:T(8,128)(2,1)S(1)}, u32[]{:S(2)}, u32[]{:S(2)}) collective-permute-start(bf16[320,896]{1,0:T(8,128)(2,1)} %collective-permute-done.11), channel_id=1, source_target_pairs={{0,112},{16,0},{32,16},{48,32},{64,48},{80,64},{96,80},{112,96},{1... | collective-permute-start | bytes 1720328 | tf_op jit(solution)/shard_map/ppermute | solution.py:11
  89.5 2.0 %bitcast_dynamic-update-slice_fusion.4 = bf16[16,320,896]{2,1,0:T(8,128)(2,1)} fusion(bf16[16,320,896]{2,1,0:T(8,128)(2,1)} %bitcast_dynamic-update-slice_fusion.5, s32[]{:T(128)S(6)} %select_n.167, bf16[320,896]{1,0:T(8,128)(2,1)} %collective-permute-done.8), kind=kLoop, calls=%fused_computation.26 | loop fusion | bytes 1146884 | tf_op jit(solution)/shard_map/dynamic_update_slice | solution.py:35
  91.5 1.9 %bitcast_dynamic-update-slice_fusion.3 = bf16[16,320,896]{2,1,0:T(8,128)(2,1)} fusion(bf16[16,320,896]{2,1,0:T(8,128)(2,1)} %bitcast_dynamic-update-slice_fusion.4, s32[]{:T(128)S(6)} %select_n.169, bf16[320,896]{1,0:T(8,128)(2,1)} %constant_dynamic-update-slice_fusion), kind=kLoop, calls=%fused_computation.25 | loop fusion | bytes 1146884 | tf_op jit(solution)/shard_map/dynamic_update_slice | solution.py:35
  93.4 0.9 bitcast_dynamic-update-slice_fusion.2
  94.3 0.9 bitcast_dynamic-update-slice_fusion.1
  95.2 1.9 %bitcast_dynamic-update-slice_fusion = bf16[16,320,896]{2,1,0:T(8,128)(2,1)} fusion(bf16[16,320,896]{2,1,0:T(8,128)(2,1)} %bitcast_dynamic-update-slice_fusion.1, s32[]{:T(128)S(6)} %select_n.172, bf16[320,896]{1,0:T(8,128)(2,1)} %collective-permute-done.11), kind=kLoop, calls=%fused_computation.22 | loop fusion | bytes 1146884 | tf_op jit(solution)/shard_map/dynamic_update_slice | solution.py:35
  97.1 9.3 %fusion.38 = f32[512,896]{1,0:T(8,128)} fusion(bf16[512,5120]{1,0:T(8,128)(2,1)S(1)} %bitcast.80, bf16[5120,896]{1,0:T(8,128)(2,1)} %bitcast.81), kind=kOutput, calls=%fused_computation.89 | convolution fusion | flops 4697620480 | bytes 16252928 | tf_op jit(solution)/shard_map/dot_general | solution.py:166
  106.4 12.7 %fusion.39 = f32[512,896]{1,0:T(8,128)S(1)} fusion(bf16[512,5120]{1,0:T(8,128)(2,1)} %bitcast.83, bf16[5120,896]{1,0:T(8,128)(2,1)} %bitcast.82), kind=kOutput, calls=%fused_computation.90 | convolution fusion | flops 4697620480 | bytes 16252928 | tf_op jit(solution)/shard_map/dot_general | solution.py:166
  119.7 2.4 %fusion.40 = f32[512,64]{0,1:T(8,128)} fusion(bf16[512,5120]{1,0:T(8,128)(2,1)S(1)} %bitcast.85, bf16[64,5120]{1,0:T(8,128)(2,1)S(1)} %copy-done), kind=kOutput, calls=%fused_computation.91 | convolution fusion | flops 335544320 | bytes 6029312 | tf_op jit(solution)/shard_map/dot_general | solution.py:148
  129.1 12.3 %all-to-all-start = ((bf16[16,8,1024]{2,1,0:T(8,128)(2,1)}), bf16[16,8,1024]{2,1,0:T(8,128)(2,1)S(1)}, u32[]{:S(2)}, u32[]{:S(2)}) async-start(bf16[16,8,1024]{2,1,0:T(8,128)(2,1)} %pad_maximum_fusion.7), calls=%async_computation | async-start | bytes 524288 | tf_op jit(solution)/shard_map/all_to_all | solution.py:188
  141.7 9.1 %all-to-all-done = bf16[16,8,1024]{2,1,0:T(8,128)(2,1)S(1)} async-done(((bf16[16,8,1024]{2,1,0:T(8,128)(2,1)}), bf16[16,8,1024]{2,1,0:T(8,128)(2,1)S(1)}, u32[]{:S(2)}, u32[]{:S(2)}) %all-to-all-start) | async-done | bytes 262176 | tf_op jit(solution)/shard_map/all_to_all | solution.py:188
  152.5 4.9 %all-to-all-start.1 = ((bf16[16,16,512]{2,1,0:T(8,128)(2,1)}), bf16[16,16,512]{2,1,0:T(8,128)(2,1)S(1)}, u32[]{:S(2)}, u32[]{:S(2)}) async-start(bf16[16,16,512]{2,1,0:T(8,128)(2,1)} %broadcast_in_dim.77), calls=%async_computation.1 | async-start | bytes 524288 | tf_op jit(solution)/shard_map/all_to_all | solution.py:204
  157.8 8.5 %all-to-all-done.1 = bf16[16,16,512]{2,1,0:T(8,128)(2,1)S(1)} async-done(((bf16[16,16,512]{2,1,0:T(8,128)(2,1)}), bf16[16,16,512]{2,1,0:T(8,128)(2,1)S(1)}, u32[]{:S(2)}, u32[]{:S(2)}) %all-to-all-start.1) | async-done | bytes 262176 | tf_op jit(solution)/shard_map/all_to_all | solution.py:204
  166.9 12.1 %all_to_all.19 = f32[16,1,640]{2,1,0:T(1,128)S(1)} all-to-all(f32[16,1,640]{2,1,0:T(1,128)S(1)} %copy.24), channel_id=1, replica_groups=mesh['ylo'=2,'z'=8,'x'=4,'core'=2,'yhi'=2] {'x','core','yhi'}, dimensions={0} | all-to-all | bytes 81920 | tf_op jit(solution)/shard_map/all_to_all | solution.py:225
  (104 shorter events, 16.4 us)
Async XLA Ops:
  6.5 29.6 %copy-start = (bf16[64,5120]{1,0:T(8,128)(2,1)S(1)}, bf16[64,5120]{1,0:T(8,128)(2,1)}, u32[]{:S(2)}) copy-start(bf16[64,5120]{1,0:T(8,128)(2,1)} %param.15) | copy-start | bytes 1966084
  6.5 99.9 %all-gather.2.cloned.1.call-start = ((), (), s32[]{:S(2)}) async-start(), calls=%async_computation.3 | async-start | bytes 5898240 | tf_op jit(solution)/shard_map/all_gather | solution.py:55
  7.9 19.3 %collective-permute-start = (bf16[320,896]{1,0:T(8,128)(2,1)S(1)}, bf16[320,896]{1,0:T(8,128)(2,1)}, u32[]{:S(2)}, u32[]{:S(2)}) collective-permute-start(bf16[320,896]{1,0:T(8,128)(2,1)S(1)} %pad_maximum_fusion.2), channel_id=1, source_target_pairs={{0,16},{16,32},{32,48},{48,64},{64,80},{80,96},{96,112},{112,0},{1... | collective-permute-start | bytes 1720328 | tf_op jit(solution)/shard_map/ppermute | solution.py:11
  10.4 16.8 %collective-permute-start.1 = (bf16[320,896]{1,0:T(8,128)(2,1)S(1)}, bf16[320,896]{1,0:T(8,128)(2,1)}, u32[]{:S(2)}, u32[]{:S(2)}) collective-permute-start(bf16[320,896]{1,0:T(8,128)(2,1)S(1)} %pad_maximum_fusion.2), channel_id=1, source_target_pairs={{0,112},{16,0},{32,16},{48,32},{64,48},{80,64},{96,80},{112,96},{1... | collective-permute-start | bytes 1720328 | tf_op jit(solution)/shard_map/ppermute | solution.py:11
  14.4 13.6 %collective-permute-start.2 = (bf16[320,896]{1,0:T(8,128)(2,1)S(1)}, bf16[320,896]{1,0:T(8,128)(2,1)S(1)}, u32[]{:S(2)}, u32[]{:S(2)}) collective-permute-start(bf16[320,896]{1,0:T(8,128)(2,1)S(1)} %pad_maximum_fusion.2), channel_id=1, source_target_pairs={{0,128},{128,0},{1,129},{129,1},{2,130},{130,2},{3,131},{131,3},{4... | collective-permute-start | bytes 1720328 | tf_op jit(solution)/shard_map/ppermute | solution.py:11
  15.7 6.5 %copy-start.5 = (bf16[8,32,896]{2,1,0:T(8,128)(2,1)S(1)}, bf16[8,32,896]{2,1,0:T(8,128)(2,1)}, u32[]{:S(2)}) copy-start(bf16[8,32,896]{2,1,0:T(8,128)(2,1)} %param.12) | copy-start | bytes 1376260
  15.7 6.5 %copy-start.6 = (bf16[8,32,896]{2,1,0:T(8,128)(2,1)S(1)}, bf16[8,32,896]{2,1,0:T(8,128)(2,1)}, u32[]{:S(2)}) copy-start(bf16[8,32,896]{2,1,0:T(8,128)(2,1)} %param.10) | copy-start | bytes 1376260
  28.0 8.1 %slice-start = ((s8[5242880]{0:T(1024)(128)(4,1)}), s8[4194304]{0:T(1024)(128)(4,1)S(1)}, s32[]{:S(2)}) async-start(s8[5242880]{0:T(1024)(128)(4,1)} %bitcast.75), calls=%async_computation.4 | async-start | bytes 8388608
  28.0 8.1 %slice-start.1 = ((s8[5242880]{0:T(1024)(128)(4,1)}), s8[1048576]{0:T(1024)(128)(4,1)S(1)}, s32[]{:S(2)}) async-start(s8[5242880]{0:T(1024)(128)(4,1)} %bitcast.75), calls=%async_computation.5 | async-start | bytes 2097152
  28.0 14.2 %collective-permute-start.3 = (bf16[320,896]{1,0:T(8,128)(2,1)}, bf16[320,896]{1,0:T(8,128)(2,1)}, u32[]{:S(2)}, u32[]{:S(2)}) collective-permute-start(bf16[320,896]{1,0:T(8,128)(2,1)} %collective-permute-done), channel_id=1, source_target_pairs={{0,16},{16,32},{32,48},{48,64},{64,80},{80,96},{96,112},{112,0},{1... | collective-permute-start | bytes 1720328 | tf_op jit(solution)/shard_map/ppermute | solution.py:11
  28.0 14.2 %collective-permute-start.4 = (bf16[320,896]{1,0:T(8,128)(2,1)}, bf16[320,896]{1,0:T(8,128)(2,1)}, u32[]{:S(2)}, u32[]{:S(2)}) collective-permute-start(bf16[320,896]{1,0:T(8,128)(2,1)} %collective-permute-done.1), channel_id=1, source_target_pairs={{0,112},{16,0},{32,16},{48,32},{64,48},{80,64},{96,80},{112,96},{1... | collective-permute-start | bytes 1720328 | tf_op jit(solution)/shard_map/ppermute | solution.py:11
  30.7 15.3 %collective-permute-start.5 = (bf16[1,64,5120]{2,1,0:T(8,128)(2,1)S(1)}, bf16[1,64,5120]{2,1,0:T(8,128)(2,1)S(1)}, u32[]{:S(2)}, u32[]{:S(2)}) collective-permute-start(bf16[1,64,5120]{2,1,0:T(8,128)(2,1)S(1)} %pad_maximum_fusion.1), channel_id=1, source_target_pairs={{0,1},{1,0},{2,3},{3,2},{4,5},{5,4},{6,7},{7,6},{8,9},{9,8},{10,11... | collective-permute-start | bytes 1966088 | tf_op jit(solution)/shard_map/ppermute | solution.py:11
  36.1 3.7 %copy-start.1 = (bf16[16,320,896]{2,1,0:T(8,128)(2,1)}, bf16[16,320,896]{2,1,0:T(8,128)(2,1)S(1)}, u32[]{:S(2)}) copy-start(bf16[16,320,896]{2,1,0:T(8,128)(2,1)S(1)} %bitcast_dynamic-update-slice_fusion.11) | copy-start | bytes 27525124
  46.0 0.8 copy-start.4
  46.9 12.6 %collective-permute-start.6 = (bf16[320,896]{1,0:T(8,128)(2,1)}, bf16[320,896]{1,0:T(8,128)(2,1)S(1)}, u32[]{:S(2)}, u32[]{:S(2)}) collective-permute-start(bf16[320,896]{1,0:T(8,128)(2,1)} %collective-permute-done.3), channel_id=1, source_target_pairs={{0,16},{16,32},{32,48},{48,64},{64,80},{80,96},{96,112},{112,0},{1... | collective-permute-start | bytes 1720328 | tf_op jit(solution)/shard_map/ppermute | solution.py:11
  47.0 12.6 %collective-permute-start.7 = (bf16[320,896]{1,0:T(8,128)(2,1)}, bf16[320,896]{1,0:T(8,128)(2,1)S(1)}, u32[]{:S(2)}, u32[]{:S(2)}) collective-permute-start(bf16[320,896]{1,0:T(8,128)(2,1)} %collective-permute-done.4), channel_id=1, source_target_pairs={{0,112},{16,0},{32,16},{48,32},{64,48},{80,64},{96,80},{112,96},{1... | collective-permute-start | bytes 1720328 | tf_op jit(solution)/shard_map/ppermute | solution.py:11
  49.6 10.9 %collective-permute-start.8 = (bf16[320,896]{1,0:T(8,128)(2,1)}, bf16[320,896]{1,0:T(8,128)(2,1)}, u32[]{:S(2)}, u32[]{:S(2)}) collective-permute-start(bf16[320,896]{1,0:T(8,128)(2,1)} %collective-permute-done.3), channel_id=1, source_target_pairs={{0,128},{128,0},{1,129},{129,1},{2,130},{130,2},{3,131},{131,3},{4... | collective-permute-start | bytes 1720328 | tf_op jit(solution)/shard_map/ppermute | solution.py:11
  52.9 21.2 %collective-permute-start.14 = (bf16[512,448]{1,0:T(8,128)(2,1)}, bf16[512,448]{1,0:T(8,128)(2,1)S(1)}, u32[]{:S(2)}, u32[]{:S(2)}) collective-permute-start(bf16[512,448]{1,0:T(8,128)(2,1)} %bitcast.90), channel_id=1, source_target_pairs={{0,1},{1,0},{2,3},{3,2},{4,5},{5,4},{6,7},{7,6},{8,9},{9,8},{10,11... | collective-permute-start | bytes 1376264 | tf_op jit(solution)/shard_map/ppermute | solution.py:11
  55.6 41.5 %slice-start.2 = ((s8[5242880]{0:T(1024)(128)(4,1)}), s8[4194304]{0:T(1024)(128)(4,1)S(1)}, s32[]{:S(2)}) async-start(s8[5242880]{0:T(1024)(128)(4,1)} %bitcast.78), calls=%async_computation.6 | async-start | bytes 8388608
  60.5 21.7 %collective-permute-start.9 = (bf16[320,896]{1,0:T(8,128)(2,1)S(1)}, bf16[320,896]{1,0:T(8,128)(2,1)S(1)}, u32[]{:S(2)}, u32[]{:S(2)}) collective-permute-start(bf16[320,896]{1,0:T(8,128)(2,1)S(1)} %collective-permute-done.2), channel_id=1, source_target_pairs={{0,16},{16,32},{32,48},{48,64},{64,80},{80,96},{96,112},{112,0},{1... | collective-permute-start | bytes 1720328 | tf_op jit(solution)/shard_map/ppermute | solution.py:11
  60.5 21.7 %collective-permute-start.10 = (bf16[320,896]{1,0:T(8,128)(2,1)S(1)}, bf16[320,896]{1,0:T(8,128)(2,1)S(1)}, u32[]{:S(2)}, u32[]{:S(2)}) collective-permute-start(bf16[320,896]{1,0:T(8,128)(2,1)S(1)} %collective-permute-done.2), channel_id=1, source_target_pairs={{0,112},{16,0},{32,16},{48,32},{64,48},{80,64},{96,80},{112,96},{1... | collective-permute-start | bytes 1720328 | tf_op jit(solution)/shard_map/ppermute | solution.py:11
  63.2 20.8 %collective-permute-start.11 = (bf16[320,896]{1,0:T(8,128)(2,1)}, bf16[320,896]{1,0:T(8,128)(2,1)}, u32[]{:S(2)}, u32[]{:S(2)}) collective-permute-start(bf16[320,896]{1,0:T(8,128)(2,1)} %collective-permute-done.4), channel_id=1, source_target_pairs={{0,128},{128,0},{1,129},{129,1},{2,130},{130,2},{3,131},{131,3},{4... | collective-permute-start | bytes 1720328 | tf_op jit(solution)/shard_map/ppermute | solution.py:11
  64.5 11.6 %collective-permute-start.12 = (bf16[160,896]{1,0:T(8,128)(2,1)S(1)}, bf16[160,896]{1,0:T(8,128)(2,1)S(1)}, u32[]{:S(2)}, u32[]{:S(2)}) collective-permute-start(bf16[160,896]{1,0:T(8,128)(2,1)S(1)} %slice.34), channel_id=1, source_target_pairs={{0,16},{16,32},{32,48},{48,64},{64,80},{80,96},{96,112},{112,0},{1... | collective-permute-start | bytes 860168 | tf_op jit(solution)/shard_map/ppermute | solution.py:11
  74.1 21.1 %copy-start.10 = (bf16[512,448]{1,0:T(8,128)(2,1)}, bf16[512,448]{1,0:T(8,128)(2,1)S(1)}, u32[]{:S(2)}) copy-start(bf16[512,448]{1,0:T(8,128)(2,1)S(1)} %collective-permute-done.14) | copy-start | bytes 1376260
  74.1 8.1 %collective-permute-start.13 = (bf16[160,896]{1,0:T(8,128)(2,1)S(1)}, bf16[160,896]{1,0:T(8,128)(2,1)S(1)}, u32[]{:S(2)}, u32[]{:S(2)}) collective-permute-start(bf16[160,896]{1,0:T(8,128)(2,1)S(1)} %slice.35), channel_id=1, source_target_pairs={{0,112},{16,0},{32,16},{48,32},{64,48},{80,64},{96,80},{112,96},{1... | collective-permute-start | bytes 860168 | tf_op jit(solution)/shard_map/ppermute | solution.py:11
  75.3 21.9 %slice-start.3 = ((s8[5242880]{0:T(1024)(128)(4,1)}), s8[1048576]{0:T(1024)(128)(4,1)S(1)}, s32[]{:S(2)}) async-start(s8[5242880]{0:T(1024)(128)(4,1)} %bitcast.78), calls=%async_computation.7 | async-start | bytes 2097152
  85.6 36.5 %collective-permute-start.15 = (bf16[320,896]{1,0:T(8,128)(2,1)}, bf16[320,896]{1,0:T(8,128)(2,1)S(1)}, u32[]{:S(2)}, u32[]{:S(2)}) collective-permute-start(bf16[320,896]{1,0:T(8,128)(2,1)} %constant_dynamic-update-slice_fusion), channel_id=1, source_target_pairs={{0,128},{128,0},{1,129},{129,1},{2,130},{130,2},{3,131},{131,3},{4... | collective-permute-start | bytes 1720328 | tf_op jit(solution)/shard_map/ppermute | solution.py:11
  86.9 35.2 %collective-permute-start.16 = (bf16[320,896]{1,0:T(8,128)(2,1)}, bf16[320,896]{1,0:T(8,128)(2,1)S(1)}, u32[]{:S(2)}, u32[]{:S(2)}) collective-permute-start(bf16[320,896]{1,0:T(8,128)(2,1)} %collective-permute-done.8), channel_id=1, source_target_pairs={{0,16},{16,32},{32,48},{48,64},{64,80},{80,96},{96,112},{112,0},{1... | collective-permute-start | bytes 1720328 | tf_op jit(solution)/shard_map/ppermute | solution.py:11
  86.9 35.2 %collective-permute-start.17 = (bf16[320,896]{1,0:T(8,128)(2,1)}, bf16[320,896]{1,0:T(8,128)(2,1)S(1)}, u32[]{:S(2)}, u32[]{:S(2)}) collective-permute-start(bf16[320,896]{1,0:T(8,128)(2,1)} %collective-permute-done.11), channel_id=1, source_target_pairs={{0,112},{16,0},{32,16},{48,32},{64,48},{80,64},{96,80},{112,96},{1... | collective-permute-start | bytes 1720328 | tf_op jit(solution)/shard_map/ppermute | solution.py:11
  106.4 12.7 %copy-start.2 = (bf16[8,64,5120]{2,1,0:T(8,128)(2,1)S(1)}, bf16[8,64,5120]{2,1,0:T(8,128)(2,1)}, u32[]{:S(2)}) copy-start(bf16[8,64,5120]{2,1,0:T(8,128)(2,1)} %all-gather.2.cloned.1.call-done) | copy-start | bytes 15728644
  122.7 1.4 copy-start.11
  122.8 1.4 copy-start.12
  123.4 1.1 copy-start.13
  124.6 2.0 %copy-start.3 = (f32[512,896]{1,0:T(8,128)S(1)}, f32[512,896]{1,0:T(8,128)}, u32[]{:S(2)}) copy-start(f32[512,896]{1,0:T(8,128)} %fusion.38) | copy-start | bytes 5505028
  125.9 1.4 copy-start.9
  127.7 13.7 %copy-start.7 = (f32[512,64]{0,1:T(8,128)S(1)}, f32[512,64]{0,1:T(8,128)}, u32[]{:S(2)}) copy-start(f32[512,64]{0,1:T(8,128)} %fusion.37) | copy-start | bytes 393220
  127.7 13.7 %copy-start.8 = (f32[512,64]{0,1:T(8,128)S(1)}, f32[512,64]{0,1:T(8,128)}, u32[]{:S(2)}) copy-start(f32[512,64]{0,1:T(8,128)} %fusion.40) | copy-start | bytes 393220
  129.1 21.7 %all-to-all-start = ((bf16[16,8,1024]{2,1,0:T(8,128)(2,1)}), bf16[16,8,1024]{2,1,0:T(8,128)(2,1)S(1)}, u32[]{:S(2)}, u32[]{:S(2)}) async-start(bf16[16,8,1024]{2,1,0:T(8,128)(2,1)} %pad_maximum_fusion.7), calls=%async_computation | async-start | bytes 524288 | tf_op jit(solution)/shard_map/all_to_all | solution.py:188
  152.5 13.8 %all-to-all-start.1 = ((bf16[16,16,512]{2,1,0:T(8,128)(2,1)}), bf16[16,16,512]{2,1,0:T(8,128)(2,1)S(1)}, u32[]{:S(2)}, u32[]{:S(2)}) async-start(bf16[16,16,512]{2,1,0:T(8,128)(2,1)} %broadcast_in_dim.77), calls=%async_computation.1 | async-start | bytes 524288 | tf_op jit(solution)/shard_map/all_to_all | solution.py:204
Sparse Core Ops, SparseCore 0:
  47.0 41.8 all-gather.1

commit v15 on v10

--- a/solution.py
+++ b/solution.py
@@ -164,9 +164,11 @@
                 for _, place in last
             ]
         )
+    shards = [shard for shard, _ in last]
+    pres, own_factor, other, chunks, shards = lax.optimization_barrier(
+        (pres, own_factor, other, chunks, shards)
+    )
     factors = (own_factor, inner_factor(other))
-    shards = [shard for shard, _ in last]
-    pres, factors, chunks, shards = lax.optimization_barrier((pres, factors, chunks, shards))
     parts = []
     for pre, pieces, rows_cot in zip(pres, chunks, (own_cot, other_cot)):
         for chunk, shard in zip(pieces, shards):

time: 178 us -> 177 us (level)
  transfers between devices with their start and end apart: 21 -> 21, of which waited for: 12 -> 12; matrix products, arithmetic and copies ran while one was open for 26% -> 24% of each run, Pallas kernels for 0% -> 0%
where the time goes in v15:
time: 177 us; the launch traced here: 176 us
  starting transfers between devices  47.1 us (27%)
  waiting for transfers between devices  43.7 us (25%)
  matrix products  27.4 us (15%)
  local copies, waits for them, and re-layouts  21.3 us (12%)
  between operations  14.8 us (8%)
  blocking collectives  12.1 us (7%)
  other arithmetic  10.1 us (6%)
    ppermute x18, starting transfers between devices, shift(): lax.ppermute(value, axis, [(i, (i + step) % size) for i in range(size)])  30.5 us
    ppermute x18, waiting for transfers between devices, shift(): lax.ppermute(value, axis, [(i, (i + step) % size) for i in range(size)])  26.1 us
    all_to_all x1, blocking collectives, body(): received = lax.all_to_all(payload, dq, 0, 0, tiled=True)  12.1 us
    all_to_all x1, starting transfers between devices, body(): swapped = lax.all_to_all(part, dq, 0, 0, tiled=True)  11.7 us
    dynamic_update_slice x13, local copies, waits for them, and re-layouts, placed(): lax.dynamic_update_slice(result, shard[None], ((z + offset) % n_z, 0, 0))  10.4 us
    all_to_all x1, waiting for transfers between devices, body(): swapped = lax.all_to_all(part, dq, 0, 0, tiled=True)  9.11 us
    dot_general x2, matrix products, body(): jnp.dot(other_flat, other_row, preferred_element_type=F32)  8.98 us
    all_to_all x1, waiting for transfers between devices, body(): lax.all_to_all(jnp.broadcast_to(queries[None], (n_fsdp,) + queries.shape)...  8.5 us
  transfers between devices with their start and end apart: 21, of which 12 were waited for; matrix products, arithmetic and copies ran while one was open for 24% of the time, Pallas kernels for 0%

profile of v15, /device:TPU:1, one launch (start us, length us, event | category | flops | bytes accessed | tf_op | source)
XLA Modules:
  0.0 176.4 jit_solution(6021955636015405446)
XLA Ops:
  6.5 1.3 pad_maximum_fusion.2
  7.9 2.5 %collective-permute-start = (bf16[320,896]{1,0:T(8,128)(2,1)S(1)}, bf16[320,896]{1,0:T(8,128)(2,1)}, u32[]{:S(2)}, u32[]{:S(2)}) collective-permute-start(bf16[320,896]{1,0:T(8,128)(2,1)S(1)} %pad_maximum_fusion.2), channel_id=1, source_target_pairs={{0,16},{16,32},{32,48},{48,64},{64,80},{80,96},{96,112},{112,0},{1... | collective-permute-start | bytes 1720328 | tf_op jit(solution)/shard_map/ppermute | solution.py:11
  10.4 4.0 %collective-permute-start.1 = (bf16[320,896]{1,0:T(8,128)(2,1)S(1)}, bf16[320,896]{1,0:T(8,128)(2,1)}, u32[]{:S(2)}, u32[]{:S(2)}) collective-permute-start(bf16[320,896]{1,0:T(8,128)(2,1)S(1)} %pad_maximum_fusion.2), channel_id=1, source_target_pairs={{0,112},{16,0},{32,16},{48,32},{64,48},{80,64},{96,80},{112,96},{1... | collective-permute-start | bytes 1720328 | tf_op jit(solution)/shard_map/ppermute | solution.py:11
  14.4 1.3 collective-permute-start.2
  15.7 5.3 %pad_maximum_fusion = bf16[8,64,5120]{2,1,0:T(8,128)(2,1)} fusion(bf16[8,32,5120]{2,1,0:T(8,128)(2,1)} %param.11, bf16[8,32,5120]{2,1,0:T(8,128)(2,1)} %param.9), kind=kLoop, calls=%fused_computation | loop fusion | flops 10485760 | bytes 10485760 | tf_op jit(solution)/shard_map/concatenate | solution.py:123
  21.0 1.1 constant_dynamic-slice_fusion.8
  22.6 0.9 pad_maximum_fusion.3
  23.5 0.8 pad_maximum_fusion.4
  24.4 2.8 %collective-permute-done = bf16[320,896]{1,0:T(8,128)(2,1)} collective-permute-done((bf16[320,896]{1,0:T(8,128)(2,1)S(1)}, bf16[320,896]{1,0:T(8,128)(2,1)}, u32[]{:S(2)}, u32[]{:S(2)}) %collective-permute-start) | collective-permute-done | bytes 573472 | tf_op jit(solution)/shard_map/ppermute | solution.py:11
  27.2 0.8 collective-permute-done.2
  28.0 2.7 %collective-permute-start.4 = (bf16[320,896]{1,0:T(8,128)(2,1)}, bf16[320,896]{1,0:T(8,128)(2,1)}, u32[]{:S(2)}, u32[]{:S(2)}) collective-permute-start(bf16[320,896]{1,0:T(8,128)(2,1)} %collective-permute-done.1), channel_id=1, source_target_pairs={{0,112},{16,0},{32,16},{48,32},{64,48},{80,64},{96,80},{112,96},{1... | collective-permute-start | bytes 1720328 | tf_op jit(solution)/shard_map/ppermute | solution.py:11
  30.7 2.9 %collective-permute-start.5 = (bf16[1,64,5120]{2,1,0:T(8,128)(2,1)S(1)}, bf16[1,64,5120]{2,1,0:T(8,128)(2,1)S(1)}, u32[]{:S(2)}, u32[]{:S(2)}) collective-permute-start(bf16[1,64,5120]{2,1,0:T(8,128)(2,1)S(1)} %pad_maximum_fusion.1), channel_id=1, source_target_pairs={{0,1},{1,0},{2,3},{3,2},{4,5},{5,4},{6,7},{7,6},{8,9},{9,8},{10,11... | collective-permute-start | bytes 1966088 | tf_op jit(solution)/shard_map/ppermute | solution.py:11
  34.3 1.1 bitcast_dynamic-update-slice_fusion.11
  35.4 2.4 %fusion.55 = f32[512,64]{0,1:T(8,128)} fusion(bf16[512,5120]{1,0:T(8,128)(2,1)S(1)} %bitcast.77, bf16[64,5120]{1,0:T(8,128)(2,1)S(1)} %copy-done), kind=kOutput, calls=%fused_computation.102 | convolution fusion | flops 335544320 | bytes 6029312 | tf_op jit(solution)/shard_map/dot_general | solution.py:138
  37.8 4.4 %collective-permute-done.3 = bf16[320,896]{1,0:T(8,128)(2,1)} collective-permute-done((bf16[320,896]{1,0:T(8,128)(2,1)}, bf16[320,896]{1,0:T(8,128)(2,1)}, u32[]{:S(2)}, u32[]{:S(2)}) %collective-permute-start.3) | collective-permute-done | bytes 573472 | tf_op jit(solution)/shard_map/ppermute | solution.py:11
  42.2 3.8 %collective-permute-done.5 = bf16[1,64,5120]{2,1,0:T(8,128)(2,1)S(1)} collective-permute-done((bf16[1,64,5120]{2,1,0:T(8,128)(2,1)S(1)}, bf16[1,64,5120]{2,1,0:T(8,128)(2,1)S(1)}, u32[]{:S(2)}, u32[]{:S(2)}) %collective-permute-start.5) | collective-permute-done | bytes 655392 | tf_op jit(solution)/shard_map/ppermute | solution.py:11
  46.0 0.8 copy-done.9
  47.1 1.4 collective-permute-start.8
  48.5 2.6 %collective-permute-start.7 = (bf16[320,896]{1,0:T(8,128)(2,1)}, bf16[320,896]{1,0:T(8,128)(2,1)S(1)}, u32[]{:S(2)}, u32[]{:S(2)}) collective-permute-start(bf16[320,896]{1,0:T(8,128)(2,1)} %collective-permute-done.4), channel_id=1, source_target_pairs={{0,112},{16,0},{32,16},{48,32},{64,48},{80,64},{96,80},{112,96},{1... | collective-permute-start | bytes 1720328 | tf_op jit(solution)/shard_map/ppermute | solution.py:11
  51.1 1.9 %constant_dynamic-slice_fusion.3 = (bf16[512,320]{1,0:T(8,128)(2,1)S(1)}, bf16[512,320]{1,0:T(8,128)(2,1)S(1)}, bf16[512,320]{1,0:T(8,128)(2,1)S(1)}) fusion(bf16[512,5120]{1,0:T(8,128)(2,1)} %bitcast.76, s32[]{:T(128)S(6)} %dynamic_slice.81, s32[]{:T(128)S(6)} %dynamic_slice.79, s32[]{:T(128)S(6)} %dynamic_slice.77), kind=kLoop, calls=%fused_computation.81 | loop fusion | bytes 1966092 | tf_op jit(solution)/shard_map/dynamic_slice | solution.py:163
  52.9 2.7 %collective-permute-start.14 = (bf16[512,448]{1,0:T(8,128)(2,1)}, bf16[512,448]{1,0:T(8,128)(2,1)S(1)}, u32[]{:S(2)}, u32[]{:S(2)}) collective-permute-start(bf16[512,448]{1,0:T(8,128)(2,1)} %bitcast.94), channel_id=1, source_target_pairs={{0,1},{1,0},{2,3},{3,2},{4,5},{5,4},{6,7},{7,6},{8,9},{9,8},{10,11... | collective-permute-start | bytes 1376264 | tf_op jit(solution)/shard_map/ppermute | solution.py:11
  55.6 1.9 %bitcast_dynamic-update-slice_fusion.10 = bf16[8,320,896]{2,1,0:T(8,128)(2,1)} fusion(bf16[8,320,896]{2,1,0:T(8,128)(2,1)} %copy-done.4, s32[]{:T(128)S(6)} %select_n.164, bf16[320,896]{1,0:T(8,128)(2,1)} %collective-permute-done.1), kind=kLoop, calls=%fused_computation.42 | loop fusion | bytes 1146884 | tf_op jit(solution)/shard_map/dynamic_update_slice | solution.py:32
  57.6 1.9 %bitcast_dynamic-update-slice_fusion.9 = bf16[8,320,896]{2,1,0:T(8,128)(2,1)} fusion(bf16[8,320,896]{2,1,0:T(8,128)(2,1)} %bitcast_dynamic-update-slice_fusion.10, s32[]{:T(128)S(6)} %select_n.166, bf16[320,896]{1,0:T(8,128)(2,1)} %collective-permute-done.3), kind=kLoop, calls=%fused_computation.41 | loop fusion | bytes 1146884 | tf_op jit(solution)/shard_map/dynamic_update_slice | solution.py:32
  60.5 2.8 %collective-permute-start.10 = (bf16[320,896]{1,0:T(8,128)(2,1)S(1)}, bf16[320,896]{1,0:T(8,128)(2,1)S(1)}, u32[]{:S(2)}, u32[]{:S(2)}) collective-permute-start(bf16[320,896]{1,0:T(8,128)(2,1)S(1)} %copy-done.13), channel_id=1, source_target_pairs={{0,112},{16,0},{32,16},{48,32},{64,48},{80,64},{96,80},{112,96},{1... | collective-permute-start | bytes 1720328 | tf_op jit(solution)/shard_map/ppermute | solution.py:11
  64.5 1.1 bitcast_dynamic-update-slice_fusion.8
  65.7 6.5 %collective-permute-done.14 = bf16[512,448]{1,0:T(8,128)(2,1)S(1)} collective-permute-done((bf16[512,448]{1,0:T(8,128)(2,1)}, bf16[512,448]{1,0:T(8,128)(2,1)S(1)}, u32[]{:S(2)}, u32[]{:S(2)}) %collective-permute-start.14) | collective-permute-done | bytes 458784 | tf_op jit(solution)/shard_map/ppermute | solution.py:11
  72.2 2.3 %collective-permute-start.13 = (bf16[160,896]{1,0:T(8,128)(2,1)S(1)}, bf16[160,896]{1,0:T(8,128)(2,1)S(1)}, u32[]{:S(2)}, u32[]{:S(2)}) collective-permute-start(bf16[160,896]{1,0:T(8,128)(2,1)S(1)} %slice.35), channel_id=1, source_target_pairs={{0,112},{16,0},{32,16},{48,32},{64,48},{80,64},{96,80},{112,96},{1... | collective-permute-start | bytes 860168 | tf_op jit(solution)/shard_map/ppermute | solution.py:11
  74.7 1.3 collective-permute-done.12
  76.0 4.4 %collective-permute-done.13 = bf16[160,896]{1,0:T(8,128)(2,1)S(1)} collective-permute-done((bf16[160,896]{1,0:T(8,128)(2,1)S(1)}, bf16[160,896]{1,0:T(8,128)(2,1)S(1)}, u32[]{:S(2)}, u32[]{:S(2)}) %collective-permute-start.13) | collective-permute-done | bytes 286752 | tf_op jit(solution)/shard_map/ppermute | solution.py:11
  80.4 1.8 collective-permute-done.11
  83.7 1.3 collective-permute-start.15
  85.0 0.9 collective-permute-start.16
  85.8 1.8 %collective-permute-start.17 = (bf16[320,896]{1,0:T(8,128)(2,1)}, bf16[320,896]{1,0:T(8,128)(2,1)S(1)}, u32[]{:S(2)}, u32[]{:S(2)}) collective-permute-start(bf16[320,896]{1,0:T(8,128)(2,1)} %collective-permute-done.11), channel_id=1, source_target_pairs={{0,112},{16,0},{32,16},{48,32},{64,48},{80,64},{96,80},{112,96},{1... | collective-permute-start | bytes 1720328 | tf_op jit(solution)/shard_map/ppermute | solution.py:11
  87.8 1.1 bitcast_dynamic-update-slice_fusion.1
  88.9 1.1 bitcast_dynamic-update-slice_fusion
  90.1 1.6 bitcast_dynamic-update-slice_fusion.5
  91.7 2.9 %fusion.4 = f32[512,896]{1,0:T(8,128)S(1)} fusion(bf16[2560,896]{1,0:T(8,128)(2,1)S(1)} %bitcast.86, bf16[512,5120]{1,0:T(8,128)(2,1)S(1)} %bitcast.80, s32[]{:T(128)S(6)} %select_n.175), kind=kOutput, calls=%fused_computation.5 | convolution fusion | flops 2348810240 | bytes 9043972 | tf_op jit(solution)/shard_map/dot_general | solution.py:160
  94.6 4.1 %fusion.8 = f32[512,896]{1,0:T(8,128)} fusion(f32[512,896]{1,0:T(8,128)S(1)} %fusion.4, bf16[2560,896]{1,0:T(8,128)(2,1)S(1)} %bitcast.88, bf16[512,5120]{1,0:T(8,128)(2,1)S(1)} %bitcast.81, s32[]{:T(128)S(6)} %select_n.158), kind=kOutput, calls=%fused_computation.11 | convolution fusion | flops 2349268992 | bytes 10878980 | tf_op jit(solution)/shard_map/dot_general | solution.py:159
  98.8 6.1 %fusion = f32[512,896]{1,0:T(8,128)S(1)} fusion(bf16[2560,896]{1,0:T(8,128)(2,1)} %bitcast.87, bf16[512,5120]{1,0:T(8,128)(2,1)} %bitcast.82, s32[]{:T(128)S(6)} %select_n.175), kind=kOutput, calls=%fused_computation.1 | convolution fusion | flops 2348810240 | bytes 9043972 | tf_op jit(solution)/shard_map/dot_general | solution.py:160
  105.5 2.9 %fusion.11 = f32[512,896]{1,0:T(8,128)S(1)} fusion(f32[512,896]{1,0:T(8,128)S(1)} %fusion, bf16[2560,896]{1,0:T(8,128)(2,1)S(1)} %bitcast.89, bf16[512,5120]{1,0:T(8,128)(2,1)S(1)} %bitcast.84, s32[]{:T(128)S(6)} %select_n.158), kind=kOutput, calls=%fused_computation.12 | convolution fusion | flops 2349268992 | bytes 10878980 | tf_op jit(solution)/shard_map/dot_general | solution.py:159
  109.7 0.8 add_add_fusion
  113.0 0.9 fusion.56
  116.0 1.7 fusion.60
  118.5 11.7 %all-to-all-start = ((bf16[16,8,1024]{2,1,0:T(8,128)(2,1)}), bf16[16,8,1024]{2,1,0:T(8,128)(2,1)S(1)}, u32[]{:S(2)}, u32[]{:S(2)}) async-start(bf16[16,8,1024]{2,1,0:T(8,128)(2,1)} %pad_maximum_fusion.7), calls=%async_computation | async-start | bytes 524288 | tf_op jit(solution)/shard_map/all_to_all | solution.py:189
  130.5 9.1 %all-to-all-done = bf16[16,8,1024]{2,1,0:T(8,128)(2,1)S(1)} async-done(((bf16[16,8,1024]{2,1,0:T(8,128)(2,1)}), bf16[16,8,1024]{2,1,0:T(8,128)(2,1)S(1)}, u32[]{:S(2)}, u32[]{:S(2)}) %all-to-all-start) | async-done | bytes 262176 | tf_op jit(solution)/shard_map/all_to_all | solution.py:189
  141.3 4.9 %all-to-all-start.1 = ((bf16[16,16,512]{2,1,0:T(8,128)(2,1)}), bf16[16,16,512]{2,1,0:T(8,128)(2,1)S(1)}, u32[]{:S(2)}, u32[]{:S(2)}) async-start(bf16[16,16,512]{2,1,0:T(8,128)(2,1)} %broadcast_in_dim.73), calls=%async_computation.1 | async-start | bytes 524288 | tf_op jit(solution)/shard_map/all_to_all | solution.py:205
  146.6 8.5 %all-to-all-done.1 = bf16[16,16,512]{2,1,0:T(8,128)(2,1)S(1)} async-done(((bf16[16,16,512]{2,1,0:T(8,128)(2,1)}), bf16[16,16,512]{2,1,0:T(8,128)(2,1)S(1)}, u32[]{:S(2)}, u32[]{:S(2)}) %all-to-all-start.1) | async-done | bytes 262176 | tf_op jit(solution)/shard_map/all_to_all | solution.py:205
  155.6 12.1 %all_to_all.19 = f32[16,1,640]{2,1,0:T(1,128)S(1)} all-to-all(f32[16,1,640]{2,1,0:T(1,128)S(1)} %copy.24), channel_id=1, replica_groups=mesh['ylo'=2,'z'=8,'x'=4,'core'=2,'yhi'=2] {'x','core','yhi'}, dimensions={0} | all-to-all | bytes 81920 | tf_op jit(solution)/shard_map/all_to_all | solution.py:226
  (114 shorter events, 16.4 us)
Async XLA Ops:
  6.5 28.9 %copy-start = (bf16[64,5120]{1,0:T(8,128)(2,1)S(1)}, bf16[64,5120]{1,0:T(8,128)(2,1)}, u32[]{:S(2)}) copy-start(bf16[64,5120]{1,0:T(8,128)(2,1)} %param.15) | copy-start | bytes 1966084
  6.5 92.2 %all-gather.2.cloned.1.call-start = ((), (), s32[]{:S(2)}) async-start(), calls=%async_computation.3 | async-start | bytes 5898240 | tf_op jit(solution)/shard_map/all_gather | solution.py:52
  7.9 19.3 %collective-permute-start = (bf16[320,896]{1,0:T(8,128)(2,1)S(1)}, bf16[320,896]{1,0:T(8,128)(2,1)}, u32[]{:S(2)}, u32[]{:S(2)}) collective-permute-start(bf16[320,896]{1,0:T(8,128)(2,1)S(1)} %pad_maximum_fusion.2), channel_id=1, source_target_pairs={{0,16},{16,32},{32,48},{48,64},{64,80},{80,96},{96,112},{112,0},{1... | collective-permute-start | bytes 1720328 | tf_op jit(solution)/shard_map/ppermute | solution.py:11
  10.4 16.8 %collective-permute-start.1 = (bf16[320,896]{1,0:T(8,128)(2,1)S(1)}, bf16[320,896]{1,0:T(8,128)(2,1)}, u32[]{:S(2)}, u32[]{:S(2)}) collective-permute-start(bf16[320,896]{1,0:T(8,128)(2,1)S(1)} %pad_maximum_fusion.2), channel_id=1, source_target_pairs={{0,112},{16,0},{32,16},{48,32},{64,48},{80,64},{96,80},{112,96},{1... | collective-permute-start | bytes 1720328 | tf_op jit(solution)/shard_map/ppermute | solution.py:11
  14.4 13.6 %collective-permute-start.2 = (bf16[320,896]{1,0:T(8,128)(2,1)S(1)}, bf16[320,896]{1,0:T(8,128)(2,1)S(1)}, u32[]{:S(2)}, u32[]{:S(2)}) collective-permute-start(bf16[320,896]{1,0:T(8,128)(2,1)S(1)} %pad_maximum_fusion.2), channel_id=1, source_target_pairs={{0,128},{128,0},{1,129},{129,1},{2,130},{130,2},{3,131},{131,3},{4... | collective-permute-start | bytes 1720328 | tf_op jit(solution)/shard_map/ppermute | solution.py:11
  15.7 6.4 %copy-start.10 = (bf16[8,32,896]{2,1,0:T(8,128)(2,1)S(1)}, bf16[8,32,896]{2,1,0:T(8,128)(2,1)}, u32[]{:S(2)}) copy-start(bf16[8,32,896]{2,1,0:T(8,128)(2,1)} %param.12) | copy-start | bytes 1376260
  15.7 6.4 %copy-start.11 = (bf16[8,32,896]{2,1,0:T(8,128)(2,1)S(1)}, bf16[8,32,896]{2,1,0:T(8,128)(2,1)}, u32[]{:S(2)}) copy-start(bf16[8,32,896]{2,1,0:T(8,128)(2,1)} %param.10) | copy-start | bytes 1376260
  24.3 11.1 %copy-start.1 = (bf16[8,64,5120]{2,1,0:T(8,128)(2,1)S(1)}, bf16[8,64,5120]{2,1,0:T(8,128)(2,1)}, u32[]{:S(2)}) copy-start(bf16[8,64,5120]{2,1,0:T(8,128)(2,1)} %pad_maximum_fusion) | copy-start | bytes 15728644
  28.0 9.8 %copy-start.12 = (bf16[320,896]{1,0:T(8,128)(2,1)}, bf16[320,896]{1,0:T(8,128)(2,1)S(1)}, u32[]{:S(2)}) copy-start(bf16[320,896]{1,0:T(8,128)(2,1)S(1)} %collective-permute-done.2) | copy-start | bytes 1720324
  28.0 14.2 %collective-permute-start.3 = (bf16[320,896]{1,0:T(8,128)(2,1)}, bf16[320,896]{1,0:T(8,128)(2,1)}, u32[]{:S(2)}, u32[]{:S(2)}) collective-permute-start(bf16[320,896]{1,0:T(8,128)(2,1)} %collective-permute-done), channel_id=1, source_target_pairs={{0,16},{16,32},{32,48},{48,64},{64,80},{80,96},{96,112},{112,0},{1... | collective-permute-start | bytes 1720328 | tf_op jit(solution)/shard_map/ppermute | solution.py:11
  28.0 14.2 %collective-permute-start.4 = (bf16[320,896]{1,0:T(8,128)(2,1)}, bf16[320,896]{1,0:T(8,128)(2,1)}, u32[]{:S(2)}, u32[]{:S(2)}) collective-permute-start(bf16[320,896]{1,0:T(8,128)(2,1)} %collective-permute-done.1), channel_id=1, source_target_pairs={{0,112},{16,0},{32,16},{48,32},{64,48},{80,64},{96,80},{112,96},{1... | collective-permute-start | bytes 1720328 | tf_op jit(solution)/shard_map/ppermute | solution.py:11
  30.7 15.3 %collective-permute-start.5 = (bf16[1,64,5120]{2,1,0:T(8,128)(2,1)S(1)}, bf16[1,64,5120]{2,1,0:T(8,128)(2,1)S(1)}, u32[]{:S(2)}, u32[]{:S(2)}) collective-permute-start(bf16[1,64,5120]{2,1,0:T(8,128)(2,1)S(1)} %pad_maximum_fusion.1), channel_id=1, source_target_pairs={{0,1},{1,0},{2,3},{3,2},{4,5},{5,4},{6,7},{7,6},{8,9},{9,8},{10,11... | collective-permute-start | bytes 1966088 | tf_op jit(solution)/shard_map/ppermute | solution.py:11
  35.4 2.4 %copy-start.4 = (bf16[8,320,896]{2,1,0:T(8,128)(2,1)}, bf16[8,320,896]{2,1,0:T(8,128)(2,1)S(1)}, u32[]{:S(2)}) copy-start(bf16[8,320,896]{2,1,0:T(8,128)(2,1)S(1)} %bitcast_dynamic-update-slice_fusion.11) | copy-start | bytes 13762564
  42.2 17.6 %copy-start.13 = (bf16[320,896]{1,0:T(8,128)(2,1)S(1)}, bf16[320,896]{1,0:T(8,128)(2,1)}, u32[]{:S(2)}) copy-start(bf16[320,896]{1,0:T(8,128)(2,1)} %copy-done.12) | copy-start | bytes 1720324
  46.0 0.9 copy-start.9
  47.0 12.6 %collective-permute-start.6 = (bf16[320,896]{1,0:T(8,128)(2,1)}, bf16[320,896]{1,0:T(8,128)(2,1)S(1)}, u32[]{:S(2)}, u32[]{:S(2)}) collective-permute-start(bf16[320,896]{1,0:T(8,128)(2,1)} %collective-permute-done.3), channel_id=1, source_target_pairs={{0,16},{16,32},{32,48},{48,64},{64,80},{80,96},{96,112},{112,0},{1... | collective-permute-start | bytes 1720328 | tf_op jit(solution)/shard_map/ppermute | solution.py:11
  47.1 12.7 %collective-permute-start.8 = (bf16[320,896]{1,0:T(8,128)(2,1)}, bf16[320,896]{1,0:T(8,128)(2,1)}, u32[]{:S(2)}, u32[]{:S(2)}) collective-permute-start(bf16[320,896]{1,0:T(8,128)(2,1)} %collective-permute-done.3), channel_id=1, source_target_pairs={{0,128},{128,0},{1,129},{129,1},{2,130},{130,2},{3,131},{131,3},{4... | collective-permute-start | bytes 1720328 | tf_op jit(solution)/shard_map/ppermute | solution.py:11
  48.5 11.3 %collective-permute-start.7 = (bf16[320,896]{1,0:T(8,128)(2,1)}, bf16[320,896]{1,0:T(8,128)(2,1)S(1)}, u32[]{:S(2)}, u32[]{:S(2)}) collective-permute-start(bf16[320,896]{1,0:T(8,128)(2,1)} %collective-permute-done.4), channel_id=1, source_target_pairs={{0,112},{16,0},{32,16},{48,32},{64,48},{80,64},{96,80},{112,96},{1... | collective-permute-start | bytes 1720328 | tf_op jit(solution)/shard_map/ppermute | solution.py:11
  52.9 19.3 %collective-permute-start.14 = (bf16[512,448]{1,0:T(8,128)(2,1)}, bf16[512,448]{1,0:T(8,128)(2,1)S(1)}, u32[]{:S(2)}, u32[]{:S(2)}) collective-permute-start(bf16[512,448]{1,0:T(8,128)(2,1)} %bitcast.94), channel_id=1, source_target_pairs={{0,1},{1,0},{2,3},{3,2},{4,5},{5,4},{6,7},{7,6},{8,9},{9,8},{10,11... | collective-permute-start | bytes 1376264 | tf_op jit(solution)/shard_map/ppermute | solution.py:11
  59.5 5.0 %copy-start.5 = (bf16[8,320,896]{2,1,0:T(8,128)(2,1)S(1)}, bf16[8,320,896]{2,1,0:T(8,128)(2,1)}, u32[]{:S(2)}) copy-start(bf16[8,320,896]{2,1,0:T(8,128)(2,1)} %bitcast_dynamic-update-slice_fusion.9) | copy-start | bytes 13762564
  59.8 20.6 %collective-permute-start.9 = (bf16[320,896]{1,0:T(8,128)(2,1)S(1)}, bf16[320,896]{1,0:T(8,128)(2,1)S(1)}, u32[]{:S(2)}, u32[]{:S(2)}) collective-permute-start(bf16[320,896]{1,0:T(8,128)(2,1)S(1)} %copy-done.13), channel_id=1, source_target_pairs={{0,16},{16,32},{32,48},{48,64},{64,80},{80,96},{96,112},{112,0},{1... | collective-permute-start | bytes 1720328 | tf_op jit(solution)/shard_map/ppermute | solution.py:11
  60.5 19.9 %collective-permute-start.10 = (bf16[320,896]{1,0:T(8,128)(2,1)S(1)}, bf16[320,896]{1,0:T(8,128)(2,1)S(1)}, u32[]{:S(2)}, u32[]{:S(2)}) collective-permute-start(bf16[320,896]{1,0:T(8,128)(2,1)S(1)} %copy-done.13), channel_id=1, source_target_pairs={{0,112},{16,0},{32,16},{48,32},{64,48},{80,64},{96,80},{112,96},{1... | collective-permute-start | bytes 1720328 | tf_op jit(solution)/shard_map/ppermute | solution.py:11
  63.3 18.8 %collective-permute-start.11 = (bf16[320,896]{1,0:T(8,128)(2,1)}, bf16[320,896]{1,0:T(8,128)(2,1)}, u32[]{:S(2)}, u32[]{:S(2)}) collective-permute-start(bf16[320,896]{1,0:T(8,128)(2,1)} %collective-permute-done.4), channel_id=1, source_target_pairs={{0,128},{128,0},{1,129},{129,1},{2,130},{130,2},{3,131},{131,3},{4... | collective-permute-start | bytes 1720328 | tf_op jit(solution)/shard_map/ppermute | solution.py:11
  63.7 12.2 %collective-permute-start.12 = (bf16[160,896]{1,0:T(8,128)(2,1)S(1)}, bf16[160,896]{1,0:T(8,128)(2,1)S(1)}, u32[]{:S(2)}, u32[]{:S(2)}) collective-permute-start(bf16[160,896]{1,0:T(8,128)(2,1)S(1)} %slice.34), channel_id=1, source_target_pairs={{0,16},{16,32},{32,48},{48,64},{64,80},{80,96},{96,112},{112,0},{1... | collective-permute-start | bytes 860168 | tf_op jit(solution)/shard_map/ppermute | solution.py:11
  63.8 27.8 %slice-start = ((s8[5242880]{0:T(1024)(128)(4,1)}), s8[1048576]{0:T(1024)(128)(4,1)S(1)}, s32[]{:S(2)}) async-start(s8[5242880]{0:T(1024)(128)(4,1)} %bitcast.78), calls=%async_computation.4 | async-start | bytes 2097152
  65.7 26.0 %slice-start.1 = ((s8[5242880]{0:T(1024)(128)(4,1)}), s8[4194304]{0:T(1024)(128)(4,1)S(1)}, s32[]{:S(2)}) async-start(s8[5242880]{0:T(1024)(128)(4,1)} %bitcast.78), calls=%async_computation.5 | async-start | bytes 8388608
  72.2 19.4 %copy-start.16 = (bf16[512,448]{1,0:T(8,128)(2,1)}, bf16[512,448]{1,0:T(8,128)(2,1)S(1)}, u32[]{:S(2)}) copy-start(bf16[512,448]{1,0:T(8,128)(2,1)S(1)} %collective-permute-done.14) | copy-start | bytes 1376260
  72.2 8.2 %collective-permute-start.13 = (bf16[160,896]{1,0:T(8,128)(2,1)S(1)}, bf16[160,896]{1,0:T(8,128)(2,1)S(1)}, u32[]{:S(2)}, u32[]{:S(2)}) collective-permute-start(bf16[160,896]{1,0:T(8,128)(2,1)S(1)} %slice.35), channel_id=1, source_target_pairs={{0,112},{16,0},{32,16},{48,32},{64,48},{80,64},{96,80},{112,96},{1... | collective-permute-start | bytes 860168 | tf_op jit(solution)/shard_map/ppermute | solution.py:11
  83.7 24.7 %collective-permute-start.15 = (bf16[320,896]{1,0:T(8,128)(2,1)}, bf16[320,896]{1,0:T(8,128)(2,1)S(1)}, u32[]{:S(2)}, u32[]{:S(2)}) collective-permute-start(bf16[320,896]{1,0:T(8,128)(2,1)} %constant_dynamic-update-slice_fusion), channel_id=1, source_target_pairs={{0,128},{128,0},{1,129},{129,1},{2,130},{130,2},{3,131},{131,3},{4... | collective-permute-start | bytes 1720328 | tf_op jit(solution)/shard_map/ppermute | solution.py:11
  85.0 23.4 %collective-permute-start.16 = (bf16[320,896]{1,0:T(8,128)(2,1)}, bf16[320,896]{1,0:T(8,128)(2,1)S(1)}, u32[]{:S(2)}, u32[]{:S(2)}) collective-permute-start(bf16[320,896]{1,0:T(8,128)(2,1)} %collective-permute-done.8), channel_id=1, source_target_pairs={{0,16},{16,32},{32,48},{48,64},{64,80},{80,96},{96,112},{112,0},{1... | collective-permute-start | bytes 1720328 | tf_op jit(solution)/shard_map/ppermute | solution.py:11
  85.8 22.6 %collective-permute-start.17 = (bf16[320,896]{1,0:T(8,128)(2,1)}, bf16[320,896]{1,0:T(8,128)(2,1)S(1)}, u32[]{:S(2)}, u32[]{:S(2)}) collective-permute-start(bf16[320,896]{1,0:T(8,128)(2,1)} %collective-permute-done.11), channel_id=1, source_target_pairs={{0,112},{16,0},{32,16},{48,32},{64,48},{80,64},{96,80},{112,96},{1... | collective-permute-start | bytes 1720328 | tf_op jit(solution)/shard_map/ppermute | solution.py:11
  90.1 4.5 %copy-start.3 = (bf16[8,320,896]{2,1,0:T(8,128)(2,1)}, bf16[8,320,896]{2,1,0:T(8,128)(2,1)S(1)}, u32[]{:S(2)}) copy-start(bf16[8,320,896]{2,1,0:T(8,128)(2,1)S(1)} %bitcast_dynamic-update-slice_fusion) | copy-start | bytes 13762564
  91.7 2.9 %copy-start.6 = (bf16[8,320,896]{2,1,0:T(8,128)(2,1)}, bf16[8,320,896]{2,1,0:T(8,128)(2,1)S(1)}, u32[]{:S(2)}) copy-start(bf16[8,320,896]{2,1,0:T(8,128)(2,1)S(1)} %bitcast_dynamic-update-slice_fusion.5) | copy-start | bytes 13762564
  98.8 6.1 %copy-start.2 = (bf16[8,64,5120]{2,1,0:T(8,128)(2,1)S(1)}, bf16[8,64,5120]{2,1,0:T(8,128)(2,1)}, u32[]{:S(2)}) copy-start(bf16[8,64,5120]{2,1,0:T(8,128)(2,1)} %all-gather.2.cloned.1.call-done) | copy-start | bytes 15728644
  98.8 6.7 %copy-start.7 = (bf16[8,320,896]{2,1,0:T(8,128)(2,1)S(1)}, bf16[8,320,896]{2,1,0:T(8,128)(2,1)}, u32[]{:S(2)}) copy-start(bf16[8,320,896]{2,1,0:T(8,128)(2,1)} %copy-done.6) | copy-start | bytes 13762564
  109.7 1.0 copy-start.17
  109.7 1.0 copy-start.18
  110.8 0.9 copy-start.19
  111.7 2.2 %copy-start.8 = (f32[512,896]{1,0:T(8,128)S(1)}, f32[512,896]{1,0:T(8,128)}, u32[]{:S(2)}) copy-start(f32[512,896]{1,0:T(8,128)} %fusion.8) | copy-start | bytes 5505028
  113.9 1.0 copy-start.15
  116.0 14.2 %copy-start.14 = (f32[512,64]{0,1:T(8,128)S(1)}, f32[512,64]{0,1:T(8,128)}, u32[]{:S(2)}) copy-start(f32[512,64]{0,1:T(8,128)} %fusion.55) | copy-start | bytes 393220
  118.5 21.1 %all-to-all-start = ((bf16[16,8,1024]{2,1,0:T(8,128)(2,1)}), bf16[16,8,1024]{2,1,0:T(8,128)(2,1)S(1)}, u32[]{:S(2)}, u32[]{:S(2)}) async-start(bf16[16,8,1024]{2,1,0:T(8,128)(2,1)} %pad_maximum_fusion.7), calls=%async_computation | async-start | bytes 524288 | tf_op jit(solution)/shard_map/all_to_all | solution.py:189
  141.3 13.8 %all-to-all-start.1 = ((bf16[16,16,512]{2,1,0:T(8,128)(2,1)}), bf16[16,16,512]{2,1,0:T(8,128)(2,1)S(1)}, u32[]{:S(2)}, u32[]{:S(2)}) async-start(bf16[16,16,512]{2,1,0:T(8,128)(2,1)} %broadcast_in_dim.73), calls=%async_computation.1 | async-start | bytes 524288 | tf_op jit(solution)/shard_map/all_to_all | solution.py:205
Sparse Core Ops, SparseCore 0:
  47.0 41.8 all-gather.1

commit v16 on v15

--- a/solution.py
+++ b/solution.py
@@ -168,7 +168,6 @@
     pres, own_factor, other, chunks, shards = lax.optimization_barrier(
         (pres, own_factor, other, chunks, shards)
     )
-    factors = (own_factor, inner_factor(other))
     parts = []
     for pre, pieces, rows_cot in zip(pres, chunks, (own_cot, other_cot)):
         for chunk, shard in zip(pieces, shards):
@@ -183,7 +182,8 @@
         return jnp.concatenate((a, b), axis=axis)
 
     part = ordered(parts, 1).astype(BF16)
-    in_factor = ordered(factors, 0)
+    part, other = lax.optimization_barrier((part, other))
+    in_factor = ordered((own_factor, inner_factor(other)), 0)
     ranks = part.shape[0] // n_dq
     part = part.reshape(n_dq, ranks, -1)
     swapped = lax.all_to_all(part, dq, 0, 0, tiled=True)

time: 177 us -> 177 us (level)
  no operation moved by 1% of the time
where the time goes in v16:
time: 177 us; the launch traced here: 176 us
  starting transfers between devices  47.1 us (27%)
  waiting for transfers between devices  43.7 us (25%)
  matrix products  27.4 us (15%)
  local copies, waits for them, and re-layouts  21.3 us (12%)
  between operations  14.8 us (8%)
  blocking collectives  12.1 us (7%)
  other arithmetic  10.1 us (6%)
    ppermute x18, starting transfers between devices, shift(): lax.ppermute(value, axis, [(i, (i + step) % size) for i in range(size)])  30.5 us
    ppermute x18, waiting for transfers between devices, shift(): lax.ppermute(value, axis, [(i, (i + step) % size) for i in range(size)])  26.1 us
    all_to_all x1, blocking collectives, body(): received = lax.all_to_all(payload, dq, 0, 0, tiled=True)  12.1 us
    all_to_all x1, starting transfers between devices, body(): swapped = lax.all_to_all(part, dq, 0, 0, tiled=True)  11.8 us
    dynamic_update_slice x13, local copies, waits for them, and re-layouts, placed(): lax.dynamic_update_slice(result, shard[None], ((z + offset) % n_z, 0, 0))  10.4 us
    all_to_all x1, waiting for transfers between devices, body(): swapped = lax.all_to_all(part, dq, 0, 0, tiled=True)  9.11 us
    dot_general x2, matrix products, body(): jnp.dot(other_flat, other_row, preferred_element_type=F32)  8.98 us
    all_to_all x1, waiting for transfers between devices, body(): lax.all_to_all(jnp.broadcast_to(queries[None], (n_fsdp,) + queries.shape)...  8.5 us
  transfers between devices with their start and end apart: 21, of which 12 were waited for; matrix products, arithmetic and copies ran while one was open for 24% of the time, Pallas kernels for 0%

profile of v16, /device:TPU:1, one launch (start us, length us, event | category | flops | bytes accessed | tf_op | source)
XLA Modules:
  0.0 176.4 jit_solution(2725246961491533329)
XLA Ops:
  6.5 1.3 pad_maximum_fusion.2
  7.9 2.5 %collective-permute-start = (bf16[320,896]{1,0:T(8,128)(2,1)S(1)}, bf16[320,896]{1,0:T(8,128)(2,1)}, u32[]{:S(2)}, u32[]{:S(2)}) collective-permute-start(bf16[320,896]{1,0:T(8,128)(2,1)S(1)} %pad_maximum_fusion.2), channel_id=1, source_target_pairs={{0,16},{16,32},{32,48},{48,64},{64,80},{80,96},{96,112},{112,0},{1... | collective-permute-start | bytes 1720328 | tf_op jit(solution)/shard_map/ppermute | solution.py:11
  10.4 4.0 %collective-permute-start.1 = (bf16[320,896]{1,0:T(8,128)(2,1)S(1)}, bf16[320,896]{1,0:T(8,128)(2,1)}, u32[]{:S(2)}, u32[]{:S(2)}) collective-permute-start(bf16[320,896]{1,0:T(8,128)(2,1)S(1)} %pad_maximum_fusion.2), channel_id=1, source_target_pairs={{0,112},{16,0},{32,16},{48,32},{64,48},{80,64},{96,80},{112,96},{1... | collective-permute-start | bytes 1720328 | tf_op jit(solution)/shard_map/ppermute | solution.py:11
  14.4 1.3 collective-permute-start.2
  15.7 5.3 %pad_maximum_fusion = bf16[8,64,5120]{2,1,0:T(8,128)(2,1)} fusion(bf16[8,32,5120]{2,1,0:T(8,128)(2,1)} %param.11, bf16[8,32,5120]{2,1,0:T(8,128)(2,1)} %param.9), kind=kLoop, calls=%fused_computation | loop fusion | flops 10485760 | bytes 10485760 | tf_op jit(solution)/shard_map/concatenate | solution.py:123
  21.0 1.1 constant_dynamic-slice_fusion.8
  22.6 0.9 pad_maximum_fusion.3
  23.5 0.8 pad_maximum_fusion.4
  24.4 2.8 %collective-permute-done = bf16[320,896]{1,0:T(8,128)(2,1)} collective-permute-done((bf16[320,896]{1,0:T(8,128)(2,1)S(1)}, bf16[320,896]{1,0:T(8,128)(2,1)}, u32[]{:S(2)}, u32[]{:S(2)}) %collective-permute-start) | collective-permute-done | bytes 573472 | tf_op jit(solution)/shard_map/ppermute | solution.py:11
  27.2 0.8 collective-permute-done.2
  28.0 2.7 %collective-permute-start.4 = (bf16[320,896]{1,0:T(8,128)(2,1)}, bf16[320,896]{1,0:T(8,128)(2,1)}, u32[]{:S(2)}, u32[]{:S(2)}) collective-permute-start(bf16[320,896]{1,0:T(8,128)(2,1)} %collective-permute-done.1), channel_id=1, source_target_pairs={{0,112},{16,0},{32,16},{48,32},{64,48},{80,64},{96,80},{112,96},{1... | collective-permute-start | bytes 1720328 | tf_op jit(solution)/shard_map/ppermute | solution.py:11
  30.7 2.9 %collective-permute-start.5 = (bf16[1,64,5120]{2,1,0:T(8,128)(2,1)S(1)}, bf16[1,64,5120]{2,1,0:T(8,128)(2,1)S(1)}, u32[]{:S(2)}, u32[]{:S(2)}) collective-permute-start(bf16[1,64,5120]{2,1,0:T(8,128)(2,1)S(1)} %pad_maximum_fusion.1), channel_id=1, source_target_pairs={{0,1},{1,0},{2,3},{3,2},{4,5},{5,4},{6,7},{7,6},{8,9},{9,8},{10,11... | collective-permute-start | bytes 1966088 | tf_op jit(solution)/shard_map/ppermute | solution.py:11
  34.3 1.1 bitcast_dynamic-update-slice_fusion.11
  35.4 2.4 %fusion.53 = f32[512,64]{0,1:T(8,128)} fusion(bf16[512,5120]{1,0:T(8,128)(2,1)S(1)} %bitcast.74, bf16[64,5120]{1,0:T(8,128)(2,1)S(1)} %copy-done), kind=kOutput, calls=%fused_computation.100 | convolution fusion | flops 335544320 | bytes 6029312 | tf_op jit(solution)/shard_map/dot_general | solution.py:138
  37.8 4.4 %collective-permute-done.3 = bf16[320,896]{1,0:T(8,128)(2,1)} collective-permute-done((bf16[320,896]{1,0:T(8,128)(2,1)}, bf16[320,896]{1,0:T(8,128)(2,1)}, u32[]{:S(2)}, u32[]{:S(2)}) %collective-permute-start.3) | collective-permute-done | bytes 573472 | tf_op jit(solution)/shard_map/ppermute | solution.py:11
  42.2 3.8 %collective-permute-done.5 = bf16[1,64,5120]{2,1,0:T(8,128)(2,1)S(1)} collective-permute-done((bf16[1,64,5120]{2,1,0:T(8,128)(2,1)S(1)}, bf16[1,64,5120]{2,1,0:T(8,128)(2,1)S(1)}, u32[]{:S(2)}, u32[]{:S(2)}) %collective-permute-start.5) | collective-permute-done | bytes 655392 | tf_op jit(solution)/shard_map/ppermute | solution.py:11
  46.0 0.8 copy-done.9
  47.1 1.4 collective-permute-start.8
  48.5 2.6 %collective-permute-start.7 = (bf16[320,896]{1,0:T(8,128)(2,1)}, bf16[320,896]{1,0:T(8,128)(2,1)S(1)}, u32[]{:S(2)}, u32[]{:S(2)}) collective-permute-start(bf16[320,896]{1,0:T(8,128)(2,1)} %collective-permute-done.4), channel_id=1, source_target_pairs={{0,112},{16,0},{32,16},{48,32},{64,48},{80,64},{96,80},{112,96},{1... | collective-permute-start | bytes 1720328 | tf_op jit(solution)/shard_map/ppermute | solution.py:11
  51.1 1.9 %constant_dynamic-slice_fusion.3 = (bf16[512,320]{1,0:T(8,128)(2,1)S(1)}, bf16[512,320]{1,0:T(8,128)(2,1)S(1)}, bf16[512,320]{1,0:T(8,128)(2,1)S(1)}) fusion(bf16[512,5120]{1,0:T(8,128)(2,1)} %bitcast.73, s32[]{:T(128)S(6)} %dynamic_slice.81, s32[]{:T(128)S(6)} %dynamic_slice.79, s32[]{:T(128)S(6)} %dynamic_slice.77), kind=kLoop, calls=%fused_computation.79 | loop fusion | bytes 1966092 | tf_op jit(solution)/shard_map/dynamic_slice | solution.py:163
  52.9 2.7 %collective-permute-start.14 = (bf16[512,448]{1,0:T(8,128)(2,1)}, bf16[512,448]{1,0:T(8,128)(2,1)S(1)}, u32[]{:S(2)}, u32[]{:S(2)}) collective-permute-start(bf16[512,448]{1,0:T(8,128)(2,1)} %bitcast.91), channel_id=1, source_target_pairs={{0,1},{1,0},{2,3},{3,2},{4,5},{5,4},{6,7},{7,6},{8,9},{9,8},{10,11... | collective-permute-start | bytes 1376264 | tf_op jit(solution)/shard_map/ppermute | solution.py:11
  55.6 1.9 %bitcast_dynamic-update-slice_fusion.10 = bf16[8,320,896]{2,1,0:T(8,128)(2,1)} fusion(bf16[8,320,896]{2,1,0:T(8,128)(2,1)} %copy-done.4, s32[]{:T(128)S(6)} %select_n.156, bf16[320,896]{1,0:T(8,128)(2,1)} %collective-permute-done.1), kind=kLoop, calls=%fused_computation.42 | loop fusion | bytes 1146884 | tf_op jit(solution)/shard_map/dynamic_update_slice | solution.py:32
  57.6 1.9 %bitcast_dynamic-update-slice_fusion.9 = bf16[8,320,896]{2,1,0:T(8,128)(2,1)} fusion(bf16[8,320,896]{2,1,0:T(8,128)(2,1)} %bitcast_dynamic-update-slice_fusion.10, s32[]{:T(128)S(6)} %select_n.158, bf16[320,896]{1,0:T(8,128)(2,1)} %collective-permute-done.3), kind=kLoop, calls=%fused_computation.41 | loop fusion | bytes 1146884 | tf_op jit(solution)/shard_map/dynamic_update_slice | solution.py:32
  60.5 2.8 %collective-permute-start.10 = (bf16[320,896]{1,0:T(8,128)(2,1)S(1)}, bf16[320,896]{1,0:T(8,128)(2,1)S(1)}, u32[]{:S(2)}, u32[]{:S(2)}) collective-permute-start(bf16[320,896]{1,0:T(8,128)(2,1)S(1)} %copy-done.13), channel_id=1, source_target_pairs={{0,112},{16,0},{32,16},{48,32},{64,48},{80,64},{96,80},{112,96},{1... | collective-permute-start | bytes 1720328 | tf_op jit(solution)/shard_map/ppermute | solution.py:11
  64.5 1.1 bitcast_dynamic-update-slice_fusion.8
  65.7 6.5 %collective-permute-done.14 = bf16[512,448]{1,0:T(8,128)(2,1)S(1)} collective-permute-done((bf16[512,448]{1,0:T(8,128)(2,1)}, bf16[512,448]{1,0:T(8,128)(2,1)S(1)}, u32[]{:S(2)}, u32[]{:S(2)}) %collective-permute-start.14) | collective-permute-done | bytes 458784 | tf_op jit(solution)/shard_map/ppermute | solution.py:11
  72.2 2.3 %collective-permute-start.13 = (bf16[160,896]{1,0:T(8,128)(2,1)S(1)}, bf16[160,896]{1,0:T(8,128)(2,1)S(1)}, u32[]{:S(2)}, u32[]{:S(2)}) collective-permute-start(bf16[160,896]{1,0:T(8,128)(2,1)S(1)} %slice.35), channel_id=1, source_target_pairs={{0,112},{16,0},{32,16},{48,32},{64,48},{80,64},{96,80},{112,96},{1... | collective-permute-start | bytes 860168 | tf_op jit(solution)/shard_map/ppermute | solution.py:11
  74.7 1.3 collective-permute-done.12
  76.0 4.4 %collective-permute-done.13 = bf16[160,896]{1,0:T(8,128)(2,1)S(1)} collective-permute-done((bf16[160,896]{1,0:T(8,128)(2,1)S(1)}, bf16[160,896]{1,0:T(8,128)(2,1)S(1)}, u32[]{:S(2)}, u32[]{:S(2)}) %collective-permute-start.13) | collective-permute-done | bytes 286752 | tf_op jit(solution)/shard_map/ppermute | solution.py:11
  80.4 1.8 collective-permute-done.11
  83.7 1.3 collective-permute-start.15
  85.0 0.9 collective-permute-start.16
  85.8 1.8 %collective-permute-start.17 = (bf16[320,896]{1,0:T(8,128)(2,1)}, bf16[320,896]{1,0:T(8,128)(2,1)S(1)}, u32[]{:S(2)}, u32[]{:S(2)}) collective-permute-start(bf16[320,896]{1,0:T(8,128)(2,1)} %collective-permute-done.11), channel_id=1, source_target_pairs={{0,112},{16,0},{32,16},{48,32},{64,48},{80,64},{96,80},{112,96},{1... | collective-permute-start | bytes 1720328 | tf_op jit(solution)/shard_map/ppermute | solution.py:11
  87.8 1.1 bitcast_dynamic-update-slice_fusion.1
  88.9 1.1 bitcast_dynamic-update-slice_fusion
  90.1 1.6 bitcast_dynamic-update-slice_fusion.5
  91.7 2.9 %fusion.4 = f32[512,896]{1,0:T(8,128)S(1)} fusion(bf16[2560,896]{1,0:T(8,128)(2,1)S(1)} %bitcast.83, bf16[512,5120]{1,0:T(8,128)(2,1)S(1)} %bitcast.77, s32[]{:T(128)S(6)} %select_n.167), kind=kOutput, calls=%fused_computation.5 | convolution fusion | flops 2348810240 | bytes 9043972 | tf_op jit(solution)/shard_map/dot_general | solution.py:160
  94.6 4.1 %fusion.8 = f32[512,896]{1,0:T(8,128)} fusion(f32[512,896]{1,0:T(8,128)S(1)} %fusion.4, bf16[2560,896]{1,0:T(8,128)(2,1)S(1)} %bitcast.85, bf16[512,5120]{1,0:T(8,128)(2,1)S(1)} %bitcast.78, s32[]{:T(128)S(6)} %select_n.150), kind=kOutput, calls=%fused_computation.11 | convolution fusion | flops 2349268992 | bytes 10878980 | tf_op jit(solution)/shard_map/dot_general | solution.py:159
  98.8 6.1 %fusion = f32[512,896]{1,0:T(8,128)S(1)} fusion(bf16[2560,896]{1,0:T(8,128)(2,1)} %bitcast.84, bf16[512,5120]{1,0:T(8,128)(2,1)} %bitcast.79, s32[]{:T(128)S(6)} %select_n.167), kind=kOutput, calls=%fused_computation.1 | convolution fusion | flops 2348810240 | bytes 9043972 | tf_op jit(solution)/shard_map/dot_general | solution.py:160
  105.5 2.9 %fusion.11 = f32[512,896]{1,0:T(8,128)S(1)} fusion(f32[512,896]{1,0:T(8,128)S(1)} %fusion, bf16[2560,896]{1,0:T(8,128)(2,1)S(1)} %bitcast.86, bf16[512,5120]{1,0:T(8,128)(2,1)S(1)} %bitcast.81, s32[]{:T(128)S(6)} %select_n.150), kind=kOutput, calls=%fused_computation.12 | convolution fusion | flops 2349268992 | bytes 10878980 | tf_op jit(solution)/shard_map/dot_general | solution.py:159
  109.7 0.8 add_add_fusion
  113.0 0.9 fusion.54
  116.8 1.7 fusion.58
  118.5 11.8 %all-to-all-start = ((bf16[16,8,1024]{2,1,0:T(8,128)(2,1)}), bf16[16,8,1024]{2,1,0:T(8,128)(2,1)S(1)}, u32[]{:S(2)}, u32[]{:S(2)}) async-start(bf16[16,8,1024]{2,1,0:T(8,128)(2,1)} %bitcast.19), calls=%async_computation | async-start | bytes 524288 | tf_op jit(solution)/shard_map/all_to_all | solution.py:189
  130.5 9.1 %all-to-all-done = bf16[16,8,1024]{2,1,0:T(8,128)(2,1)S(1)} async-done(((bf16[16,8,1024]{2,1,0:T(8,128)(2,1)}), bf16[16,8,1024]{2,1,0:T(8,128)(2,1)S(1)}, u32[]{:S(2)}, u32[]{:S(2)}) %all-to-all-start) | async-done | bytes 262176 | tf_op jit(solution)/shard_map/all_to_all | solution.py:189
  141.3 4.9 %all-to-all-start.1 = ((bf16[16,16,512]{2,1,0:T(8,128)(2,1)}), bf16[16,16,512]{2,1,0:T(8,128)(2,1)S(1)}, u32[]{:S(2)}, u32[]{:S(2)}) async-start(bf16[16,16,512]{2,1,0:T(8,128)(2,1)} %broadcast_in_dim.73), calls=%async_computation.1 | async-start | bytes 524288 | tf_op jit(solution)/shard_map/all_to_all | solution.py:205
  146.6 8.5 %all-to-all-done.1 = bf16[16,16,512]{2,1,0:T(8,128)(2,1)S(1)} async-done(((bf16[16,16,512]{2,1,0:T(8,128)(2,1)}), bf16[16,16,512]{2,1,0:T(8,128)(2,1)S(1)}, u32[]{:S(2)}, u32[]{:S(2)}) %all-to-all-start.1) | async-done | bytes 262176 | tf_op jit(solution)/shard_map/all_to_all | solution.py:205
  155.6 12.1 %all_to_all.19 = f32[16,1,640]{2,1,0:T(1,128)S(1)} all-to-all(f32[16,1,640]{2,1,0:T(1,128)S(1)} %copy.24), channel_id=1, replica_groups=mesh['ylo'=2,'z'=8,'x'=4,'core'=2,'yhi'=2] {'x','core','yhi'}, dimensions={0} | all-to-all | bytes 81920 | tf_op jit(solution)/shard_map/all_to_all | solution.py:226
  (114 shorter events, 16.4 us)
Async XLA Ops:
  6.5 28.9 %copy-start = (bf16[64,5120]{1,0:T(8,128)(2,1)S(1)}, bf16[64,5120]{1,0:T(8,128)(2,1)}, u32[]{:S(2)}) copy-start(bf16[64,5120]{1,0:T(8,128)(2,1)} %param.15) | copy-start | bytes 1966084
  6.5 92.2 %all-gather.2.cloned.1.call-start = ((), (), s32[]{:S(2)}) async-start(), calls=%async_computation.3 | async-start | bytes 5898240 | tf_op jit(solution)/shard_map/all_gather | solution.py:52
  7.9 19.3 %collective-permute-start = (bf16[320,896]{1,0:T(8,128)(2,1)S(1)}, bf16[320,896]{1,0:T(8,128)(2,1)}, u32[]{:S(2)}, u32[]{:S(2)}) collective-permute-start(bf16[320,896]{1,0:T(8,128)(2,1)S(1)} %pad_maximum_fusion.2), channel_id=1, source_target_pairs={{0,16},{16,32},{32,48},{48,64},{64,80},{80,96},{96,112},{112,0},{1... | collective-permute-start | bytes 1720328 | tf_op jit(solution)/shard_map/ppermute | solution.py:11
  10.4 16.8 %collective-permute-start.1 = (bf16[320,896]{1,0:T(8,128)(2,1)S(1)}, bf16[320,896]{1,0:T(8,128)(2,1)}, u32[]{:S(2)}, u32[]{:S(2)}) collective-permute-start(bf16[320,896]{1,0:T(8,128)(2,1)S(1)} %pad_maximum_fusion.2), channel_id=1, source_target_pairs={{0,112},{16,0},{32,16},{48,32},{64,48},{80,64},{96,80},{112,96},{1... | collective-permute-start | bytes 1720328 | tf_op jit(solution)/shard_map/ppermute | solution.py:11
  14.4 13.6 %collective-permute-start.2 = (bf16[320,896]{1,0:T(8,128)(2,1)S(1)}, bf16[320,896]{1,0:T(8,128)(2,1)S(1)}, u32[]{:S(2)}, u32[]{:S(2)}) collective-permute-start(bf16[320,896]{1,0:T(8,128)(2,1)S(1)} %pad_maximum_fusion.2), channel_id=1, source_target_pairs={{0,128},{128,0},{1,129},{129,1},{2,130},{130,2},{3,131},{131,3},{4... | collective-permute-start | bytes 1720328 | tf_op jit(solution)/shard_map/ppermute | solution.py:11
  15.7 6.4 %copy-start.10 = (bf16[8,32,896]{2,1,0:T(8,128)(2,1)S(1)}, bf16[8,32,896]{2,1,0:T(8,128)(2,1)}, u32[]{:S(2)}) copy-start(bf16[8,32,896]{2,1,0:T(8,128)(2,1)} %param.12) | copy-start | bytes 1376260
  15.7 6.4 %copy-start.11 = (bf16[8,32,896]{2,1,0:T(8,128)(2,1)S(1)}, bf16[8,32,896]{2,1,0:T(8,128)(2,1)}, u32[]{:S(2)}) copy-start(bf16[8,32,896]{2,1,0:T(8,128)(2,1)} %param.10) | copy-start | bytes 1376260
  24.3 11.1 %copy-start.1 = (bf16[8,64,5120]{2,1,0:T(8,128)(2,1)S(1)}, bf16[8,64,5120]{2,1,0:T(8,128)(2,1)}, u32[]{:S(2)}) copy-start(bf16[8,64,5120]{2,1,0:T(8,128)(2,1)} %pad_maximum_fusion) | copy-start | bytes 15728644
  28.0 9.8 %copy-start.12 = (bf16[320,896]{1,0:T(8,128)(2,1)}, bf16[320,896]{1,0:T(8,128)(2,1)S(1)}, u32[]{:S(2)}) copy-start(bf16[320,896]{1,0:T(8,128)(2,1)S(1)} %collective-permute-done.2) | copy-start | bytes 1720324
  28.0 14.2 %collective-permute-start.3 = (bf16[320,896]{1,0:T(8,128)(2,1)}, bf16[320,896]{1,0:T(8,128)(2,1)}, u32[]{:S(2)}, u32[]{:S(2)}) collective-permute-start(bf16[320,896]{1,0:T(8,128)(2,1)} %collective-permute-done), channel_id=1, source_target_pairs={{0,16},{16,32},{32,48},{48,64},{64,80},{80,96},{96,112},{112,0},{1... | collective-permute-start | bytes 1720328 | tf_op jit(solution)/shard_map/ppermute | solution.py:11
  28.0 14.2 %collective-permute-start.4 = (bf16[320,896]{1,0:T(8,128)(2,1)}, bf16[320,896]{1,0:T(8,128)(2,1)}, u32[]{:S(2)}, u32[]{:S(2)}) collective-permute-start(bf16[320,896]{1,0:T(8,128)(2,1)} %collective-permute-done.1), channel_id=1, source_target_pairs={{0,112},{16,0},{32,16},{48,32},{64,48},{80,64},{96,80},{112,96},{1... | collective-permute-start | bytes 1720328 | tf_op jit(solution)/shard_map/ppermute | solution.py:11
  30.7 15.3 %collective-permute-start.5 = (bf16[1,64,5120]{2,1,0:T(8,128)(2,1)S(1)}, bf16[1,64,5120]{2,1,0:T(8,128)(2,1)S(1)}, u32[]{:S(2)}, u32[]{:S(2)}) collective-permute-start(bf16[1,64,5120]{2,1,0:T(8,128)(2,1)S(1)} %pad_maximum_fusion.1), channel_id=1, source_target_pairs={{0,1},{1,0},{2,3},{3,2},{4,5},{5,4},{6,7},{7,6},{8,9},{9,8},{10,11... | collective-permute-start | bytes 1966088 | tf_op jit(solution)/shard_map/ppermute | solution.py:11
  35.4 2.4 %copy-start.4 = (bf16[8,320,896]{2,1,0:T(8,128)(2,1)}, bf16[8,320,896]{2,1,0:T(8,128)(2,1)S(1)}, u32[]{:S(2)}) copy-start(bf16[8,320,896]{2,1,0:T(8,128)(2,1)S(1)} %bitcast_dynamic-update-slice_fusion.11) | copy-start | bytes 13762564
  42.2 17.6 %copy-start.13 = (bf16[320,896]{1,0:T(8,128)(2,1)S(1)}, bf16[320,896]{1,0:T(8,128)(2,1)}, u32[]{:S(2)}) copy-start(bf16[320,896]{1,0:T(8,128)(2,1)} %copy-done.12) | copy-start | bytes 1720324
  46.0 0.9 copy-start.9
  47.0 12.6 %collective-permute-start.6 = (bf16[320,896]{1,0:T(8,128)(2,1)}, bf16[320,896]{1,0:T(8,128)(2,1)S(1)}, u32[]{:S(2)}, u32[]{:S(2)}) collective-permute-start(bf16[320,896]{1,0:T(8,128)(2,1)} %collective-permute-done.3), channel_id=1, source_target_pairs={{0,16},{16,32},{32,48},{48,64},{64,80},{80,96},{96,112},{112,0},{1... | collective-permute-start | bytes 1720328 | tf_op jit(solution)/shard_map/ppermute | solution.py:11
  47.1 12.7 %collective-permute-start.8 = (bf16[320,896]{1,0:T(8,128)(2,1)}, bf16[320,896]{1,0:T(8,128)(2,1)}, u32[]{:S(2)}, u32[]{:S(2)}) collective-permute-start(bf16[320,896]{1,0:T(8,128)(2,1)} %collective-permute-done.3), channel_id=1, source_target_pairs={{0,128},{128,0},{1,129},{129,1},{2,130},{130,2},{3,131},{131,3},{4... | collective-permute-start | bytes 1720328 | tf_op jit(solution)/shard_map/ppermute | solution.py:11
  48.5 11.3 %collective-permute-start.7 = (bf16[320,896]{1,0:T(8,128)(2,1)}, bf16[320,896]{1,0:T(8,128)(2,1)S(1)}, u32[]{:S(2)}, u32[]{:S(2)}) collective-permute-start(bf16[320,896]{1,0:T(8,128)(2,1)} %collective-permute-done.4), channel_id=1, source_target_pairs={{0,112},{16,0},{32,16},{48,32},{64,48},{80,64},{96,80},{112,96},{1... | collective-permute-start | bytes 1720328 | tf_op jit(solution)/shard_map/ppermute | solution.py:11
  52.9 19.3 %collective-permute-start.14 = (bf16[512,448]{1,0:T(8,128)(2,1)}, bf16[512,448]{1,0:T(8,128)(2,1)S(1)}, u32[]{:S(2)}, u32[]{:S(2)}) collective-permute-start(bf16[512,448]{1,0:T(8,128)(2,1)} %bitcast.91), channel_id=1, source_target_pairs={{0,1},{1,0},{2,3},{3,2},{4,5},{5,4},{6,7},{7,6},{8,9},{9,8},{10,11... | collective-permute-start | bytes 1376264 | tf_op jit(solution)/shard_map/ppermute | solution.py:11
  59.5 5.0 %copy-start.5 = (bf16[8,320,896]{2,1,0:T(8,128)(2,1)S(1)}, bf16[8,320,896]{2,1,0:T(8,128)(2,1)}, u32[]{:S(2)}) copy-start(bf16[8,320,896]{2,1,0:T(8,128)(2,1)} %bitcast_dynamic-update-slice_fusion.9) | copy-start | bytes 13762564
  59.8 20.6 %collective-permute-start.9 = (bf16[320,896]{1,0:T(8,128)(2,1)S(1)}, bf16[320,896]{1,0:T(8,128)(2,1)S(1)}, u32[]{:S(2)}, u32[]{:S(2)}) collective-permute-start(bf16[320,896]{1,0:T(8,128)(2,1)S(1)} %copy-done.13), channel_id=1, source_target_pairs={{0,16},{16,32},{32,48},{48,64},{64,80},{80,96},{96,112},{112,0},{1... | collective-permute-start | bytes 1720328 | tf_op jit(solution)/shard_map/ppermute | solution.py:11
  60.5 19.9 %collective-permute-start.10 = (bf16[320,896]{1,0:T(8,128)(2,1)S(1)}, bf16[320,896]{1,0:T(8,128)(2,1)S(1)}, u32[]{:S(2)}, u32[]{:S(2)}) collective-permute-start(bf16[320,896]{1,0:T(8,128)(2,1)S(1)} %copy-done.13), channel_id=1, source_target_pairs={{0,112},{16,0},{32,16},{48,32},{64,48},{80,64},{96,80},{112,96},{1... | collective-permute-start | bytes 1720328 | tf_op jit(solution)/shard_map/ppermute | solution.py:11
  63.3 18.8 %collective-permute-start.11 = (bf16[320,896]{1,0:T(8,128)(2,1)}, bf16[320,896]{1,0:T(8,128)(2,1)}, u32[]{:S(2)}, u32[]{:S(2)}) collective-permute-start(bf16[320,896]{1,0:T(8,128)(2,1)} %collective-permute-done.4), channel_id=1, source_target_pairs={{0,128},{128,0},{1,129},{129,1},{2,130},{130,2},{3,131},{131,3},{4... | collective-permute-start | bytes 1720328 | tf_op jit(solution)/shard_map/ppermute | solution.py:11
  63.7 12.2 %collective-permute-start.12 = (bf16[160,896]{1,0:T(8,128)(2,1)S(1)}, bf16[160,896]{1,0:T(8,128)(2,1)S(1)}, u32[]{:S(2)}, u32[]{:S(2)}) collective-permute-start(bf16[160,896]{1,0:T(8,128)(2,1)S(1)} %slice.34), channel_id=1, source_target_pairs={{0,16},{16,32},{32,48},{48,64},{64,80},{80,96},{96,112},{112,0},{1... | collective-permute-start | bytes 860168 | tf_op jit(solution)/shard_map/ppermute | solution.py:11
  63.8 27.8 %slice-start = ((s8[5242880]{0:T(1024)(128)(4,1)}), s8[1048576]{0:T(1024)(128)(4,1)S(1)}, s32[]{:S(2)}) async-start(s8[5242880]{0:T(1024)(128)(4,1)} %bitcast.75), calls=%async_computation.4 | async-start | bytes 2097152
  65.7 26.0 %slice-start.1 = ((s8[5242880]{0:T(1024)(128)(4,1)}), s8[4194304]{0:T(1024)(128)(4,1)S(1)}, s32[]{:S(2)}) async-start(s8[5242880]{0:T(1024)(128)(4,1)} %bitcast.75), calls=%async_computation.5 | async-start | bytes 8388608
  72.2 19.4 %copy-start.16 = (bf16[512,448]{1,0:T(8,128)(2,1)}, bf16[512,448]{1,0:T(8,128)(2,1)S(1)}, u32[]{:S(2)}) copy-start(bf16[512,448]{1,0:T(8,128)(2,1)S(1)} %collective-permute-done.14) | copy-start | bytes 1376260
  72.2 8.2 %collective-permute-start.13 = (bf16[160,896]{1,0:T(8,128)(2,1)S(1)}, bf16[160,896]{1,0:T(8,128)(2,1)S(1)}, u32[]{:S(2)}, u32[]{:S(2)}) collective-permute-start(bf16[160,896]{1,0:T(8,128)(2,1)S(1)} %slice.35), channel_id=1, source_target_pairs={{0,112},{16,0},{32,16},{48,32},{64,48},{80,64},{96,80},{112,96},{1... | collective-permute-start | bytes 860168 | tf_op jit(solution)/shard_map/ppermute | solution.py:11
  83.7 24.7 %collective-permute-start.15 = (bf16[320,896]{1,0:T(8,128)(2,1)}, bf16[320,896]{1,0:T(8,128)(2,1)S(1)}, u32[]{:S(2)}, u32[]{:S(2)}) collective-permute-start(bf16[320,896]{1,0:T(8,128)(2,1)} %constant_dynamic-update-slice_fusion), channel_id=1, source_target_pairs={{0,128},{128,0},{1,129},{129,1},{2,130},{130,2},{3,131},{131,3},{4... | collective-permute-start | bytes 1720328 | tf_op jit(solution)/shard_map/ppermute | solution.py:11
  85.0 23.4 %collective-permute-start.16 = (bf16[320,896]{1,0:T(8,128)(2,1)}, bf16[320,896]{1,0:T(8,128)(2,1)S(1)}, u32[]{:S(2)}, u32[]{:S(2)}) collective-permute-start(bf16[320,896]{1,0:T(8,128)(2,1)} %collective-permute-done.8), channel_id=1, source_target_pairs={{0,16},{16,32},{32,48},{48,64},{64,80},{80,96},{96,112},{112,0},{1... | collective-permute-start | bytes 1720328 | tf_op jit(solution)/shard_map/ppermute | solution.py:11
  85.8 22.6 %collective-permute-start.17 = (bf16[320,896]{1,0:T(8,128)(2,1)}, bf16[320,896]{1,0:T(8,128)(2,1)S(1)}, u32[]{:S(2)}, u32[]{:S(2)}) collective-permute-start(bf16[320,896]{1,0:T(8,128)(2,1)} %collective-permute-done.11), channel_id=1, source_target_pairs={{0,112},{16,0},{32,16},{48,32},{64,48},{80,64},{96,80},{112,96},{1... | collective-permute-start | bytes 1720328 | tf_op jit(solution)/shard_map/ppermute | solution.py:11
  90.1 4.5 %copy-start.3 = (bf16[8,320,896]{2,1,0:T(8,128)(2,1)}, bf16[8,320,896]{2,1,0:T(8,128)(2,1)S(1)}, u32[]{:S(2)}) copy-start(bf16[8,320,896]{2,1,0:T(8,128)(2,1)S(1)} %bitcast_dynamic-update-slice_fusion) | copy-start | bytes 13762564
  91.7 2.9 %copy-start.6 = (bf16[8,320,896]{2,1,0:T(8,128)(2,1)}, bf16[8,320,896]{2,1,0:T(8,128)(2,1)S(1)}, u32[]{:S(2)}) copy-start(bf16[8,320,896]{2,1,0:T(8,128)(2,1)S(1)} %bitcast_dynamic-update-slice_fusion.5) | copy-start | bytes 13762564
  98.8 6.1 %copy-start.2 = (bf16[8,64,5120]{2,1,0:T(8,128)(2,1)S(1)}, bf16[8,64,5120]{2,1,0:T(8,128)(2,1)}, u32[]{:S(2)}) copy-start(bf16[8,64,5120]{2,1,0:T(8,128)(2,1)} %all-gather.2.cloned.1.call-done) | copy-start | bytes 15728644
  98.8 6.7 %copy-start.7 = (bf16[8,320,896]{2,1,0:T(8,128)(2,1)S(1)}, bf16[8,320,896]{2,1,0:T(8,128)(2,1)}, u32[]{:S(2)}) copy-start(bf16[8,320,896]{2,1,0:T(8,128)(2,1)} %copy-done.6) | copy-start | bytes 13762564
  109.7 1.0 copy-start.17
  109.7 1.0 copy-start.18
  110.8 0.9 copy-start.19
  111.7 2.2 %copy-start.8 = (f32[512,896]{1,0:T(8,128)S(1)}, f32[512,896]{1,0:T(8,128)}, u32[]{:S(2)}) copy-start(f32[512,896]{1,0:T(8,128)} %fusion.8) | copy-start | bytes 5505028
  113.9 1.0 copy-start.15
  116.0 14.3 %copy-start.14 = (f32[512,64]{0,1:T(8,128)S(1)}, f32[512,64]{0,1:T(8,128)}, u32[]{:S(2)}) copy-start(f32[512,64]{0,1:T(8,128)} %fusion.53) | copy-start | bytes 393220
  118.5 21.1 %all-to-all-start = ((bf16[16,8,1024]{2,1,0:T(8,128)(2,1)}), bf16[16,8,1024]{2,1,0:T(8,128)(2,1)S(1)}, u32[]{:S(2)}, u32[]{:S(2)}) async-start(bf16[16,8,1024]{2,1,0:T(8,128)(2,1)} %bitcast.19), calls=%async_computation | async-start | bytes 524288 | tf_op jit(solution)/shard_map/all_to_all | solution.py:189
  141.3 13.8 %all-to-all-start.1 = ((bf16[16,16,512]{2,1,0:T(8,128)(2,1)}), bf16[16,16,512]{2,1,0:T(8,128)(2,1)S(1)}, u32[]{:S(2)}, u32[]{:S(2)}) async-start(bf16[16,16,512]{2,1,0:T(8,128)(2,1)} %broadcast_in_dim.73), calls=%async_computation.1 | async-start | bytes 524288 | tf_op jit(solution)/shard_map/all_to_all | solution.py:205
Sparse Core Ops, SparseCore 0:
  47.0 41.8 all-gather.1
